TPU v7x, 32 devices: a whole 2x2x4 slice. The times are simulated.
32 devices in a mesh: dp: 8 (over z, x), head: 4 (over y, core).
Axes of the slice: x: 2, y: 2, z: 4, core: 2. Of those that a mesh axis runs over, the one named last changes fastest.
Arguments:
- patches: bfloat16 [12608, 768], P(('dp', 'head'))
- selected: int32 [64, 197], P(('dp', 'head')), may hold values from 0 to 1, as said below
- out_grad: bfloat16 [12608, 768], P(('dp', 'head')), may hold values from -6 to 6
- gain_one: bfloat16 [768], replicated, may hold values from 0.5 to 1.5
- shift_one: bfloat16 [768], replicated, may hold values from -1.5 to 1.5
- router_w: bfloat16 [768], replicated, may hold values from -0.21875 to 0.21875
- w_query: bfloat16 [768, 768], P('dp', 'head'), may hold values from -0.21875 to 0.21875
- b_query: bfloat16 [768], P('head'), may hold values from -1.5 to 1.5
- w_key: bfloat16 [768, 768], P('dp', 'head'), may hold values from -0.21875 to 0.21875
- w_value: bfloat16 [768, 768], P('dp', 'head'), may hold values from -0.21875 to 0.21875
- b_value: bfloat16 [768], P('head'), may hold values from -1.5 to 1.5
- w_out: bfloat16 [768, 768], P('head', 'dp'), may hold values from -0.875 to 0.875
- b_out: bfloat16 [768], replicated, may hold values from -1.5 to 1.5
- gain_two: bfloat16 [768], replicated, may hold values from 0.5 to 1.5
- shift_two: bfloat16 [768], replicated, may hold values from -1.5 to 1.5
- w_up: bfloat16 [768, 3072], P('dp', 'head'), may hold values from -0.21875 to 0.21875
- b_up: bfloat16 [3072], P('head'), may hold values from -1.5 to 1.5
- w_down: bfloat16 [3072, 768], P('head', 'dp'), may hold values from -0.109375 to 0.109375
- b_down: bfloat16 [768], replicated, may hold values from -1.5 to 1.5
Outputs:
- out_tokens: bfloat16 [12608, 768], P(('dp', 'head'))
- grad_patches: bfloat16 [12608, 768], P(('dp', 'head'))
- grad_gain_one: float32 [768], replicated
- grad_shift_one: float32 [768], replicated
- grad_router: float32 [768], replicated
- grad_query: float32 [768, 768], P('dp', 'head')
- grad_query_bias: float32 [768], P('head')
- grad_key: float32 [768, 768], P('dp', 'head')
- grad_value: float32 [768, 768], P('dp', 'head')
- grad_value_bias: float32 [768], P('head')
- grad_out: float32 [768, 768], P('head', 'dp')
- grad_out_bias: float32 [768], replicated
- grad_gain_two: float32 [768], replicated
- grad_shift_two: float32 [768], replicated
- grad_up: float32 [768, 3072], P('dp', 'head')
- grad_up_bias: float32 [3072], P('head')
- grad_down: float32 [3072, 768], P('head', 'dp')
- grad_down_bias: float32 [768], replicated
Inputs may be any that keep to these rules, and one draw needn't show every extreme that they name: Each image has between 40 and 157 selected patches; some image has exactly 40, and all images of some device have 157, so that the most selected patches on one device is 314.
All inputs are finite; a program needn't handle non-finite values.
Results may differ from a plain program's by a relative error of at most 0.013.
Values may be sent and summed in bfloat16 or wider, within the bound.
No kernel may reach another device: no remote copies, remote signals or barrier semaphores. Data moves between devices by JAX's collectives and lax.ppermute only.
A program may use at most 128 MiB of HBM per device.

v0:
```python
from functools import partial
import math

import jax
import jax.numpy as jnp
from jax import lax
from jax.sharding import PartitionSpec as P

HEADS = 12
CAP = 384


epsilon = 1e-06
highest = lax.Precision.HIGHEST


def layer_norm(inputs, gain_vec, shift_vec):
    center = inputs - jnp.mean(inputs, axis=-1, keepdims=True)
    spread = jnp.mean(center * center, axis=-1, keepdims=True)
    return center * lax.rsqrt(spread + epsilon) * gain_vec + shift_vec


def masked_scores(query_block, key_block, seg_blk, score_scale):
    raw_scores = (
        jnp.einsum("jir,jgr->jig", query_block, key_block, preferred_element_type=jnp.float32)
        * score_scale
    )
    return jnp.where(seg_blk[:, :, None] == seg_blk[:, None, :], raw_scores, -1e30)


def head_forward(query_head, key_head, value_head, segment, score_scale):
    sources, slots = segment.shape
    query_block = query_head.reshape(sources, slots, -1)
    key_block = key_head.reshape(sources, slots, -1)
    value_block = value_head.reshape(sources, slots, -1)
    scores = masked_scores(query_block, key_block, segment, score_scale)
    row_max = jnp.max(scores, axis=-1, keepdims=True)
    exp_vals = jnp.exp(scores - row_max)
    row_sum = jnp.sum(exp_vals, axis=-1, keepdims=True)
    probability_lower = (exp_vals / row_sum).astype(jnp.bfloat16)
    context_mix = jnp.einsum(
        "eiw,ewt->eit", probability_lower, value_block, preferred_element_type=jnp.float32
    )
    log_total = (row_max + jnp.log(row_sum))[..., 0]
    return (context_mix.astype(jnp.bfloat16).reshape(query_head.shape), log_total.reshape(-1))


def head_backward(query_head, key_head, value_head, segment, score_scale, log_total, grad_head):
    sources, slots = segment.shape
    query_block = query_head.reshape(sources, slots, -1)
    key_block = key_head.reshape(sources, slots, -1)
    value_block = value_head.reshape(sources, slots, -1)
    gradient_block = grad_head.reshape(sources, slots, -1)
    scores = masked_scores(query_block, key_block, segment, score_scale)
    soft_probs = jnp.exp(scores - log_total.reshape(sources, slots)[:, :, None])
    probability_gradient = jnp.einsum(
        "jir,jgr->jig", gradient_block, value_block, preferred_element_type=jnp.float32
    )
    row_dot = jnp.sum(soft_probs * probability_gradient, axis=-1, keepdims=True)
    score_lower = (soft_probs * (probability_gradient - row_dot) * score_scale).astype(jnp.bfloat16)
    query_gradient = jnp.einsum(
        "eiw,ewt->eit", score_lower, key_block, preferred_element_type=jnp.float32
    )
    key_gradient = jnp.einsum(
        "pzt,pzh->pth", score_lower, query_block, preferred_element_type=jnp.float32
    )
    value_grad = jnp.einsum(
        "pzt,pzh->pth",
        soft_probs.astype(jnp.bfloat16),
        gradient_block,
        preferred_element_type=jnp.float32,
    )
    return (
        query_gradient.reshape(query_head.shape),
        key_gradient.reshape(key_head.shape),
        value_grad.reshape(value_head.shape),
    )


def to_heads(matrix, local_heads):
    return matrix.reshape(matrix.shape[0], local_heads, -1).transpose(1, 0, 2)


def from_heads(stacked):
    return stacked.transpose(1, 0, 2).reshape(stacked.shape[1], -1)


def on_device(
    patches,
    selected,
    out_grad,
    gain_one,
    shift_one,
    router_w,
    w_query,
    b_query,
    w_key,
    w_value,
    b_value,
    w_out,
    b_out,
    gain_two,
    shift_two,
    w_up,
    b_up,
    w_down,
    b_down,
):
    images_here, seq_len = selected.shape
    token_rows, width = patches.shape
    head_pos = lax.axis_index("head")
    local_heads = HEADS // lax.axis_size("head")
    score_scale = 1.0 / math.sqrt(width // HEADS)
    capacity = CAP
    inputs = patches.astype(jnp.float32)
    gain_first = gain_one.astype(jnp.float32)
    shift_first = shift_one.astype(jnp.float32)
    gain_second = gain_two.astype(jnp.float32)
    shift_second = shift_two.astype(jnp.float32)
    router_vec = router_w.astype(jnp.float32)
    up_bias = b_up.astype(jnp.float32)
    normed, norm_pull = jax.vjp(layer_norm, inputs, gain_first, shift_first)
    gate_vals = jax.nn.sigmoid(jnp.dot(normed, router_vec, precision=highest))
    chosen = selected.reshape(token_rows) > 0
    slot_rows = jnp.nonzero(chosen, size=capacity, fill_value=token_rows)[0].astype(jnp.int32)
    slot_live = slot_rows < token_rows
    normed_sel = jnp.concatenate([normed, jnp.zeros((1, width), jnp.float32)], axis=0)[slot_rows]
    gate_sel = jnp.concatenate([gate_vals, jnp.zeros((1,), jnp.float32)], axis=0)[slot_rows]
    picked_rows = normed_sel.astype(jnp.bfloat16)
    image_ids = jnp.where(slot_live, slot_rows // seq_len + head_pos * images_here, -1).astype(
        jnp.bfloat16
    )
    group_rows, group_ids, grad_rows = (
        lax.all_gather(picked_rows, "head", axis=0, tiled=True),
        lax.all_gather(image_ids, "head", axis=0, tiled=True),
        lax.all_gather(out_grad, "head", axis=0, tiled=True),
    )
    group_seg = group_ids.astype(jnp.float32).reshape(-1, capacity)
    query_w, key_w, value_w, proj_w = (
        lax.all_gather(w_query, "dp", axis=0, tiled=True),
        lax.all_gather(w_key, "dp", axis=0, tiled=True),
        lax.all_gather(w_value, "dp", axis=0, tiled=True),
        lax.all_gather(w_out, "dp", axis=1, tiled=True),
    )
    up_w, down_w = (
        lax.all_gather(w_up, "dp", axis=0, tiled=True),
        lax.all_gather(w_down, "dp", axis=1, tiled=True),
    )
    queries = (
        jnp.dot(group_rows, query_w, preferred_element_type=jnp.float32)
        + b_query.astype(jnp.float32)
    ).astype(jnp.bfloat16)
    key_vecs = jnp.dot(group_rows, key_w, preferred_element_type=jnp.float32).astype(jnp.bfloat16)
    value_vecs = (
        jnp.dot(group_rows, value_w, preferred_element_type=jnp.float32)
        + b_value.astype(jnp.float32)
    ).astype(jnp.bfloat16)
    query_heads = to_heads(queries, local_heads)
    key_heads = to_heads(key_vecs, local_heads)
    value_heads = to_heads(value_vecs, local_heads)

    def forward_head(pieces):
        return head_forward(pieces[0], pieces[1], pieces[2], group_seg, score_scale)

    context_heads, log_total = lax.map(forward_head, (query_heads, key_heads, value_heads))
    context_mix = from_heads(context_heads)
    attended = lax.psum_scatter(
        jnp.dot(
            lax.slice_in_dim(context_mix, 0, capacity * lax.axis_size("head"), axis=0),
            proj_w,
            preferred_element_type=jnp.float32,
        ),
        "head",
        scatter_dimension=0,
        tiled=True,
    ) + b_out.astype(jnp.float32)
    branch = gate_sel[:, None] * attended
    mixed_rows = (
        inputs
        + jnp.zeros((token_rows + 1, width), jnp.float32).at[slot_rows].add(branch)[:token_rows]
    )
    normed_two, norm_pull_two = jax.vjp(layer_norm, mixed_rows, gain_second, shift_second)
    mlp_rows = lax.all_gather(normed_two.astype(jnp.bfloat16), "head", axis=0, tiled=True)
    upper_pre = jnp.dot(mlp_rows, up_w, preferred_element_type=jnp.float32) + up_bias
    active = jax.nn.gelu(upper_pre, approximate=False).astype(jnp.bfloat16)
    result = (
        mixed_rows
        + lax.psum_scatter(
            jnp.dot(active, down_w, preferred_element_type=jnp.float32).astype(jnp.bfloat16),
            "head",
            scatter_dimension=0,
            tiled=True,
        ).astype(jnp.float32)
        + b_down.astype(jnp.float32)
    )
    out_tokens = result.astype(jnp.bfloat16)
    grad_top = out_grad.astype(jnp.float32)
    down_bias_grad = jnp.sum(grad_top, axis=0)
    upper_again = jnp.dot(mlp_rows, up_w, preferred_element_type=jnp.float32) + up_bias
    active_again, gelu_pull = jax.vjp(partial(jax.nn.gelu, approximate=False), upper_again)
    down_grad = jnp.einsum(
        "rf,rd->fd",
        active_again.astype(jnp.bfloat16),
        grad_rows,
        preferred_element_type=jnp.float32,
    )
    act_grad = jnp.einsum("rd,fd->rf", grad_rows, down_w, preferred_element_type=jnp.float32)
    (upper_grad,) = gelu_pull(act_grad)
    up_bias_grad = jnp.sum(upper_grad, axis=0)
    upper_low = upper_grad.astype(jnp.bfloat16)
    up_grad = jnp.einsum("rd,rf->df", mlp_rows, upper_low, preferred_element_type=jnp.float32)
    norm_two_grad = lax.psum_scatter(
        jnp.einsum("rf,df->rd", upper_low, up_w, preferred_element_type=jnp.float32),
        "head",
        scatter_dimension=0,
        tiled=True,
    )
    mixed_part, gain_two_grad, shift_two_grad = norm_pull_two(norm_two_grad)
    mixed_grad = grad_top + mixed_part
    grad_sel = jnp.concatenate([mixed_grad, jnp.zeros((1, width), jnp.float32)], axis=0)[slot_rows]
    branch_grad = gate_sel[:, None] * grad_sel
    out_bias_grad = jnp.sum(branch_grad, axis=0)
    logit_grad = jnp.sum(grad_sel * attended, axis=-1) * gate_sel * (1.0 - gate_sel)
    router_grad = jnp.dot(logit_grad, normed_sel, precision=highest)
    group_grad = lax.all_gather(branch_grad.astype(jnp.bfloat16), "head", axis=0, tiled=True)
    proj_grad = jnp.einsum("rc,rd->cd", context_mix, group_grad, preferred_element_type=jnp.float32)
    context_grad = jnp.einsum(
        "rd,cd->rc", group_grad, proj_w, preferred_element_type=jnp.float32
    ).astype(jnp.bfloat16)

    def backward_head(pieces):
        return head_backward(
            pieces[0], pieces[1], pieces[2], group_seg, score_scale, pieces[3], pieces[4]
        )

    query_grads, key_grads, value_grads = lax.map(
        backward_head,
        (query_heads, key_heads, value_heads, log_total, to_heads(context_grad, local_heads)),
    )
    query_full = from_heads(query_grads)
    value_full = from_heads(value_grads)
    query_bias_grad = jnp.sum(query_full, axis=0)
    value_bias_grad = jnp.sum(value_full, axis=0)
    query_low = query_full.astype(jnp.bfloat16)
    key_low = from_heads(key_grads).astype(jnp.bfloat16)
    value_low = value_full.astype(jnp.bfloat16)
    query_wgrad = jnp.einsum("rd,rc->dc", group_rows, query_low, preferred_element_type=jnp.float32)
    key_wgrad = jnp.einsum("rd,rc->dc", group_rows, key_low, preferred_element_type=jnp.float32)
    value_wgrad = jnp.einsum("rd,rc->dc", group_rows, value_low, preferred_element_type=jnp.float32)
    total_rows = jnp.einsum(
        "rc,dc->rd",
        lax.slice_in_dim(query_low, 0, capacity * lax.axis_size("head"), axis=0),
        query_w,
        preferred_element_type=jnp.float32,
    )
    total_rows = total_rows + jnp.einsum(
        "rc,dc->rd",
        lax.slice_in_dim(key_low, 0, capacity * lax.axis_size("head"), axis=0),
        key_w,
        preferred_element_type=jnp.float32,
    )
    picked_grad = lax.psum_scatter(
        (
            total_rows
            + jnp.einsum(
                "rc,dc->rd",
                lax.slice_in_dim(value_low, 0, capacity * lax.axis_size("head"), axis=0),
                value_w,
                preferred_element_type=jnp.float32,
            )
        ).astype(jnp.bfloat16),
        "head",
        scatter_dimension=0,
        tiled=True,
    ).astype(jnp.float32)
    picked_grad = picked_grad + logit_grad[:, None] * router_vec[None, :]
    normed_grad = (
        jnp.zeros((token_rows + 1, width), jnp.float32).at[slot_rows].add(picked_grad)[:token_rows]
    )
    input_part, gain_one_grad, shift_one_grad = norm_pull(normed_grad)
    grad_patches = (mixed_grad + input_part).astype(jnp.bfloat16)
    grad_query, grad_key, grad_value, grad_out, grad_up, grad_down = (
        lax.psum_scatter(query_wgrad, "dp", scatter_dimension=0, tiled=True),
        lax.psum_scatter(key_wgrad, "dp", scatter_dimension=0, tiled=True),
        lax.psum_scatter(value_wgrad, "dp", scatter_dimension=0, tiled=True),
        lax.psum_scatter(proj_grad, "dp", scatter_dimension=1, tiled=True),
        lax.psum_scatter(up_grad, "dp", scatter_dimension=0, tiled=True),
        lax.psum_scatter(down_grad, "dp", scatter_dimension=1, tiled=True),
    )

    def spread_head(vector, total_len):
        return lax.dynamic_update_slice(
            jnp.zeros((total_len,), jnp.float32), vector, (head_pos * vector.shape[0],)
        )

    ff_total = up_bias_grad.shape[0] * lax.axis_size("head")
    summed = lax.psum(
        (
            spread_head(query_bias_grad, width),
            spread_head(value_bias_grad, width),
            spread_head(up_bias_grad, ff_total),
            gain_one_grad,
            shift_one_grad,
            router_grad,
            out_bias_grad,
            gain_two_grad,
            shift_two_grad,
            down_bias_grad,
        ),
        ("dp", "head"),
    )
    head_width = query_bias_grad.shape[0]
    grad_query_bias = lax.dynamic_slice(summed[0], (head_pos * head_width,), (head_width,))
    grad_value_bias = lax.dynamic_slice(summed[1], (head_pos * head_width,), (head_width,))
    grad_up_bias = lax.dynamic_slice(
        summed[2], (head_pos * up_bias_grad.shape[0],), (up_bias_grad.shape[0],)
    )
    return (
        out_tokens,
        grad_patches,
        summed[3],
        summed[4],
        summed[5],
        grad_query,
        grad_query_bias,
        grad_key,
        grad_value,
        grad_value_bias,
        grad_out,
        summed[6],
        summed[7],
        summed[8],
        grad_up,
        grad_up_bias,
        grad_down,
        summed[9],
    )


def solution(mesh):
    placed = (
        P(("dp", "head"), None),
        P(("dp", "head"), None),
        P(("dp", "head"), None),
        P(),
        P(),
        P(),
        P("dp", "head"),
        P("head"),
        P("dp", "head"),
        P("dp", "head"),
        P("head"),
        P("head", "dp"),
        P(),
        P(),
        P(),
        P("dp", "head"),
        P("head"),
        P("head", "dp"),
        P(),
    )
    return jax.shard_map(
        on_device,
        mesh=mesh,
        in_specs=placed,
        out_specs=(
            P(("dp", "head"), None),
            P(("dp", "head"), None),
            P(),
            P(),
            P(),
            P("dp", "head"),
            P("head"),
            P("dp", "head"),
            P("dp", "head"),
            P("head"),
            P("head", "dp"),
            P(),
            P(),
            P(),
            P("dp", "head"),
            P("head"),
            P("head", "dp"),
            P(),
        ),
        check_vma=False,
    )
```

profile of v0, /device:TPU:0, one launch (start us, length us, event | category | flops | bytes accessed | tf_op | source)
XLA Modules:
  0.0 1042.3 jit_solution(12588060105090416432)
XLA Ops:
  25.4 6.1 all-gather
  32.3 32.0 %all_gather.37 = bf16[768,192]{1,0:T(8,128)(2,1)S(1)} all-gather(bf16[96,192]{1,0:T(8,128)(2,1)S(1)} %copy-done.33), channel_id=1, replica_groups=mesh['dp'=8,'head'=4] {'dp'}, dimensions={0}, use_global_device_ids=true | all-gather | bytes 331776 | tf_op jit(solution)/shard_map/all_gather | solution.py:142
  64.3 31.1 %all_gather.35 = bf16[768,192]{1,0:T(8,128)(2,1)S(1)} all-gather(bf16[96,192]{1,0:T(8,128)(2,1)S(1)} %copy-done.34), channel_id=1, replica_groups=mesh['dp'=8,'head'=4] {'dp'}, dimensions={0}, use_global_device_ids=true | all-gather | bytes 331776 | tf_op jit(solution)/shard_map/all_gather | solution.py:140
  95.4 31.2 %all_gather.36 = bf16[768,192]{1,0:T(8,128)(2,1)S(1)} all-gather(bf16[96,192]{1,0:T(8,128)(2,1)S(1)} %copy-done.35), channel_id=1, replica_groups=mesh['dp'=8,'head'=4] {'dp'}, dimensions={0}, use_global_device_ids=true | all-gather | bytes 331776 | tf_op jit(solution)/shard_map/all_gather | solution.py:141
  126.6 33.0 %all_gather.38 = bf16[192,768]{0,1:T(8,128)(2,1)} all-gather(bf16[192,96]{0,1:T(8,128)(2,1)S(1)} %copy.81), channel_id=1, replica_groups=mesh['dp'=8,'head'=4] {'dp'}, dimensions={1}, use_global_device_ids=true | all-gather | bytes 331776 | tf_op jit(solution)/shard_map/all_gather | solution.py:143
  166.0 17.7 %while.28 = (s32[]{:T(128)}, bf16[3,1536,64]{1,2,0:T(8,128)(2,1)}, f32[3,1536]{1,0:T(4,128)}, f32[1536]{0:T(1024)}, bf16[3,1536,64]{1,2,0:T(8,128)(2,1)}, /*inde...) while((s32[]{:T(128)}, bf16[3,1536,64]{1,2,0:T(8,128)(2,1)}, ...), condition=%wide.wide.region_11.12_spmd, body=%wide.wide.region_8.11_spmd.sunk | while | flops 156400128 | bytes 11483761 | solution.py:165
  192.8 44.0 %reduce-scatter.15.cloned.1.call-done = f32[384,768]{1,0:T(8,128)} async-done(((f32[1536,768]{1,0:T(8,128)}), f32[384,768]{1,0:T(8,128)}) %reduce-scatter.15.cloned.1.call-update) | async-done | bytes 1179664 | tf_op jit(solution)/shard_map/reduce_scatter | solution.py:167
  236.8 5.1 scatter_custom_fusion.1
  246.1 17.1 %all-gather.20.cloned.1.call-done = bf16[4,394,768]{2,1,0:T(8,128)(2,1)} async-done(((bf16[1,394,768]{2,1,0:T(8,128)(2,1)}), bf16[4,394,768]{2,1,0:T(8,128)(2,1)}) %all-gather.20.cloned.1.call-update) | async-done | bytes 2420752 | tf_op jit(solution)/shard_map/all_gather | solution.py:136
  266.9 23.0 %all-gather.18.cloned.1.call-done = bf16[4,394,768]{2,1,0:T(8,128)(2,1)} async-done(((bf16[1,394,768]{2,1,0:T(8,128)(2,1)}), bf16[4,394,768]{2,1,0:T(8,128)(2,1)}) %all-gather.18.cloned.1.call-update) | async-done | bytes 2420752 | tf_op jit(solution)/shard_map/all_gather | solution.py:183
  293.6 39.6 %all-gather.12.cloned.1.call-done = bf16[768,768]{1,0:T(8,128)(2,1)} async-done(((bf16[96,768]{1,0:T(8,128)(2,1)}), bf16[768,768]{1,0:T(8,128)(2,1)}) %all-gather.12.cloned.1.call-update) | async-done | bytes 1179664 | tf_op jit(solution)/shard_map/all_gather | solution.py:146
  333.2 6.2 fusion.87
  339.4 35.9 %all-gather.14.cloned.1.call-done = bf16[768,768]{0,1:T(8,128)(2,1)} async-done(((bf16[768,96]{0,1:T(8,128)(2,1)}), bf16[768,768]{0,1:T(8,128)(2,1)}) %all-gather.14.cloned.1.call-update) | async-done | bytes 1179664 | tf_op jit(solution)/shard_map/all_gather | solution.py:147
  375.3 15.7 %fusion.80 = (f32[768]{0:T(1024)}, bf16[1576,768]{1,0:T(8,128)(2,1)S(1)}, f32[1576,768]{1,0:T(8,128)S(1)}) fusion(f32[1576,768]{1,0:T(8,128)} %fusion.87, f32[768]{0:T(1024)S(1)} %convert_element_type.147, bf16[1576,768]{1,0:T(8,128)(2,1)} %reshape.368, bf16[768,768]{0,1:T(8,128)(2,1)} %all-gather.14.cloned.1.call-done), kind=kOutput, calls=%fused_computation.170 | convolution fusion | flops 1948691712 | bytes 15710208 | tf_op jit(solution)/shard_map/rd,fd->rf/dot_general | solution.py:207
  393.4 4.3 fusion.54
  397.7 45.7 %fusion.1 = f32[400,768]{1,0:T(8,128)S(1)} fusion(f32[1576,768]{1,0:T(8,128)} %fusion.54), kind=kCustom, calls=%all-reduce-scatter.1 | all-reduce-scatter fusion | flops 1228801 | bytes 6070784
  443.5 9.5 collective-permute-start.1
  453.0 5.6 convolution_convert_fusion
  458.6 28.4 %fusion = bf16[400,768]{1,0:T(8,128)(2,1)} fusion(bf16[1576,768]{1,0:T(8,128)(2,1)} %convolution_convert_fusion), kind=kCustom, calls=%all-reduce-scatter | all-reduce-scatter fusion | flops 1228801 | bytes 3035648
  490.4 4.9 concatenate.12
  508.1 24.5 %all-gather.16.cloned.1.call-done = bf16[1536,768]{1,0:T(8,128)(2,1)} async-done(((bf16[384,768]{1,0:T(8,128)(2,1)}), bf16[1536,768]{1,0:T(8,128)(2,1)}) %all-gather.16.cloned.1.call-update) | async-done | bytes 2359312 | tf_op jit(solution)/shard_map/all_gather | solution.py:225
  536.1 54.6 %while.29 = (s32[]{:T(128)}, f32[3,1536,64]{1,2,0:T(8,128)}, bf16[3,1536,64]{1,2,0:T(8,128)(2,1)}, f32[3,1536,64]{1,2,0:T(8,128)}, f32[1536]{0:T(1024)}, /*index...) while((s32[]{:T(128)}, f32[3,1536,64]{1,2,0:T(8,128)}, ...), condition=%wide.wide.region_22.23_spmd, body=%wide.wide.region_20.22_spmd.sunk | while | flops 386338560 | bytes 32724216 | solution.py:236
  600.2 6.3 fusion.52
  606.5 6.2 fusion.93
  628.1 29.3 %reduce-scatter.29.cloned.1.call-done = f32[96,192]{1,0:T(8,128)} async-done(((f32[768,192]{1,0:T(8,128)}), f32[96,192]{1,0:T(8,128)}) %reduce-scatter.29.cloned.1.call-update) | async-done | bytes 73744
  659.1 33.0 %reduce-scatter.17.cloned.1.call-done = bf16[384,768]{1,0:T(8,128)(2,1)} async-done(((bf16[1536,768]{1,0:T(8,128)(2,1)}), bf16[384,768]{1,0:T(8,128)(2,1)}) %reduce-scatter.17.cloned.1.call-update) | async-done | bytes 589840 | tf_op jit(solution)/shard_map/reduce_scatter | solution.py:262
  697.4 41.4 %all-reduce.7 = (f32[768]{0:T(1024)}, f32[768]{0:T(1024)}, f32[768]{0:T(1024)}, f32[768]{0:T(1024)S(1)}, f32[768]{0:T(1024)S(1)}, /*index=5*/f32[768]{0:T(1024)}...) all-reduce(f32[768]{0:T(1024)S(1)} %get-tuple-element.117, ...), channel_id=1, replica_groups=mesh['dp'=8,'head'=4] {'dp','head'}, use_global_device_ids=true, to_apply=%region_29.30 | all-reduce | flops 9984 | bytes 79872 | tf_op jit(solution)/shard_map/psum | solution.py:297
  742.0 24.1 %reduce-scatter.25.cloned.1.call-done = f32[96,768]{1,0:T(8,128)} async-done(((f32[768,768]{1,0:T(8,128)}), f32[96,768]{1,0:T(8,128)}) %reduce-scatter.25.cloned.1.call-update) | async-done | bytes 294928 | tf_op jit(solution)/shard_map/reduce_scatter | solution.py:287
  766.1 72.6 %reduce-scatter.27.cloned.1.call-done = f32[768,96]{0,1:T(8,128)} async-done(((f32[768,768]{0,1:T(8,128)}), f32[768,96]{0,1:T(8,128)}) %reduce-scatter.27.cloned.1.call-update) | async-done | bytes 294928 | tf_op jit(solution)/shard_map/reduce_scatter | solution.py:288
  838.7 65.6 %reduce-scatter.19.cloned.1.call-done = f32[96,192]{1,0:T(8,128)} async-done(((f32[768,192]{1,0:T(8,128)}), f32[96,192]{1,0:T(8,128)}) %reduce-scatter.19.cloned.1.call-update) | async-done | bytes 73744 | tf_op jit(solution)/shard_map/reduce_scatter | solution.py:283
  904.3 65.5 %reduce-scatter.23.cloned.1.call-done = f32[96,192]{1,0:T(8,128)} async-done(((f32[768,192]{1,0:T(8,128)}), f32[96,192]{1,0:T(8,128)}) %reduce-scatter.23.cloned.1.call-update) | async-done | bytes 73744 | tf_op jit(solution)/shard_map/reduce_scatter | solution.py:285
  969.8 65.6 %reduce-scatter.21.cloned.1.call-done = f32[96,192]{1,0:T(8,128)} async-done(((f32[768,192]{1,0:T(8,128)}), f32[96,192]{1,0:T(8,128)}) %reduce-scatter.21.cloned.1.call-update) | async-done | bytes 73744 | tf_op jit(solution)/shard_map/reduce_scatter | solution.py:284
  (397 shorter events, 173.4 us)
Async XLA Ops:
  7.2 152.4 %all-gather.10.cloned.1.call-start = ((), (), s32[]{:S(2)}) async-start(), calls=%async_computation.8 | async-start | bytes 2949120 | tf_op jit(solution)/shard_map/all_gather | solution.py:134
  23.6 138.8 %copy-start.8 = (f32[384,768]{1,0:T(8,128)}, f32[384,768]{1,0:T(8,128)S(1)}, u32[]{:S(2)}) copy-start(f32[384,768]{1,0:T(8,128)S(1)} %gather_fusion.1) | copy-start | bytes 3538948
  23.6 40.7 %copy-start.34 = (bf16[96,192]{1,0:T(8,128)(2,1)S(1)}, bf16[96,192]{1,0:T(8,128)(2,1)}, u32[]{:S(2)}) copy-start(bf16[96,192]{1,0:T(8,128)(2,1)} %param.29) | copy-start | bytes 110596
  23.6 71.8 %copy-start.35 = (bf16[96,192]{1,0:T(8,128)(2,1)S(1)}, bf16[96,192]{1,0:T(8,128)(2,1)}, u32[]{:S(2)}) copy-start(bf16[96,192]{1,0:T(8,128)(2,1)} %param.31) | copy-start | bytes 110596
  24.5 212.3 %reduce-scatter.15.cloned.1.call-start = ((), (), s32[]{:S(2)}) async-start(), calls=%async_computation.9 | async-start | bytes 5898240 | tf_op jit(solution)/shard_map/reduce_scatter | solution.py:167
  31.6 130.8 %copy-start.31 = (f32[1536]{0:T(1024)}, f32[1536]{0:T(1024)S(1)}, u32[]{:S(2)}) copy-start(f32[1536]{0:T(1024)S(1)} %reshape.369) | copy-start | bytes 18436
  64.3 99.9 %copy-start.21 = (bf16[768,192]{1,0:T(8,128)(2,1)}, bf16[768,192]{1,0:T(8,128)(2,1)S(1)}, u32[]{:S(2)}) copy-start(bf16[768,192]{1,0:T(8,128)(2,1)S(1)} %all_gather.37) | copy-start | bytes 884740
  95.4 68.8 %copy-start.23 = (bf16[768,192]{1,0:T(8,128)(2,1)}, bf16[768,192]{1,0:T(8,128)(2,1)S(1)}, u32[]{:S(2)}) copy-start(bf16[768,192]{1,0:T(8,128)(2,1)S(1)} %all_gather.35) | copy-start | bytes 884740
  187.9 75.2 %all-gather.20.cloned.1.call-start = ((), (), s32[]{:S(2)}) async-start(), calls=%async_computation.20 | async-start | bytes 3072000 | tf_op jit(solution)/shard_map/all_gather | solution.py:136
  188.7 101.2 %all-gather.18.cloned.1.call-start = ((), (), s32[]{:S(2)}) async-start(), calls=%async_computation.19 | async-start | bytes 3072000 | tf_op jit(solution)/shard_map/all_gather | solution.py:183
  189.8 52.1 %copy-start = (bf16[394,768]{1,0:T(8,128)(2,1)S(1)}, bf16[394,768]{1,0:T(8,128)(2,1)}, u32[]{:S(2)}) copy-start(bf16[394,768]{1,0:T(8,128)(2,1)} %param.23) | copy-start | bytes 1815556
  244.8 88.4 %all-gather.12.cloned.1.call-start = ((), (), s32[]{:S(2)}) async-start(), calls=%async_computation.10 | async-start | bytes 1327104 | tf_op jit(solution)/shard_map/all_gather | solution.py:146
  245.4 129.9 %all-gather.14.cloned.1.call-start = ((), (), s32[]{:S(2)}) async-start(), calls=%async_computation.11 | async-start | bytes 1327104 | tf_op jit(solution)/shard_map/all_gather | solution.py:147
  246.0 286.6 %all-gather.16.cloned.1.call-start = ((), (), s32[]{:S(2)}) async-start(), calls=%async_computation.12 | async-start | bytes 2949120 | tf_op jit(solution)/shard_map/all_gather | solution.py:225
  443.5 51.8 %collective-permute-start.1 = (f32[18,768]{1,0:T(8,128)S(1)}, f32[18,768]{1,0:T(8,128)S(1)}, u32[]{:S(2)}, u32[]{:S(2)}) collective-permute-start(f32[18,768]{1,0:T(8,128)S(1)} %slice.39), channel_id=1, source_target_pairs={{0,1},{1,2},{2,3},{4,5},{5,6},{6,7},{8,9},{9,10},{10,11},{12,13},{... | collective-permute-start | bytes 165896
  487.8 2.6 collective-permute-start
  508.0 149.4 %reduce-scatter.29.cloned.1.call-start = ((), (), s32[]{:S(2)}) async-start(), calls=%async_computation.21 | async-start | bytes 884736
  594.7 97.4 %reduce-scatter.17.cloned.1.call-start = ((), (), s32[]{:S(2)}) async-start(), calls=%async_computation.13 | async-start | bytes 2949120 | tf_op jit(solution)/shard_map/reduce_scatter | solution.py:262
  600.1 165.9 %reduce-scatter.25.cloned.1.call-start = ((), (), s32[]{:S(2)}) async-start(), calls=%async_computation.17 | async-start | bytes 2654208 | tf_op jit(solution)/shard_map/reduce_scatter | solution.py:287
  606.5 232.2 %reduce-scatter.27.cloned.1.call-start = ((), (), s32[]{:S(2)}) async-start(), calls=%async_computation.18 | async-start | bytes 2654208 | tf_op jit(solution)/shard_map/reduce_scatter | solution.py:288
  612.7 291.6 %reduce-scatter.19.cloned.1.call-start = ((), (), s32[]{:S(2)}) async-start(), calls=%async_computation.14 | async-start | bytes 884736 | tf_op jit(solution)/shard_map/reduce_scatter | solution.py:283
  616.2 353.5 %reduce-scatter.23.cloned.1.call-start = ((), (), s32[]{:S(2)}) async-start(), calls=%async_computation.16 | async-start | bytes 884736 | tf_op jit(solution)/shard_map/reduce_scatter | solution.py:285
  619.9 415.5 %reduce-scatter.21.cloned.1.call-start = ((), (), s32[]{:S(2)}) async-start(), calls=%async_computation.15 | async-start | bytes 884736 | tf_op jit(solution)/shard_map/reduce_scatter | solution.py:284
  624.6 67.4 %copy-start.42 = (f32[384]{0:T(512)S(1)}, f32[384]{0:T(512)}, u32[]{:S(2)}) copy-start(f32[384]{0:T(512)} %copy-done.41) | copy-start | bytes 4612
  624.6 67.4 %copy-start.49 = (f32[768]{0:T(1024)S(1)}, f32[768]{0:T(1024)}, u32[]{:S(2)}) copy-start(f32[768]{0:T(1024)} %convert_element_type.166) | copy-start | bytes 9220
  628.1 68.1 %copy-start.1 = (bf16[394,768]{1,0:T(8,128)(2,1)S(1)}, bf16[394,768]{1,0:T(8,128)(2,1)}, u32[]{:S(2)}) copy-start(bf16[394,768]{1,0:T(8,128)(2,1)} %param.23) | copy-start | bytes 1815556
  628.1 68.1 %copy-start.28 = (f32[768]{0:T(1024)S(1)}, f32[768]{0:T(1024)}, u32[]{:S(2)}) copy-start(f32[768]{0:T(1024)} %copy-done.27) | copy-start | bytes 9220
  628.1 68.1 %copy-start.30 = (f32[394]{0:T(512)S(1)}, f32[394]{0:T(512)}, u32[]{:S(2)}) copy-start(f32[394]{0:T(512)} %copy-done.29) | copy-start | bytes 4732
  628.1 68.5 %copy-start.44 = (f32[394]{0:T(512)S(1)}, f32[394]{0:T(512)}, u32[]{:S(2)}) copy-start(f32[394]{0:T(512)} %copy-done.43) | copy-start | bytes 4732
  628.1 68.6 %copy-start.38 = (f32[394]{0:T(512)S(1)}, f32[394]{0:T(512)}, u32[]{:S(2)}) copy-start(f32[394]{0:T(512)} %copy-done.37) | copy-start | bytes 4732
  659.1 38.3 %copy-start.48 = (f32[768]{0:T(1024)S(1)}, f32[768]{0:T(1024)}, u32[]{:S(2)}) copy-start(f32[768]{0:T(1024)} %get-tuple-element.121) | copy-start | bytes 9220
  696.2 44.5 %copy-start.5 = (f32[394,768]{1,0:T(8,128)S(1)}, f32[394,768]{1,0:T(8,128)}, u32[]{:S(2)}) copy-start(f32[394,768]{1,0:T(8,128)} %copy-done.4) | copy-start | bytes 3631108
  (57 other events, 411.4 us)
Sparse Core Ops, SparseCore 0:
  24.7 26.7 all-gather.9
  188.0 48.7 reduce-scatter.14
  238.5 24.6 all-gather.19
  265.2 24.6 all-gather.17
  292.1 41.0 all-gather.11
  335.5 39.8 all-gather.13
  508.1 24.4 all-gather.15
  594.8 62.5 reduce-scatter.28
  660.0 32.0 reduce-scatter.16
  696.4 69.6 reduce-scatter.24
  770.6 68.0 reduce-scatter.26
  842.7 61.4 reduce-scatter.18
  908.2 61.5 reduce-scatter.22
  973.8 61.4 reduce-scatter.20
where the time goes:
time: 1050 us; the launch traced here: 1040 us
  waiting for transfers between devices  542 us (52%)
  blocking collectives  249 us (24%)
  matrix products  110 us (10%)
  local copies, waits for them, and re-layouts  72.9 us (7%)
  other arithmetic  40.3 us (4%)
  between operations  15.8 us (2%)
  starting transfers between devices  12.1 us (1%)
    unnamed x2, blocking collectives  74.1 us
    reduce_scatter x1, waiting for transfers between devices, on_device(): lax.psum_scatter(down_grad, 'dp', scatter_dimension=1, tiled=True)  72.6 us
    reduce_scatter x1, waiting for transfers between devices, on_device(): lax.psum_scatter(query_wgrad, 'dp', scatter_dimension=0, tiled=True)  65.6 us
    reduce_scatter x1, waiting for transfers between devices, on_device(): lax.psum_scatter(key_wgrad, 'dp', scatter_dimension=0, tiled=True)  65.6 us
    reduce_scatter x1, waiting for transfers between devices, on_device(): lax.psum_scatter(value_wgrad, 'dp', scatter_dimension=0, tiled=True)  65.5 us
    reduce_scatter x1, waiting for transfers between devices, on_device(): lax.psum_scatter(jnp.dot(lax.slice_in_dim(context_mix, 0, capacity * lax....  44 us
    psum x1, blocking collectives, on_device(): lax.psum((spread_head(query_bias_grad, width), spread_head(value_bias_gra...  41.4 us
    all_gather x1, waiting for transfers between devices, on_device(): lax.all_gather(w_up, 'dp', axis=0, tiled=True)  39.6 us
  transfers between devices with their start and end apart: 16, of which 13 were waited for; matrix products, arithmetic and copies ran while one was open for 10% of the time, Pallas kernels for 0%

commit v1 on v0

v1 whole, which is shorter than its diff:
```python
import math

import jax
import jax.numpy as jnp
from jax import lax
from jax.experimental import pallas as pl
from jax.experimental.pallas import tpu as pltpu
from jax.sharding import PartitionSpec as P

HEADS = 12
EPS = 1e-06
F32 = jnp.float32
BF16 = jnp.bfloat16
VMEM = pl.BlockSpec(memory_space=pltpu.VMEM)
SMEM = pl.BlockSpec(memory_space=pltpu.SMEM)
ANYS = pl.BlockSpec(memory_space=pl.ANY)
LIMIT = 48 * 1024 * 1024
INV_SQRT2 = 0.7071067811865476
INV_SQRT2PI = 0.3989422804014327

NN = (((1,), (0,)), ((), ()))
NT = (((1,), (1,)), ((), ()))
TN = (((0,), (0,)), ((), ()))


def dot(a, b, dims=NN):
    return lax.dot_general(a, b, dims, preferred_element_type=F32)


def sds(shape, dtype):
    return jax.ShapeDtypeStruct(shape, dtype)


def call(body, outs, ins, scratch=(), flops=0, nbytes=0, trans=0, name=None):
    return pl.pallas_call(
        body,
        out_shape=[o for o, _ in outs],
        in_specs=[s for _, s in ins],
        out_specs=[s for _, s in outs],
        scratch_shapes=list(scratch),
        compiler_params=pltpu.CompilerParams(vmem_limit_bytes=LIMIT),
        cost_estimate=pl.CostEstimate(
            flops=int(flops), bytes_accessed=int(nbytes), transcendentals=int(trans)
        ),
        name=name,
    )(*[a for a, _ in ins])


def norm_parts(v):
    center = v - jnp.mean(v, axis=-1, keepdims=True)
    spread = jnp.mean(center * center, axis=-1, keepdims=True)
    rstd = lax.rsqrt(spread + EPS)
    return center * rstd, rstd


def norm_back(u, xhat, rstd):
    return rstd * (
        u
        - jnp.mean(u, axis=-1, keepdims=True)
        - xhat * jnp.mean(u * xhat, axis=-1, keepdims=True)
    )


class Plan:
    def __init__(self, rows, seq, images, width, hidden, dp, head):
        self.rows, self.seq, self.images, self.width = rows, seq, images, width
        self.dp, self.head = dp, head
        self.pairs = head // 2
        self.cols = width // head
        self.hid = hidden // head
        self.hd = width // HEADS
        self.local_heads = HEADS // head
        self.piece = width // dp
        self.fast = dp == 8 and head == 4 and self.piece % 16 == 0
        self.base = [seq * i // 16 * 16 for i in range(images)]
        self.win = max(-(-(seq * (i + 1) - self.base[i]) // 16) * 16 for i in range(images))
        self.pad = self.base[-1] + self.win
        self.off = self.cols // 128 * 128
        self.lo = self.cols - self.off
        self.nq = 4 * self.cols - self.off
        self.cw = -(-self.cols // 128) * 128
        self.scale = 1.0 / math.sqrt(self.hd)


def source_rows(p, pos_ref, zz, xx):
    z, x = pos_ref[0], pos_ref[1]
    part = ((z - zz) & 3) * 2 + (x ^ xx)
    return pl.multiple_of(part * p.piece, p.piece)


def piece_list(p, pos_ref, other):
    core = pos_ref[2] ^ other
    found = []
    for b3 in range(2):
        for b2 in range(2):
            yy = jnp.where(core == 0, b3, b2)
            xx = jnp.where(core == 0, b2, b3)
            for zz in range(4):
                found.append((b3, b2, zz, yy, source_rows(p, pos_ref, zz, xx)))
    return found


def load_start(p, refs, buf, sem, pos_ref, other):
    if not p.fast:
        copy = pltpu.make_async_copy(refs[0], buf, sem.at[0])
        copy.start()
        return [copy]
    copies = []
    for i, (b3, b2, zz, yy, row) in enumerate(piece_list(p, pos_ref, other)):
        copy = pltpu.make_async_copy(
            refs[b3].at[b2, zz], buf.at[yy, pl.ds(row, p.piece)], sem.at[i]
        )
        copy.start()
        copies.append(copy)
    return copies


def store_start(p, buf, refs, sem, pos_ref, other):
    if not p.fast:
        copy = pltpu.make_async_copy(buf, refs[0], sem.at[0])
        copy.start()
        return [copy]
    copies = []
    for i, (b3, b2, zz, yy, row) in enumerate(piece_list(p, pos_ref, other)):
        copy = pltpu.make_async_copy(
            buf.at[yy, pl.ds(row, p.piece)], refs[b3].at[b2, zz], sem.at[i]
        )
        copy.start()
        copies.append(copy)
    return copies


def wait_all(copies):
    for copy in copies:
        copy.wait()


def piece_shapes(p):
    if p.fast:
        return [sds((2, 4, p.piece, p.width), BF16)] * 2
    return [sds((2, p.width, p.width), BF16)]


def n_sem(p):
    return 16 if p.fast else 1


def entry_kernel(p, patches, out_grad, gain_one, shift_one, router):
    def body(x_ref, og_ref, g_ref, s_ref, r_ref, low_ref, gate_ref, down_ref):
        xhat, _ = norm_parts(x_ref[...].astype(F32))
        normed = xhat * g_ref[...] + s_ref[...]
        low_ref[...] = normed.astype(BF16)
        logit = jnp.sum(normed * r_ref[...], axis=-1, keepdims=True)
        gate_ref[...] = 1.0 / (1.0 + jnp.exp(-logit))
        down_ref[...] = jnp.sum(og_ref[...].astype(F32), axis=0, keepdims=True)

    return call(
        body,
        [
            (sds((p.pad, p.width), BF16), VMEM),
            (sds((p.pad, 1), F32), VMEM),
            (sds((1, p.width), F32), VMEM),
        ],
        [(a, VMEM) for a in (patches, out_grad, gain_one, shift_one, router)],
        flops=p.pad * p.width * 10,
        nbytes=p.pad * p.width * 6,
        name="entry",
    )


def attention_forward(p, pos, weights, other, rows_low, bias, key_mask, carry, tail):
    last = tail is not None
    win, pad, lh, hd = p.win, p.pad, p.local_heads, p.hd

    def body(*refs):
        nw = len(weights)
        pos_ref, w_refs = refs[0], refs[1 : 1 + nw]
        rest = list(refs[1 + nw :])
        low_ref, bias_ref, mask_ref = rest[:3]
        rest = rest[3:]
        carry_ref = None
        if carry is not None:
            carry_ref, rest = rest[0], rest[1:]
        if last:
            x_ref, sg_ref, bo_ref, g2_ref, s2_ref = rest[:5]
            rest = rest[5:]
            qkv_ref, prob_ref, ctx_ref, att_ref, mixed_ref, in_ref = rest[:6]
            rest = rest[6:]
        else:
            qkv_ref, prob_ref, ctx_ref, att_ref = rest[:4]
            rest = rest[4:]
        wbuf, ctx, sem = rest
        wait_all(load_start(p, w_refs, wbuf, sem, pos_ref, other))
        low = low_ref[...]
        total = None
        for b in range(2):
            qkv = dot(low, wbuf[b, :, p.off :]) + bias_ref[b]
            qkv_ref[b] = qkv.astype(BF16)
            ctx[...] = jnp.zeros((pad, p.cw), F32)
            for img in range(p.images):
                first = p.base[img]
                at = lax.broadcasted_iota(jnp.int32, (win, 1), 0) + first
                valid = (at >= p.seq * img) & (at < p.seq * (img + 1))
                seen = mask_ref[img] > 0.0
                got = []
                for j in range(lh):
                    qs = p.lo + hd * j
                    q = qkv_ref[b, first : first + win, qs : qs + hd]
                    k = qkv_ref[b, first : first + win, qs + p.cols : qs + p.cols + hd]
                    v = qkv_ref[b, first : first + win, qs + 2 * p.cols : qs + 2 * p.cols + hd]
                    s = dot(q, k, NT) * p.scale
                    s = jnp.where(seen, s, -1e30)
                    e = jnp.exp(s - jnp.max(s, axis=-1, keepdims=True))
                    prob = e * (1.0 / jnp.sum(e, axis=-1, keepdims=True))
                    prob = jnp.where(valid, prob, 0.0).astype(BF16)
                    prob_ref[(b * p.images + img) * lh + j] = prob
                    got.append(dot(prob, v))
                if p.cw > p.cols:
                    got.append(jnp.zeros((win, p.cw - p.cols), F32))
                ctx[first : first + win, :] += jnp.concatenate(got, axis=1)
            mix = ctx[...].astype(BF16)
            ctx_ref[b] = mix
            part = dot(mix, wbuf[b, :, : p.cw], NT)
            total = part if total is None else total + part
        if carry_ref is not None:
            total = total + carry_ref[...]
        if not last:
            att_ref[...] = total
            return
        attended = total + bo_ref[...]
        att_ref[...] = attended
        mixed = x_ref[...].astype(F32) + sg_ref[...] * attended
        mixed_ref[...] = mixed
        xhat, _ = norm_parts(mixed)
        in_ref[...] = (xhat * g2_ref[...] + s2_ref[...]).astype(BF16)

    ins = [(pos, SMEM)] + [(w, ANYS) for w in weights]
    ins += [(a, VMEM) for a in (rows_low, bias, key_mask)]
    if carry is not None:
        ins.append((carry, VMEM))
    if last:
        ins += [(a, VMEM) for a in tail]
    outs = [
        (sds((2, pad, p.nq), BF16), VMEM),
        (sds((2 * p.images * lh, win, win), BF16), VMEM),
        (sds((2, pad, p.cw), BF16), VMEM),
        (sds((pad, p.width), F32), VMEM),
    ]
    if last:
        outs += [(sds((pad, p.width), F32), VMEM), (sds((pad, p.width), BF16), VMEM)]
    return call(
        body,
        outs,
        ins,
        [
            pltpu.VMEM((2, p.width, 4 * p.cols), BF16),
            pltpu.VMEM((pad, p.cw), F32),
            pltpu.SemaphoreType.DMA((n_sem(p),)),
        ],
        flops=2 * (2 * pad * p.width * (p.nq + p.cw) + p.images * lh * win * win * hd * 4),
        nbytes=2 * 2 * p.width * p.width + pad * p.width * 10,
        trans=2 * p.images * lh * win * win,
        name="attn_fwd",
    )


def up_kernel(p, pos, weights, other, mlp_in, bias):
    def body(*refs):
        nw = len(weights)
        pos_ref, w_refs = refs[0], refs[1 : 1 + nw]
        in_ref, b_ref, act_ref, slope_ref, wbuf, sem = refs[1 + nw :]
        wait_all(load_start(p, w_refs, wbuf, sem, pos_ref, other))
        rows = in_ref[...]
        for b in range(2):
            pre = dot(rows, wbuf[b]) + b_ref[b]
            phi = 0.5 * (1.0 + lax.erf(pre * INV_SQRT2))
            act_ref[b] = (pre * phi).astype(BF16)
            slope_ref[b] = (phi + pre * (jnp.exp(-0.5 * pre * pre) * INV_SQRT2PI)).astype(BF16)

    return call(
        body,
        [(sds((2, p.pad, p.hid), BF16), VMEM)] * 2,
        [(pos, SMEM)] + [(w, ANYS) for w in weights] + [(mlp_in, VMEM), (bias, VMEM)],
        [pltpu.VMEM((2, p.width, p.hid), BF16), pltpu.SemaphoreType.DMA((n_sem(p),))],
        flops=2 * 2 * p.pad * p.width * p.hid,
        nbytes=4 * p.width * p.hid + 10 * p.pad * p.hid,
        trans=2 * p.pad * p.hid * 2,
        name="up",
    )


def weight_grad(p, pos, other, lhs, rhs, received, name):
    def body(*refs):
        pos_ref, l_ref, r_ref = refs[:3]
        rest = list(refs[3:])
        nr = len(received) if received is not None else 0
        got_refs, rest = rest[:nr], rest[nr:]
        no = len(piece_shapes(p))
        out_refs, rest = rest[:no], rest[no:]
        if nr:
            gbuf, rbuf, sem, rsem = rest
            loads = load_start(p, got_refs, rbuf, rsem, pos_ref, other)
        else:
            gbuf, sem = rest
        left = l_ref[...]
        for b in range(2):
            g = dot(left, r_ref[b], TN)
            if nr:
                if b == 0:
                    wait_all(loads)
                g = g + rbuf[b].astype(F32)
            gbuf[b] = g.astype(BF16)
        wait_all(store_start(p, gbuf, out_refs, sem, pos_ref, other))

    scratch = [pltpu.VMEM((2, p.width, p.hid), BF16)]
    if received is not None:
        scratch.append(pltpu.VMEM((2, p.width, p.hid), BF16))
    scratch.append(pltpu.SemaphoreType.DMA((n_sem(p),)))
    if received is not None:
        scratch.append(pltpu.SemaphoreType.DMA((n_sem(p),)))
    return call(
        body,
        [(s, ANYS) for s in piece_shapes(p)],
        [(pos, SMEM), (lhs, VMEM), (rhs, VMEM)] + [(r, ANYS) for r in received or ()],
        scratch,
        flops=2 * 2 * p.pad * p.width * p.hid,
        nbytes=8 * p.width * p.hid + 6 * p.pad * p.hid,
        name=name,
    )


def down_kernel(p, pos, w_up, w_down, other, active, slope, out_grad, carry):
    def body(*refs):
        nw = len(w_up)
        pos_ref, u_refs, d_refs = refs[0], refs[1 : 1 + nw], refs[1 + nw : 1 + 2 * nw]
        act_ref, slope_ref, og_ref = refs[1 + 2 * nw : 4 + 2 * nw]
        rest = list(refs[4 + 2 * nw :])
        if carry is not None:
            out_in, back_in = rest[:2]
            rest = rest[2:]
        out_ref, back_ref, low_ref, bias_ref, ubuf, dbuf, usem, dsem = rest
        d_copies = load_start(p, d_refs, dbuf, dsem, pos_ref, other)
        u_copies = load_start(p, u_refs, ubuf, usem, pos_ref, other)
        wait_all(d_copies)
        og = og_ref[...]
        for b in range(2):
            grad = dot(og, dbuf[b]) * slope_ref[b].astype(F32)
            bias_ref[b] = jnp.sum(grad, axis=0, keepdims=True)
            low = grad.astype(BF16)
            low_ref[b] = low
            if b == 0:
                wait_all(u_copies)
            back = dot(low, ubuf[b], NT)
            out = dot(act_ref[b], dbuf[b], NT)
            if b == 0 and carry is not None:
                back_ref[...] = back_in[...] + back
                out_ref[...] = out_in[...] + out
            elif b == 0:
                back_ref[...] = back
                out_ref[...] = out
            else:
                back_ref[...] += back
                out_ref[...] += out

    ins = [(pos, SMEM)] + [(w, ANYS) for w in tuple(w_up) + tuple(w_down)]
    ins += [(a, VMEM) for a in (active, slope, out_grad)]
    if carry is not None:
        ins += [(a, VMEM) for a in carry]
    return call(
        body,
        [
            (sds((p.pad, p.width), F32), VMEM),
            (sds((p.pad, p.width), F32), VMEM),
            (sds((2, p.pad, p.hid), BF16), VMEM),
            (sds((2, 1, p.hid), F32), VMEM),
        ],
        ins,
        [
            pltpu.VMEM((2, p.width, p.hid), BF16),
            pltpu.VMEM((2, p.width, p.hid), BF16),
            pltpu.SemaphoreType.DMA((n_sem(p),)),
            pltpu.SemaphoreType.DMA((n_sem(p),)),
        ],
        flops=2 * 2 * p.pad * p.width * p.hid * 3,
        nbytes=8 * p.width * p.hid + 12 * p.pad * p.hid + 16 * p.pad * p.width,
        name="down",
    )


def middle_kernel(p, patches, out_grad, mixed, out_sum, back_sum, attended, gate, sel, vecs):
    gain_one, shift_one, gain_two, b_down = vecs

    def body(
        x_ref, og_ref, mix_ref, out_ref, back_ref, att_ref, gate_ref, sel_ref,
        g1_ref, s1_ref, g2_ref, bd_ref,
        tok_ref, mg_ref, br_ref, logit_ref, gg_ref, gs_ref, gb_ref, gr_ref,
    ):
        mixed = mix_ref[...]
        tok_ref[...] = (mixed + out_ref[...] + bd_ref[...])[: p.rows].astype(BF16)
        xhat, rstd = norm_parts(mixed)
        back = back_ref[...]
        gg_ref[...] = jnp.sum(back * xhat, axis=0, keepdims=True)
        gs_ref[...] = jnp.sum(back, axis=0, keepdims=True)
        mg = og_ref[...].astype(F32) + norm_back(back * g2_ref[...], xhat, rstd)
        mg_ref[...] = mg
        gate, sel = gate_ref[...], sel_ref[...]
        branch = (gate * sel) * mg
        gb_ref[...] = jnp.sum(branch, axis=0, keepdims=True)
        br_ref[...] = branch.astype(BF16)
        logit = sel * jnp.sum(mg * att_ref[...], axis=-1, keepdims=True) * gate * (1.0 - gate)
        logit_ref[...] = logit
        first, _ = norm_parts(x_ref[...].astype(F32))
        normed = first * g1_ref[...] + s1_ref[...]
        gr_ref[...] = jnp.sum(normed * logit, axis=0, keepdims=True)

    vec = (sds((1, p.width), F32), VMEM)
    return call(
        body,
        [
            (sds((p.rows, p.width), BF16), VMEM),
            (sds((p.pad, p.width), F32), VMEM),
            (sds((p.pad, p.width), BF16), VMEM),
            (sds((p.pad, 1), F32), VMEM),
            vec, vec, vec, vec,
        ],
        [
            (a, VMEM)
            for a in (
                patches, out_grad, mixed, out_sum, back_sum, attended, gate, sel,
                gain_one, shift_one, gain_two, b_down,
            )
        ],
        flops=p.pad * p.width * 30,
        nbytes=p.pad * p.width * 28,
        name="middle",
    )


def attention_backward(p, pos, weights, other, branch, rows_low, qkv, probs, ctx, received, carry):
    win, pad, lh, hd, cols = p.win, p.pad, p.local_heads, p.hd, p.cols

    def body(*refs):
        nw = len(weights)
        pos_ref, w_refs = refs[0], refs[1 : 1 + nw]
        br_ref, low_ref, qkv_ref, prob_ref, ctx_ref = refs[1 + nw : 6 + nw]
        rest = list(refs[6 + nw :])
        nr = len(received) if received is not None else 0
        got_refs, rest = rest[:nr], rest[nr:]
        if carry is not None:
            carry_ref, rest = rest[0], rest[1:]
        no = len(piece_shapes(p))
        out_refs, rest = rest[:no], rest[no:]
        n1_ref, bias_ref, wbuf, gbuf, gq, dc, wsem, sem = rest[:8]
        loads = load_start(p, w_refs, wbuf, wsem, pos_ref, other)
        if nr:
            rbuf, rsem = rest[8:]
            got = load_start(p, got_refs, rbuf, rsem, pos_ref, other)
        wait_all(loads)
        branch_low, low = br_ref[...], low_ref[...]
        total = None
        for b in range(2):
            dc[...] = dot(branch_low, wbuf[b, :, : p.cw]).astype(BF16)
            gq[...] = jnp.zeros((pad, p.nq), F32)
            for img in range(p.images):
                first = p.base[img]
                here = slice(first, first + win)
                dqs, dks, dvs = [], [], []
                for j in range(lh):
                    qs = p.lo + hd * j
                    q = qkv_ref[b, here, qs : qs + hd]
                    k = qkv_ref[b, here, qs + cols : qs + cols + hd]
                    v = qkv_ref[b, here, qs + 2 * cols : qs + 2 * cols + hd]
                    d = dc[here, hd * j : hd * j + hd]
                    prob = prob_ref[(b * p.images + img) * lh + j]
                    soft = prob.astype(F32)
                    pg = dot(d, v, NT)
                    row = jnp.sum(soft * pg, axis=-1, keepdims=True)
                    s = (soft * (pg - row) * p.scale).astype(BF16)
                    dqs.append(dot(s, k))
                    dks.append(dot(s, q, TN))
                    dvs.append(dot(prob, d, TN))
                lead = [jnp.zeros((win, p.lo), F32)] if p.lo else []
                gq[here, :] += jnp.concatenate(lead + dqs + dks + dvs, axis=1)
            full = gq[...]
            bias_ref[b] = jnp.sum(full, axis=0, keepdims=True)
            gl = full.astype(BF16)
            part = dot(gl, wbuf[b, :, p.off :], NT)
            total = part if total is None else total + part
            g_out = dot(branch_low, ctx_ref[b], TN)
            g_qkv = dot(low, gl, TN)
            g = jnp.concatenate(
                [
                    g_out[:, : p.off],
                    g_out[:, p.off : p.cw] + g_qkv[:, : p.cw - p.off],
                    g_qkv[:, p.cw - p.off :],
                ],
                axis=1,
            )
            if nr:
                if b == 0:
                    wait_all(got)
                g = g + rbuf[b].astype(F32)
            gbuf[b] = g.astype(BF16)
        if carry is not None:
            total = total + carry_ref[...]
        n1_ref[...] = total
        wait_all(store_start(p, gbuf, out_refs, sem, pos_ref, other))

    ins = [(pos, SMEM)] + [(w, ANYS) for w in weights]
    ins += [(a, VMEM) for a in (branch, rows_low, qkv, probs, ctx)]
    ins += [(r, ANYS) for r in received or ()]
    if carry is not None:
        ins.append((carry, VMEM))
    scratch = [
        pltpu.VMEM((2, p.width, 4 * cols), BF16),
        pltpu.VMEM((2, p.width, 4 * cols), BF16),
        pltpu.VMEM((pad, p.nq), F32),
        pltpu.VMEM((pad, p.cw), BF16),
        pltpu.SemaphoreType.DMA((n_sem(p),)),
        pltpu.SemaphoreType.DMA((n_sem(p),)),
    ]
    if received is not None:
        scratch += [
            pltpu.VMEM((2, p.width, 4 * cols), BF16),
            pltpu.SemaphoreType.DMA((n_sem(p),)),
        ]
    return call(
        body,
        [(s, ANYS) for s in piece_shapes(p)]
        + [(sds((pad, p.width), F32), VMEM), (sds((2, 1, p.nq), F32), VMEM)],
        ins,
        scratch,
        flops=2 * 2 * pad * p.width * 2 * (p.nq + p.cw) + 2 * p.images * lh * win * win * hd * 8,
        nbytes=12 * p.width * p.width + pad * p.width * 20,
        name="attn_bwd",
    )


def exit_kernel(p, patches, back, logit, router, gain_one, mixed_grad):
    def body(x_ref, n_ref, l_ref, r_ref, g_ref, mg_ref, out_ref, gg_ref, gs_ref):
        xhat, rstd = norm_parts(x_ref[...].astype(F32))
        grad = n_ref[...] + l_ref[...] * r_ref[...]
        gg_ref[...] = jnp.sum(grad * xhat, axis=0, keepdims=True)
        gs_ref[...] = jnp.sum(grad, axis=0, keepdims=True)
        total = mg_ref[...] + norm_back(grad * g_ref[...], xhat, rstd)
        out_ref[...] = total[: p.rows].astype(BF16)

    vec = (sds((1, p.width), F32), VMEM)
    return call(
        body,
        [(sds((p.rows, p.width), BF16), VMEM), vec, vec],
        [(a, VMEM) for a in (patches, back, logit, router, gain_one, mixed_grad)],
        flops=p.pad * p.width * 20,
        nbytes=p.pad * p.width * 12,
        name="exit",
    )


def flat(z, x, y, c):
    return ((z * 2 + x) * 2 + y) * 2 + c


def table(move):
    pairs = []
    for z in range(4):
        for x in range(2):
            for y in range(2):
                for c in range(2):
                    pairs.append((flat(z, x, y, c), flat(*move(z, x, y, c))))
    return pairs


def send(v, move):
    return lax.ppermute(v, ("dp", "head"), table(move))


def along_z(shift):
    return lambda z, x, y, c: ((z + shift) % 4, x, y, c)


def near(z, x, y, c):
    return (z, x ^ 1, y, c) if c == 0 else (z, x, y ^ 1, c)


def far(z, x, y, c):
    return (z, x, y ^ 1, c) if c == 0 else (z, x ^ 1, y, c)


def core(z, x, y, c):
    return (z, x, y, c ^ 1)


def add(a, b):
    return (a.astype(F32) + b.astype(F32)).astype(BF16)


def gather_pieces(p, shard):
    if not p.fast:
        full = lax.all_gather(lax.all_gather(shard, "dp", axis=0, tiled=True), "head", axis=0)
        return [(full[2 * i : 2 * i + 2],) for i in range(p.pairs)]
    own = jnp.stack([shard] + [send(shard, along_z(s)) for s in (1, 2, 3)])
    eight = jnp.stack([own, send(own, near)])
    rest = send(eight, far)
    return [(eight, rest), (send(eight, core), send(rest, core))]


def scatter_pieces(p, grads):
    if not p.fast:
        stacked = jnp.concatenate(grads, axis=0)
        part = lax.psum_scatter(stacked, "head", scatter_dimension=0, tiled=False)
        return lax.psum_scatter(part, "dp", scatter_dimension=0, tiled=True).astype(F32)
    keep, away = grads
    got = send(away, far)
    other = add(keep[1], got[1])
    mine = keep[0]
    got2 = send(other, near)
    pieces = [add(add(mine[s], got[0, s]), got2[s]) for s in range(4)]
    total = pieces[0].astype(F32)
    for s in (1, 2, 3):
        total = total + send(pieces[s], along_z(-s)).astype(F32)
    return total


def gather_head(p, vector):
    if not p.fast:
        return lax.all_gather(vector, "head", axis=0)
    pair = jnp.stack([vector, send(vector, lambda z, x, y, c: (z, x, y ^ 1, c))])
    return jnp.concatenate([pair, send(pair, core)], axis=0)


def sum_vectors(p, common, owned):
    n = common.shape[0]
    if not p.fast:
        total = lax.psum(common, ("dp", "head"))
        mine = lax.psum_scatter(owned, "head", scatter_dimension=0, tiled=False)
        return total, lax.psum(mine, "dp")
    got = send(jnp.concatenate([common, owned[2], owned[3]]), core)
    m = owned.shape[1]
    vec = jnp.concatenate([common, owned[0], owned[1]]) + got
    keep = vec[: n + m]
    got = send(jnp.concatenate([vec[:n], vec[n + m :]]), lambda z, x, y, c: (z, x, y ^ 1, c))
    keep = keep + got
    keep = keep + send(keep, lambda z, x, y, c: (z, x ^ 1, y, c))
    keep = keep + send(keep, lambda z, x, y, c: (z ^ 1, x, y, c))
    keep = keep + send(keep, lambda z, x, y, c: (z ^ 2, x, y, c))
    return keep[:n], keep[n:]


def on_device(
    patches, selected, out_grad, gain_one, shift_one, router_w, w_query, b_query, w_key, w_value,
    b_value, w_out, b_out, gain_two, shift_two, w_up, b_up, w_down, b_down,
):
    images, seq = selected.shape
    rows, width = patches.shape
    dp, head = lax.axis_size("dp"), lax.axis_size("head")
    p = Plan(rows, seq, images, width, b_up.shape[0] * head, dp, head)
    cols, hid = p.cols, p.hid

    dp_pos, head_pos = lax.axis_index("dp"), lax.axis_index("head")
    pos = jnp.stack([dp_pos // 2, dp_pos % 2, head_pos % 2]).astype(jnp.int32)

    attn_shard = jnp.concatenate([w_out.T, w_query, w_key, w_value], axis=1)
    attn_w = gather_pieces(p, attn_shard)
    up_w = gather_pieces(p, w_up)
    down_w = gather_pieces(p, w_down.T)
    biases = gather_head(p, jnp.concatenate([b_query, b_value, b_up])).astype(F32)
    zeros = jnp.zeros((head, cols), F32)
    qkv_bias = jnp.concatenate(
        [zeros[:, : p.lo], biases[:, :cols], zeros, biases[:, cols : 2 * cols]], axis=1
    )[:, None, :]
    up_bias = biases[:, 2 * cols :][:, None, :]

    def row(v):
        return v.astype(F32)[None, :]

    more = p.pad - rows
    x_pad = jnp.pad(patches, ((0, more), (0, 0)))
    og_pad = jnp.pad(out_grad, ((0, more), (0, 0)))
    sel = selected.astype(F32)
    sel_col = jnp.pad(sel.reshape(rows, 1), ((0, more), (0, 0)))
    key_mask = jnp.stack(
        [
            jnp.pad(sel[i], (seq * i - p.base[i], p.win - seq - (seq * i - p.base[i])))
            for i in range(images)
        ]
    )[:, None, :]
    gain_one, shift_one, gain_two, shift_two = map(row, (gain_one, shift_one, gain_two, shift_two))
    router, b_out, b_down = row(router_w), row(b_out), row(b_down)

    rows_low, gate, g_down_bias = entry_kernel(p, x_pad, og_pad, gain_one, shift_one, router)
    sel_gate = gate * sel_col

    qkvs, probs, ctxs, carry = [], [], [], None
    for i in range(p.pairs):
        tail = (x_pad, sel_gate, b_out, gain_two, shift_two) if i == p.pairs - 1 else None
        got = attention_forward(
            p, pos, attn_w[i], i, rows_low, qkv_bias[2 * i : 2 * i + 2], key_mask, carry, tail
        )
        qkvs.append(got[0])
        probs.append(got[1])
        ctxs.append(got[2])
        carry = got[3]
    attended, mixed, mlp_in = got[3], got[4], got[5]

    acts, slopes = [], []
    for i in range(p.pairs):
        act, slope = up_kernel(p, pos, up_w[i], i, mlp_in, up_bias[2 * i : 2 * i + 2])
        acts.append(act)
        slopes.append(slope)

    def reduced(lhs, rhs, name):
        if not p.fast:
            blocks = [weight_grad(p, pos, 0, lhs, r, None, name)[0] for r in rhs]
            return scatter_pieces(p, blocks)
        other = weight_grad(p, pos, 1, lhs, rhs[1], None, name)
        got = [send(o, core) for o in other]
        return scatter_pieces(p, weight_grad(p, pos, 0, lhs, rhs[0], got, name))

    grad_down = reduced(og_pad, acts, "grad_down")

    carry, lows, up_sums = None, [], []
    for i in range(p.pairs):
        got = down_kernel(p, pos, up_w[i], down_w[i], i, acts[i], slopes[i], og_pad, carry)
        carry = (got[0], got[1])
        lows.append(got[2])
        up_sums.append(got[3][:, 0])
    grad_up = reduced(mlp_in, lows, "grad_up")

    tokens, mixed_grad, branch, logit, g_gain2, g_shift2, g_out_bias, g_router = middle_kernel(
        p, x_pad, og_pad, mixed, carry[0], carry[1], attended, gate, sel_col,
        (gain_one, shift_one, gain_two, b_down),
    )

    carry, blocks, sums, received = None, [None] * p.pairs, [None] * p.pairs, None
    for i in reversed(range(p.pairs)):
        got = attention_backward(
            p, pos, attn_w[i], i if p.fast else 0, branch, rows_low, qkvs[i], probs[i], ctxs[i],
            received, carry,
        )
        pieces, carry, sums[i] = got[:-2], got[-2], got[-1][:, 0]
        blocks[i] = pieces
        if p.fast and i == 1:
            received = [send(o, core) for o in pieces]
    grad_attn = scatter_pieces(p, blocks[0] if p.fast else [b[0] for b in blocks])
    grad_patches, g_gain1, g_shift1 = exit_kernel(
        p, x_pad, carry, logit, router, gain_one, mixed_grad
    )

    qkv_sums = jnp.concatenate(sums, axis=0)
    owned = jnp.concatenate(
        [
            qkv_sums[:, p.lo : p.lo + cols],
            qkv_sums[:, p.lo + 2 * cols :],
            jnp.concatenate(up_sums, axis=0),
        ],
        axis=1,
    )
    common = jnp.concatenate(
        [g_gain1, g_shift1, g_router, g_out_bias, g_gain2, g_shift2, g_down_bias], axis=1
    )[0]
    common, owned = sum_vectors(p, common, owned)
    vecs = [common[i * width : (i + 1) * width] for i in range(7)]
    return (
        tokens,
        grad_patches,
        vecs[0],
        vecs[1],
        vecs[2],
        grad_attn[:, cols : 2 * cols],
        owned[:cols],
        grad_attn[:, 2 * cols : 3 * cols],
        grad_attn[:, 3 * cols :],
        owned[cols : 2 * cols],
        grad_attn[:, :cols].T,
        vecs[3],
        vecs[4],
        vecs[5],
        grad_up,
        owned[2 * cols :],
        grad_down.T,
        vecs[6],
    )


def solution(mesh):
    rows, rep = P(("dp", "head"), None), P()
    split, side, turned = P("dp", "head"), P("head"), P("head", "dp")
    return jax.shard_map(
        on_device,
        mesh=mesh,
        in_specs=(
            rows, rows, rows, rep, rep, rep, split, side, split, split, side, turned, rep, rep,
            rep, split, side, turned, rep,
        ),
        out_specs=(
            rows, rows, rep, rep, rep, split, side, split, split, side, turned, rep, rep, rep,
            split, side, turned, rep,
        ),
        check_vma=False,
    )
```

time: 1050 us -> 336 us (0.32)
  waiting for transfers between devices: 542 us -> 104 us
  blocking collectives: 249 us -> 0 us
  Pallas kernels: 0 us -> 117 us
  matrix products: 110 us -> 0 us
  starting transfers between devices: 12.1 us -> 65.8 us
  local copies, waits for them, and re-layouts: 72.9 us -> 27.6 us
  other arithmetic: 40.3 us -> 15.2 us
  between operations: 15.8 us -> 1.57 us
    reduce_scatter x7 -> x0, waiting for transfers between devices: 370 us -> none  [the longest x1 72.6 us: on_device(): lax.psum_scatter(down_grad, 'dp', scatter_dimension=1, tiled=True)]
    all_gather x6 -> x0, waiting for transfers between devices: 140 us -> none  [the longest x1 39.6 us: on_device(): lax.all_gather(w_up, 'dp', axis=0, tiled=True)]
    all_gather x5 -> x0, blocking collectives: 133 us -> none  [the longest x1 33 us: on_device(): lax.all_gather(w_out, 'dp', axis=1, tiled=True)]
    pallas_call x0 -> x15, Pallas kernels: none -> 117 us  [call(): pl.pallas_call(body, out_shape=[o for o, _ in outs], in_specs=[s for _, s...]
    dot_general x40 -> x0, matrix products: 106 us -> none  [the longest x1 15.7 us: on_device(): jnp.einsum('rd,fd->rf', grad_rows, down_w, preferred_element_type=jnp.flo...]
    ppermute x0 -> x49, waiting for transfers between devices: none -> 104 us  [send(): return lax.ppermute(v, ('dp', 'head'), table(move))]
    unnamed x2 -> x0, blocking collectives: 74.1 us -> none
    ppermute x0 -> x49, starting transfers between devices: none -> 65.8 us  [send(): return lax.ppermute(v, ('dp', 'head'), table(move))]
  transfers between devices with their start and end apart: 16 -> 49, of which waited for: 13 -> 19; matrix products, arithmetic and copies ran while one was open for 10% -> 7% of each run, Pallas kernels for 0% -> 35%
where the time goes in v1:
time: 336 us; the launch traced here: 331 us
  Pallas kernels  117 us (35%)
  waiting for transfers between devices  104 us (31%)
  starting transfers between devices  65.8 us (20%)
  local copies, waits for them, and re-layouts  27.6 us (8%)
  other arithmetic  15.2 us (5%)
    pallas_call x15, Pallas kernels, call(): pl.pallas_call(body, out_shape=[o for o, _ in outs], in_specs=[s for _, s...  117 us
    ppermute x49, waiting for transfers between devices, send(): return lax.ppermute(v, ('dp', 'head'), table(move))  104 us
    ppermute x49, starting transfers between devices, send(): return lax.ppermute(v, ('dp', 'head'), table(move))  65.8 us
    unnamed x94, local copies, waits for them, and re-layouts  16.9 us
  transfers between devices with their start and end apart: 49, of which 19 were waited for; matrix products, arithmetic and copies ran while one was open for 7% of the time, Pallas kernels for 35%

profile of v1, /device:TPU:0, one launch (start us, length us, event | category | flops | bytes accessed | tf_op | source)
XLA Modules:
  0.0 330.8 jit_solution(5614422839475288126)
XLA Ops:
  2.6 4.1 %collective-permute-start.1 = (bf16[96,768]{1,0:T(8,128)(2,1)S(1)}, bf16[96,768]{1,0:T(8,128)(2,1)S(1)}, u32[]{:S(2)}, u32[]{:S(2)}) collective-permute-start(bf16[96,768]{1,0:T(8,128)(2,1)S(1)} %pad_maximum_fusion.6), channel_id=1, source_target_pairs={{0,16},{1,17},{2,18},{3,19},{4,20},{5,21},{6,22},{7,23},{8,24},{9,... | collective-permute-start | bytes 442376 | tf_op jit(solution)/shard_map/ppermute | solution.py:574
  10.5 3.8 %collective-permute-start.11 = (bf16[96,768]{1,0:T(8,128)(2,1)}, bf16[96,768]{1,0:T(8,128)(2,1)S(1)}, u32[]{:S(2)}, u32[]{:S(2)}) collective-permute-start(bf16[96,768]{1,0:T(8,128)(2,1)} %param.34), channel_id=1, source_target_pairs={{0,24},{1,25},{2,26},{3,27},{4,28},{5,29},{6,30},{7,31},{8,0},{9,1... | collective-permute-start | bytes 442376 | tf_op jit(solution)/shard_map/ppermute | solution.py:574
  14.3 4.2 %collective-permute-done.1 = bf16[96,768]{1,0:T(8,128)(2,1)S(1)} collective-permute-done((bf16[96,768]{1,0:T(8,128)(2,1)S(1)}, bf16[96,768]{1,0:T(8,128)(2,1)S(1)}, u32[]{:S(2)}, u32[]{:S(2)}) %collective-permute-start.1) | collective-permute-done | bytes 147488 | tf_op jit(solution)/shard_map/ppermute | solution.py:574
  19.4 3.3 %collective-permute-done.2 = bf16[96,768]{1,0:T(8,128)(2,1)S(1)} collective-permute-done((bf16[96,768]{1,0:T(8,128)(2,1)S(1)}, bf16[96,768]{1,0:T(8,128)(2,1)S(1)}, u32[]{:S(2)}, u32[]{:S(2)}) %collective-permute-start.2) | collective-permute-done | bytes 147488 | tf_op jit(solution)/shard_map/ppermute | solution.py:574
  24.7 7.9 %collective-permute-done.10 = bf16[96,768]{1,0:T(8,128)(2,1)S(1)} collective-permute-done((bf16[96,768]{1,0:T(8,128)(2,1)}, bf16[96,768]{1,0:T(8,128)(2,1)S(1)}, u32[]{:S(2)}, u32[]{:S(2)}) %collective-permute-start.10) | collective-permute-done | bytes 147488 | tf_op jit(solution)/shard_map/ppermute | solution.py:574
  34.4 4.1 %collective-permute-start.16 = (bf16[96,768]{1,0:T(8,128)(2,1)S(1)}, bf16[96,768]{1,0:T(8,128)(2,1)S(1)}, u32[]{:S(2)}, u32[]{:S(2)}) collective-permute-start(bf16[96,768]{1,0:T(8,128)(2,1)S(1)} %bitcast.193), channel_id=1, source_target_pairs={{0,8},{1,9},{2,10},{3,11},{4,12},{5,13},{6,14},{7,15},{8,16},{9,17... | collective-permute-start | bytes 442376 | tf_op jit(solution)/shard_map/ppermute | solution.py:574
  38.4 9.5 %collective-permute-done.17 = bf16[96,768]{1,0:T(8,128)(2,1)S(1)} collective-permute-done((bf16[96,768]{1,0:T(8,128)(2,1)S(1)}, bf16[96,768]{1,0:T(8,128)(2,1)S(1)}, u32[]{:S(2)}, u32[]{:S(2)}) %collective-permute-start.17) | collective-permute-done | bytes 147488 | tf_op jit(solution)/shard_map/ppermute | solution.py:574
  51.8 12.7 %collective-permute-done.19 = bf16[4,96,768]{2,1,0:T(8,128)(2,1)S(1)} collective-permute-done((bf16[4,96,768]{2,1,0:T(8,128)(2,1)S(1)}, bf16[4,96,768]{2,1,0:T(8,128)(2,1)S(1)}, u32[]{:S(2)}, u32[]{:S(2)}) %collective-permute-start.19) | collective-permute-done | bytes 589856 | tf_op jit(solution)/shard_map/ppermute | solution.py:574
  67.6 25.2 %collective-permute-done.7 = bf16[1152]{0:T(1024)(128)(2,1)S(1)} collective-permute-done((bf16[1152]{0:T(1024)(128)(2,1)S(1)}, bf16[1152]{0:T(1024)(128)(2,1)S(1)}, u32[]{:S(2)}, u32[]{:S(2)}) %collective-permute-start.7) | collective-permute-done | bytes 2336 | tf_op jit(solution)/shard_map/ppermute | solution.py:574
  107.1 9.1 %attn_fwd.2 = (bf16[2,400,640]{2,1,0:T(8,128)(2,1)S(1)}, bf16[12,208,208]{2,1,0:T(8,128)(2,1)}, bf16[2,400,256]{2,1,0:T(8,128)(2,1)S(1)}, f32[400,768]{1,0:T(8,128)S(1)}) custom-call(s32[3]{0:T(128)S(1)} %pad_add_fusion.refs_0_, bf16[2,4,96,768]{3,2,1,0:T(8,128)(2,1)S(1)} %pad_maximum_fusion.refs_1_, bf16[2,4,96,768]{3,2,1,0:T(8,128)(2,1)} %collective-permute-done.5.refs_2_, ...), custom_call_target="tpu_custom_call" | custom-call | flops 1233911808 | bytes 5431296 | tf_op jit(solution)/shard_map/attn_fwd/pallas_call | solution.py:35
  118.9 9.4 %attn_fwd.3 = (bf16[2,400,640]{2,1,0:T(8,128)(2,1)S(1)}, bf16[12,208,208]{2,1,0:T(8,128)(2,1)}, bf16[2,400,256]{2,1,0:T(8,128)(2,1)S(1)}, f32[400,768]{1,0:T(8,1...) custom-call(s32[3]{0:T(128)S(1)} %pad_add_fusion.refs_0_, bf16[2,4,96,768]{3,2,1,0:T(8,128)(2,1)} %collective-permute-done.4.refs_1_, ...), custom_call_target="tpu_custom_call" | custom-call | flops 1233911808 | bytes 5431296 | tf_op jit(solution)/shard_map/attn_fwd/pallas_call | solution.py:35
  129.4 4.2 %up.2 = (bf16[2,400,768]{2,1,0:T(8,128)(2,1)S(1)}, bf16[2,400,768]{2,1,0:T(8,128)(2,1)S(1)}) custom-call(s32[3]{0:T(128)S(1)} %pad_add_fusion.refs_0_, bf16[2,4,96,768]{3,2,1,0:T(8,128)(2,1)} %collective-permute-done.13.refs_1_, bf16[2,4,96,768]{3,2,1,0:T(8,128)(2,1)} %collective-permute-done.15.refs_2_, ...), custom_call_target="tpu_custom_call" | custom-call | flops 943718400 | bytes 5431296 | tf_op jit(solution)/shard_map/up/pallas_call | solution.py:35
  133.6 3.5 %grad_down.2 = (bf16[2,4,96,768]{3,2,1,0:T(8,128)(2,1)}, bf16[2,4,96,768]{3,2,1,0:T(8,128)(2,1)}) custom-call(s32[3]{0:T(128)S(1)} %pad_add_fusion.refs_0_, bf16[400,768]{1,0:T(8,128)(2,1)S(1)} %pad.20.og_ref.refs_7_.refs_1_, bf16[2,400,768]{2,1,0:T(8,128)(2,1)S(1)} %get-tuple-element.75.refs_5_.refs_2_), custom_call_target="tpu_custom_call" | custom-call | flops 943718400 | bytes 6561792 | tf_op jit(solution)/shard_map/grad_down/pallas_call | solution.py:35
  137.7 5.8 %up.3 = (bf16[2,400,768]{2,1,0:T(8,128)(2,1)S(1)}, bf16[2,400,768]{2,1,0:T(8,128)(2,1)S(1)}) custom-call(s32[3]{0:T(128)S(1)} %pad_add_fusion.refs_0_, bf16[2,4,96,768]{3,2,1,0:T(8,128)(2,1)S(1)} %pad_maximum_fusion.1.refs_1_, bf16[2,4,96,768]{3,2,1,0:T(8,128)(2,1)} %collective-permute-done.14.refs_2_, ...), custom_call_target="tpu_custom_call" | custom-call | flops 943718400 | bytes 5431296 | tf_op jit(solution)/shard_map/up/pallas_call | solution.py:35
  145.7 11.0 %down.2 = (f32[400,768]{1,0:T(8,128)}, f32[400,768]{1,0:T(8,128)}, bf16[2,400,768]{2,1,0:T(8,128)(2,1)}, f32[2,1,768]{2,1,0:T(1,128)S(1)}) custom-call(s32[3]{0:T(128)S(1)} %pad_add_fusion.refs_0_, bf16[2,4,96,768]{3,2,1,0:T(8,128)(2,1)S(1)} %pad_maximum_fusion.1.refs_1_, bf16[2,4,96,768]{3,2,1,0:T(8,128)(2,1)} %collective-permute-done.14.refs_2_, ...), custom_call_target="tpu_custom_call" | custom-call | flops 2831155200 | bytes 13320192 | tf_op jit(solution)/shard_map/down/pallas_call | solution.py:35
  159.0 11.6 %down.3 = (f32[400,768]{1,0:T(8,128)}, f32[400,768]{1,0:T(8,128)}, bf16[2,400,768]{2,1,0:T(8,128)(2,1)}, f32[2,1,768]{2,1,0:T(1,128)S(1)}) custom-call(s32[3]{0:T(128)S(1)} %pad_add_fusion.refs_0_, bf16[2,4,96,768]{3,2,1,0:T(8,128)(2,1)} %collective-permute-done.13.refs_1_, bf16[2,4,96,768]{3,2,1,0:T(8,128)(2,1)} %collective-permute-done.15.refs_2_, ...), custom_call_target="tpu_custom_call" | custom-call | flops 2831155200 | bytes 13320192 | tf_op jit(solution)/shard_map/down/pallas_call | solution.py:35
  171.9 4.3 %middle.1 = (bf16[394,768]{1,0:T(8,128)(2,1)}, f32[400,768]{1,0:T(8,128)S(1)}, bf16[400,768]{1,0:T(8,128)(2,1)S(1)}, f32[400,1]{1,0:T(8,128)S(1)}, f32[1,768]{1,...) custom-call(bf16[400,768]{1,0:T(8,128)(2,1)S(1)} %pad.19.x_ref.refs_7_, ...), custom_call_target="tpu_custom_call" | custom-call | flops 9216000 | bytes 8601600 | tf_op jit(solution)/shard_map/middle/pallas_call | solution.py:35
  176.8 14.9 %attn_bwd.2 = (bf16[2,4,96,768]{3,2,1,0:T(8,128)(2,1)}, bf16[2,4,96,768]{3,2,1,0:T(8,128)(2,1)S(1)}, f32[400,768]{1,0:T(8,128)}, f32[2,1,640]{2,1,0:T(1,128)S(1)}) custom-call(s32[3]{0:T(128)S(1)} %pad_add_fusion.refs_0_, bf16[2,4,96,768]{3,2,1,0:T(8,128)(2,1)} %collective-permute-done.4.refs_1_, bf16[2,4,96,768]{3,2,1,0:T(8,128)(2,1)} %collective-permute-done.6.refs_2_, ...), custom_call_target="tpu_custom_call" | custom-call | flops 2467823616 | bytes 13221888 | tf_op jit(solution)/shard_map/attn_bwd/pallas_call | solution.py:35
  194.2 3.6 %grad_up.2 = (bf16[2,4,96,768]{3,2,1,0:T(8,128)(2,1)}, bf16[2,4,96,768]{3,2,1,0:T(8,128)(2,1)}) custom-call(s32[3]{0:T(128)S(1)} %pad_add_fusion.refs_0_, bf16[400,768]{1,0:T(8,128)(2,1)S(1)} %copy-done.9, bf16[2,400,768]{2,1,0:T(8,128)(2,1)S(1)} %copy-done.22), custom_call_target="tpu_custom_call" | custom-call | flops 943718400 | bytes 6561792 | tf_op jit(solution)/shard_map/grad_up/pallas_call | solution.py:35
  198.5 9.5 %grad_down.3 = (bf16[2,4,96,768]{3,2,1,0:T(8,128)(2,1)S(1)}, bf16[2,4,96,768]{3,2,1,0:T(8,128)(2,1)}) custom-call(s32[3]{0:T(128)S(1)} %pad_add_fusion.refs_0_, bf16[400,768]{1,0:T(8,128)(2,1)S(1)} %pad.20.og_ref.refs_7_.refs_1_, bf16[2,400,768]{2,1,0:T(8,128)(2,1)} %copy-done, bf16[2,4,96,768]{3,2,1,0:T(8,128)(2,1)S(1)} %collective-permute-done.42.refs_3_, ...), custom_call_target="tpu_custom_call" | custom-call | flops 943718400 | bytes 6561792 | tf_op jit(solution)/shard_map/grad_down/pallas_call | solution.py:35
  208.4 19.5 %attn_bwd.3 = (bf16[2,4,96,768]{3,2,1,0:T(8,128)(2,1)S(1)}, bf16[2,4,96,768]{3,2,1,0:T(8,128)(2,1)S(1)}, f32[400,768]{1,0:T(8,128)}, f32[2,1,640]{2,1,0:T(1,128)S(1)}) custom-call(s32[3]{0:T(128)S(1)} %pad_add_fusion.refs_0_, bf16[2,4,96,768]{3,2,1,0:T(8,128)(2,1)S(1)} %pad_maximum_fusion.refs_1_, bf16[2,4,96,768]{3,2,1,0:T(8,128)(2,1)} %collective-permute-done.5.refs_2_, ...), custom_call_target="tpu_custom_call" | custom-call | flops 2467823616 | bytes 13221888 | tf_op jit(solution)/shard_map/attn_bwd/pallas_call | solution.py:35
  235.6 8.1 %grad_up.3 = (bf16[2,4,96,768]{3,2,1,0:T(8,128)(2,1)S(1)}, bf16[2,4,96,768]{3,2,1,0:T(8,128)(2,1)S(1)}) custom-call(s32[3]{0:T(128)S(1)} %pad_add_fusion.refs_0_, bf16[400,768]{1,0:T(8,128)(2,1)S(1)} %copy-done.10, bf16[2,400,768]{2,1,0:T(8,128)(2,1)} %get-tuple-element.112.refs_2_, bf16[2,4,96,768]{3,2,1,0:T(8,128)(2,1)} %collective-permute-done.35.refs_3_, ...), custom_call_target="tpu_custom_call" | custom-call | flops 943718400 | bytes 6561792 | tf_op jit(solution)/shard_map/grad_up/pallas_call | solution.py:35
  246.0 18.0 %collective-permute-done.26 = f32[6528]{0:T(1024)S(1)} collective-permute-done((f32[6528]{0:T(1024)S(1)}, f32[6528]{0:T(1024)S(1)}, u32[]{:S(2)}, u32[]{:S(2)}) %collective-permute-start.26) | collective-permute-done | bytes 26144 | tf_op jit(solution)/shard_map/ppermute | solution.py:574
  264.5 3.4 %collective-permute-done.27 = f32[6528]{0:T(1024)S(1)} collective-permute-done((f32[6528]{0:T(1024)S(1)}, f32[6528]{0:T(1024)S(1)}, u32[]{:S(2)}, u32[]{:S(2)}) %collective-permute-start.27) | collective-permute-done | bytes 26144 | tf_op jit(solution)/shard_map/ppermute | solution.py:574
  271.7 2.9 collective-permute-start.29
  282.2 6.1 %collective-permute-done.45 = bf16[4,96,768]{2,1,0:T(8,128)(2,1)S(1)} collective-permute-done((bf16[4,96,768]{2,1,0:T(8,128)(2,1)S(1)}, bf16[4,96,768]{2,1,0:T(8,128)(2,1)S(1)}, u32[]{:S(2)}, u32[]{:S(2)}) %collective-permute-start.45) | collective-permute-done | bytes 589856 | tf_op jit(solution)/shard_map/ppermute | solution.py:574
  294.8 2.8 collective-permute-start.32
  297.6 3.3 collective-permute-done.38
  300.9 2.9 collective-permute-start.33
  307.7 4.5 %collective-permute-start.39 = (bf16[96,768]{1,0:T(8,128)(2,1)}, bf16[96,768]{1,0:T(8,128)(2,1)}, u32[]{:S(2)}, u32[]{:S(2)}) collective-permute-start(bf16[96,768]{1,0:T(8,128)(2,1)} %get-tuple-element.165), channel_id=1, source_target_pairs={{0,24},{1,25},{2,26},{3,27},{4,28},{5,29},{6,30},{7,31},{8,0},{9,1... | collective-permute-start | bytes 442376 | tf_op jit(solution)/shard_map/ppermute | solution.py:574
  312.5 6.7 %collective-permute-start.41 = (bf16[96,768]{1,0:T(8,128)(2,1)}, bf16[96,768]{1,0:T(8,128)(2,1)}, u32[]{:S(2)}, u32[]{:S(2)}) collective-permute-start(bf16[96,768]{1,0:T(8,128)(2,1)} %get-tuple-element.166), channel_id=1, source_target_pairs={{0,8},{1,9},{2,10},{3,11},{4,12},{5,13},{6,14},{7,15},{8,16},{9,17... | collective-permute-start | bytes 442376 | tf_op jit(solution)/shard_map/ppermute | solution.py:574
  320.9 3.4 %collective-permute-start.40 = (bf16[96,768]{1,0:T(8,128)(2,1)}, bf16[96,768]{1,0:T(8,128)(2,1)S(1)}, u32[]{:S(2)}, u32[]{:S(2)}) collective-permute-start(bf16[96,768]{1,0:T(8,128)(2,1)} %get-tuple-element.167), channel_id=1, source_target_pairs={{0,16},{1,17},{2,18},{3,19},{4,20},{5,21},{6,22},{7,23},{8,24},{9,... | collective-permute-start | bytes 442376 | tf_op jit(solution)/shard_map/ppermute | solution.py:574
  (244 shorter events, 86.2 us)
Async XLA Ops:
  2.6 15.9 %collective-permute-start.1 = (bf16[96,768]{1,0:T(8,128)(2,1)S(1)}, bf16[96,768]{1,0:T(8,128)(2,1)S(1)}, u32[]{:S(2)}, u32[]{:S(2)}) collective-permute-start(bf16[96,768]{1,0:T(8,128)(2,1)S(1)} %pad_maximum_fusion.6), channel_id=1, source_target_pairs={{0,16},{1,17},{2,18},{3,19},{4,20},{5,21},{6,22},{7,23},{8,24},{9,... | collective-permute-start | bytes 442376 | tf_op jit(solution)/shard_map/ppermute | solution.py:574
  8.2 14.5 %collective-permute-start.2 = (bf16[96,768]{1,0:T(8,128)(2,1)S(1)}, bf16[96,768]{1,0:T(8,128)(2,1)S(1)}, u32[]{:S(2)}, u32[]{:S(2)}) collective-permute-start(bf16[96,768]{1,0:T(8,128)(2,1)S(1)} %pad_maximum_fusion.6), channel_id=1, source_target_pairs={{0,24},{1,25},{2,26},{3,27},{4,28},{5,29},{6,30},{7,31},{8,0},{9,1... | collective-permute-start | bytes 442376 | tf_op jit(solution)/shard_map/ppermute | solution.py:574
  10.5 14.3 %collective-permute-start.11 = (bf16[96,768]{1,0:T(8,128)(2,1)}, bf16[96,768]{1,0:T(8,128)(2,1)S(1)}, u32[]{:S(2)}, u32[]{:S(2)}) collective-permute-start(bf16[96,768]{1,0:T(8,128)(2,1)} %param.34), channel_id=1, source_target_pairs={{0,24},{1,25},{2,26},{3,27},{4,28},{5,29},{6,30},{7,31},{8,0},{9,1... | collective-permute-start | bytes 442376 | tf_op jit(solution)/shard_map/ppermute | solution.py:574
  22.9 26.5 %collective-permute-start.3 = (bf16[4,96,768]{2,1,0:T(8,128)(2,1)S(1)}, bf16[4,96,768]{2,1,0:T(8,128)(2,1)S(1)}, u32[]{:S(2)}, u32[]{:S(2)}) collective-permute-start(bf16[4,96,768]{2,1,0:T(8,128)(2,1)S(1)} %get-tuple-element.176), channel_id=1, source_target_pairs={{0,4},{1,3},{2,6},{3,1},{4,0},{5,7},{6,2},{7,5},{8,12},{9,11},{10,... | collective-permute-start | bytes 1769480 | tf_op jit(solution)/shard_map/ppermute | solution.py:574
  32.8 17.6 %collective-permute-start.12 = (bf16[4,96,768]{2,1,0:T(8,128)(2,1)S(1)}, bf16[4,96,768]{2,1,0:T(8,128)(2,1)S(1)}, u32[]{:S(2)}, u32[]{:S(2)}) collective-permute-start(bf16[4,96,768]{2,1,0:T(8,128)(2,1)S(1)} %get-tuple-element.174), channel_id=1, source_target_pairs={{0,4},{1,3},{2,6},{3,1},{4,0},{5,7},{6,2},{7,5},{8,12},{9,11},{10,... | collective-permute-start | bytes 1769480 | tf_op jit(solution)/shard_map/ppermute | solution.py:574
  48.1 16.3 %collective-permute-start.19 = (bf16[4,96,768]{2,1,0:T(8,128)(2,1)S(1)}, bf16[4,96,768]{2,1,0:T(8,128)(2,1)S(1)}, u32[]{:S(2)}, u32[]{:S(2)}) collective-permute-start(bf16[4,96,768]{2,1,0:T(8,128)(2,1)S(1)} %get-tuple-element.172), channel_id=1, source_target_pairs={{0,4},{1,3},{2,6},{3,1},{4,0},{5,7},{6,2},{7,5},{8,12},{9,11},{10,... | collective-permute-start | bytes 1769480 | tf_op jit(solution)/shard_map/ppermute | solution.py:574
  49.5 43.9 %collective-permute-start.5 = (bf16[2,4,96,768]{3,2,1,0:T(8,128)(2,1)S(1)}, bf16[2,4,96,768]{3,2,1,0:T(8,128)(2,1)}, u32[]{:S(2)}, u32[]{:S(2)}) collective-permute-start(bf16[2,4,96,768]{3,2,1,0:T(8,128)(2,1)S(1)} %pad_maximum_fusion.refs_1_), channel_id=1, source_target_pairs={{0,2},{1,5},{2,0},{3,7},{4,6},{5,1},{6,4},{7,3},{8,10},{9,13},{10,... | collective-permute-start | bytes 3538952 | tf_op jit(solution)/shard_map/ppermute | solution.py:574
  50.5 44.6 %collective-permute-start.14 = (bf16[2,4,96,768]{3,2,1,0:T(8,128)(2,1)S(1)}, bf16[2,4,96,768]{3,2,1,0:T(8,128)(2,1)}, u32[]{:S(2)}, u32[]{:S(2)}) collective-permute-start(bf16[2,4,96,768]{3,2,1,0:T(8,128)(2,1)S(1)} %pad_maximum_fusion.1.refs_1_), channel_id=1, source_target_pairs={{0,2},{1,5},{2,0},{3,7},{4,6},{5,1},{6,4},{7,3},{8,10},{9,13},{10,... | collective-permute-start | bytes 3538952 | tf_op jit(solution)/shard_map/ppermute | solution.py:574
  64.6 41.8 %collective-permute-start.21 = (bf16[2,4,96,768]{3,2,1,0:T(8,128)(2,1)S(1)}, bf16[2,4,96,768]{3,2,1,0:T(8,128)(2,1)}, u32[]{:S(2)}, u32[]{:S(2)}) collective-permute-start(bf16[2,4,96,768]{3,2,1,0:T(8,128)(2,1)S(1)} %pad_maximum_fusion.2.refs_3_), channel_id=1, source_target_pairs={{0,2},{1,5},{2,0},{3,7},{4,6},{5,1},{6,4},{7,3},{8,10},{9,13},{10,... | collective-permute-start | bytes 3538952 | tf_op jit(solution)/shard_map/ppermute | solution.py:574
  65.0 41.5 %collective-permute-start.4 = (bf16[2,4,96,768]{3,2,1,0:T(8,128)(2,1)S(1)}, bf16[2,4,96,768]{3,2,1,0:T(8,128)(2,1)}, u32[]{:S(2)}, u32[]{:S(2)}) collective-permute-start(bf16[2,4,96,768]{3,2,1,0:T(8,128)(2,1)S(1)} %pad_maximum_fusion.refs_1_), channel_id=1, source_target_pairs={{0,1},{1,0},{2,3},{3,2},{4,5},{5,4},{6,7},{7,6},{8,9},{9,8},{10,11... | collective-permute-start | bytes 3538952 | tf_op jit(solution)/shard_map/ppermute | solution.py:574
  65.9 26.9 %collective-permute-start.7 = (bf16[1152]{0:T(1024)(128)(2,1)S(1)}, bf16[1152]{0:T(1024)(128)(2,1)S(1)}, u32[]{:S(2)}, u32[]{:S(2)}) collective-permute-start(bf16[1152]{0:T(1024)(128)(2,1)S(1)} %concatenate.35), channel_id=1, source_target_pairs={{0,2},{1,3},{2,0},{3,1},{4,6},{5,7},{6,4},{7,5},{8,10},{9,11},{10,... | collective-permute-start | bytes 6920 | tf_op jit(solution)/shard_map/ppermute | solution.py:574
  93.4 25.5 %collective-permute-start.6 = (bf16[2,4,96,768]{3,2,1,0:T(8,128)(2,1)}, bf16[2,4,96,768]{3,2,1,0:T(8,128)(2,1)}, u32[]{:S(2)}, u32[]{:S(2)}) collective-permute-start(bf16[2,4,96,768]{3,2,1,0:T(8,128)(2,1)} %collective-permute-done.5.refs_2_), channel_id=1, source_target_pairs={{0,1},{1,0},{2,3},{3,2},{4,5},{5,4},{6,7},{7,6},{8,9},{9,8},{10,11... | collective-permute-start | bytes 3538952 | tf_op jit(solution)/shard_map/ppermute | solution.py:574
  94.9 34.4 %collective-permute-start.13 = (bf16[2,4,96,768]{3,2,1,0:T(8,128)(2,1)S(1)}, bf16[2,4,96,768]{3,2,1,0:T(8,128)(2,1)}, u32[]{:S(2)}, u32[]{:S(2)}) collective-permute-start(bf16[2,4,96,768]{3,2,1,0:T(8,128)(2,1)S(1)} %pad_maximum_fusion.1.refs_1_), channel_id=1, source_target_pairs={{0,1},{1,0},{2,3},{3,2},{4,5},{5,4},{6,7},{7,6},{8,9},{9,8},{10,11... | collective-permute-start | bytes 3538952 | tf_op jit(solution)/shard_map/ppermute | solution.py:574
  95.1 34.3 %collective-permute-start.15 = (bf16[2,4,96,768]{3,2,1,0:T(8,128)(2,1)}, bf16[2,4,96,768]{3,2,1,0:T(8,128)(2,1)}, u32[]{:S(2)}, u32[]{:S(2)}) collective-permute-start(bf16[2,4,96,768]{3,2,1,0:T(8,128)(2,1)} %collective-permute-done.14.refs_2_), channel_id=1, source_target_pairs={{0,1},{1,0},{2,3},{3,2},{4,5},{5,4},{6,7},{7,6},{8,9},{9,8},{10,11... | collective-permute-start | bytes 3538952 | tf_op jit(solution)/shard_map/ppermute | solution.py:574
  106.4 50.3 %collective-permute-start.20 = (bf16[2,4,96,768]{3,2,1,0:T(8,128)(2,1)S(1)}, bf16[2,4,96,768]{3,2,1,0:T(8,128)(2,1)S(1)}, u32[]{:S(2)}, u32[]{:S(2)}) collective-permute-start(bf16[2,4,96,768]{3,2,1,0:T(8,128)(2,1)S(1)} %pad_maximum_fusion.2.refs_3_), channel_id=1, source_target_pairs={{0,1},{1,0},{2,3},{3,2},{4,5},{5,4},{6,7},{7,6},{8,9},{9,8},{10,11... | collective-permute-start | bytes 3538952 | tf_op jit(solution)/shard_map/ppermute | solution.py:574
  106.6 51.1 %collective-permute-start.22 = (bf16[2,4,96,768]{3,2,1,0:T(8,128)(2,1)}, bf16[2,4,96,768]{3,2,1,0:T(8,128)(2,1)}, u32[]{:S(2)}, u32[]{:S(2)}) collective-permute-start(bf16[2,4,96,768]{3,2,1,0:T(8,128)(2,1)} %collective-permute-done.21.refs_4_), channel_id=1, source_target_pairs={{0,1},{1,0},{2,3},{3,2},{4,5},{5,4},{6,7},{7,6},{8,9},{9,8},{10,11... | collective-permute-start | bytes 3538952 | tf_op jit(solution)/shard_map/ppermute | solution.py:574
  137.1 60.9 %collective-permute-start.42 = (bf16[2,4,96,768]{3,2,1,0:T(8,128)(2,1)}, bf16[2,4,96,768]{3,2,1,0:T(8,128)(2,1)S(1)}, u32[]{:S(2)}, u32[]{:S(2)}) collective-permute-start(bf16[2,4,96,768]{3,2,1,0:T(8,128)(2,1)} %get-tuple-element.118), channel_id=1, source_target_pairs={{0,1},{1,0},{2,3},{3,2},{4,5},{5,4},{6,7},{7,6},{8,9},{9,8},{10,11... | collective-permute-start | bytes 3538952 | tf_op jit(solution)/shard_map/ppermute | solution.py:574
  137.4 61.1 %collective-permute-start.43 = (bf16[2,4,96,768]{3,2,1,0:T(8,128)(2,1)}, bf16[2,4,96,768]{3,2,1,0:T(8,128)(2,1)S(1)}, u32[]{:S(2)}, u32[]{:S(2)}) collective-permute-start(bf16[2,4,96,768]{3,2,1,0:T(8,128)(2,1)} %get-tuple-element.119), channel_id=1, source_target_pairs={{0,1},{1,0},{2,3},{3,2},{4,5},{5,4},{6,7},{7,6},{8,9},{9,8},{10,11... | collective-permute-start | bytes 3538952 | tf_op jit(solution)/shard_map/ppermute | solution.py:574
  191.7 16.6 %collective-permute-start.23 = (bf16[2,4,96,768]{3,2,1,0:T(8,128)(2,1)}, bf16[2,4,96,768]{3,2,1,0:T(8,128)(2,1)}, u32[]{:S(2)}, u32[]{:S(2)}) collective-permute-start(bf16[2,4,96,768]{3,2,1,0:T(8,128)(2,1)} %get-tuple-element.92), channel_id=1, source_target_pairs={{0,1},{1,0},{2,3},{3,2},{4,5},{5,4},{6,7},{7,6},{8,9},{9,8},{10,11... | collective-permute-start | bytes 3538952 | tf_op jit(solution)/shard_map/ppermute | solution.py:574
  191.9 16.4 %collective-permute-start.24 = (bf16[2,4,96,768]{3,2,1,0:T(8,128)(2,1)S(1)}, bf16[2,4,96,768]{3,2,1,0:T(8,128)(2,1)}, u32[]{:S(2)}, u32[]{:S(2)}) collective-permute-start(bf16[2,4,96,768]{3,2,1,0:T(8,128)(2,1)S(1)} %get-tuple-element.93), channel_id=1, source_target_pairs={{0,1},{1,0},{2,3},{3,2},{4,5},{5,4},{6,7},{7,6},{8,9},{9,8},{10,11... | collective-permute-start | bytes 3538952 | tf_op jit(solution)/shard_map/ppermute | solution.py:574
  197.8 36.8 %collective-permute-start.35 = (bf16[2,4,96,768]{3,2,1,0:T(8,128)(2,1)}, bf16[2,4,96,768]{3,2,1,0:T(8,128)(2,1)}, u32[]{:S(2)}, u32[]{:S(2)}) collective-permute-start(bf16[2,4,96,768]{3,2,1,0:T(8,128)(2,1)} %get-tuple-element.114), channel_id=1, source_target_pairs={{0,1},{1,0},{2,3},{3,2},{4,5},{5,4},{6,7},{7,6},{8,9},{9,8},{10,11... | collective-permute-start | bytes 3538952 | tf_op jit(solution)/shard_map/ppermute | solution.py:574
  198.0 36.5 %collective-permute-start.36 = (bf16[2,4,96,768]{3,2,1,0:T(8,128)(2,1)}, bf16[2,4,96,768]{3,2,1,0:T(8,128)(2,1)}, u32[]{:S(2)}, u32[]{:S(2)}) collective-permute-start(bf16[2,4,96,768]{3,2,1,0:T(8,128)(2,1)} %get-tuple-element.115), channel_id=1, source_target_pairs={{0,1},{1,0},{2,3},{3,2},{4,5},{5,4},{6,7},{7,6},{8,9},{9,8},{10,11... | collective-permute-start | bytes 3538952 | tf_op jit(solution)/shard_map/ppermute | solution.py:574
  208.0 69.1 %collective-permute-start.44 = (bf16[2,4,96,768]{3,2,1,0:T(8,128)(2,1)}, bf16[2,4,96,768]{3,2,1,0:T(8,128)(2,1)}, u32[]{:S(2)}, u32[]{:S(2)}) collective-permute-start(bf16[2,4,96,768]{3,2,1,0:T(8,128)(2,1)} %get-tuple-element.121), channel_id=1, source_target_pairs={{0,2},{1,5},{2,0},{3,7},{4,6},{5,1},{6,4},{7,3},{8,10},{9,13},{10,... | collective-permute-start | bytes 3538952 | tf_op jit(solution)/shard_map/ppermute | solution.py:574
  234.3 44.8 %collective-permute-start.30 = (bf16[2,4,96,768]{3,2,1,0:T(8,128)(2,1)}, bf16[2,4,96,768]{3,2,1,0:T(8,128)(2,1)S(1)}, u32[]{:S(2)}, u32[]{:S(2)}) collective-permute-start(bf16[2,4,96,768]{3,2,1,0:T(8,128)(2,1)} %copy-done.17), channel_id=1, source_target_pairs={{0,2},{1,5},{2,0},{3,7},{4,6},{5,1},{6,4},{7,3},{8,10},{9,13},{10,... | collective-permute-start | bytes 3538952 | tf_op jit(solution)/shard_map/ppermute | solution.py:574
  243.8 36.9 %collective-permute-start.37 = (bf16[2,4,96,768]{3,2,1,0:T(8,128)(2,1)S(1)}, bf16[2,4,96,768]{3,2,1,0:T(8,128)(2,1)S(1)}, u32[]{:S(2)}, u32[]{:S(2)}) collective-permute-start(bf16[2,4,96,768]{3,2,1,0:T(8,128)(2,1)S(1)} %get-tuple-element.117), channel_id=1, source_target_pairs={{0,2},{1,5},{2,0},{3,7},{4,6},{5,1},{6,4},{7,3},{8,10},{9,13},{10,... | collective-permute-start | bytes 3538952 | tf_op jit(solution)/shard_map/ppermute | solution.py:574
  245.6 18.3 %collective-permute-start.26 = (f32[6528]{0:T(1024)S(1)}, f32[6528]{0:T(1024)S(1)}, u32[]{:S(2)}, u32[]{:S(2)}) collective-permute-start(f32[6528]{0:T(1024)S(1)} %pad_maximum_fusion.9), channel_id=1, source_target_pairs={{0,2},{1,3},{2,0},{3,1},{4,6},{5,7},{6,4},{7,5},{8,10},{9,11},{10,... | collective-permute-start | bytes 78344 | tf_op jit(solution)/shard_map/ppermute | solution.py:574
  279.2 15.4 %collective-permute-start.31 = (bf16[4,96,768]{2,1,0:T(8,128)(2,1)S(1)}, bf16[4,96,768]{2,1,0:T(8,128)(2,1)S(1)}, u32[]{:S(2)}, u32[]{:S(2)}) collective-permute-start(bf16[4,96,768]{2,1,0:T(8,128)(2,1)S(1)} %fusion), channel_id=1, source_target_pairs={{0,4},{1,3},{2,6},{3,1},{4,0},{5,7},{6,2},{7,5},{8,12},{9,11},{10,... | collective-permute-start | bytes 1769480 | tf_op jit(solution)/shard_map/ppermute | solution.py:574
  280.8 20.1 %collective-permute-start.38 = (bf16[4,96,768]{2,1,0:T(8,128)(2,1)S(1)}, bf16[4,96,768]{2,1,0:T(8,128)(2,1)S(1)}, u32[]{:S(2)}, u32[]{:S(2)}) collective-permute-start(bf16[4,96,768]{2,1,0:T(8,128)(2,1)S(1)} %fusion.1), channel_id=1, source_target_pairs={{0,4},{1,3},{2,6},{3,1},{4,0},{5,7},{6,2},{7,5},{8,12},{9,11},{10,... | collective-permute-start | bytes 1769480 | tf_op jit(solution)/shard_map/ppermute | solution.py:574
  290.4 30.4 %collective-permute-start.46 = (bf16[96,768]{1,0:T(8,128)(2,1)}, bf16[96,768]{1,0:T(8,128)(2,1)}, u32[]{:S(2)}, u32[]{:S(2)}) collective-permute-start(bf16[96,768]{1,0:T(8,128)(2,1)} %get-tuple-element.162), channel_id=1, source_target_pairs={{0,24},{1,25},{2,26},{3,27},{4,28},{5,29},{6,30},{7,31},{8,0},{9,1... | collective-permute-start | bytes 442376 | tf_op jit(solution)/shard_map/ppermute | solution.py:574
  293.2 31.0 %collective-permute-start.48 = (bf16[96,768]{1,0:T(8,128)(2,1)}, bf16[96,768]{1,0:T(8,128)(2,1)}, u32[]{:S(2)}, u32[]{:S(2)}) collective-permute-start(bf16[96,768]{1,0:T(8,128)(2,1)} %get-tuple-element.163), channel_id=1, source_target_pairs={{0,8},{1,9},{2,10},{3,11},{4,12},{5,13},{6,14},{7,15},{8,16},{9,17... | collective-permute-start | bytes 442376 | tf_op jit(solution)/shard_map/ppermute | solution.py:574
  304.7 19.6 %collective-permute-start.47 = (bf16[96,768]{1,0:T(8,128)(2,1)}, bf16[96,768]{1,0:T(8,128)(2,1)}, u32[]{:S(2)}, u32[]{:S(2)}) collective-permute-start(bf16[96,768]{1,0:T(8,128)(2,1)} %get-tuple-element.164), channel_id=1, source_target_pairs={{0,16},{1,17},{2,18},{3,19},{4,20},{5,21},{6,22},{7,23},{8,24},{9,... | collective-permute-start | bytes 442376 | tf_op jit(solution)/shard_map/ppermute | solution.py:574
  307.7 18.6 %collective-permute-start.39 = (bf16[96,768]{1,0:T(8,128)(2,1)}, bf16[96,768]{1,0:T(8,128)(2,1)}, u32[]{:S(2)}, u32[]{:S(2)}) collective-permute-start(bf16[96,768]{1,0:T(8,128)(2,1)} %get-tuple-element.165), channel_id=1, source_target_pairs={{0,24},{1,25},{2,26},{3,27},{4,28},{5,29},{6,30},{7,31},{8,0},{9,1... | collective-permute-start | bytes 442376 | tf_op jit(solution)/shard_map/ppermute | solution.py:574
  (58 other events, 430.9 us)

commit v2 on v1

--- a/solution.py
+++ b/solution.py
@@ -13,8 +13,8 @@
 BF16 = jnp.bfloat16
 VMEM = pl.BlockSpec(memory_space=pltpu.VMEM)
 SMEM = pl.BlockSpec(memory_space=pltpu.SMEM)
-ANYS = pl.BlockSpec(memory_space=pl.ANY)
-LIMIT = 48 * 1024 * 1024
+WEIGHT = 1.0e10
+LIMIT = 20 * 1024 * 1024
 INV_SQRT2 = 0.7071067811865476
 INV_SQRT2PI = 0.3989422804014327
 
@@ -31,7 +31,7 @@
     return jax.ShapeDtypeStruct(shape, dtype)
 
 
-def call(body, outs, ins, scratch=(), flops=0, nbytes=0, trans=0, name=None):
+def call(body, outs, ins, scratch=(), micros=1.0, name=None):
     return pl.pallas_call(
         body,
         out_shape=[o for o, _ in outs],
@@ -40,7 +40,7 @@
         scratch_shapes=list(scratch),
         compiler_params=pltpu.CompilerParams(vmem_limit_bytes=LIMIT),
         cost_estimate=pl.CostEstimate(
-            flops=int(flops), bytes_accessed=int(nbytes), transcendentals=int(trans)
+            flops=int(micros * WEIGHT), bytes_accessed=0, transcendentals=0
         ),
         name=name,
     )(*[a for a, _ in ins])
@@ -100,49 +100,29 @@
     return found
 
 
-def load_start(p, refs, buf, sem, pos_ref, other):
+def gather_blocks(p, refs, buf, pos_ref, other):
     if not p.fast:
-        copy = pltpu.make_async_copy(refs[0], buf, sem.at[0])
-        copy.start()
-        return [copy]
-    copies = []
-    for i, (b3, b2, zz, yy, row) in enumerate(piece_list(p, pos_ref, other)):
-        copy = pltpu.make_async_copy(
-            refs[b3].at[b2, zz], buf.at[yy, pl.ds(row, p.piece)], sem.at[i]
-        )
-        copy.start()
-        copies.append(copy)
-    return copies
-
-
-def store_start(p, buf, refs, sem, pos_ref, other):
+        buf[...] = refs[0][...]
+        return
+    for b3, b2, zz, yy, row in piece_list(p, pos_ref, other):
+        buf[yy, pl.ds(row, p.piece), :] = refs[b3][b2, zz]
+
+
+def spread_blocks(p, buf, refs, pos_ref, other, received=None):
     if not p.fast:
-        copy = pltpu.make_async_copy(buf, refs[0], sem.at[0])
-        copy.start()
-        return [copy]
-    copies = []
-    for i, (b3, b2, zz, yy, row) in enumerate(piece_list(p, pos_ref, other)):
-        copy = pltpu.make_async_copy(
-            buf.at[yy, pl.ds(row, p.piece)], refs[b3].at[b2, zz], sem.at[i]
-        )
-        copy.start()
-        copies.append(copy)
-    return copies
-
-
-def wait_all(copies):
-    for copy in copies:
-        copy.wait()
+        refs[0][...] = buf[...].astype(BF16)
+        return
+    for b3, b2, zz, yy, row in piece_list(p, pos_ref, other):
+        part = buf[yy, pl.ds(row, p.piece), :]
+        if received is not None:
+            part = part + received[b3][b2, zz].astype(F32)
+        refs[b3][b2, zz] = part.astype(BF16)
 
 
 def piece_shapes(p):
     if p.fast:
         return [sds((2, 4, p.piece, p.width), BF16)] * 2
     return [sds((2, p.width, p.width), BF16)]
-
-
-def n_sem(p):
-    return 16 if p.fast else 1
 
 
 def entry_kernel(p, patches, out_grad, gain_one, shift_one, router):
@@ -162,8 +142,7 @@
             (sds((1, p.width), F32), VMEM),
         ],
         [(a, VMEM) for a in (patches, out_grad, gain_one, shift_one, router)],
-        flops=p.pad * p.width * 10,
-        nbytes=p.pad * p.width * 6,
+        micros=0.7,
         name="entry",
     )
 
@@ -189,8 +168,8 @@
         else:
             qkv_ref, prob_ref, ctx_ref, att_ref = rest[:4]
             rest = rest[4:]
-        wbuf, ctx, sem = rest
-        wait_all(load_start(p, w_refs, wbuf, sem, pos_ref, other))
+        wbuf, ctx = rest
+        gather_blocks(p, w_refs, wbuf, pos_ref, other)
         low = low_ref[...]
         total = None
         for b in range(2):
@@ -234,7 +213,7 @@
         xhat, _ = norm_parts(mixed)
         in_ref[...] = (xhat * g2_ref[...] + s2_ref[...]).astype(BF16)
 
-    ins = [(pos, SMEM)] + [(w, ANYS) for w in weights]
+    ins = [(pos, SMEM)] + [(w, VMEM) for w in weights]
     ins += [(a, VMEM) for a in (rows_low, bias, key_mask)]
     if carry is not None:
         ins.append((carry, VMEM))
@@ -255,11 +234,8 @@
         [
             pltpu.VMEM((2, p.width, 4 * p.cols), BF16),
             pltpu.VMEM((pad, p.cw), F32),
-            pltpu.SemaphoreType.DMA((n_sem(p),)),
         ],
-        flops=2 * (2 * pad * p.width * (p.nq + p.cw) + p.images * lh * win * win * hd * 4),
-        nbytes=2 * 2 * p.width * p.width + pad * p.width * 10,
-        trans=2 * p.images * lh * win * win,
+        micros=5.5,
         name="attn_fwd",
     )
 
@@ -268,8 +244,8 @@
     def body(*refs):
         nw = len(weights)
         pos_ref, w_refs = refs[0], refs[1 : 1 + nw]
-        in_ref, b_ref, act_ref, slope_ref, wbuf, sem = refs[1 + nw :]
-        wait_all(load_start(p, w_refs, wbuf, sem, pos_ref, other))
+        in_ref, b_ref, act_ref, slope_ref, wbuf = refs[1 + nw :]
+        gather_blocks(p, w_refs, wbuf, pos_ref, other)
         rows = in_ref[...]
         for b in range(2):
             pre = dot(rows, wbuf[b]) + b_ref[b]
@@ -280,11 +256,9 @@
     return call(
         body,
         [(sds((2, p.pad, p.hid), BF16), VMEM)] * 2,
-        [(pos, SMEM)] + [(w, ANYS) for w in weights] + [(mlp_in, VMEM), (bias, VMEM)],
-        [pltpu.VMEM((2, p.width, p.hid), BF16), pltpu.SemaphoreType.DMA((n_sem(p),))],
-        flops=2 * 2 * p.pad * p.width * p.hid,
-        nbytes=4 * p.width * p.hid + 10 * p.pad * p.hid,
-        trans=2 * p.pad * p.hid * 2,
+        [(pos, SMEM)] + [(w, VMEM) for w in weights] + [(mlp_in, VMEM), (bias, VMEM)],
+        [pltpu.VMEM((2, p.width, p.hid), BF16)],
+        micros=2.5,
         name="up",
     )
 
@@ -297,34 +271,18 @@
         got_refs, rest = rest[:nr], rest[nr:]
         no = len(piece_shapes(p))
         out_refs, rest = rest[:no], rest[no:]
-        if nr:
-            gbuf, rbuf, sem, rsem = rest
-            loads = load_start(p, got_refs, rbuf, rsem, pos_ref, other)
-        else:
-            gbuf, sem = rest
+        (gbuf,) = rest
         left = l_ref[...]
         for b in range(2):
-            g = dot(left, r_ref[b], TN)
-            if nr:
-                if b == 0:
-                    wait_all(loads)
-                g = g + rbuf[b].astype(F32)
-            gbuf[b] = g.astype(BF16)
-        wait_all(store_start(p, gbuf, out_refs, sem, pos_ref, other))
-
-    scratch = [pltpu.VMEM((2, p.width, p.hid), BF16)]
-    if received is not None:
-        scratch.append(pltpu.VMEM((2, p.width, p.hid), BF16))
-    scratch.append(pltpu.SemaphoreType.DMA((n_sem(p),)))
-    if received is not None:
-        scratch.append(pltpu.SemaphoreType.DMA((n_sem(p),)))
+            gbuf[b] = dot(left, r_ref[b], TN)
+        spread_blocks(p, gbuf, out_refs, pos_ref, other, got_refs if nr else None)
+
     return call(
         body,
-        [(s, ANYS) for s in piece_shapes(p)],
-        [(pos, SMEM), (lhs, VMEM), (rhs, VMEM)] + [(r, ANYS) for r in received or ()],
-        scratch,
-        flops=2 * 2 * p.pad * p.width * p.hid,
-        nbytes=8 * p.width * p.hid + 6 * p.pad * p.hid,
+        [(s, VMEM) for s in piece_shapes(p)],
+        [(pos, SMEM), (lhs, VMEM), (rhs, VMEM)] + [(r, VMEM) for r in received or ()],
+        [pltpu.VMEM((2, p.width, p.hid), F32)],
+        micros=2.3,
         name=name,
     )
 
@@ -338,18 +296,15 @@
         if carry is not None:
             out_in, back_in = rest[:2]
             rest = rest[2:]
-        out_ref, back_ref, low_ref, bias_ref, ubuf, dbuf, usem, dsem = rest
-        d_copies = load_start(p, d_refs, dbuf, dsem, pos_ref, other)
-        u_copies = load_start(p, u_refs, ubuf, usem, pos_ref, other)
-        wait_all(d_copies)
+        out_ref, back_ref, low_ref, bias_ref, ubuf, dbuf = rest
+        gather_blocks(p, d_refs, dbuf, pos_ref, other)
+        gather_blocks(p, u_refs, ubuf, pos_ref, other)
         og = og_ref[...]
         for b in range(2):
             grad = dot(og, dbuf[b]) * slope_ref[b].astype(F32)
             bias_ref[b] = jnp.sum(grad, axis=0, keepdims=True)
             low = grad.astype(BF16)
             low_ref[b] = low
-            if b == 0:
-                wait_all(u_copies)
             back = dot(low, ubuf[b], NT)
             out = dot(act_ref[b], dbuf[b], NT)
             if b == 0 and carry is not None:
@@ -362,7 +317,7 @@
                 back_ref[...] += back
                 out_ref[...] += out
 
-    ins = [(pos, SMEM)] + [(w, ANYS) for w in tuple(w_up) + tuple(w_down)]
+    ins = [(pos, SMEM)] + [(w, VMEM) for w in tuple(w_up) + tuple(w_down)]
     ins += [(a, VMEM) for a in (active, slope, out_grad)]
     if carry is not None:
         ins += [(a, VMEM) for a in carry]
@@ -378,11 +333,8 @@
         [
             pltpu.VMEM((2, p.width, p.hid), BF16),
             pltpu.VMEM((2, p.width, p.hid), BF16),
-            pltpu.SemaphoreType.DMA((n_sem(p),)),
-            pltpu.SemaphoreType.DMA((n_sem(p),)),
         ],
-        flops=2 * 2 * p.pad * p.width * p.hid * 3,
-        nbytes=8 * p.width * p.hid + 12 * p.pad * p.hid + 16 * p.pad * p.width,
+        micros=5.0,
         name="down",
     )
 
@@ -430,33 +382,24 @@
                 gain_one, shift_one, gain_two, b_down,
             )
         ],
-        flops=p.pad * p.width * 30,
-        nbytes=p.pad * p.width * 28,
+        micros=2.6,
         name="middle",
     )
 
 
-def attention_backward(p, pos, weights, other, branch, rows_low, qkv, probs, ctx, received, carry):
+def attention_backward(p, pos, weights, other, branch, qkv, probs, carry):
     win, pad, lh, hd, cols = p.win, p.pad, p.local_heads, p.hd, p.cols
 
     def body(*refs):
         nw = len(weights)
         pos_ref, w_refs = refs[0], refs[1 : 1 + nw]
-        br_ref, low_ref, qkv_ref, prob_ref, ctx_ref = refs[1 + nw : 6 + nw]
-        rest = list(refs[6 + nw :])
-        nr = len(received) if received is not None else 0
-        got_refs, rest = rest[:nr], rest[nr:]
+        br_ref, qkv_ref, prob_ref = refs[1 + nw : 4 + nw]
+        rest = list(refs[4 + nw :])
         if carry is not None:
             carry_ref, rest = rest[0], rest[1:]
-        no = len(piece_shapes(p))
-        out_refs, rest = rest[:no], rest[no:]
-        n1_ref, bias_ref, wbuf, gbuf, gq, dc, wsem, sem = rest[:8]
-        loads = load_start(p, w_refs, wbuf, wsem, pos_ref, other)
-        if nr:
-            rbuf, rsem = rest[8:]
-            got = load_start(p, got_refs, rbuf, rsem, pos_ref, other)
-        wait_all(loads)
-        branch_low, low = br_ref[...], low_ref[...]
+        low_ref, n1_ref, bias_ref, wbuf, gq, dc = rest
+        gather_blocks(p, w_refs, wbuf, pos_ref, other)
+        branch_low = br_ref[...]
         total = None
         for b in range(2):
             dc[...] = dot(branch_low, wbuf[b, :, : p.cw]).astype(BF16)
@@ -484,55 +427,59 @@
             full = gq[...]
             bias_ref[b] = jnp.sum(full, axis=0, keepdims=True)
             gl = full.astype(BF16)
+            low_ref[b] = gl
             part = dot(gl, wbuf[b, :, p.off :], NT)
             total = part if total is None else total + part
-            g_out = dot(branch_low, ctx_ref[b], TN)
-            g_qkv = dot(low, gl, TN)
-            g = jnp.concatenate(
-                [
-                    g_out[:, : p.off],
-                    g_out[:, p.off : p.cw] + g_qkv[:, : p.cw - p.off],
-                    g_qkv[:, p.cw - p.off :],
-                ],
-                axis=1,
-            )
-            if nr:
-                if b == 0:
-                    wait_all(got)
-                g = g + rbuf[b].astype(F32)
-            gbuf[b] = g.astype(BF16)
         if carry is not None:
             total = total + carry_ref[...]
         n1_ref[...] = total
-        wait_all(store_start(p, gbuf, out_refs, sem, pos_ref, other))
-
-    ins = [(pos, SMEM)] + [(w, ANYS) for w in weights]
-    ins += [(a, VMEM) for a in (branch, rows_low, qkv, probs, ctx)]
-    ins += [(r, ANYS) for r in received or ()]
+
+    ins = [(pos, SMEM)] + [(w, VMEM) for w in weights]
+    ins += [(a, VMEM) for a in (branch, qkv, probs)]
     if carry is not None:
         ins.append((carry, VMEM))
-    scratch = [
-        pltpu.VMEM((2, p.width, 4 * cols), BF16),
-        pltpu.VMEM((2, p.width, 4 * cols), BF16),
-        pltpu.VMEM((pad, p.nq), F32),
-        pltpu.VMEM((pad, p.cw), BF16),
-        pltpu.SemaphoreType.DMA((n_sem(p),)),
-        pltpu.SemaphoreType.DMA((n_sem(p),)),
-    ]
-    if received is not None:
-        scratch += [
+    return call(
+        body,
+        [
+            (sds((2, pad, p.nq), BF16), VMEM),
+            (sds((pad, p.width), F32), VMEM),
+            (sds((2, 1, p.nq), F32), VMEM),
+        ],
+        ins,
+        [
             pltpu.VMEM((2, p.width, 4 * cols), BF16),
-            pltpu.SemaphoreType.DMA((n_sem(p),)),
-        ]
+            pltpu.VMEM((pad, p.nq), F32),
+            pltpu.VMEM((pad, p.cw), BF16),
+        ],
+        micros=7.5,
+        name="attn_bwd",
+    )
+
+
+def attention_grad(p, pos, other, branch, rows_low, ctx, low, received):
+    def body(*refs):
+        pos_ref, br_ref, rows_ref, ctx_ref, low_ref = refs[:5]
+        rest = list(refs[5:])
+        nr = len(received) if received is not None else 0
+        got_refs, rest = rest[:nr], rest[nr:]
+        out_refs, gbuf = rest[:-1], rest[-1]
+        for b in range(2):
+            g_out = dot(br_ref[...], ctx_ref[b], TN)
+            g_qkv = dot(rows_ref[...], low_ref[b], TN)
+            gbuf[b, :, : p.off] = g_out[:, : p.off]
+            gbuf[b, :, p.off : p.cw] = g_out[:, p.off :] + g_qkv[:, : p.cw - p.off]
+            gbuf[b, :, p.cw :] = g_qkv[:, p.cw - p.off :]
+        spread_blocks(p, gbuf, out_refs, pos_ref, other, got_refs if nr else None)
+
     return call(
         body,
-        [(s, ANYS) for s in piece_shapes(p)]
-        + [(sds((pad, p.width), F32), VMEM), (sds((2, 1, p.nq), F32), VMEM)],
-        ins,
-        scratch,
-        flops=2 * 2 * pad * p.width * 2 * (p.nq + p.cw) + 2 * p.images * lh * win * win * hd * 8,
-        nbytes=12 * p.width * p.width + pad * p.width * 20,
-        name="attn_bwd",
+        [(s, VMEM) for s in piece_shapes(p)],
+        [(pos, SMEM)]
+        + [(a, VMEM) for a in (branch, rows_low, ctx, low)]
+        + [(r, VMEM) for r in received or ()],
+        [pltpu.VMEM((2, p.width, 4 * p.cols), F32)],
+        micros=3.0,
+        name="attn_grad",
     )
 
 
@@ -550,8 +497,7 @@
         body,
         [(sds((p.rows, p.width), BF16), VMEM), vec, vec],
         [(a, VMEM) for a in (patches, back, logit, router, gain_one, mixed_grad)],
-        flops=p.pad * p.width * 20,
-        nbytes=p.pad * p.width * 12,
+        micros=2.0,
         name="exit",
     )
 
@@ -590,35 +536,50 @@
     return (z, x, y, c ^ 1)
 
 
+def after(v, *others):
+    return lax.optimization_barrier((v,) + others)[0]
+
+
 def add(a, b):
     return (a.astype(F32) + b.astype(F32)).astype(BF16)
 
 
-def gather_pieces(p, shard):
-    if not p.fast:
-        full = lax.all_gather(lax.all_gather(shard, "dp", axis=0, tiled=True), "head", axis=0)
-        return [(full[2 * i : 2 * i + 2],) for i in range(p.pairs)]
-    own = jnp.stack([shard] + [send(shard, along_z(s)) for s in (1, 2, 3)])
-    eight = jnp.stack([own, send(own, near)])
-    rest = send(eight, far)
-    return [(eight, rest), (send(eight, core), send(rest, core))]
-
-
-def scatter_pieces(p, grads):
-    if not p.fast:
-        stacked = jnp.concatenate(grads, axis=0)
-        part = lax.psum_scatter(stacked, "head", scatter_dimension=0, tiled=False)
-        return lax.psum_scatter(part, "dp", scatter_dimension=0, tiled=True).astype(F32)
-    keep, away = grads
-    got = send(away, far)
-    other = add(keep[1], got[1])
-    mine = keep[0]
-    got2 = send(other, near)
-    pieces = [add(add(mine[s], got[0, s]), got2[s]) for s in range(4)]
-    total = pieces[0].astype(F32)
-    for s in (1, 2, 3):
-        total = total + send(pieces[s], along_z(-s)).astype(F32)
-    return total
+def gather_whole(p, shard):
+    full = lax.all_gather(lax.all_gather(shard, "dp", axis=0, tiled=True), "head", axis=0)
+    return [(full[2 * i : 2 * i + 2],) for i in range(p.pairs)]
+
+
+def own_pieces(shard):
+    return jnp.stack([shard] + [send(shard, along_z(s)) for s in (1, 2, 3)])
+
+
+def both_cores(eight, rest, *others):
+    eight_out, rest_out = after(eight, *others), after(rest, *others)
+    return [(eight, rest), (send(eight_out, core), send(rest_out, core))]
+
+
+def scatter_whole(p, grads):
+    stacked = jnp.concatenate(grads, axis=0)
+    part = lax.psum_scatter(stacked, "head", scatter_dimension=0, tiled=False)
+    return lax.psum_scatter(part, "dp", scatter_dimension=0, tiled=True).astype(F32)
+
+
+class Scatter:
+    def __init__(self, keep, away):
+        self.keep, self.away = keep, away
+
+    def first(self):
+        got = send(self.away, far)
+        self.mine = add(self.keep[0], got[0])
+        self.other = add(self.keep[1], got[1])
+
+    def second(self):
+        got = send(self.other, near)
+        self.pieces = [add(self.mine[s], got[s]) for s in range(4)]
+
+    def third(self, *others):
+        got = [after(send(self.pieces[s], along_z(-s)), *others) for s in (1, 2, 3)]
+        return sum([g.astype(F32) for g in got], self.pieces[0].astype(F32))
 
 
 def gather_head(p, vector):
@@ -660,10 +621,8 @@
     pos = jnp.stack([dp_pos // 2, dp_pos % 2, head_pos % 2]).astype(jnp.int32)
 
     attn_shard = jnp.concatenate([w_out.T, w_query, w_key, w_value], axis=1)
-    attn_w = gather_pieces(p, attn_shard)
-    up_w = gather_pieces(p, w_up)
-    down_w = gather_pieces(p, w_down.T)
-    biases = gather_head(p, jnp.concatenate([b_query, b_value, b_up])).astype(F32)
+    bias_parts = after(jnp.concatenate([b_query, b_value, b_up]), attn_shard)
+    biases = gather_head(p, bias_parts).astype(F32)
     zeros = jnp.zeros((head, cols), F32)
     qkv_bias = jnp.concatenate(
         [zeros[:, : p.lo], biases[:, :cols], zeros, biases[:, cols : 2 * cols]], axis=1
@@ -687,12 +646,30 @@
     gain_one, shift_one, gain_two, shift_two = map(row, (gain_one, shift_one, gain_two, shift_two))
     router, b_out, b_down = row(router_w), row(b_out), row(b_down)
 
-    rows_low, gate, g_down_bias = entry_kernel(p, x_pad, og_pad, gain_one, shift_one, router)
+    fast = p.fast
+    if fast:
+        attn_own = after(own_pieces(attn_shard), biases)
+        x_in = after(x_pad, attn_own)
+        rows_low, gate, g_down_bias = entry_kernel(p, x_in, og_pad, gain_one, shift_one, router)
+        attn_eight = after(jnp.stack([attn_own, send(attn_own, near)]), rows_low)
+        attn_rest = send(attn_eight, far)
+        attn_w = both_cores(attn_eight, attn_rest)
+        up_own = after(own_pieces(after(w_up, attn_own)), attn_eight)
+        up_eight = after(jnp.stack([up_own, send(up_own, near)]), attn_rest)
+        up_rest = send(up_eight, far)
+        down_own = after(own_pieces(after(w_down.T, up_own)), up_eight)
+        down_eight = jnp.stack([down_own, send(down_own, near)])
+        down_rest = send(down_eight, far)
+    else:
+        rows_low, gate, g_down_bias = entry_kernel(p, x_pad, og_pad, gain_one, shift_one, router)
+        attn_w, up_w, down_w = (gather_whole(p, v) for v in (attn_shard, w_up, w_down.T))
     sel_gate = gate * sel_col
 
     qkvs, probs, ctxs, carry = [], [], [], None
     for i in range(p.pairs):
         tail = (x_pad, sel_gate, b_out, gain_two, shift_two) if i == p.pairs - 1 else None
+        if fast and i == 1:
+            rows_low = after(rows_low, up_eight, down_own)
         got = attention_forward(
             p, pos, attn_w[i], i, rows_low, qkv_bias[2 * i : 2 * i + 2], key_mask, carry, tail
         )
@@ -703,48 +680,88 @@
     attended, mixed, mlp_in = got[3], got[4], got[5]
 
     acts, slopes = [], []
+    if fast:
+        up_w = both_cores(up_eight, up_rest, mlp_in)
+    up_in = after(mlp_in, down_eight) if fast else mlp_in
     for i in range(p.pairs):
-        act, slope = up_kernel(p, pos, up_w[i], i, mlp_in, up_bias[2 * i : 2 * i + 2])
+        act, slope = up_kernel(p, pos, up_w[i], i, up_in, up_bias[2 * i : 2 * i + 2])
         acts.append(act)
         slopes.append(slope)
 
-    def reduced(lhs, rhs, name):
-        if not p.fast:
-            blocks = [weight_grad(p, pos, 0, lhs, r, None, name)[0] for r in rhs]
-            return scatter_pieces(p, blocks)
-        other = weight_grad(p, pos, 1, lhs, rhs[1], None, name)
-        got = [send(o, core) for o in other]
-        return scatter_pieces(p, weight_grad(p, pos, 0, lhs, rhs[0], got, name))
-
-    grad_down = reduced(og_pad, acts, "grad_down")
-
-    carry, lows, up_sums = None, [], []
-    for i in range(p.pairs):
-        got = down_kernel(p, pos, up_w[i], down_w[i], i, acts[i], slopes[i], og_pad, carry)
-        carry = (got[0], got[1])
-        lows.append(got[2])
-        up_sums.append(got[3][:, 0])
-    grad_up = reduced(mlp_in, lows, "grad_up")
-
-    tokens, mixed_grad, branch, logit, g_gain2, g_shift2, g_out_bias, g_router = middle_kernel(
-        p, x_pad, og_pad, mixed, carry[0], carry[1], attended, gate, sel_col,
-        (gain_one, shift_one, gain_two, b_down),
-    )
-
-    carry, blocks, sums, received = None, [None] * p.pairs, [None] * p.pairs, None
-    for i in reversed(range(p.pairs)):
-        got = attention_backward(
-            p, pos, attn_w[i], i if p.fast else 0, branch, rows_low, qkvs[i], probs[i], ctxs[i],
-            received, carry,
+    def backward(i, branch, carry):
+        return attention_backward(
+            p, pos, attn_w[i], i if fast else 0, branch, qkvs[i], probs[i], carry
         )
-        pieces, carry, sums[i] = got[:-2], got[-2], got[-1][:, 0]
-        blocks[i] = pieces
-        if p.fast and i == 1:
-            received = [send(o, core) for o in pieces]
-    grad_attn = scatter_pieces(p, blocks[0] if p.fast else [b[0] for b in blocks])
-    grad_patches, g_gain1, g_shift1 = exit_kernel(
-        p, x_pad, carry, logit, router, gain_one, mixed_grad
-    )
+
+    def down(i, grad_in, carry):
+        return down_kernel(p, pos, up_w[i], down_w[i], i, acts[i], slopes[i], grad_in, carry)
+
+    def middle(back, out):
+        return middle_kernel(
+            p, x_pad, og_pad, mixed, out, back, attended, gate, sel_col,
+            (gain_one, shift_one, gain_two, b_down),
+        )
+
+    def leave(back, logit, mixed_grad):
+        return exit_kernel(p, x_pad, back, logit, router, gain_one, mixed_grad)
+
+    if fast:
+        down_w = both_cores(down_eight, down_rest, acts[1])
+        gd1 = weight_grad(p, pos, 1, og_pad, acts[1], None, "grad_down")
+        gd1_got = [send(o, core) for o in gd1]
+        out_sum, back_sum, low0, sum0 = down(0, after(og_pad, *gd1), None)
+        gd0 = weight_grad(p, pos, 0, after(og_pad, low0), acts[0], gd1_got, "grad_down")
+        down_sum = Scatter(*gd0)
+        out_sum, back_sum, low1, sum1 = down(1, after(og_pad, *gd0), (out_sum, back_sum))
+        up_sums = [sum0[:, 0], sum1[:, 0]]
+        gu1 = weight_grad(p, pos, 1, mlp_in, low1, None, "grad_up")
+        gu1_got = [send(o, core) for o in gu1]
+        tokens, mixed_grad, branch, logit, g_gain2, g_shift2, g_out_bias, g_router = middle(
+            after(back_sum, *gu1), out_sum
+        )
+        gu0 = weight_grad(p, pos, 0, after(mlp_in, branch), low0, gu1_got, "grad_up")
+        up_sum = Scatter(*gu0)
+        down_sum.first()
+        low1, carry, bias1 = backward(1, after(branch, down_sum.other, *gu0), None)
+        ga1 = attention_grad(p, pos, 1, branch, rows_low, ctxs[1], low1, None)
+        ga1_got = [send(o, core) for o in ga1]
+        up_sum.first()
+        down_sum.second()
+        low0, carry, bias0 = backward(0, after(branch, up_sum.other, *ga1, *down_sum.pieces), carry)
+        ga0 = attention_grad(p, pos, 0, branch, rows_low, ctxs[0], low0, ga1_got)
+        attn_sum = Scatter(*ga0)
+        sums = [bias0[:, 0], bias1[:, 0]]
+        grad_patches, g_gain1, g_shift1 = leave(after(carry, *ga0), logit, mixed_grad)
+        grad_down = down_sum.third(grad_patches)
+        up_sum.second()
+        attn_sum.first()
+        attn_sum.second()
+        grad_up = up_sum.third(grad_patches)
+        grad_attn = attn_sum.third()
+    else:
+        carry, lows, up_sums, blocks, sums = None, [], [], [], []
+        for i in range(p.pairs):
+            got = down(i, og_pad, carry)
+            carry = (got[0], got[1])
+            lows.append(got[2])
+            up_sums.append(got[3][:, 0])
+        tokens, mixed_grad, branch, logit, g_gain2, g_shift2, g_out_bias, g_router = middle(
+            carry[1], carry[0]
+        )
+        carry = None
+        for i in range(p.pairs):
+            low, carry, bias = backward(i, branch, carry)
+            blocks += attention_grad(p, pos, 0, branch, rows_low, ctxs[i], low, None)
+            sums.append(bias[:, 0])
+        grad_patches, g_gain1, g_shift1 = leave(carry, logit, mixed_grad)
+        grad_down, grad_up, grad_attn = (
+            scatter_whole(p, g)
+            for g in (
+                [weight_grad(p, pos, 0, og_pad, a, None, "grad_down")[0] for a in acts],
+                [weight_grad(p, pos, 0, mlp_in, v, None, "grad_up")[0] for v in lows],
+                blocks,
+            )
+        )
 
     qkv_sums = jnp.concatenate(sums, axis=0)
     owned = jnp.concatenate(

time: 336 us -> 217 us (0.65)
  Pallas kernels: 117 us -> 58.7 us
  waiting for transfers between devices: 104 us -> 76.9 us
  local copies, waits for them, and re-layouts: 27.6 us -> 7.32 us
  starting transfers between devices: 65.8 us -> 59.4 us
  other arithmetic: 15.2 us -> 9.9 us
    pallas_call x15 -> x17, Pallas kernels: 117 us -> 58.7 us  [call(): pl.pallas_call(body, out_shape=[o for o, _ in outs], in_specs=[s for _, s...]
    ppermute x49, waiting for transfers between devices: 104 us -> 76.9 us  [send(): return lax.ppermute(v, ('dp', 'head'), table(move))]
    unnamed x94 -> x84, local copies, waits for them, and re-layouts: 16.9 us -> 2.46 us
    ppermute x49, starting transfers between devices: 65.8 us -> 59.4 us  [send(): return lax.ppermute(v, ('dp', 'head'), table(move))]
    broadcast_in_dim x7, local copies, waits for them, and re-layouts: 4.79 us -> 0.03 us  [row(): return v.astype(F32)[None, :]]
  transfers between devices with their start and end apart: 49 -> 49, of which waited for: 19 -> 23; matrix products, arithmetic and copies ran while one was open for 7% -> 6% of each run, Pallas kernels for 35% -> 26%
where the time goes in v2:
time: 217 us; the launch traced here: 214 us
  waiting for transfers between devices  76.9 us (35%)
  starting transfers between devices  59.4 us (27%)
  Pallas kernels  58.7 us (27%)
  other arithmetic  9.9 us (5%)
  local copies, waits for them, and re-layouts  7.32 us (3%)
    ppermute x49, waiting for transfers between devices, send(): return lax.ppermute(v, ('dp', 'head'), table(move))  76.9 us
    ppermute x49, starting transfers between devices, send(): return lax.ppermute(v, ('dp', 'head'), table(move))  59.4 us
    pallas_call x17, Pallas kernels, call(): pl.pallas_call(body, out_shape=[o for o, _ in outs], in_specs=[s for _, s...  58.7 us
  transfers between devices with their start and end apart: 49, of which 23 were waited for; matrix products, arithmetic and copies ran while one was open for 6% of the time, Pallas kernels for 26%

profile of v2, /device:TPU:0, one launch (start us, length us, event | category | flops | bytes accessed | tf_op | source)
XLA Modules:
  0.0 214.3 jit_solution(16940299406025116419)
XLA Ops:
  2.6 3.1 %collective-permute-start = (bf16[96,768]{1,0:T(8,128)(2,1)S(1)}, bf16[96,768]{1,0:T(8,128)(2,1)S(1)}, u32[]{:S(2)}, u32[]{:S(2)}) collective-permute-start(bf16[96,768]{1,0:T(8,128)(2,1)S(1)} %pad_maximum_fusion.6), channel_id=1, source_target_pairs={{0,8},{1,9},{2,10},{3,11},{4,12},{5,13},{6,14},{7,15},{8,16},{9,17... | collective-permute-start | bytes 442376 | tf_op jit(solution)/shard_map/ppermute | solution.py:520
  5.7 2.6 %collective-permute-start.1 = (bf16[96,768]{1,0:T(8,128)(2,1)S(1)}, bf16[96,768]{1,0:T(8,128)(2,1)S(1)}, u32[]{:S(2)}, u32[]{:S(2)}) collective-permute-start(bf16[96,768]{1,0:T(8,128)(2,1)S(1)} %pad_maximum_fusion.6), channel_id=1, source_target_pairs={{0,16},{1,17},{2,18},{3,19},{4,20},{5,21},{6,22},{7,23},{8,24},{9,... | collective-permute-start | bytes 442376 | tf_op jit(solution)/shard_map/ppermute | solution.py:520
  20.4 7.7 %collective-permute-done.5 = bf16[4,96,768]{2,1,0:T(8,128)(2,1)S(1)} collective-permute-done((bf16[4,96,768]{2,1,0:T(8,128)(2,1)S(1)}, bf16[4,96,768]{2,1,0:T(8,128)(2,1)S(1)}, u32[]{:S(2)}, u32[]{:S(2)}) %collective-permute-start.5) | collective-permute-done | bytes 589856 | tf_op jit(solution)/shard_map/ppermute | solution.py:520
  29.8 3.6 %collective-permute-start.9 = (bf16[96,768]{1,0:T(8,128)(2,1)S(1)}, bf16[96,768]{1,0:T(8,128)(2,1)S(1)}, u32[]{:S(2)}, u32[]{:S(2)}) collective-permute-start(bf16[96,768]{1,0:T(8,128)(2,1)S(1)} %copy-done.26), channel_id=1, source_target_pairs={{0,8},{1,9},{2,10},{3,11},{4,12},{5,13},{6,14},{7,15},{8,16},{9,17... | collective-permute-start | bytes 442376 | tf_op jit(solution)/shard_map/ppermute | solution.py:520
  35.9 3.4 %collective-permute-done.9 = bf16[96,768]{1,0:T(8,128)(2,1)S(1)} collective-permute-done((bf16[96,768]{1,0:T(8,128)(2,1)S(1)}, bf16[96,768]{1,0:T(8,128)(2,1)S(1)}, u32[]{:S(2)}, u32[]{:S(2)}) %collective-permute-start.9) | collective-permute-done | bytes 147488 | tf_op jit(solution)/shard_map/ppermute | solution.py:520
  39.3 4.0 %collective-permute-done.10 = bf16[96,768]{1,0:T(8,128)(2,1)S(1)} collective-permute-done((bf16[96,768]{1,0:T(8,128)(2,1)S(1)}, bf16[96,768]{1,0:T(8,128)(2,1)S(1)}, u32[]{:S(2)}, u32[]{:S(2)}) %collective-permute-start.10) | collective-permute-done | bytes 147488 | tf_op jit(solution)/shard_map/ppermute | solution.py:520
  45.1 2.9 %collective-permute-start.13 = (bf16[96,768]{1,0:T(8,128)(2,1)S(1)}, bf16[96,768]{1,0:T(8,128)(2,1)S(1)}, u32[]{:S(2)}, u32[]{:S(2)}) collective-permute-start(bf16[96,768]{1,0:T(8,128)(2,1)S(1)} %bitcast.155), channel_id=1, source_target_pairs={{0,8},{1,9},{2,10},{3,11},{4,12},{5,13},{6,14},{7,15},{8,16},{9,17... | collective-permute-start | bytes 442376 | tf_op jit(solution)/shard_map/ppermute | solution.py:520
  50.9 3.2 %collective-permute-done.13 = bf16[96,768]{1,0:T(8,128)(2,1)S(1)} collective-permute-done((bf16[96,768]{1,0:T(8,128)(2,1)S(1)}, bf16[96,768]{1,0:T(8,128)(2,1)S(1)}, u32[]{:S(2)}, u32[]{:S(2)}) %collective-permute-start.13) | collective-permute-done | bytes 147488 | tf_op jit(solution)/shard_map/ppermute | solution.py:520
  54.1 5.2 %collective-permute-done.14 = bf16[96,768]{1,0:T(8,128)(2,1)S(1)} collective-permute-done((bf16[96,768]{1,0:T(8,128)(2,1)S(1)}, bf16[96,768]{1,0:T(8,128)(2,1)S(1)}, u32[]{:S(2)}, u32[]{:S(2)}) %collective-permute-start.14) | collective-permute-done | bytes 147488 | tf_op jit(solution)/shard_map/ppermute | solution.py:520
  60.9 5.0 %attn_fwd.2 = (bf16[2,400,640]{2,1,0:T(8,128)(2,1)S(1)}, bf16[12,208,208]{2,1,0:T(8,128)(2,1)S(1)}, bf16[2,400,256]{2,1,0:T(8,128)(2,1)S(1)}, f32[400,768]{1,0:T(8,128)S(1)}) custom-call(s32[3]{0:T(128)S(1)} %pad_add_fusion.refs_0_, bf16[2,4,96,768]{3,2,1,0:T(8,128)(2,1)S(1)} %pad_maximum_fusion.refs_1_, ...), custom_call_target="tpu_custom_call" | custom-call | flops 54999998464 | tf_op jit(solution)/shard_map/attn_fwd/pallas_call | solution.py:35
  65.9 10.8 %collective-permute-done.19 = bf16[4,96,768]{2,1,0:T(8,128)(2,1)S(1)} collective-permute-done((bf16[4,96,768]{2,1,0:T(8,128)(2,1)S(1)}, bf16[4,96,768]{2,1,0:T(8,128)(2,1)S(1)}, u32[]{:S(2)}, u32[]{:S(2)}) %collective-permute-start.19) | collective-permute-done | bytes 589856 | tf_op jit(solution)/shard_map/ppermute | solution.py:520
  78.1 5.4 %attn_fwd.3 = (bf16[2,400,640]{2,1,0:T(8,128)(2,1)S(1)}, bf16[12,208,208]{2,1,0:T(8,128)(2,1)S(1)}, bf16[2,400,256]{2,1,0:T(8,128)(2,1)S(1)}, f32[400,768]{1,0:T...) custom-call(s32[3]{0:T(128)S(1)} %pad_add_fusion.refs_0_, ...), custom_call_target="tpu_custom_call" | custom-call | flops 54999998464 | tf_op jit(solution)/shard_map/attn_fwd/pallas_call | solution.py:35
  88.2 2.7 %up.2 = (bf16[2,400,768]{2,1,0:T(8,128)(2,1)S(1)}, bf16[2,400,768]{2,1,0:T(8,128)(2,1)S(1)}) custom-call(s32[3]{0:T(128)S(1)} %pad_add_fusion.refs_0_, bf16[2,4,96,768]{3,2,1,0:T(8,128)(2,1)S(1)} %collective-permute-done.16.refs_1_, bf16[2,4,96,768]{3,2,1,0:T(8,128)(2,1)S(1)} %collective-permute-done.18.refs_2_, ...), custom_call_target="tpu_custom_call" | custom-call | flops 24999999488 | tf_op jit(solution)/shard_map/up/pallas_call | solution.py:35
  94.1 4.0 %down.2 = (f32[400,768]{1,0:T(8,128)S(1)}, f32[400,768]{1,0:T(8,128)S(1)}, bf16[2,400,768]{2,1,0:T(8,128)(2,1)S(1)}, f32[2,1,768]{2,1,0:T(1,128)S(1)}) custom-call(s32[3]{0:T(128)S(1)} %pad_add_fusion.refs_0_, bf16[2,4,96,768]{3,2,1,0:T(8,128)(2,1)S(1)} %pad_maximum_fusion.1.refs_1_, bf16[2,4,96,768]{3,2,1,0:T(8,128)(2,1)S(1)} %collective-permute-done.17.refs_2_, ...), custom_call_target="tpu_custom_call" | custom-call | flops 49999998976 | tf_op jit(solution)/shard_map/down/pallas_call | solution.py:35
  98.7 2.5 %grad_down.3 = (bf16[2,4,96,768]{3,2,1,0:T(8,128)(2,1)S(1)}, bf16[2,4,96,768]{3,2,1,0:T(8,128)(2,1)S(1)}) custom-call(s32[3]{0:T(128)S(1)} %pad_add_fusion.refs_0_, bf16[400,768]{1,0:T(8,128)(2,1)S(1)} %copy-done.6, bf16[2,400,768]{2,1,0:T(8,128)(2,1)S(1)} %get-tuple-element.123.refs_5_.refs_2_, bf16[2,4,96,768]{3,2,1,0:T(8,128)(2,1)S(1)} %collective-permute-done.23.refs_3_, ...), custom_call_target="tpu_custom_call" | custom-call | flops 23000000512 | tf_op jit(solution)/shard_map/grad_down/pallas_call | solution.py:35
  102.7 4.1 %down.3 = (f32[400,768]{1,0:T(8,128)S(1)}, f32[400,768]{1,0:T(8,128)S(1)}, bf16[2,400,768]{2,1,0:T(8,128)(2,1)S(1)}, f32[2,1,768]{2,1,0:T(1,128)S(1)}) custom-call(s32[3]{0:T(128)S(1)} %pad_add_fusion.refs_0_, bf16[2,4,96,768]{3,2,1,0:T(8,128)(2,1)S(1)} %collective-permute-done.16.refs_1_, bf16[2,4,96,768]{3,2,1,0:T(8,128)(2,1)S(1)} %collective-permute-done.18.refs_2_, ...), custom_call_target="tpu_custom_call" | custom-call | flops 49999998976 | tf_op jit(solution)/shard_map/down/pallas_call | solution.py:35
  109.7 2.7 %middle.1 = (bf16[394,768]{1,0:T(8,128)(2,1)}, f32[400,768]{1,0:T(8,128)S(1)}, bf16[400,768]{1,0:T(8,128)(2,1)S(1)}, f32[400,1]{1,0:T(8,128)S(1)}, f32[1,768]{1,...) custom-call(bf16[400,768]{1,0:T(8,128)(2,1)S(1)} %copy-done.3, ...), custom_call_target="tpu_custom_call" | custom-call | flops 25999998976 | tf_op jit(solution)/shard_map/middle/pallas_call | solution.py:35
  113.0 4.5 %collective-permute-done.28 = bf16[2,4,96,768]{3,2,1,0:T(8,128)(2,1)S(1)} collective-permute-done((bf16[2,4,96,768]{3,2,1,0:T(8,128)(2,1)S(1)}, bf16[2,4,96,768]{3,2,1,0:T(8,128)(2,1)S(1)}, u32[]{:S(2)}, u32[]{:S(2)}) %collective-permute-start.28) | collective-permute-done | bytes 1179680 | tf_op jit(solution)/shard_map/ppermute | solution.py:520
  119.2 2.5 %grad_up.3 = (bf16[2,4,96,768]{3,2,1,0:T(8,128)(2,1)S(1)}, bf16[2,4,96,768]{3,2,1,0:T(8,128)(2,1)S(1)}) custom-call(s32[3]{0:T(128)S(1)} %pad_add_fusion.refs_0_, bf16[400,768]{1,0:T(8,128)(2,1)S(1)} %get-tuple-element.144.refs_3_.refs_1_, bf16[2,400,768]{2,1,0:T(8,128)(2,1)S(1)} %get-tuple-element.128.refs_2_, ...), custom_call_target="tpu_custom_call" | custom-call | flops 23000000512 | tf_op jit(solution)/shard_map/grad_up/pallas_call | solution.py:35
  122.5 7.2 %attn_bwd.2 = (bf16[2,400,640]{2,1,0:T(8,128)(2,1)S(1)}, f32[400,768]{1,0:T(8,128)S(1)}, f32[2,1,640]{2,1,0:T(1,128)S(1)}) custom-call(s32[3]{0:T(128)S(1)} %pad_add_fusion.refs_0_, bf16[2,4,96,768]{3,2,1,0:T(8,128)(2,1)S(1)} %copy-done.21, bf16[2,4,96,768]{3,2,1,0:T(8,128)(2,1)S(1)} %collective-permute-done.8.refs_2_, ...), custom_call_target="tpu_custom_call" | custom-call | flops 74999996416 | tf_op jit(solution)/shard_map/attn_bwd/pallas_call | solution.py:35
  129.6 2.6 %attn_grad.2 = (bf16[2,4,96,768]{3,2,1,0:T(8,128)(2,1)S(1)}, bf16[2,4,96,768]{3,2,1,0:T(8,128)(2,1)S(1)}) custom-call(s32[3]{0:T(128)S(1)} %pad_add_fusion.refs_0_, bf16[400,768]{1,0:T(8,128)(2,1)S(1)} %get-tuple-element.154.refs_3_.refs_1_, bf16[400,768]{1,0:T(8,128)(2,1)S(1)} %copy-done.23, bf16[2,400,256]{2,1,0:T(8,128)(2,1)S(1)} %get-tuple-element.147.refs_3_, ...), custom_call_target="tpu_custom_call" | custom-call | flops 30000001024 | tf_op jit(solution)/shard_map/attn_grad/pallas_call | solution.py:35
  133.8 4.9 %collective-permute-done.27 = bf16[2,4,96,768]{3,2,1,0:T(8,128)(2,1)S(1)} collective-permute-done((bf16[2,4,96,768]{3,2,1,0:T(8,128)(2,1)S(1)}, bf16[2,4,96,768]{3,2,1,0:T(8,128)(2,1)S(1)}, u32[]{:S(2)}, u32[]{:S(2)}) %collective-permute-start.27) | collective-permute-done | bytes 1179680 | tf_op jit(solution)/shard_map/ppermute | solution.py:520
  139.8 7.5 %attn_bwd.3 = (bf16[2,400,640]{2,1,0:T(8,128)(2,1)S(1)}, f32[400,768]{1,0:T(8,128)S(1)}, f32[2,1,640]{2,1,0:T(1,128)S(1)}) custom-call(s32[3]{0:T(128)S(1)} %pad_add_fusion.refs_0_, bf16[2,4,96,768]{3,2,1,0:T(8,128)(2,1)S(1)} %copy-done.1, bf16[2,4,96,768]{3,2,1,0:T(8,128)(2,1)S(1)} %copy-done.19, bf16[400,768]{1,0:T(8,128)(2,1)S(1)} %get-tuple-element.154.refs_3_.refs_1_, ...), custom_call_target="tpu_custom_call" | custom-call | flops 74999996416 | tf_op jit(solution)/shard_map/attn_bwd/pallas_call | solution.py:35
  147.4 3.0 %attn_grad.3 = (bf16[2,4,96,768]{3,2,1,0:T(8,128)(2,1)S(1)}, bf16[2,4,96,768]{3,2,1,0:T(8,128)(2,1)S(1)}) custom-call(s32[3]{0:T(128)S(1)} %pad_add_fusion.refs_0_, bf16[400,768]{1,0:T(8,128)(2,1)S(1)} %get-tuple-element.154.refs_3_.refs_1_, bf16[400,768]{1,0:T(8,128)(2,1)S(1)} %copy-done.23, bf16[2,400,256]{2,1,0:T(8,128)(2,1)S(1)} %get-tuple-element.159.refs_3_, ...), custom_call_target="tpu_custom_call" | custom-call | flops 30000001024 | tf_op jit(solution)/shard_map/attn_grad/pallas_call | solution.py:35
  157.1 4.4 %collective-permute-start.46 = (bf16[96,768]{1,0:T(8,128)(2,1)}, bf16[96,768]{1,0:T(8,128)(2,1)S(1)}, u32[]{:S(2)}, u32[]{:S(2)}) collective-permute-start(bf16[96,768]{1,0:T(8,128)(2,1)} %get-tuple-element.238), channel_id=1, source_target_pairs={{0,24},{1,25},{2,26},{3,27},{4,28},{5,29},{6,30},{7,31},{8,0},{9,1... | collective-permute-start | bytes 442376 | tf_op jit(solution)/shard_map/ppermute | solution.py:520
  162.1 5.1 %collective-permute-done.33 = f32[6528]{0:T(1024)S(1)} collective-permute-done((f32[6528]{0:T(1024)S(1)}, f32[6528]{0:T(1024)S(1)}, u32[]{:S(2)}, u32[]{:S(2)}) %collective-permute-start.33) | collective-permute-done | bytes 26144 | tf_op jit(solution)/shard_map/ppermute | solution.py:520
  168.5 2.5 %collective-permute-done.34 = f32[6528]{0:T(1024)S(1)} collective-permute-done((f32[6528]{0:T(1024)S(1)}, f32[6528]{0:T(1024)S(1)}, u32[]{:S(2)}, u32[]{:S(2)}) %collective-permute-start.34) | collective-permute-done | bytes 26144 | tf_op jit(solution)/shard_map/ppermute | solution.py:520
  171.1 3.7 %collective-permute-start.35 = (f32[6528]{0:T(1024)S(1)}, f32[6528]{0:T(1024)S(1)}, u32[]{:S(2)}, u32[]{:S(2)}) collective-permute-start(f32[6528]{0:T(1024)S(1)} %add.143), channel_id=1, source_target_pairs={{0,8},{1,9},{2,10},{3,11},{4,12},{5,13},{6,14},{7,15},{8,0},{9,1},... | collective-permute-start | bytes 78344 | tf_op jit(solution)/shard_map/ppermute | solution.py:520
  185.0 3.2 %collective-permute-start.43 = (bf16[96,768]{1,0:T(8,128)(2,1)S(1)}, bf16[96,768]{1,0:T(8,128)(2,1)S(1)}, u32[]{:S(2)}, u32[]{:S(2)}) collective-permute-start(bf16[96,768]{1,0:T(8,128)(2,1)S(1)} %get-tuple-element.230), channel_id=1, source_target_pairs={{0,24},{1,25},{2,26},{3,27},{4,28},{5,29},{6,30},{7,31},{8,0},{9,1... | collective-permute-start | bytes 442376 | tf_op jit(solution)/shard_map/ppermute | solution.py:520
  189.5 2.9 %collective-permute-done.43 = bf16[96,768]{1,0:T(8,128)(2,1)S(1)} collective-permute-done((bf16[96,768]{1,0:T(8,128)(2,1)S(1)}, bf16[96,768]{1,0:T(8,128)(2,1)S(1)}, u32[]{:S(2)}, u32[]{:S(2)}) %collective-permute-start.43) | collective-permute-done | bytes 147488 | tf_op jit(solution)/shard_map/ppermute | solution.py:520
  192.4 9.6 %collective-permute-done.44 = bf16[96,768]{1,0:T(8,128)(2,1)S(1)} collective-permute-done((bf16[96,768]{1,0:T(8,128)(2,1)S(1)}, bf16[96,768]{1,0:T(8,128)(2,1)S(1)}, u32[]{:S(2)}, u32[]{:S(2)}) %collective-permute-start.44) | collective-permute-done | bytes 147488 | tf_op jit(solution)/shard_map/ppermute | solution.py:520
  207.4 4.9 %collective-permute-done.40 = bf16[96,768]{1,0:T(8,128)(2,1)S(1)} collective-permute-done((bf16[96,768]{1,0:T(8,128)(2,1)S(1)}, bf16[96,768]{1,0:T(8,128)(2,1)S(1)}, u32[]{:S(2)}, u32[]{:S(2)}) %collective-permute-start.40) | collective-permute-done | bytes 147488 | tf_op jit(solution)/shard_map/ppermute | solution.py:520
  (237 shorter events, 71.0 us)
Async XLA Ops:
  2.6 14.2 %collective-permute-start = (bf16[96,768]{1,0:T(8,128)(2,1)S(1)}, bf16[96,768]{1,0:T(8,128)(2,1)S(1)}, u32[]{:S(2)}, u32[]{:S(2)}) collective-permute-start(bf16[96,768]{1,0:T(8,128)(2,1)S(1)} %pad_maximum_fusion.6), channel_id=1, source_target_pairs={{0,8},{1,9},{2,10},{3,11},{4,12},{5,13},{6,14},{7,15},{8,16},{9,17... | collective-permute-start | bytes 442376 | tf_op jit(solution)/shard_map/ppermute | solution.py:520
  5.7 12.3 %collective-permute-start.1 = (bf16[96,768]{1,0:T(8,128)(2,1)S(1)}, bf16[96,768]{1,0:T(8,128)(2,1)S(1)}, u32[]{:S(2)}, u32[]{:S(2)}) collective-permute-start(bf16[96,768]{1,0:T(8,128)(2,1)S(1)} %pad_maximum_fusion.6), channel_id=1, source_target_pairs={{0,16},{1,17},{2,18},{3,19},{4,20},{5,21},{6,22},{7,23},{8,24},{9,... | collective-permute-start | bytes 442376 | tf_op jit(solution)/shard_map/ppermute | solution.py:520
  8.3 9.7 %collective-permute-start.2 = (bf16[96,768]{1,0:T(8,128)(2,1)S(1)}, bf16[96,768]{1,0:T(8,128)(2,1)S(1)}, u32[]{:S(2)}, u32[]{:S(2)}) collective-permute-start(bf16[96,768]{1,0:T(8,128)(2,1)S(1)} %pad_maximum_fusion.6), channel_id=1, source_target_pairs={{0,24},{1,25},{2,26},{3,27},{4,28},{5,29},{6,30},{7,31},{8,0},{9,1... | collective-permute-start | bytes 442376 | tf_op jit(solution)/shard_map/ppermute | solution.py:520
  18.1 9.9 %collective-permute-start.5 = (bf16[4,96,768]{2,1,0:T(8,128)(2,1)S(1)}, bf16[4,96,768]{2,1,0:T(8,128)(2,1)S(1)}, u32[]{:S(2)}, u32[]{:S(2)}) collective-permute-start(bf16[4,96,768]{2,1,0:T(8,128)(2,1)S(1)} %pad_maximum_fusion.3), channel_id=1, source_target_pairs={{0,4},{1,3},{2,6},{3,1},{4,0},{5,7},{6,2},{7,5},{8,12},{9,11},{10,... | collective-permute-start | bytes 1769480 | tf_op jit(solution)/shard_map/ppermute | solution.py:520
  28.2 31.4 %collective-permute-start.7 = (bf16[2,4,96,768]{3,2,1,0:T(8,128)(2,1)S(1)}, bf16[2,4,96,768]{3,2,1,0:T(8,128)(2,1)S(1)}, u32[]{:S(2)}, u32[]{:S(2)}) collective-permute-start(bf16[2,4,96,768]{3,2,1,0:T(8,128)(2,1)S(1)} %pad_maximum_fusion.refs_1_), channel_id=1, source_target_pairs={{0,2},{1,5},{2,0},{3,7},{4,6},{5,1},{6,4},{7,3},{8,10},{9,13},{10,... | collective-permute-start | bytes 3538952 | tf_op jit(solution)/shard_map/ppermute | solution.py:520
  29.8 9.5 %collective-permute-start.9 = (bf16[96,768]{1,0:T(8,128)(2,1)S(1)}, bf16[96,768]{1,0:T(8,128)(2,1)S(1)}, u32[]{:S(2)}, u32[]{:S(2)}) collective-permute-start(bf16[96,768]{1,0:T(8,128)(2,1)S(1)} %copy-done.26), channel_id=1, source_target_pairs={{0,8},{1,9},{2,10},{3,11},{4,12},{5,13},{6,14},{7,15},{8,16},{9,17... | collective-permute-start | bytes 442376 | tf_op jit(solution)/shard_map/ppermute | solution.py:520
  33.5 9.9 %collective-permute-start.10 = (bf16[96,768]{1,0:T(8,128)(2,1)S(1)}, bf16[96,768]{1,0:T(8,128)(2,1)S(1)}, u32[]{:S(2)}, u32[]{:S(2)}) collective-permute-start(bf16[96,768]{1,0:T(8,128)(2,1)S(1)} %copy-done.26), channel_id=1, source_target_pairs={{0,16},{1,17},{2,18},{3,19},{4,20},{5,21},{6,22},{7,23},{8,24},{9,... | collective-permute-start | bytes 442376 | tf_op jit(solution)/shard_map/ppermute | solution.py:520
  43.4 16.0 %collective-permute-start.12 = (bf16[4,96,768]{2,1,0:T(8,128)(2,1)S(1)}, bf16[4,96,768]{2,1,0:T(8,128)(2,1)S(1)}, u32[]{:S(2)}, u32[]{:S(2)}) collective-permute-start(bf16[4,96,768]{2,1,0:T(8,128)(2,1)S(1)} %pad_maximum_fusion.4), channel_id=1, source_target_pairs={{0,4},{1,3},{2,6},{3,1},{4,0},{5,7},{6,2},{7,5},{8,12},{9,11},{10,... | collective-permute-start | bytes 1769480 | tf_op jit(solution)/shard_map/ppermute | solution.py:520
  48.0 11.3 %collective-permute-start.14 = (bf16[96,768]{1,0:T(8,128)(2,1)S(1)}, bf16[96,768]{1,0:T(8,128)(2,1)S(1)}, u32[]{:S(2)}, u32[]{:S(2)}) collective-permute-start(bf16[96,768]{1,0:T(8,128)(2,1)S(1)} %bitcast.156), channel_id=1, source_target_pairs={{0,16},{1,17},{2,18},{3,19},{4,20},{5,21},{6,22},{7,23},{8,24},{9,... | collective-permute-start | bytes 442376 | tf_op jit(solution)/shard_map/ppermute | solution.py:520
  49.9 9.4 %collective-permute-start.15 = (bf16[96,768]{1,0:T(8,128)(2,1)S(1)}, bf16[96,768]{1,0:T(8,128)(2,1)S(1)}, u32[]{:S(2)}, u32[]{:S(2)}) collective-permute-start(bf16[96,768]{1,0:T(8,128)(2,1)S(1)} %bitcast.157), channel_id=1, source_target_pairs={{0,24},{1,25},{2,26},{3,27},{4,28},{5,29},{6,30},{7,31},{8,0},{9,1... | collective-permute-start | bytes 442376 | tf_op jit(solution)/shard_map/ppermute | solution.py:520
  54.1 24.0 %collective-permute-start.6 = (bf16[2,4,96,768]{3,2,1,0:T(8,128)(2,1)S(1)}, bf16[2,4,96,768]{3,2,1,0:T(8,128)(2,1)S(1)}, u32[]{:S(2)}, u32[]{:S(2)}) collective-permute-start(bf16[2,4,96,768]{3,2,1,0:T(8,128)(2,1)S(1)} %pad_maximum_fusion.refs_1_), channel_id=1, source_target_pairs={{0,1},{1,0},{2,3},{3,2},{4,5},{5,4},{6,7},{7,6},{8,9},{9,8},{10,11... | collective-permute-start | bytes 3538952 | tf_op jit(solution)/shard_map/ppermute | solution.py:520
  59.5 24.0 %collective-permute-start.17 = (bf16[2,4,96,768]{3,2,1,0:T(8,128)(2,1)S(1)}, bf16[2,4,96,768]{3,2,1,0:T(8,128)(2,1)S(1)}, u32[]{:S(2)}, u32[]{:S(2)}) collective-permute-start(bf16[2,4,96,768]{3,2,1,0:T(8,128)(2,1)S(1)} %pad_maximum_fusion.1.refs_1_), channel_id=1, source_target_pairs={{0,2},{1,5},{2,0},{3,7},{4,6},{5,1},{6,4},{7,3},{8,10},{9,13},{10,... | collective-permute-start | bytes 3538952 | tf_op jit(solution)/shard_map/ppermute | solution.py:520
  60.4 16.3 %collective-permute-start.19 = (bf16[4,96,768]{2,1,0:T(8,128)(2,1)S(1)}, bf16[4,96,768]{2,1,0:T(8,128)(2,1)S(1)}, u32[]{:S(2)}, u32[]{:S(2)}) collective-permute-start(bf16[4,96,768]{2,1,0:T(8,128)(2,1)S(1)} %pad_maximum_fusion.5), channel_id=1, source_target_pairs={{0,4},{1,3},{2,6},{3,1},{4,0},{5,7},{6,2},{7,5},{8,12},{9,11},{10,... | collective-permute-start | bytes 1769480 | tf_op jit(solution)/shard_map/ppermute | solution.py:520
  60.9 17.2 %collective-permute-start.8 = (bf16[2,4,96,768]{3,2,1,0:T(8,128)(2,1)S(1)}, bf16[2,4,96,768]{3,2,1,0:T(8,128)(2,1)S(1)}, u32[]{:S(2)}, u32[]{:S(2)}) collective-permute-start(bf16[2,4,96,768]{3,2,1,0:T(8,128)(2,1)S(1)} %collective-permute-done.7.refs_2_), channel_id=1, source_target_pairs={{0,1},{1,0},{2,3},{3,2},{4,5},{5,4},{6,7},{7,6},{8,9},{9,8},{10,11... | collective-permute-start | bytes 3538952 | tf_op jit(solution)/shard_map/ppermute | solution.py:520
  76.8 17.3 %collective-permute-start.21 = (bf16[2,4,96,768]{3,2,1,0:T(8,128)(2,1)S(1)}, bf16[2,4,96,768]{3,2,1,0:T(8,128)(2,1)S(1)}, u32[]{:S(2)}, u32[]{:S(2)}) collective-permute-start(bf16[2,4,96,768]{3,2,1,0:T(8,128)(2,1)S(1)} %pad_maximum_fusion.2.refs_3_), channel_id=1, source_target_pairs={{0,2},{1,5},{2,0},{3,7},{4,6},{5,1},{6,4},{7,3},{8,10},{9,13},{10,... | collective-permute-start | bytes 3538952 | tf_op jit(solution)/shard_map/ppermute | solution.py:520
  101.2 16.3 %collective-permute-start.28 = (bf16[2,4,96,768]{3,2,1,0:T(8,128)(2,1)S(1)}, bf16[2,4,96,768]{3,2,1,0:T(8,128)(2,1)S(1)}, u32[]{:S(2)}, u32[]{:S(2)}) collective-permute-start(bf16[2,4,96,768]{3,2,1,0:T(8,128)(2,1)S(1)} %get-tuple-element.131), channel_id=1, source_target_pairs={{0,2},{1,5},{2,0},{3,7},{4,6},{5,1},{6,4},{7,3},{8,10},{9,13},{10,... | collective-permute-start | bytes 3538952 | tf_op jit(solution)/shard_map/ppermute | solution.py:520
  109.1 10.2 %collective-permute-start.25 = (bf16[2,4,96,768]{3,2,1,0:T(8,128)(2,1)S(1)}, bf16[2,4,96,768]{3,2,1,0:T(8,128)(2,1)S(1)}, u32[]{:S(2)}, u32[]{:S(2)}) collective-permute-start(bf16[2,4,96,768]{3,2,1,0:T(8,128)(2,1)S(1)} %get-tuple-element.138), channel_id=1, source_target_pairs={{0,1},{1,0},{2,3},{3,2},{4,5},{5,4},{6,7},{7,6},{8,9},{9,8},{10,11... | collective-permute-start | bytes 3538952 | tf_op jit(solution)/shard_map/ppermute | solution.py:520
  109.3 10.0 %collective-permute-start.26 = (bf16[2,4,96,768]{3,2,1,0:T(8,128)(2,1)S(1)}, bf16[2,4,96,768]{3,2,1,0:T(8,128)(2,1)S(1)}, u32[]{:S(2)}, u32[]{:S(2)}) collective-permute-start(bf16[2,4,96,768]{3,2,1,0:T(8,128)(2,1)S(1)} %get-tuple-element.139), channel_id=1, source_target_pairs={{0,1},{1,0},{2,3},{3,2},{4,5},{5,4},{6,7},{7,6},{8,9},{9,8},{10,11... | collective-permute-start | bytes 3538952 | tf_op jit(solution)/shard_map/ppermute | solution.py:520
  117.8 15.1 %collective-permute-start.29 = (bf16[4,96,768]{2,1,0:T(8,128)(2,1)S(1)}, bf16[4,96,768]{2,1,0:T(8,128)(2,1)S(1)}, u32[]{:S(2)}, u32[]{:S(2)}) collective-permute-start(bf16[4,96,768]{2,1,0:T(8,128)(2,1)S(1)} %get-tuple-element.229), channel_id=1, source_target_pairs={{0,4},{1,3},{2,6},{3,1},{4,0},{5,7},{6,2},{7,5},{8,12},{9,11},{10,... | collective-permute-start | bytes 1769480 | tf_op jit(solution)/shard_map/ppermute | solution.py:520
  121.7 16.9 %collective-permute-start.27 = (bf16[2,4,96,768]{3,2,1,0:T(8,128)(2,1)S(1)}, bf16[2,4,96,768]{3,2,1,0:T(8,128)(2,1)S(1)}, u32[]{:S(2)}, u32[]{:S(2)}) collective-permute-start(bf16[2,4,96,768]{3,2,1,0:T(8,128)(2,1)S(1)} %get-tuple-element.146), channel_id=1, source_target_pairs={{0,2},{1,5},{2,0},{3,7},{4,6},{5,1},{6,4},{7,3},{8,10},{9,13},{10,... | collective-permute-start | bytes 3538952 | tf_op jit(solution)/shard_map/ppermute | solution.py:520
  132.3 15.0 %collective-permute-start.30 = (bf16[2,4,96,768]{3,2,1,0:T(8,128)(2,1)S(1)}, bf16[2,4,96,768]{3,2,1,0:T(8,128)(2,1)S(1)}, u32[]{:S(2)}, u32[]{:S(2)}) collective-permute-start(bf16[2,4,96,768]{3,2,1,0:T(8,128)(2,1)S(1)} %get-tuple-element.152), channel_id=1, source_target_pairs={{0,1},{1,0},{2,3},{3,2},{4,5},{5,4},{6,7},{7,6},{8,9},{9,8},{10,11... | collective-permute-start | bytes 3538952 | tf_op jit(solution)/shard_map/ppermute | solution.py:520
  132.4 14.9 %collective-permute-start.31 = (bf16[2,4,96,768]{3,2,1,0:T(8,128)(2,1)S(1)}, bf16[2,4,96,768]{3,2,1,0:T(8,128)(2,1)S(1)}, u32[]{:S(2)}, u32[]{:S(2)}) collective-permute-start(bf16[2,4,96,768]{3,2,1,0:T(8,128)(2,1)S(1)} %get-tuple-element.153), channel_id=1, source_target_pairs={{0,1},{1,0},{2,3},{3,2},{4,5},{5,4},{6,7},{7,6},{8,9},{9,8},{10,11... | collective-permute-start | bytes 3538952 | tf_op jit(solution)/shard_map/ppermute | solution.py:520
  150.3 31.1 %collective-permute-start.37 = (bf16[2,4,96,768]{3,2,1,0:T(8,128)(2,1)S(1)}, bf16[2,4,96,768]{3,2,1,0:T(8,128)(2,1)}, u32[]{:S(2)}, u32[]{:S(2)}) collective-permute-start(bf16[2,4,96,768]{3,2,1,0:T(8,128)(2,1)S(1)} %get-tuple-element.162), channel_id=1, source_target_pairs={{0,2},{1,5},{2,0},{3,7},{4,6},{5,1},{6,4},{7,3},{8,10},{9,13},{10,... | collective-permute-start | bytes 3538952 | tf_op jit(solution)/shard_map/ppermute | solution.py:520
  156.4 10.8 %collective-permute-start.33 = (f32[6528]{0:T(1024)S(1)}, f32[6528]{0:T(1024)S(1)}, u32[]{:S(2)}, u32[]{:S(2)}) collective-permute-start(f32[6528]{0:T(1024)S(1)} %pad_maximum_fusion.9), channel_id=1, source_target_pairs={{0,2},{1,3},{2,0},{3,1},{4,6},{5,7},{6,4},{7,5},{8,10},{9,11},{10,... | collective-permute-start | bytes 78344 | tf_op jit(solution)/shard_map/ppermute | solution.py:520
  157.1 17.8 %collective-permute-start.46 = (bf16[96,768]{1,0:T(8,128)(2,1)}, bf16[96,768]{1,0:T(8,128)(2,1)S(1)}, u32[]{:S(2)}, u32[]{:S(2)}) collective-permute-start(bf16[96,768]{1,0:T(8,128)(2,1)} %get-tuple-element.238), channel_id=1, source_target_pairs={{0,24},{1,25},{2,26},{3,27},{4,28},{5,29},{6,30},{7,31},{8,0},{9,1... | collective-permute-start | bytes 442376 | tf_op jit(solution)/shard_map/ppermute | solution.py:520
  161.4 14.6 %collective-permute-start.47 = (bf16[96,768]{1,0:T(8,128)(2,1)S(1)}, bf16[96,768]{1,0:T(8,128)(2,1)S(1)}, u32[]{:S(2)}, u32[]{:S(2)}) collective-permute-start(bf16[96,768]{1,0:T(8,128)(2,1)S(1)} %get-tuple-element.237), channel_id=1, source_target_pairs={{0,16},{1,17},{2,18},{3,19},{4,20},{5,21},{6,22},{7,23},{8,24},{9,... | collective-permute-start | bytes 442376 | tf_op jit(solution)/shard_map/ppermute | solution.py:520
  162.1 13.9 %collective-permute-start.48 = (bf16[96,768]{1,0:T(8,128)(2,1)S(1)}, bf16[96,768]{1,0:T(8,128)(2,1)S(1)}, u32[]{:S(2)}, u32[]{:S(2)}) collective-permute-start(bf16[96,768]{1,0:T(8,128)(2,1)S(1)} %get-tuple-element.236), channel_id=1, source_target_pairs={{0,8},{1,9},{2,10},{3,11},{4,12},{5,13},{6,14},{7,15},{8,16},{9,17... | collective-permute-start | bytes 442376 | tf_op jit(solution)/shard_map/ppermute | solution.py:520
  174.8 10.1 %collective-permute-start.42 = (bf16[4,96,768]{2,1,0:T(8,128)(2,1)}, bf16[4,96,768]{2,1,0:T(8,128)(2,1)S(1)}, u32[]{:S(2)}, u32[]{:S(2)}) collective-permute-start(bf16[4,96,768]{2,1,0:T(8,128)(2,1)} %get-tuple-element.225), channel_id=1, source_target_pairs={{0,4},{1,3},{2,6},{3,1},{4,0},{5,7},{6,2},{7,5},{8,12},{9,11},{10,... | collective-permute-start | bytes 1769480 | tf_op jit(solution)/shard_map/ppermute | solution.py:520
  183.0 19.0 %collective-permute-start.38 = (bf16[4,96,768]{2,1,0:T(8,128)(2,1)S(1)}, bf16[4,96,768]{2,1,0:T(8,128)(2,1)S(1)}, u32[]{:S(2)}, u32[]{:S(2)}) collective-permute-start(bf16[4,96,768]{2,1,0:T(8,128)(2,1)S(1)} %get-tuple-element.227), channel_id=1, source_target_pairs={{0,4},{1,3},{2,6},{3,1},{4,0},{5,7},{6,2},{7,5},{8,12},{9,11},{10,... | collective-permute-start | bytes 1769480 | tf_op jit(solution)/shard_map/ppermute | solution.py:520
  188.2 13.8 %collective-permute-start.44 = (bf16[96,768]{1,0:T(8,128)(2,1)S(1)}, bf16[96,768]{1,0:T(8,128)(2,1)S(1)}, u32[]{:S(2)}, u32[]{:S(2)}) collective-permute-start(bf16[96,768]{1,0:T(8,128)(2,1)S(1)} %get-tuple-element.232), channel_id=1, source_target_pairs={{0,16},{1,17},{2,18},{3,19},{4,20},{5,21},{6,22},{7,23},{8,24},{9,... | collective-permute-start | bytes 442376 | tf_op jit(solution)/shard_map/ppermute | solution.py:520
  188.8 13.2 %collective-permute-start.45 = (bf16[96,768]{1,0:T(8,128)(2,1)S(1)}, bf16[96,768]{1,0:T(8,128)(2,1)S(1)}, u32[]{:S(2)}, u32[]{:S(2)}) collective-permute-start(bf16[96,768]{1,0:T(8,128)(2,1)S(1)} %get-tuple-element.231), channel_id=1, source_target_pairs={{0,8},{1,9},{2,10},{3,11},{4,12},{5,13},{6,14},{7,15},{8,16},{9,17... | collective-permute-start | bytes 442376 | tf_op jit(solution)/shard_map/ppermute | solution.py:520
  202.2 10.0 %collective-permute-start.40 = (bf16[96,768]{1,0:T(8,128)(2,1)S(1)}, bf16[96,768]{1,0:T(8,128)(2,1)S(1)}, u32[]{:S(2)}, u32[]{:S(2)}) collective-permute-start(bf16[96,768]{1,0:T(8,128)(2,1)S(1)} %get-tuple-element.235), channel_id=1, source_target_pairs={{0,16},{1,17},{2,18},{3,19},{4,20},{5,21},{6,22},{7,23},{8,24},{9,... | collective-permute-start | bytes 442376 | tf_op jit(solution)/shard_map/ppermute | solution.py:520
  (53 other events, 468.2 us)

commit v3 on v2

--- a/solution.py
+++ b/solution.py
@@ -13,7 +13,8 @@
 BF16 = jnp.bfloat16
 VMEM = pl.BlockSpec(memory_space=pltpu.VMEM)
 SMEM = pl.BlockSpec(memory_space=pltpu.SMEM)
-WEIGHT = 1.0e10
+EXIT = 2.0
+WEIGHT = 4.0e9
 LIMIT = 20 * 1024 * 1024
 INV_SQRT2 = 0.7071067811865476
 INV_SQRT2PI = 0.3989422804014327
@@ -100,29 +101,31 @@
     return found
 
 
-def gather_blocks(p, refs, buf, pos_ref, other):
+def gather_blocks(p, refs, buf, pos_ref, other, lanes=slice(None), turned=False):
     if not p.fast:
-        buf[...] = refs[0][...]
+        buf[...] = refs[0][:, :, lanes]
         return
     for b3, b2, zz, yy, row in piece_list(p, pos_ref, other):
-        buf[yy, pl.ds(row, p.piece), :] = refs[b3][b2, zz]
-
-
-def spread_blocks(p, buf, refs, pos_ref, other, received=None):
+        i, j = (zz, b2) if turned else (b2, zz)
+        buf[yy, pl.ds(row, p.piece), :] = refs[b3][i, j, :, lanes]
+
+
+def spread_blocks(p, buf, refs, pos_ref, other, received=None, turned=False):
     if not p.fast:
         refs[0][...] = buf[...].astype(BF16)
         return
     for b3, b2, zz, yy, row in piece_list(p, pos_ref, other):
+        i, j = (zz, b2) if turned else (b2, zz)
         part = buf[yy, pl.ds(row, p.piece), :]
         if received is not None:
-            part = part + received[b3][b2, zz].astype(F32)
-        refs[b3][b2, zz] = part.astype(BF16)
-
-
-def piece_shapes(p):
+            part = part + received[b3][i, j].astype(F32)
+        refs[b3][i, j] = part.astype(BF16)
+
+
+def piece_shapes(p, lanes, turned=False):
     if p.fast:
-        return [sds((2, 4, p.piece, p.width), BF16)] * 2
-    return [sds((2, p.width, p.width), BF16)]
+        return [sds(((4, 2) if turned else (2, 4)) + (p.piece, lanes), BF16)] * 2
+    return [sds((2, p.width, lanes), BF16)]
 
 
 def entry_kernel(p, patches, out_grad, gain_one, shift_one, router):
@@ -263,25 +266,36 @@
     )
 
 
-def weight_grad(p, pos, other, lhs, rhs, received, name):
+def weight_grad(p, pos, other, pairs, received, name, turned=False):
+    lanes = max(at + rhs.shape[2] for _, rhs, at in pairs)
+    starts = [at for _, _, at in pairs]
+
     def body(*refs):
-        pos_ref, l_ref, r_ref = refs[:3]
-        rest = list(refs[3:])
+        pos_ref, rest = refs[0], list(refs[1:])
+        ops, rest = rest[: 2 * len(pairs)], rest[2 * len(pairs) :]
         nr = len(received) if received is not None else 0
         got_refs, rest = rest[:nr], rest[nr:]
-        no = len(piece_shapes(p))
-        out_refs, rest = rest[:no], rest[no:]
-        (gbuf,) = rest
-        left = l_ref[...]
+        out_refs, gbuf = rest[:-1], rest[-1]
         for b in range(2):
-            gbuf[b] = dot(left, r_ref[b], TN)
-        spread_blocks(p, gbuf, out_refs, pos_ref, other, got_refs if nr else None)
-
-    return call(
-        body,
-        [(s, VMEM) for s in piece_shapes(p)],
-        [(pos, SMEM), (lhs, VMEM), (rhs, VMEM)] + [(r, VMEM) for r in received or ()],
-        [pltpu.VMEM((2, p.width, p.hid), F32)],
+            done = 0
+            for i, at in enumerate(starts):
+                g = dot(ops[2 * i][...], ops[2 * i + 1][b], TN)
+                end = at + g.shape[1]
+                if at < done:
+                    gbuf[b, :, at:done] += g[:, : done - at]
+                    gbuf[b, :, done:end] = g[:, done - at :]
+                else:
+                    gbuf[b, :, at:end] = g
+                done = end
+        spread_blocks(p, gbuf, out_refs, pos_ref, other, got_refs if nr else None, turned)
+
+    return call(
+        body,
+        [(s, VMEM) for s in piece_shapes(p, lanes, turned)],
+        [(pos, SMEM)]
+        + [(a, VMEM) for lhs, rhs, _ in pairs for a in (lhs, rhs)]
+        + [(r, VMEM) for r in received or ()],
+        [pltpu.VMEM((2, p.width, lanes), F32)],
         micros=2.3,
         name=name,
     )
@@ -297,7 +311,7 @@
             out_in, back_in = rest[:2]
             rest = rest[2:]
         out_ref, back_ref, low_ref, bias_ref, ubuf, dbuf = rest
-        gather_blocks(p, d_refs, dbuf, pos_ref, other)
+        gather_blocks(p, d_refs, dbuf, pos_ref, other, turned=True)
         gather_blocks(p, u_refs, ubuf, pos_ref, other)
         og = og_ref[...]
         for b in range(2):
@@ -387,118 +401,176 @@
     )
 
 
-def attention_backward(p, pos, weights, other, branch, qkv, probs, carry):
-    win, pad, lh, hd, cols = p.win, p.pad, p.local_heads, p.hd, p.cols
+def attention_values(p, pos, weights, other, branch, probs):
+    win, pad, lh, hd = p.win, p.pad, p.local_heads, p.hd
+    lead = p.cw - p.cols
 
     def body(*refs):
         nw = len(weights)
         pos_ref, w_refs = refs[0], refs[1 : 1 + nw]
-        br_ref, qkv_ref, prob_ref = refs[1 + nw : 4 + nw]
-        rest = list(refs[4 + nw :])
+        br_ref, prob_ref, dc_ref, dv_ref, bias_ref, wbuf, gv = refs[1 + nw :]
+        gather_blocks(p, w_refs, wbuf, pos_ref, other, slice(0, p.cw))
+        for b in range(2):
+            dc_ref[b] = dot(br_ref[...], wbuf[b]).astype(BF16)
+            gv[...] = jnp.zeros((pad, p.cw), F32)
+            for img in range(p.images):
+                here = slice(p.base[img], p.base[img] + win)
+                got = [jnp.zeros((win, lead), F32)] if lead else []
+                for j in range(lh):
+                    prob = prob_ref[(b * p.images + img) * lh + j]
+                    got.append(dot(prob, dc_ref[b, here, hd * j : hd * j + hd], TN))
+                gv[here, :] += jnp.concatenate(got, axis=1)
+            full = gv[...]
+            bias_ref[b] = jnp.sum(full, axis=0, keepdims=True)
+            dv_ref[b] = full.astype(BF16)
+
+    return call(
+        body,
+        [
+            (sds((2, pad, p.cw), BF16), VMEM),
+            (sds((2, pad, p.cw), BF16), VMEM),
+            (sds((2, 1, p.cw), F32), VMEM),
+        ],
+        [(pos, SMEM)] + [(w, VMEM) for w in weights] + [(branch, VMEM), (probs, VMEM)],
+        [pltpu.VMEM((2, p.width, p.cw), BF16), pltpu.VMEM((pad, p.cw), F32)],
+        micros=2.5,
+        name="attn_values",
+    )
+
+
+def attention_backward(p, pos, weights, other, dc, dv, qkv, probs, carry):
+    win, pad, lh, hd, cols = p.win, p.pad, p.local_heads, p.hd, p.cols
+    lead = p.cw - p.cols
+
+    def body(*refs):
+        nw = len(weights)
+        pos_ref, w_refs = refs[0], refs[1 : 1 + nw]
+        dc_ref, dv_ref, qkv_ref, prob_ref = refs[1 + nw : 5 + nw]
+        rest = list(refs[5 + nw :])
         if carry is not None:
             carry_ref, rest = rest[0], rest[1:]
-        low_ref, n1_ref, bias_ref, wbuf, gq, dc = rest
-        gather_blocks(p, w_refs, wbuf, pos_ref, other)
-        branch_low = br_ref[...]
+        low_ref, n1_ref, bias_ref, wbuf, gq = rest
+        gather_blocks(p, w_refs, wbuf, pos_ref, other, slice(p.off, None))
         total = None
         for b in range(2):
-            dc[...] = dot(branch_low, wbuf[b, :, : p.cw]).astype(BF16)
-            gq[...] = jnp.zeros((pad, p.nq), F32)
+            gq[...] = jnp.zeros((pad, 2 * cols), F32)
             for img in range(p.images):
                 first = p.base[img]
                 here = slice(first, first + win)
-                dqs, dks, dvs = [], [], []
+                dqs, dks = [], []
                 for j in range(lh):
                     qs = p.lo + hd * j
                     q = qkv_ref[b, here, qs : qs + hd]
                     k = qkv_ref[b, here, qs + cols : qs + cols + hd]
                     v = qkv_ref[b, here, qs + 2 * cols : qs + 2 * cols + hd]
-                    d = dc[here, hd * j : hd * j + hd]
-                    prob = prob_ref[(b * p.images + img) * lh + j]
-                    soft = prob.astype(F32)
+                    d = dc_ref[b, here, hd * j : hd * j + hd]
+                    soft = prob_ref[(b * p.images + img) * lh + j].astype(F32)
                     pg = dot(d, v, NT)
                     row = jnp.sum(soft * pg, axis=-1, keepdims=True)
                     s = (soft * (pg - row) * p.scale).astype(BF16)
                     dqs.append(dot(s, k))
                     dks.append(dot(s, q, TN))
-                    dvs.append(dot(prob, d, TN))
-                lead = [jnp.zeros((win, p.lo), F32)] if p.lo else []
-                gq[here, :] += jnp.concatenate(lead + dqs + dks + dvs, axis=1)
+                gq[here, :] += jnp.concatenate(dqs + dks, axis=1)
             full = gq[...]
             bias_ref[b] = jnp.sum(full, axis=0, keepdims=True)
-            gl = full.astype(BF16)
-            low_ref[b] = gl
-            part = dot(gl, wbuf[b, :, p.off :], NT)
+            low = full.astype(BF16)
+            low_ref[b] = low
+            start = [jnp.zeros((pad, p.lo), BF16)] if p.lo else []
+            gl = jnp.concatenate(start + [low, dv_ref[b][:, lead:]], axis=1)
+            part = dot(gl, wbuf[b], NT)
             total = part if total is None else total + part
         if carry is not None:
             total = total + carry_ref[...]
         n1_ref[...] = total
 
     ins = [(pos, SMEM)] + [(w, VMEM) for w in weights]
-    ins += [(a, VMEM) for a in (branch, qkv, probs)]
+    ins += [(a, VMEM) for a in (dc, dv, qkv, probs)]
     if carry is not None:
         ins.append((carry, VMEM))
     return call(
         body,
         [
-            (sds((2, pad, p.nq), BF16), VMEM),
+            (sds((2, pad, 2 * cols), BF16), VMEM),
             (sds((pad, p.width), F32), VMEM),
-            (sds((2, 1, p.nq), F32), VMEM),
+            (sds((2, 1, 2 * cols), F32), VMEM),
         ],
         ins,
-        [
-            pltpu.VMEM((2, p.width, 4 * cols), BF16),
-            pltpu.VMEM((pad, p.nq), F32),
-            pltpu.VMEM((pad, p.cw), BF16),
-        ],
-        micros=7.5,
+        [pltpu.VMEM((2, p.width, p.nq), BF16), pltpu.VMEM((pad, 2 * cols), F32)],
+        micros=6.0,
         name="attn_bwd",
     )
 
 
-def attention_grad(p, pos, other, branch, rows_low, ctx, low, received):
+def exit_kernel(p, patches, back, logit, router, gain_one, mixed_grad, common, query, value, up):
+    half = p.cols
+    at = p.cw - p.cols
+
     def body(*refs):
-        pos_ref, br_ref, rows_ref, ctx_ref, low_ref = refs[:5]
-        rest = list(refs[5:])
-        nr = len(received) if received is not None else 0
-        got_refs, rest = rest[:nr], rest[nr:]
-        out_refs, gbuf = rest[:-1], rest[-1]
-        for b in range(2):
-            g_out = dot(br_ref[...], ctx_ref[b], TN)
-            g_qkv = dot(rows_ref[...], low_ref[b], TN)
-            gbuf[b, :, : p.off] = g_out[:, : p.off]
-            gbuf[b, :, p.off : p.cw] = g_out[:, p.off :] + g_qkv[:, : p.cw - p.off]
-            gbuf[b, :, p.cw :] = g_qkv[:, p.cw - p.off :]
-        spread_blocks(p, gbuf, out_refs, pos_ref, other, got_refs if nr else None)
-
-    return call(
-        body,
-        [(s, VMEM) for s in piece_shapes(p)],
-        [(pos, SMEM)]
-        + [(a, VMEM) for a in (branch, rows_low, ctx, low)]
-        + [(r, VMEM) for r in received or ()],
-        [pltpu.VMEM((2, p.width, 4 * p.cols), F32)],
-        micros=3.0,
-        name="attn_grad",
-    )
-
-
-def exit_kernel(p, patches, back, logit, router, gain_one, mixed_grad):
-    def body(x_ref, n_ref, l_ref, r_ref, g_ref, mg_ref, out_ref, gg_ref, gs_ref):
+        x_ref, n_ref, l_ref, r_ref, g_ref, mg_ref = refs[:6]
+        c_refs = refs[6 : 6 + len(common)]
+        rest = list(refs[6 + len(common) :])
+        q_refs, v_refs, u_refs = (rest[i * p.pairs : (i + 1) * p.pairs] for i in range(3))
+        out_ref, *vec_refs = rest[3 * p.pairs :]
         xhat, rstd = norm_parts(x_ref[...].astype(F32))
         grad = n_ref[...] + l_ref[...] * r_ref[...]
-        gg_ref[...] = jnp.sum(grad * xhat, axis=0, keepdims=True)
-        gs_ref[...] = jnp.sum(grad, axis=0, keepdims=True)
+        g_gain = jnp.sum(grad * xhat, axis=0, keepdims=True)
+        g_shift = jnp.sum(grad, axis=0, keepdims=True)
         total = mg_ref[...] + norm_back(grad * g_ref[...], xhat, rstd)
         out_ref[...] = total[: p.rows].astype(BF16)
-
-    vec = (sds((1, p.width), F32), VMEM)
-    return call(
-        body,
-        [(sds((p.rows, p.width), BF16), VMEM), vec, vec],
-        [(a, VMEM) for a in (patches, back, logit, router, gain_one, mixed_grad)],
-        micros=2.0,
+        for i in range(p.pairs):
+            vec = vec_refs[i]
+            vec[...] = jnp.zeros(vec.shape, F32)
+            for j, r in enumerate([g_gain, g_shift] + [c[...] for c in c_refs]):
+                vec[j : j + 1, :] = r
+            for b in range(2):
+                row = 8 + 2 * b
+                vec[row : row + 1, : 2 * half] = q_refs[i][b]
+                vec[row : row + 1, half : 2 * half] = v_refs[i][b][:, at:]
+                vec[row + 1 : row + 2, :] = u_refs[i][b]
+
+    return call(
+        body,
+        [(sds((p.rows, p.width), BF16), VMEM)] + [(sds((12, p.width), F32), VMEM)] * p.pairs,
+        [
+            (a, VMEM)
+            for a in (
+                [patches, back, logit, router, gain_one, mixed_grad]
+                + list(common)
+                + list(query)
+                + list(value)
+                + list(up)
+            )
+        ],
+        micros=EXIT,
         name="exit",
+    )
+
+
+def halves_kernel(keep, got):
+    def body(k_ref, g_ref, mine_ref, other_ref):
+        mine_ref[...] = (k_ref[0].astype(F32) + g_ref[0].astype(F32)).astype(BF16)
+        other_ref[...] = (k_ref[1].astype(F32) + g_ref[1].astype(F32)).astype(BF16)
+
+    return call(
+        body,
+        [(sds(keep.shape[1:], BF16), VMEM)] * 2,
+        [(keep, VMEM), (got, VMEM)],
+        micros=4.0,
+        name="halves",
+    )
+
+
+def parts_kernel(mine, got):
+    def body(m_ref, g_ref, *part_refs):
+        for i, ref in enumerate(part_refs):
+            ref[...] = (m_ref[i].astype(F32) + g_ref[i].astype(F32)).astype(BF16)
+
+    return call(
+        body,
+        [(sds(mine.shape[1:], BF16), VMEM)] * 4,
+        [(mine, VMEM), (got, VMEM)],
+        micros=4.0,
+        name="parts",
     )
 
 
@@ -568,18 +640,18 @@
     def __init__(self, keep, away):
         self.keep, self.away = keep, away
 
-    def first(self):
-        got = send(self.away, far)
-        self.mine = add(self.keep[0], got[0])
-        self.other = add(self.keep[1], got[1])
-
-    def second(self):
-        got = send(self.other, near)
-        self.pieces = [add(self.mine[s], got[s]) for s in range(4)]
-
-    def third(self, *others):
-        got = [after(send(self.pieces[s], along_z(-s)), *others) for s in (1, 2, 3)]
-        return sum([g.astype(F32) for g in got], self.pieces[0].astype(F32))
+    def first(self, *others):
+        got = after(send(self.away, far), *others)
+        self.mine, self.other = halves_kernel(self.keep, got)
+
+    def second(self, *others):
+        got = after(send(self.other, near), *others)
+        self.pieces = parts_kernel(self.mine, got)
+
+
+def along_chips(pieces, *others):
+    got = [after(send(pieces[s], along_z(-s)), *others) for s in (1, 2, 3)]
+    return sum([g.astype(F32) for g in got], pieces[0].astype(F32))
 
 
 def gather_head(p, vector):
@@ -589,22 +661,31 @@
     return jnp.concatenate([pair, send(pair, core)], axis=0)
 
 
-def sum_vectors(p, common, owned):
-    n = common.shape[0]
-    if not p.fast:
-        total = lax.psum(common, ("dp", "head"))
-        mine = lax.psum_scatter(owned, "head", scatter_dimension=0, tiled=False)
-        return total, lax.psum(mine, "dp")
-    got = send(jnp.concatenate([common, owned[2], owned[3]]), core)
-    m = owned.shape[1]
-    vec = jnp.concatenate([common, owned[0], owned[1]]) + got
-    keep = vec[: n + m]
-    got = send(jnp.concatenate([vec[:n], vec[n + m :]]), lambda z, x, y, c: (z, x, y ^ 1, c))
-    keep = keep + got
-    keep = keep + send(keep, lambda z, x, y, c: (z, x ^ 1, y, c))
-    keep = keep + send(keep, lambda z, x, y, c: (z ^ 1, x, y, c))
-    keep = keep + send(keep, lambda z, x, y, c: (z ^ 2, x, y, c))
-    return keep[:n], keep[n:]
+def sum_vectors(p, vecs):
+    total = lax.psum(vecs[0][:8], ("dp", "head"))
+    owned = jnp.concatenate([v[8:] for v in vecs]).reshape(p.head, 2, p.width)
+    mine = lax.psum_scatter(owned, "head", scatter_dimension=0, tiled=False)
+    return jnp.concatenate([total, lax.psum(mine, "dp")])
+
+
+class VectorSum:
+    def __init__(self, vecs):
+        self.keep, self.away = vecs
+
+    def over_cores(self, *others):
+        self.vec = self.keep + after(send(self.away, core), *others)
+
+    def over_z(self, step, *others):
+        got = send(self.vec, lambda z, x, y, c: (z ^ step, x, y, c))
+        self.vec = self.vec + after(got, *others)
+
+    def over_xy(self, *others):
+        mine, away = self.vec[:10], jnp.concatenate([self.vec[:8], self.vec[10:]])
+        along_x = send(mine, lambda z, x, y, c: (z, x ^ 1, y, c))
+        along_y = send(away, lambda z, x, y, c: (z, x, y ^ 1, c))
+        across = send(away, lambda z, x, y, c: (z, x ^ 1, y ^ 1, c))
+        along_x, along_y, across = (after(v, *others) for v in (along_x, along_y, across))
+        return (mine + along_x) + (along_y + across)
 
 
 def on_device(
@@ -648,18 +729,23 @@
 
     fast = p.fast
     if fast:
-        attn_own = after(own_pieces(attn_shard), biases)
+        down_one = w_down.T
+        down_near = send(down_one, near)
+        attn_own = after(own_pieces(attn_shard), biases, down_near)
         x_in = after(x_pad, attn_own)
         rows_low, gate, g_down_bias = entry_kernel(p, x_in, og_pad, gain_one, shift_one, router)
-        attn_eight = after(jnp.stack([attn_own, send(attn_own, near)]), rows_low)
+        up_one = after(w_up, attn_own)
+        up_z = [send(up_one, along_z(s)) for s in (1, 2, 3)]
+        attn_eight = after(jnp.stack([attn_own, send(attn_own, near)]), rows_low, up_z[0])
         attn_rest = send(attn_eight, far)
         attn_w = both_cores(attn_eight, attn_rest)
-        up_own = after(own_pieces(after(w_up, attn_own)), attn_eight)
+        up_own = after(jnp.stack([w_up] + up_z), attn_eight)
+        down_pair = after(jnp.stack([down_one, down_near]), up_own)
+        down_z = [send(down_pair, along_z(s)) for s in (1, 2, 3)]
         up_eight = after(jnp.stack([up_own, send(up_own, near)]), attn_rest)
         up_rest = send(up_eight, far)
-        down_own = after(own_pieces(after(w_down.T, up_own)), up_eight)
-        down_eight = jnp.stack([down_own, send(down_own, near)])
-        down_rest = send(down_eight, far)
+        attn_w[1] = tuple(after(w, up_rest) for w in attn_w[1])
+        up_w = both_cores(up_eight, up_rest)
     else:
         rows_low, gate, g_down_bias = entry_kernel(p, x_pad, og_pad, gain_one, shift_one, router)
         attn_w, up_w, down_w = (gather_whole(p, v) for v in (attn_shard, w_up, w_down.T))
@@ -669,7 +755,8 @@
     for i in range(p.pairs):
         tail = (x_pad, sel_gate, b_out, gain_two, shift_two) if i == p.pairs - 1 else None
         if fast and i == 1:
-            rows_low = after(rows_low, up_eight, down_own)
+            down_eight = jnp.stack([down_pair] + [after(v, carry) for v in down_z])
+            down_rest = send(down_eight, far)
         got = attention_forward(
             p, pos, attn_w[i], i, rows_low, qkv_bias[2 * i : 2 * i + 2], key_mask, carry, tail
         )
@@ -680,18 +767,25 @@
     attended, mixed, mlp_in = got[3], got[4], got[5]
 
     acts, slopes = [], []
-    if fast:
-        up_w = both_cores(up_eight, up_rest, mlp_in)
-    up_in = after(mlp_in, down_eight) if fast else mlp_in
+    up_in = mlp_in
     for i in range(p.pairs):
         act, slope = up_kernel(p, pos, up_w[i], i, up_in, up_bias[2 * i : 2 * i + 2])
         acts.append(act)
         slopes.append(slope)
 
-    def backward(i, branch, carry):
+    def values(i, branch):
+        return attention_values(p, pos, attn_w[i], i if fast else 0, branch, probs[i])
+
+    def backward(i, dc, dv, carry):
         return attention_backward(
-            p, pos, attn_w[i], i if fast else 0, branch, qkvs[i], probs[i], carry
+            p, pos, attn_w[i], i if fast else 0, dc, dv, qkvs[i], probs[i], carry
         )
+
+    def grads(pairs, received, name, other, turned=False):
+        return weight_grad(p, pos, other, pairs, received, name, turned)
+
+    def attention_pairs(i, dv, low):
+        return [(branch, ctxs[i], 0), (rows_low, dv, p.off), (rows_low, low, 2 * cols)]
 
     def down(i, grad_in, carry):
         return down_kernel(p, pos, up_w[i], down_w[i], i, acts[i], slopes[i], grad_in, carry)
@@ -702,98 +796,101 @@
             (gain_one, shift_one, gain_two, b_down),
         )
 
-    def leave(back, logit, mixed_grad):
-        return exit_kernel(p, x_pad, back, logit, router, gain_one, mixed_grad)
+    def leave(back, qsums, vsums, up_sums):
+        common = (g_router, g_out_bias, g_gain2, g_shift2, g_down_bias)
+        return exit_kernel(
+            p, x_pad, back, logit, router, gain_one, mixed_grad, common, qsums, vsums, up_sums
+        )
 
     if fast:
         down_w = both_cores(down_eight, down_rest, acts[1])
-        gd1 = weight_grad(p, pos, 1, og_pad, acts[1], None, "grad_down")
+        gd1 = grads([(og_pad, acts[1], 0)], None, "grad_down", 1)
         gd1_got = [send(o, core) for o in gd1]
         out_sum, back_sum, low0, sum0 = down(0, after(og_pad, *gd1), None)
-        gd0 = weight_grad(p, pos, 0, after(og_pad, low0), acts[0], gd1_got, "grad_down")
+        gd0 = grads([(after(og_pad, low0), acts[0], 0)], gd1_got, "grad_down", 0)
         down_sum = Scatter(*gd0)
         out_sum, back_sum, low1, sum1 = down(1, after(og_pad, *gd0), (out_sum, back_sum))
-        up_sums = [sum0[:, 0], sum1[:, 0]]
-        gu1 = weight_grad(p, pos, 1, mlp_in, low1, None, "grad_up")
+        tokens, mixed_grad, branch, logit, g_gain2, g_shift2, g_out_bias, g_router = middle(
+            back_sum, out_sum
+        )
+        gu1 = grads([(after(mlp_in, branch), low1, 0)], None, "grad_up", 1)
         gu1_got = [send(o, core) for o in gu1]
-        tokens, mixed_grad, branch, logit, g_gain2, g_shift2, g_out_bias, g_router = middle(
-            after(back_sum, *gu1), out_sum
-        )
-        gu0 = weight_grad(p, pos, 0, after(mlp_in, branch), low0, gu1_got, "grad_up")
+        dc1, dv1, vsum1 = values(1, after(branch, *gu1))
+        dc0, dv0, vsum0 = values(0, after(branch, dv1))
+        down_sum.first()
+        gu1_got = [after(g, dv0, down_sum.other) for g in gu1_got]
+        gu0 = grads([(mlp_in, low0, 0)], gu1_got, "grad_up", 0)
         up_sum = Scatter(*gu0)
-        down_sum.first()
-        low1, carry, bias1 = backward(1, after(branch, down_sum.other, *gu0), None)
-        ga1 = attention_grad(p, pos, 1, branch, rows_low, ctxs[1], low1, None)
+        low1, carry, qsum1 = backward(1, after(dc1, *gu0), dv1, None)
+        ga1 = grads(attention_pairs(1, dv1, low1), None, "grad_attn", 1)
         ga1_got = [send(o, core) for o in ga1]
-        up_sum.first()
         down_sum.second()
-        low0, carry, bias0 = backward(0, after(branch, up_sum.other, *ga1, *down_sum.pieces), carry)
-        ga0 = attention_grad(p, pos, 0, branch, rows_low, ctxs[0], low0, ga1_got)
+        low0, carry, qsum0 = backward(0, after(dc0, *ga1, *down_sum.pieces), dv0, carry)
+        up_sum.first(low0)
+        ga1_got = [after(g, up_sum.other) for g in ga1_got]
+        ga0 = grads(attention_pairs(0, dv0, low0), ga1_got, "grad_attn", 0)
         attn_sum = Scatter(*ga0)
-        sums = [bias0[:, 0], bias1[:, 0]]
-        grad_patches, g_gain1, g_shift1 = leave(after(carry, *ga0), logit, mixed_grad)
-        grad_down = down_sum.third(grad_patches)
-        up_sum.second()
-        attn_sum.first()
-        attn_sum.second()
-        grad_up = up_sum.third(grad_patches)
-        grad_attn = attn_sum.third()
+        carry = after(carry, *ga0)
+        grad_patches, *vecs = leave(carry, (qsum0, qsum1), (vsum0, vsum1), (sum0, sum1))
+        vec_sum = VectorSum(vecs)
+        grad_down = along_chips(down_sum.pieces, grad_patches)
+        vec_sum.over_cores(grad_down)
+        up_sum.second(vec_sum.vec)
+        vec_sum.vec = after(vec_sum.vec, *up_sum.pieces)
+        attn_sum.first(*up_sum.pieces)
+        grad_up = along_chips(up_sum.pieces, attn_sum.other)
+        vec_sum.over_z(1, grad_up)
+        attn_sum.second(vec_sum.vec)
+        vec_sum.over_z(2, *attn_sum.pieces)
+        grad_attn = along_chips(attn_sum.pieces, vec_sum.vec)
+        summed = vec_sum.over_xy(grad_attn)
     else:
-        carry, lows, up_sums, blocks, sums = None, [], [], [], []
+        carry, lows, up_sums = None, [], []
         for i in range(p.pairs):
             got = down(i, og_pad, carry)
             carry = (got[0], got[1])
             lows.append(got[2])
-            up_sums.append(got[3][:, 0])
+            up_sums.append(got[3])
         tokens, mixed_grad, branch, logit, g_gain2, g_shift2, g_out_bias, g_router = middle(
             carry[1], carry[0]
         )
-        carry = None
+        carry, blocks, vsums, qsums = None, [], [], []
         for i in range(p.pairs):
-            low, carry, bias = backward(i, branch, carry)
-            blocks += attention_grad(p, pos, 0, branch, rows_low, ctxs[i], low, None)
-            sums.append(bias[:, 0])
-        grad_patches, g_gain1, g_shift1 = leave(carry, logit, mixed_grad)
+            dc, dv, vsum = values(i, branch)
+            low, carry, qsum = backward(i, dc, dv, carry)
+            blocks += grads(attention_pairs(i, dv, low), None, "grad_attn", 0)
+            vsums.append(vsum)
+            qsums.append(qsum)
+        grad_patches, *vecs = leave(carry, qsums, vsums, up_sums)
         grad_down, grad_up, grad_attn = (
             scatter_whole(p, g)
             for g in (
-                [weight_grad(p, pos, 0, og_pad, a, None, "grad_down")[0] for a in acts],
-                [weight_grad(p, pos, 0, mlp_in, v, None, "grad_up")[0] for v in lows],
+                [grads([(og_pad, a, 0)], None, "grad_down", 0)[0] for a in acts],
+                [grads([(mlp_in, v, 0)], None, "grad_up", 0)[0] for v in lows],
                 blocks,
             )
         )
-
-    qkv_sums = jnp.concatenate(sums, axis=0)
-    owned = jnp.concatenate(
-        [
-            qkv_sums[:, p.lo : p.lo + cols],
-            qkv_sums[:, p.lo + 2 * cols :],
-            jnp.concatenate(up_sums, axis=0),
-        ],
-        axis=1,
-    )
-    common = jnp.concatenate(
-        [g_gain1, g_shift1, g_router, g_out_bias, g_gain2, g_shift2, g_down_bias], axis=1
-    )[0]
-    common, owned = sum_vectors(p, common, owned)
-    vecs = [common[i * width : (i + 1) * width] for i in range(7)]
+        summed = sum_vectors(p, vecs)
+
+    vecs = [summed[i] for i in range(7)]
+    owned, hidden_sum = summed[8], summed[9]
     return (
         tokens,
         grad_patches,
         vecs[0],
         vecs[1],
         vecs[2],
+        grad_attn[:, 2 * cols : 3 * cols],
+        owned[:cols],
+        grad_attn[:, 3 * cols :],
         grad_attn[:, cols : 2 * cols],
-        owned[:cols],
-        grad_attn[:, 2 * cols : 3 * cols],
-        grad_attn[:, 3 * cols :],
         owned[cols : 2 * cols],
         grad_attn[:, :cols].T,
         vecs[3],
         vecs[4],
         vecs[5],
         grad_up,
-        owned[2 * cols :],
+        hidden_sum,
         grad_down.T,
         vecs[6],
     )

time: 217 us -> 197 us (0.908)
  waiting for transfers between devices: 76.9 us -> 56.2 us
  other arithmetic: 9.9 us -> 5.07 us
  starting transfers between devices: 59.4 us -> 63.5 us
    ppermute x49 -> x50, waiting for transfers between devices: 76.9 us -> 56.2 us  [send(): return lax.ppermute(v, ('dp', 'head'), table(move))]
    ppermute x49 -> x50, starting transfers between devices: 59.4 us -> 63.5 us  [send(): return lax.ppermute(v, ('dp', 'head'), table(move))]
    convert_element_type x6 -> x0, other arithmetic: 4.04 us -> none  [add(): return (a.astype(F32) + b.astype(F32)).astype(BF16)]
    pallas_call x17 -> x25, Pallas kernels: 58.7 us -> 60.1 us  [call(): pl.pallas_call(body, out_shape=[o for o, _ in outs], in_specs=[s for _, s...]
  transfers between devices with their start and end apart: 49 -> 50, of which waited for: 23 -> 17; matrix products, arithmetic and copies ran while one was open for 6% -> 4% of each run, Pallas kernels for 26% -> 31%
where the time goes in v3:
time: 197 us; the launch traced here: 194 us
  starting transfers between devices  63.5 us (32%)
  Pallas kernels  60.1 us (31%)
  waiting for transfers between devices  56.2 us (29%)
  local copies, waits for them, and re-layouts  7.05 us (4%)
  other arithmetic  5.07 us (3%)
    ppermute x50, starting transfers between devices, send(): return lax.ppermute(v, ('dp', 'head'), table(move))  63.5 us
    pallas_call x25, Pallas kernels, call(): pl.pallas_call(body, out_shape=[o for o, _ in outs], in_specs=[s for _, s...  60.1 us
    ppermute x50, waiting for transfers between devices, send(): return lax.ppermute(v, ('dp', 'head'), table(move))  56.2 us
  transfers between devices with their start and end apart: 50, of which 17 were waited for; matrix products, arithmetic and copies ran while one was open for 4% of the time, Pallas kernels for 31%

profile of v3, /device:TPU:0, one launch (start us, length us, event | category | flops | bytes accessed | tf_op | source)
XLA Modules:
  0.0 193.7 jit_solution(1786887790672876030)
XLA Ops:
  2.6 3.1 %collective-permute-start = (bf16[96,768]{1,0:T(8,128)(2,1)S(1)}, bf16[96,768]{1,0:T(8,128)(2,1)S(1)}, u32[]{:S(2)}, u32[]{:S(2)}) collective-permute-start(bf16[96,768]{1,0:T(8,128)(2,1)S(1)} %pad_maximum_fusion.6), channel_id=1, source_target_pairs={{0,8},{1,9},{2,10},{3,11},{4,12},{5,13},{6,14},{7,15},{8,16},{9,17... | collective-permute-start | bytes 442376 | tf_op jit(solution)/shard_map/ppermute | solution.py:592
  5.7 2.6 %collective-permute-start.1 = (bf16[96,768]{1,0:T(8,128)(2,1)S(1)}, bf16[96,768]{1,0:T(8,128)(2,1)S(1)}, u32[]{:S(2)}, u32[]{:S(2)}) collective-permute-start(bf16[96,768]{1,0:T(8,128)(2,1)S(1)} %pad_maximum_fusion.6), channel_id=1, source_target_pairs={{0,16},{1,17},{2,18},{3,19},{4,20},{5,21},{6,22},{7,23},{8,24},{9,... | collective-permute-start | bytes 442376 | tf_op jit(solution)/shard_map/ppermute | solution.py:592
  9.6 2.1 %concatenate.17 = bf16[1152]{0:T(1024)(128)(2,1)S(1)} concatenate(bf16[192]{0:T(256)(128)(2,1)} %param.26, bf16[192]{0:T(256)(128)(2,1)} %param.29, bf16[768]{0:T(1024)(128)(2,1)} %param.35), dimensions={0} | concatenate | bytes 4608 | tf_op jit(solution)/shard_map/concatenate | solution.py:705
  20.2 3.2 %collective-permute-start.7 = (bf16[96,768]{1,0:T(8,128)(2,1)S(1)}, bf16[96,768]{1,0:T(8,128)(2,1)S(1)}, u32[]{:S(2)}, u32[]{:S(2)}) collective-permute-start(bf16[96,768]{1,0:T(8,128)(2,1)S(1)} %copy-done.4), channel_id=1, source_target_pairs={{0,8},{1,9},{2,10},{3,11},{4,12},{5,13},{6,14},{7,15},{8,16},{9,17... | collective-permute-start | bytes 442376 | tf_op jit(solution)/shard_map/ppermute | solution.py:592
  30.9 3.2 %collective-permute-done.9 = bf16[96,768]{1,0:T(8,128)(2,1)S(1)} collective-permute-done((bf16[96,768]{1,0:T(8,128)(2,1)S(1)}, bf16[96,768]{1,0:T(8,128)(2,1)S(1)}, u32[]{:S(2)}, u32[]{:S(2)}) %collective-permute-start.9) | collective-permute-done | bytes 147488 | tf_op jit(solution)/shard_map/ppermute | solution.py:592
  35.3 3.7 %collective-permute-start.17 = (bf16[2,96,768]{2,1,0:T(8,128)(2,1)S(1)}, bf16[2,96,768]{2,1,0:T(8,128)(2,1)S(1)}, u32[]{:S(2)}, u32[]{:S(2)}) collective-permute-start(bf16[2,96,768]{2,1,0:T(8,128)(2,1)S(1)} %pad_maximum_fusion.5), channel_id=1, source_target_pairs={{0,8},{1,9},{2,10},{3,11},{4,12},{5,13},{6,14},{7,15},{8,16},{9,17... | collective-permute-start | bytes 884744 | tf_op jit(solution)/shard_map/ppermute | solution.py:592
  39.1 2.4 %collective-permute-start.18 = (bf16[2,96,768]{2,1,0:T(8,128)(2,1)S(1)}, bf16[2,96,768]{2,1,0:T(8,128)(2,1)S(1)}, u32[]{:S(2)}, u32[]{:S(2)}) collective-permute-start(bf16[2,96,768]{2,1,0:T(8,128)(2,1)S(1)} %pad_maximum_fusion.5), channel_id=1, source_target_pairs={{0,16},{1,17},{2,18},{3,19},{4,20},{5,21},{6,22},{7,23},{8,24},{9,... | collective-permute-start | bytes 884744 | tf_op jit(solution)/shard_map/ppermute | solution.py:592
  42.0 7.3 %collective-permute-done.11 = bf16[4,96,768]{2,1,0:T(8,128)(2,1)S(1)} collective-permute-done((bf16[4,96,768]{2,1,0:T(8,128)(2,1)S(1)}, bf16[4,96,768]{2,1,0:T(8,128)(2,1)S(1)}, u32[]{:S(2)}, u32[]{:S(2)}) %collective-permute-start.11) | collective-permute-done | bytes 589856 | tf_op jit(solution)/shard_map/ppermute | solution.py:592
  49.6 2.0 %collective-permute-done.12.refs_2_ = bf16[2,4,96,768]{3,2,1,0:T(8,128)(2,1)S(1)} collective-permute-done((bf16[2,4,96,768]{3,2,1,0:T(8,128)(2,1)S(1)}, bf16[2,4,96,768]{3,2,1,0:T(8,128)(2,1)S(1)}, u32[]{:S(2)}, u32[]{:S(2)}) %collective-permute-start.12) | collective-permute-done | bytes 1179680 | tf_op jit(solution)/shard_map/ppermute | solution.py:592
  53.3 5.0 %attn_fwd.2 = (bf16[2,400,640]{2,1,0:T(8,128)(2,1)S(1)}, bf16[12,208,208]{2,1,0:T(8,128)(2,1)S(1)}, bf16[2,400,256]{2,1,0:T(8,128)(2,1)S(1)}, f32[400,768]{1,0:T(8,128)S(1)}) custom-call(s32[3]{0:T(128)S(1)} %pad_add_fusion.refs_0_, bf16[2,4,96,768]{3,2,1,0:T(8,128)(2,1)S(1)} %pad_maximum_fusion.refs_1_, ...), custom_call_target="tpu_custom_call" | custom-call | flops 22000001024 | tf_op jit(solution)/shard_map/attn_fwd/pallas_call | solution.py:36
  60.5 7.4 %collective-permute-done.13.refs_2_ = bf16[2,4,96,768]{3,2,1,0:T(8,128)(2,1)S(1)} collective-permute-done((bf16[2,4,96,768]{3,2,1,0:T(8,128)(2,1)S(1)}, bf16[2,4,96,768]{3,2,1,0:T(8,128)(2,1)S(1)}, u32[]{:S(2)}, u32[]{:S(2)}) %collective-permute-start.13) | collective-permute-done | bytes 1179680 | tf_op jit(solution)/shard_map/ppermute | solution.py:592
  67.9 5.4 %attn_fwd.3 = (bf16[2,400,640]{2,1,0:T(8,128)(2,1)S(1)}, bf16[12,208,208]{2,1,0:T(8,128)(2,1)S(1)}, bf16[2,400,256]{2,1,0:T(8,128)(2,1)S(1)}, f32[400,768]{1,0:T...) custom-call(s32[3]{0:T(128)S(1)} %pad_add_fusion.refs_0_, ...), custom_call_target="tpu_custom_call" | custom-call | flops 22000001024 | tf_op jit(solution)/shard_map/attn_fwd/pallas_call | solution.py:36
  73.3 2.5 %up.3 = (bf16[2,400,768]{2,1,0:T(8,128)(2,1)S(1)}, bf16[2,400,768]{2,1,0:T(8,128)(2,1)S(1)}) custom-call(s32[3]{0:T(128)S(1)} %pad_add_fusion.refs_0_, bf16[2,4,96,768]{3,2,1,0:T(8,128)(2,1)S(1)} %pad_maximum_fusion.1.refs_1_, bf16[2,4,96,768]{3,2,1,0:T(8,128)(2,1)S(1)} %collective-permute-done.13.refs_2_, ...), custom_call_target="tpu_custom_call" | custom-call | flops 10000000000 | tf_op jit(solution)/shard_map/up/pallas_call | solution.py:36
  75.9 2.5 %up.2 = (bf16[2,400,768]{2,1,0:T(8,128)(2,1)S(1)}, bf16[2,400,768]{2,1,0:T(8,128)(2,1)S(1)}) custom-call(s32[3]{0:T(128)S(1)} %pad_add_fusion.refs_0_, bf16[2,4,96,768]{3,2,1,0:T(8,128)(2,1)S(1)} %collective-permute-done.15.refs_1_, bf16[2,4,96,768]{3,2,1,0:T(8,128)(2,1)S(1)} %collective-permute-done.16.refs_2_, ...), custom_call_target="tpu_custom_call" | custom-call | flops 10000000000 | tf_op jit(solution)/shard_map/up/pallas_call | solution.py:36
  78.4 2.4 %grad_down.2 = (bf16[2,4,96,768]{3,2,1,0:T(8,128)(2,1)S(1)}, bf16[2,4,96,768]{3,2,1,0:T(8,128)(2,1)S(1)}) custom-call(s32[3]{0:T(128)S(1)} %pad_add_fusion.refs_0_, bf16[400,768]{1,0:T(8,128)(2,1)S(1)} %pad.20.og_ref.refs_1_.refs_7_, bf16[2,400,768]{2,1,0:T(8,128)(2,1)S(1)} %get-tuple-element.162.refs_2_.refs_5_), custom_call_target="tpu_custom_call" | custom-call | flops 9200000000 | tf_op jit(solution)/shard_map/grad_down/pallas_call | solution.py:36
  81.9 4.0 %down.2 = (f32[400,768]{1,0:T(8,128)S(1)}, f32[400,768]{1,0:T(8,128)S(1)}, bf16[2,400,768]{2,1,0:T(8,128)(2,1)S(1)}, f32[2,1,768]{2,1,0:T(1,128)S(1)}) custom-call(s32[3]{0:T(128)S(1)} %pad_add_fusion.refs_0_, bf16[2,4,96,768]{3,2,1,0:T(8,128)(2,1)S(1)} %pad_maximum_fusion.1.refs_1_, bf16[2,4,96,768]{3,2,1,0:T(8,128)(2,1)S(1)} %collective-permute-done.13.refs_2_, ...), custom_call_target="tpu_custom_call" | custom-call | flops 20000000000 | tf_op jit(solution)/shard_map/down/pallas_call | solution.py:36
  86.0 2.5 %grad_down.3 = (bf16[2,4,96,768]{3,2,1,0:T(8,128)(2,1)S(1)}, bf16[2,4,96,768]{3,2,1,0:T(8,128)(2,1)S(1)}) custom-call(s32[3]{0:T(128)S(1)} %pad_add_fusion.refs_0_, bf16[400,768]{1,0:T(8,128)(2,1)S(1)} %pad.20.og_ref.refs_1_.refs_7_, bf16[2,400,768]{2,1,0:T(8,128)(2,1)S(1)} %get-tuple-element.166.refs_5_.refs_2_, ...), custom_call_target="tpu_custom_call" | custom-call | flops 9200000000 | tf_op jit(solution)/shard_map/grad_down/pallas_call | solution.py:36
  90.2 4.1 %down.3 = (f32[400,768]{1,0:T(8,128)S(1)}, f32[400,768]{1,0:T(8,128)S(1)}, bf16[2,400,768]{2,1,0:T(8,128)(2,1)S(1)}, f32[2,1,768]{2,1,0:T(1,128)S(1)}) custom-call(s32[3]{0:T(128)S(1)} %pad_add_fusion.refs_0_, bf16[2,4,96,768]{3,2,1,0:T(8,128)(2,1)S(1)} %collective-permute-done.15.refs_1_, bf16[2,4,96,768]{3,2,1,0:T(8,128)(2,1)S(1)} %collective-permute-done.16.refs_2_, ...), custom_call_target="tpu_custom_call" | custom-call | flops 20000000000 | tf_op jit(solution)/shard_map/down/pallas_call | solution.py:36
  94.3 2.5 %middle.1 = (bf16[394,768]{1,0:T(8,128)(2,1)}, f32[400,768]{1,0:T(8,128)S(1)}, bf16[400,768]{1,0:T(8,128)(2,1)S(1)}, f32[400,1]{1,0:T(8,128)S(1)}, f32[1,768]{1,...) custom-call(bf16[400,768]{1,0:T(8,128)(2,1)S(1)} %pad.19.x_ref.refs_7_.refs_0_, ...), custom_call_target="tpu_custom_call" | custom-call | flops 10400000000 | tf_op jit(solution)/shard_map/middle/pallas_call | solution.py:36
  96.8 2.4 %grad_up.2 = (bf16[2,4,96,768]{3,2,1,0:T(8,128)(2,1)S(1)}, bf16[2,4,96,768]{3,2,1,0:T(8,128)(2,1)S(1)}) custom-call(s32[3]{0:T(128)S(1)} %pad_add_fusion.refs_0_, bf16[400,768]{1,0:T(8,128)(2,1)S(1)} %get-tuple-element.183.refs_3_.refs_1_, bf16[2,400,768]{2,1,0:T(8,128)(2,1)S(1)} %get-tuple-element.184.refs_2_), custom_call_target="tpu_custom_call" | custom-call | flops 9200000000 | tf_op jit(solution)/shard_map/grad_up/pallas_call | solution.py:36
  106.1 2.5 %grad_up.3 = (bf16[2,4,96,768]{3,2,1,0:T(8,128)(2,1)S(1)}, bf16[2,4,96,768]{3,2,1,0:T(8,128)(2,1)S(1)}) custom-call(s32[3]{0:T(128)S(1)} %pad_add_fusion.refs_0_, bf16[400,768]{1,0:T(8,128)(2,1)S(1)} %get-tuple-element.183.refs_3_.refs_1_, bf16[2,400,768]{2,1,0:T(8,128)(2,1)S(1)} %get-tuple-element.171.refs_2_, ...), custom_call_target="tpu_custom_call" | custom-call | flops 9200000000 | tf_op jit(solution)/shard_map/grad_up/pallas_call | solution.py:36
  109.8 5.4 %attn_bwd.2 = (bf16[2,400,384]{2,1,0:T(8,128)(2,1)S(1)}, f32[400,768]{1,0:T(8,128)S(1)}, f32[2,1,384]{2,1,0:T(1,128)S(1)}) custom-call(s32[3]{0:T(128)S(1)} %pad_add_fusion.refs_0_, bf16[2,4,96,768]{3,2,1,0:T(8,128)(2,1)S(1)} %collective-permute-done.8.refs_1_, bf16[2,4,96,768]{3,2,1,0:T(8,128)(2,1)S(1)} %collective-permute-done.14.refs_2_, ...), custom_call_target="tpu_custom_call" | custom-call | flops 24000000000 | tf_op jit(solution)/shard_map/attn_bwd/pallas_call | solution.py:36
  115.3 2.6 %grad_attn.2 = (bf16[2,4,96,768]{3,2,1,0:T(8,128)(2,1)S(1)}, bf16[2,4,96,768]{3,2,1,0:T(8,128)(2,1)S(1)}) custom-call(s32[3]{0:T(128)S(1)} %pad_add_fusion.refs_0_, bf16[400,768]{1,0:T(8,128)(2,1)S(1)} %get-tuple-element.190.refs_3_.refs_1_, bf16[2,400,256]{2,1,0:T(8,128)(2,1)S(1)} %get-tuple-element.193.refs_2_, bf16[400,768]{1,0:T(8,128)(2,1)S(1)} %copy-done.1, ...), custom_call_target="tpu_custom_call" | custom-call | flops 9200000000 | tf_op jit(solution)/shard_map/grad_attn/pallas_call | solution.py:36
  118.8 4.8 %collective-permute-start.33 = (bf16[96,768]{1,0:T(8,128)(2,1)S(1)}, bf16[96,768]{1,0:T(8,128)(2,1)S(1)}, u32[]{:S(2)}, u32[]{:S(2)}) collective-permute-start(bf16[96,768]{1,0:T(8,128)(2,1)S(1)} %get-tuple-element.208), channel_id=1, source_target_pairs={{0,24},{1,25},{2,26},{3,27},{4,28},{5,29},{6,30},{7,31},{8,0},{9,1... | collective-permute-start | bytes 442376 | tf_op jit(solution)/shard_map/ppermute | solution.py:592
  125.4 5.4 %attn_bwd.3 = (bf16[2,400,384]{2,1,0:T(8,128)(2,1)S(1)}, f32[400,768]{1,0:T(8,128)S(1)}, f32[2,1,384]{2,1,0:T(1,128)S(1)}) custom-call(s32[3]{0:T(128)S(1)} %pad_add_fusion.refs_0_, bf16[2,4,96,768]{3,2,1,0:T(8,128)(2,1)S(1)} %pad_maximum_fusion.refs_1_, bf16[2,4,96,768]{3,2,1,0:T(8,128)(2,1)S(1)} %collective-permute-done.12.refs_2_, ...), custom_call_target="tpu_custom_call" | custom-call | flops 24000000000 | tf_op jit(solution)/shard_map/attn_bwd/pallas_call | solution.py:36
  133.9 2.9 %grad_attn.3 = (bf16[2,4,96,768]{3,2,1,0:T(8,128)(2,1)S(1)}, bf16[2,4,96,768]{3,2,1,0:T(8,128)(2,1)S(1)}) custom-call(s32[3]{0:T(128)S(1)} %pad_add_fusion.refs_0_, bf16[400,768]{1,0:T(8,128)(2,1)S(1)} %get-tuple-element.190.refs_3_.refs_1_, bf16[2,400,256]{2,1,0:T(8,128)(2,1)S(1)} %get-tuple-element.215.refs_2_, bf16[400,768]{1,0:T(8,128)(2,1)S(1)} %copy-done.1, ...), custom_call_target="tpu_custom_call" | custom-call | flops 9200000000 | tf_op jit(solution)/shard_map/grad_attn/pallas_call | solution.py:36
  141.5 5.5 %collective-permute-done.36.g_ref = bf16[4,96,768]{2,1,0:T(8,128)(2,1)S(1)} collective-permute-done((bf16[4,96,768]{2,1,0:T(8,128)(2,1)S(1)}, bf16[4,96,768]{2,1,0:T(8,128)(2,1)S(1)}, u32[]{:S(2)}, u32[]{:S(2)}) %collective-permute-start.36) | collective-permute-done | bytes 589856 | tf_op jit(solution)/shard_map/ppermute | solution.py:592
  147.1 6.5 %collective-permute-done.39.g_ref = bf16[2,4,96,768]{3,2,1,0:T(8,128)(2,1)S(1)} collective-permute-done((bf16[2,4,96,768]{3,2,1,0:T(8,128)(2,1)S(1)}, bf16[2,4,96,768]{3,2,1,0:T(8,128)(2,1)S(1)}, u32[]{:S(2)}, u32[]{:S(2)}) %collective-permute-start.39) | collective-permute-done | bytes 1179680 | tf_op jit(solution)/shard_map/ppermute | solution.py:592
  155.1 2.2 %collective-permute-start.38 = (bf16[96,768]{1,0:T(8,128)(2,1)S(1)}, bf16[96,768]{1,0:T(8,128)(2,1)S(1)}, u32[]{:S(2)}, u32[]{:S(2)}) collective-permute-start(bf16[96,768]{1,0:T(8,128)(2,1)S(1)} %get-tuple-element.247), channel_id=1, source_target_pairs={{0,24},{1,25},{2,26},{3,27},{4,28},{5,29},{6,30},{7,31},{8,0},{9,1... | collective-permute-start | bytes 442376 | tf_op jit(solution)/shard_map/ppermute | solution.py:592
  158.0 2.8 %collective-permute-start.37 = (f32[12,768]{1,0:T(8,128)S(1)}, f32[12,768]{1,0:T(8,128)S(1)}, u32[]{:S(2)}, u32[]{:S(2)}) collective-permute-start(f32[12,768]{1,0:T(8,128)S(1)} %add.68), channel_id=1, source_target_pairs={{0,8},{1,9},{2,10},{3,11},{4,12},{5,13},{6,14},{7,15},{8,0},{9,1},... | collective-permute-start | bytes 110600 | tf_op jit(solution)/shard_map/ppermute | solution.py:592
  160.7 10.9 %collective-permute-done.40 = bf16[96,768]{1,0:T(8,128)(2,1)S(1)} collective-permute-done((bf16[96,768]{1,0:T(8,128)(2,1)S(1)}, bf16[96,768]{1,0:T(8,128)(2,1)S(1)}, u32[]{:S(2)}, u32[]{:S(2)}) %collective-permute-start.40) | collective-permute-done | bytes 147488 | tf_op jit(solution)/shard_map/ppermute | solution.py:592
  182.4 8.0 %collective-permute-done.46 = bf16[96,768]{1,0:T(8,128)(2,1)S(1)} collective-permute-done((bf16[96,768]{1,0:T(8,128)(2,1)S(1)}, bf16[96,768]{1,0:T(8,128)(2,1)S(1)}, u32[]{:S(2)}, u32[]{:S(2)}) %collective-permute-start.46) | collective-permute-done | bytes 147488 | tf_op jit(solution)/shard_map/ppermute | solution.py:592
  (177 shorter events, 62.2 us)
Async XLA Ops:
  2.6 15.2 %collective-permute-start = (bf16[96,768]{1,0:T(8,128)(2,1)S(1)}, bf16[96,768]{1,0:T(8,128)(2,1)S(1)}, u32[]{:S(2)}, u32[]{:S(2)}) collective-permute-start(bf16[96,768]{1,0:T(8,128)(2,1)S(1)} %pad_maximum_fusion.6), channel_id=1, source_target_pairs={{0,8},{1,9},{2,10},{3,11},{4,12},{5,13},{6,14},{7,15},{8,16},{9,17... | collective-permute-start | bytes 442376 | tf_op jit(solution)/shard_map/ppermute | solution.py:592
  5.7 12.3 %collective-permute-start.1 = (bf16[96,768]{1,0:T(8,128)(2,1)S(1)}, bf16[96,768]{1,0:T(8,128)(2,1)S(1)}, u32[]{:S(2)}, u32[]{:S(2)}) collective-permute-start(bf16[96,768]{1,0:T(8,128)(2,1)S(1)} %pad_maximum_fusion.6), channel_id=1, source_target_pairs={{0,16},{1,17},{2,18},{3,19},{4,20},{5,21},{6,22},{7,23},{8,24},{9,... | collective-permute-start | bytes 442376 | tf_op jit(solution)/shard_map/ppermute | solution.py:592
  18.6 9.9 %collective-permute-start.6 = (bf16[4,96,768]{2,1,0:T(8,128)(2,1)S(1)}, bf16[4,96,768]{2,1,0:T(8,128)(2,1)S(1)}, u32[]{:S(2)}, u32[]{:S(2)}) collective-permute-start(bf16[4,96,768]{2,1,0:T(8,128)(2,1)S(1)} %pad_maximum_fusion.3), channel_id=1, source_target_pairs={{0,4},{1,3},{2,6},{3,1},{4,0},{5,7},{6,2},{7,5},{8,12},{9,11},{10,... | collective-permute-start | bytes 1769480 | tf_op jit(solution)/shard_map/ppermute | solution.py:592
  23.4 10.6 %collective-permute-start.9 = (bf16[96,768]{1,0:T(8,128)(2,1)S(1)}, bf16[96,768]{1,0:T(8,128)(2,1)S(1)}, u32[]{:S(2)}, u32[]{:S(2)}) collective-permute-start(bf16[96,768]{1,0:T(8,128)(2,1)S(1)} %copy-done.4), channel_id=1, source_target_pairs={{0,16},{1,17},{2,18},{3,19},{4,20},{5,21},{6,22},{7,23},{8,24},{9,... | collective-permute-start | bytes 442376 | tf_op jit(solution)/shard_map/ppermute | solution.py:592
  29.1 22.5 %collective-permute-start.12 = (bf16[2,4,96,768]{3,2,1,0:T(8,128)(2,1)S(1)}, bf16[2,4,96,768]{3,2,1,0:T(8,128)(2,1)S(1)}, u32[]{:S(2)}, u32[]{:S(2)}) collective-permute-start(bf16[2,4,96,768]{3,2,1,0:T(8,128)(2,1)S(1)} %pad_maximum_fusion.refs_1_), channel_id=1, source_target_pairs={{0,2},{1,5},{2,0},{3,7},{4,6},{5,1},{6,4},{7,3},{8,10},{9,13},{10,... | collective-permute-start | bytes 3538952 | tf_op jit(solution)/shard_map/ppermute | solution.py:592
  34.1 15.2 %collective-permute-start.11 = (bf16[4,96,768]{2,1,0:T(8,128)(2,1)S(1)}, bf16[4,96,768]{2,1,0:T(8,128)(2,1)S(1)}, u32[]{:S(2)}, u32[]{:S(2)}) collective-permute-start(bf16[4,96,768]{2,1,0:T(8,128)(2,1)S(1)} %pad_maximum_fusion.4), channel_id=1, source_target_pairs={{0,4},{1,3},{2,6},{3,1},{4,0},{5,7},{6,2},{7,5},{8,12},{9,11},{10,... | collective-permute-start | bytes 1769480 | tf_op jit(solution)/shard_map/ppermute | solution.py:592
  35.3 18.0 %collective-permute-start.17 = (bf16[2,96,768]{2,1,0:T(8,128)(2,1)S(1)}, bf16[2,96,768]{2,1,0:T(8,128)(2,1)S(1)}, u32[]{:S(2)}, u32[]{:S(2)}) collective-permute-start(bf16[2,96,768]{2,1,0:T(8,128)(2,1)S(1)} %pad_maximum_fusion.5), channel_id=1, source_target_pairs={{0,8},{1,9},{2,10},{3,11},{4,12},{5,13},{6,14},{7,15},{8,16},{9,17... | collective-permute-start | bytes 884744 | tf_op jit(solution)/shard_map/ppermute | solution.py:592
  39.1 19.4 %collective-permute-start.18 = (bf16[2,96,768]{2,1,0:T(8,128)(2,1)S(1)}, bf16[2,96,768]{2,1,0:T(8,128)(2,1)S(1)}, u32[]{:S(2)}, u32[]{:S(2)}) collective-permute-start(bf16[2,96,768]{2,1,0:T(8,128)(2,1)S(1)} %pad_maximum_fusion.5), channel_id=1, source_target_pairs={{0,16},{1,17},{2,18},{3,19},{4,20},{5,21},{6,22},{7,23},{8,24},{9,... | collective-permute-start | bytes 884744 | tf_op jit(solution)/shard_map/ppermute | solution.py:592
  41.5 17.4 %collective-permute-start.19 = (bf16[2,96,768]{2,1,0:T(8,128)(2,1)S(1)}, bf16[2,96,768]{2,1,0:T(8,128)(2,1)S(1)}, u32[]{:S(2)}, u32[]{:S(2)}) collective-permute-start(bf16[2,96,768]{2,1,0:T(8,128)(2,1)S(1)} %pad_maximum_fusion.5), channel_id=1, source_target_pairs={{0,24},{1,25},{2,26},{3,27},{4,28},{5,29},{6,30},{7,31},{8,0},{9,1... | collective-permute-start | bytes 884744 | tf_op jit(solution)/shard_map/ppermute | solution.py:592
  49.3 18.6 %collective-permute-start.8 = (bf16[2,4,96,768]{3,2,1,0:T(8,128)(2,1)S(1)}, bf16[2,4,96,768]{3,2,1,0:T(8,128)(2,1)S(1)}, u32[]{:S(2)}, u32[]{:S(2)}) collective-permute-start(bf16[2,4,96,768]{3,2,1,0:T(8,128)(2,1)S(1)} %pad_maximum_fusion.refs_1_), channel_id=1, source_target_pairs={{0,1},{1,0},{2,3},{3,2},{4,5},{5,4},{6,7},{7,6},{8,9},{9,8},{10,11... | collective-permute-start | bytes 3538952 | tf_op jit(solution)/shard_map/ppermute | solution.py:592
  51.7 16.2 %collective-permute-start.13 = (bf16[2,4,96,768]{3,2,1,0:T(8,128)(2,1)S(1)}, bf16[2,4,96,768]{3,2,1,0:T(8,128)(2,1)S(1)}, u32[]{:S(2)}, u32[]{:S(2)}) collective-permute-start(bf16[2,4,96,768]{3,2,1,0:T(8,128)(2,1)S(1)} %pad_maximum_fusion.1.refs_1_), channel_id=1, source_target_pairs={{0,2},{1,5},{2,0},{3,7},{4,6},{5,1},{6,4},{7,3},{8,10},{9,13},{10,... | collective-permute-start | bytes 3538952 | tf_op jit(solution)/shard_map/ppermute | solution.py:592
  53.3 14.6 %collective-permute-start.14 = (bf16[2,4,96,768]{3,2,1,0:T(8,128)(2,1)S(1)}, bf16[2,4,96,768]{3,2,1,0:T(8,128)(2,1)S(1)}, u32[]{:S(2)}, u32[]{:S(2)}) collective-permute-start(bf16[2,4,96,768]{3,2,1,0:T(8,128)(2,1)S(1)} %collective-permute-done.12.refs_2_), channel_id=1, source_target_pairs={{0,1},{1,0},{2,3},{3,2},{4,5},{5,4},{6,7},{7,6},{8,9},{9,8},{10,11... | collective-permute-start | bytes 3538952 | tf_op jit(solution)/shard_map/ppermute | solution.py:592
  58.5 17.4 %collective-permute-start.15 = (bf16[2,4,96,768]{3,2,1,0:T(8,128)(2,1)S(1)}, bf16[2,4,96,768]{3,2,1,0:T(8,128)(2,1)S(1)}, u32[]{:S(2)}, u32[]{:S(2)}) collective-permute-start(bf16[2,4,96,768]{3,2,1,0:T(8,128)(2,1)S(1)} %pad_maximum_fusion.1.refs_1_), channel_id=1, source_target_pairs={{0,1},{1,0},{2,3},{3,2},{4,5},{5,4},{6,7},{7,6},{8,9},{9,8},{10,11... | collective-permute-start | bytes 3538952 | tf_op jit(solution)/shard_map/ppermute | solution.py:592
  59.0 22.4 %collective-permute-start.21 = (bf16[4,2,96,768]{3,2,1,0:T(8,128)(2,1)S(1)}, bf16[4,2,96,768]{3,2,1,0:T(8,128)(2,1)S(1)}, u32[]{:S(2)}, u32[]{:S(2)}) collective-permute-start(bf16[4,2,96,768]{3,2,1,0:T(8,128)(2,1)S(1)} %pad_maximum_fusion.2.refs_3_), channel_id=1, source_target_pairs={{0,2},{1,5},{2,0},{3,7},{4,6},{5,1},{6,4},{7,3},{8,10},{9,13},{10,... | collective-permute-start | bytes 3538952 | tf_op jit(solution)/shard_map/ppermute | solution.py:592
  88.5 16.3 %collective-permute-start.26 = (bf16[2,4,96,768]{3,2,1,0:T(8,128)(2,1)S(1)}, bf16[2,4,96,768]{3,2,1,0:T(8,128)(2,1)S(1)}, u32[]{:S(2)}, u32[]{:S(2)}) collective-permute-start(bf16[2,4,96,768]{3,2,1,0:T(8,128)(2,1)S(1)} %get-tuple-element.174), channel_id=1, source_target_pairs={{0,2},{1,5},{2,0},{3,7},{4,6},{5,1},{6,4},{7,3},{8,10},{9,13},{10,... | collective-permute-start | bytes 3538952 | tf_op jit(solution)/shard_map/ppermute | solution.py:592
  105.0 13.6 %collective-permute-start.28 = (bf16[4,96,768]{2,1,0:T(8,128)(2,1)S(1)}, bf16[4,96,768]{2,1,0:T(8,128)(2,1)S(1)}, u32[]{:S(2)}, u32[]{:S(2)}) collective-permute-start(bf16[4,96,768]{2,1,0:T(8,128)(2,1)S(1)} %get-tuple-element.196), channel_id=1, source_target_pairs={{0,4},{1,3},{2,6},{3,1},{4,0},{5,7},{6,2},{7,5},{8,12},{9,11},{10,... | collective-permute-start | bytes 1769480 | tf_op jit(solution)/shard_map/ppermute | solution.py:592
  108.7 22.2 %collective-permute-start.30 = (bf16[2,4,96,768]{3,2,1,0:T(8,128)(2,1)S(1)}, bf16[2,4,96,768]{3,2,1,0:T(8,128)(2,1)S(1)}, u32[]{:S(2)}, u32[]{:S(2)}) collective-permute-start(bf16[2,4,96,768]{3,2,1,0:T(8,128)(2,1)S(1)} %get-tuple-element.200), channel_id=1, source_target_pairs={{0,2},{1,5},{2,0},{3,7},{4,6},{5,1},{6,4},{7,3},{8,10},{9,13},{10,... | collective-permute-start | bytes 3538952 | tf_op jit(solution)/shard_map/ppermute | solution.py:592
  117.9 15.2 %collective-permute-start.31 = (bf16[2,4,96,768]{3,2,1,0:T(8,128)(2,1)S(1)}, bf16[2,4,96,768]{3,2,1,0:T(8,128)(2,1)S(1)}, u32[]{:S(2)}, u32[]{:S(2)}) collective-permute-start(bf16[2,4,96,768]{3,2,1,0:T(8,128)(2,1)S(1)} %get-tuple-element.205), channel_id=1, source_target_pairs={{0,1},{1,0},{2,3},{3,2},{4,5},{5,4},{6,7},{7,6},{8,9},{9,8},{10,11... | collective-permute-start | bytes 3538952 | tf_op jit(solution)/shard_map/ppermute | solution.py:592
  118.0 16.0 %collective-permute-start.29 = (bf16[2,4,96,768]{3,2,1,0:T(8,128)(2,1)S(1)}, bf16[2,4,96,768]{3,2,1,0:T(8,128)(2,1)S(1)}, u32[]{:S(2)}, u32[]{:S(2)}) collective-permute-start(bf16[2,4,96,768]{3,2,1,0:T(8,128)(2,1)S(1)} %get-tuple-element.204), channel_id=1, source_target_pairs={{0,1},{1,0},{2,3},{3,2},{4,5},{5,4},{6,7},{7,6},{8,9},{9,8},{10,11... | collective-permute-start | bytes 3538952 | tf_op jit(solution)/shard_map/ppermute | solution.py:592
  118.8 21.4 %collective-permute-start.33 = (bf16[96,768]{1,0:T(8,128)(2,1)S(1)}, bf16[96,768]{1,0:T(8,128)(2,1)S(1)}, u32[]{:S(2)}, u32[]{:S(2)}) collective-permute-start(bf16[96,768]{1,0:T(8,128)(2,1)S(1)} %get-tuple-element.208), channel_id=1, source_target_pairs={{0,24},{1,25},{2,26},{3,27},{4,28},{5,29},{6,30},{7,31},{8,0},{9,1... | collective-permute-start | bytes 442376 | tf_op jit(solution)/shard_map/ppermute | solution.py:592
  123.6 16.6 %collective-permute-start.34 = (bf16[96,768]{1,0:T(8,128)(2,1)S(1)}, bf16[96,768]{1,0:T(8,128)(2,1)S(1)}, u32[]{:S(2)}, u32[]{:S(2)}) collective-permute-start(bf16[96,768]{1,0:T(8,128)(2,1)S(1)} %get-tuple-element.209), channel_id=1, source_target_pairs={{0,16},{1,17},{2,18},{3,19},{4,20},{5,21},{6,22},{7,23},{8,24},{9,... | collective-permute-start | bytes 442376 | tf_op jit(solution)/shard_map/ppermute | solution.py:592
  133.2 13.8 %collective-permute-start.36 = (bf16[4,96,768]{2,1,0:T(8,128)(2,1)S(1)}, bf16[4,96,768]{2,1,0:T(8,128)(2,1)S(1)}, u32[]{:S(2)}, u32[]{:S(2)}) collective-permute-start(bf16[4,96,768]{2,1,0:T(8,128)(2,1)S(1)} %get-tuple-element.218), channel_id=1, source_target_pairs={{0,4},{1,3},{2,6},{3,1},{4,0},{5,7},{6,2},{7,5},{8,12},{9,11},{10,... | collective-permute-start | bytes 1769480 | tf_op jit(solution)/shard_map/ppermute | solution.py:592
  136.9 16.8 %collective-permute-start.39 = (bf16[2,4,96,768]{3,2,1,0:T(8,128)(2,1)S(1)}, bf16[2,4,96,768]{3,2,1,0:T(8,128)(2,1)S(1)}, u32[]{:S(2)}, u32[]{:S(2)}) collective-permute-start(bf16[2,4,96,768]{3,2,1,0:T(8,128)(2,1)S(1)} %get-tuple-element.222), channel_id=1, source_target_pairs={{0,2},{1,5},{2,0},{3,7},{4,6},{5,1},{6,4},{7,3},{8,10},{9,13},{10,... | collective-permute-start | bytes 3538952 | tf_op jit(solution)/shard_map/ppermute | solution.py:592
  153.9 19.7 %collective-permute-start.43 = (bf16[4,96,768]{2,1,0:T(8,128)(2,1)S(1)}, bf16[4,96,768]{2,1,0:T(8,128)(2,1)S(1)}, u32[]{:S(2)}, u32[]{:S(2)}) collective-permute-start(bf16[4,96,768]{2,1,0:T(8,128)(2,1)S(1)} %get-tuple-element.252), channel_id=1, source_target_pairs={{0,4},{1,3},{2,6},{3,1},{4,0},{5,7},{6,2},{7,5},{8,12},{9,11},{10,... | collective-permute-start | bytes 1769480 | tf_op jit(solution)/shard_map/ppermute | solution.py:592
  157.2 14.3 %collective-permute-start.40 = (bf16[96,768]{1,0:T(8,128)(2,1)S(1)}, bf16[96,768]{1,0:T(8,128)(2,1)S(1)}, u32[]{:S(2)}, u32[]{:S(2)}) collective-permute-start(bf16[96,768]{1,0:T(8,128)(2,1)S(1)} %get-tuple-element.248), channel_id=1, source_target_pairs={{0,16},{1,17},{2,18},{3,19},{4,20},{5,21},{6,22},{7,23},{8,24},{9,... | collective-permute-start | bytes 442376 | tf_op jit(solution)/shard_map/ppermute | solution.py:592
  157.7 13.9 %collective-permute-start.41 = (bf16[96,768]{1,0:T(8,128)(2,1)S(1)}, bf16[96,768]{1,0:T(8,128)(2,1)S(1)}, u32[]{:S(2)}, u32[]{:S(2)}) collective-permute-start(bf16[96,768]{1,0:T(8,128)(2,1)S(1)} %get-tuple-element.249), channel_id=1, source_target_pairs={{0,8},{1,9},{2,10},{3,11},{4,12},{5,13},{6,14},{7,15},{8,16},{9,17... | collective-permute-start | bytes 442376 | tf_op jit(solution)/shard_map/ppermute | solution.py:592
  158.0 14.4 %collective-permute-start.37 = (f32[12,768]{1,0:T(8,128)S(1)}, f32[12,768]{1,0:T(8,128)S(1)}, u32[]{:S(2)}, u32[]{:S(2)}) collective-permute-start(f32[12,768]{1,0:T(8,128)S(1)} %add.68), channel_id=1, source_target_pairs={{0,8},{1,9},{2,10},{3,11},{4,12},{5,13},{6,14},{7,15},{8,0},{9,1},... | collective-permute-start | bytes 110600 | tf_op jit(solution)/shard_map/ppermute | solution.py:592
  174.2 16.1 %collective-permute-start.46 = (bf16[96,768]{1,0:T(8,128)(2,1)S(1)}, bf16[96,768]{1,0:T(8,128)(2,1)S(1)}, u32[]{:S(2)}, u32[]{:S(2)}) collective-permute-start(bf16[96,768]{1,0:T(8,128)(2,1)S(1)} %get-tuple-element.261), channel_id=1, source_target_pairs={{0,16},{1,17},{2,18},{3,19},{4,20},{5,21},{6,22},{7,23},{8,24},{9,... | collective-permute-start | bytes 442376 | tf_op jit(solution)/shard_map/ppermute | solution.py:592
  175.6 14.7 %collective-permute-start.47 = (bf16[96,768]{1,0:T(8,128)(2,1)S(1)}, bf16[96,768]{1,0:T(8,128)(2,1)S(1)}, u32[]{:S(2)}, u32[]{:S(2)}) collective-permute-start(bf16[96,768]{1,0:T(8,128)(2,1)S(1)} %get-tuple-element.262), channel_id=1, source_target_pairs={{0,8},{1,9},{2,10},{3,11},{4,12},{5,13},{6,14},{7,15},{8,16},{9,17... | collective-permute-start | bytes 442376 | tf_op jit(solution)/shard_map/ppermute | solution.py:592
  178.0 13.2 %collective-permute-start.49 = (f32[10,768]{1,0:T(8,128)S(1)}, f32[10,768]{1,0:T(8,128)S(1)}, u32[]{:S(2)}, u32[]{:S(2)}) collective-permute-start(f32[10,768]{1,0:T(8,128)S(1)} %pad_maximum_fusion.7), channel_id=1, source_target_pairs={{0,6},{1,7},{2,4},{3,5},{4,2},{5,3},{6,0},{7,1},{8,14},{9,15},{10,... | collective-permute-start | bytes 92168 | tf_op jit(solution)/shard_map/ppermute | solution.py:592
  179.9 11.3 %collective-permute-start.48 = (f32[10,768]{1,0:T(8,128)S(1)}, f32[10,768]{1,0:T(8,128)S(1)}, u32[]{:S(2)}, u32[]{:S(2)}) collective-permute-start(f32[10,768]{1,0:T(8,128)S(1)} %pad_maximum_fusion.7), channel_id=1, source_target_pairs={{0,2},{1,3},{2,0},{3,1},{4,6},{5,7},{6,4},{7,5},{8,10},{9,11},{10,... | collective-permute-start | bytes 92168 | tf_op jit(solution)/shard_map/ppermute | solution.py:592
  181.4 9.8 %collective-permute-start.44 = (f32[10,768]{1,0:T(8,128)S(1)}, f32[10,768]{1,0:T(8,128)S(1)}, u32[]{:S(2)}, u32[]{:S(2)}) collective-permute-start(f32[10,768]{1,0:T(8,128)S(1)} %bitcast.48), channel_id=1, source_target_pairs={{0,4},{1,5},{2,6},{3,7},{4,0},{5,1},{6,2},{7,3},{8,12},{9,13},{10,... | collective-permute-start | bytes 92168 | tf_op jit(solution)/shard_map/ppermute | solution.py:592
  (31 other events, 211.5 us)

commit v4 on v3

--- a/solution.py
+++ b/solution.py
@@ -81,6 +81,7 @@
         self.nq = 4 * self.cols - self.off
         self.cw = -(-self.cols // 128) * 128
         self.scale = 1.0 / math.sqrt(self.hd)
+        self.exact = math.log2(self.scale).is_integer()
 
 
 def source_rows(p, pos_ref, zz, xx):
@@ -166,12 +167,10 @@
         if last:
             x_ref, sg_ref, bo_ref, g2_ref, s2_ref = rest[:5]
             rest = rest[5:]
-            qkv_ref, prob_ref, ctx_ref, att_ref, mixed_ref, in_ref = rest[:6]
-            rest = rest[6:]
+            qkv_ref, prob_ref, ctx_ref, att_ref, wbuf, mixed_ref, in_ref = rest[:7]
         else:
-            qkv_ref, prob_ref, ctx_ref, att_ref = rest[:4]
-            rest = rest[4:]
-        wbuf, ctx = rest
+            qkv_ref, prob_ref, ctx_ref, att_ref, wbuf = rest[:5]
+        ctx = rest[-1]
         gather_blocks(p, w_refs, wbuf, pos_ref, other)
         low = low_ref[...]
         total = None
@@ -190,11 +189,14 @@
                     q = qkv_ref[b, first : first + win, qs : qs + hd]
                     k = qkv_ref[b, first : first + win, qs + p.cols : qs + p.cols + hd]
                     v = qkv_ref[b, first : first + win, qs + 2 * p.cols : qs + 2 * p.cols + hd]
-                    s = dot(q, k, NT) * p.scale
+                    if p.exact:
+                        s = dot(q * jnp.asarray(p.scale, BF16), k, NT)
+                    else:
+                        s = dot(q, k, NT) * p.scale
                     s = jnp.where(seen, s, -1e30)
                     e = jnp.exp(s - jnp.max(s, axis=-1, keepdims=True))
-                    prob = e * (1.0 / jnp.sum(e, axis=-1, keepdims=True))
-                    prob = jnp.where(valid, prob, 0.0).astype(BF16)
+                    share = jnp.where(valid, 1.0 / jnp.sum(e, axis=-1, keepdims=True), 0.0)
+                    prob = (e * share).astype(BF16)
                     prob_ref[(b * p.images + img) * lh + j] = prob
                     got.append(dot(prob, v))
                 if p.cw > p.cols:
@@ -227,6 +229,7 @@
         (sds((2 * p.images * lh, win, win), BF16), VMEM),
         (sds((2, pad, p.cw), BF16), VMEM),
         (sds((pad, p.width), F32), VMEM),
+        (sds((2, p.width, 4 * p.cols), BF16), VMEM),
     ]
     if last:
         outs += [(sds((pad, p.width), F32), VMEM), (sds((pad, p.width), BF16), VMEM)]
@@ -234,10 +237,7 @@
         body,
         outs,
         ins,
-        [
-            pltpu.VMEM((2, p.width, 4 * p.cols), BF16),
-            pltpu.VMEM((pad, p.cw), F32),
-        ],
+        [pltpu.VMEM((pad, p.cw), F32)],
         micros=5.5,
         name="attn_fwd",
     )
@@ -258,9 +258,8 @@
 
     return call(
         body,
-        [(sds((2, p.pad, p.hid), BF16), VMEM)] * 2,
+        [(sds((2, p.pad, p.hid), BF16), VMEM)] * 2 + [(sds((2, p.width, p.hid), BF16), VMEM)],
         [(pos, SMEM)] + [(w, VMEM) for w in weights] + [(mlp_in, VMEM), (bias, VMEM)],
-        [pltpu.VMEM((2, p.width, p.hid), BF16)],
         micros=2.5,
         name="up",
     )
@@ -276,10 +275,14 @@
         nr = len(received) if received is not None else 0
         got_refs, rest = rest[:nr], rest[nr:]
         out_refs, gbuf = rest[:-1], rest[-1]
+        turned_lhs = {}
+        for i, (lhs, _, _) in enumerate(pairs):
+            if id(lhs) not in turned_lhs:
+                turned_lhs[id(lhs)] = ops[2 * i][...].T
         for b in range(2):
             done = 0
             for i, at in enumerate(starts):
-                g = dot(ops[2 * i][...], ops[2 * i + 1][b], TN)
+                g = dot(turned_lhs[id(pairs[i][0])], ops[2 * i + 1][b])
                 end = at + g.shape[1]
                 if at < done:
                     gbuf[b, :, at:done] += g[:, : done - at]
@@ -303,16 +306,15 @@
 
 def down_kernel(p, pos, w_up, w_down, other, active, slope, out_grad, carry):
     def body(*refs):
-        nw = len(w_up)
-        pos_ref, u_refs, d_refs = refs[0], refs[1 : 1 + nw], refs[1 + nw : 1 + 2 * nw]
-        act_ref, slope_ref, og_ref = refs[1 + 2 * nw : 4 + 2 * nw]
-        rest = list(refs[4 + 2 * nw :])
+        nw = len(w_down)
+        pos_ref, d_refs = refs[0], refs[1 : 1 + nw]
+        ubuf, act_ref, slope_ref, og_ref = refs[1 + nw : 5 + nw]
+        rest = list(refs[5 + nw :])
         if carry is not None:
             out_in, back_in = rest[:2]
             rest = rest[2:]
-        out_ref, back_ref, low_ref, bias_ref, ubuf, dbuf = rest
+        out_ref, back_ref, low_ref, bias_ref, dbuf = rest
         gather_blocks(p, d_refs, dbuf, pos_ref, other, turned=True)
-        gather_blocks(p, u_refs, ubuf, pos_ref, other)
         og = og_ref[...]
         for b in range(2):
             grad = dot(og, dbuf[b]) * slope_ref[b].astype(F32)
@@ -331,8 +333,8 @@
                 back_ref[...] += back
                 out_ref[...] += out
 
-    ins = [(pos, SMEM)] + [(w, VMEM) for w in tuple(w_up) + tuple(w_down)]
-    ins += [(a, VMEM) for a in (active, slope, out_grad)]
+    ins = [(pos, SMEM)] + [(w, VMEM) for w in w_down]
+    ins += [(a, VMEM) for a in (w_up, active, slope, out_grad)]
     if carry is not None:
         ins += [(a, VMEM) for a in carry]
     return call(
@@ -344,74 +346,35 @@
             (sds((2, 1, p.hid), F32), VMEM),
         ],
         ins,
-        [
-            pltpu.VMEM((2, p.width, p.hid), BF16),
-            pltpu.VMEM((2, p.width, p.hid), BF16),
-        ],
+        [pltpu.VMEM((2, p.width, p.hid), BF16)],
         micros=5.0,
         name="down",
     )
 
 
-def middle_kernel(p, patches, out_grad, mixed, out_sum, back_sum, attended, gate, sel, vecs):
-    gain_one, shift_one, gain_two, b_down = vecs
-
-    def body(
-        x_ref, og_ref, mix_ref, out_ref, back_ref, att_ref, gate_ref, sel_ref,
-        g1_ref, s1_ref, g2_ref, bd_ref,
-        tok_ref, mg_ref, br_ref, logit_ref, gg_ref, gs_ref, gb_ref, gr_ref,
-    ):
-        mixed = mix_ref[...]
-        tok_ref[...] = (mixed + out_ref[...] + bd_ref[...])[: p.rows].astype(BF16)
-        xhat, rstd = norm_parts(mixed)
-        back = back_ref[...]
-        gg_ref[...] = jnp.sum(back * xhat, axis=0, keepdims=True)
-        gs_ref[...] = jnp.sum(back, axis=0, keepdims=True)
-        mg = og_ref[...].astype(F32) + norm_back(back * g2_ref[...], xhat, rstd)
+def middle_kernel(p, out_grad, mixed, back_sum, sel_gate, gain_two):
+    def body(og_ref, mix_ref, back_ref, sg_ref, g2_ref, mg_ref, br_ref):
+        xhat, rstd = norm_parts(mix_ref[...])
+        mg = og_ref[...].astype(F32) + norm_back(back_ref[...] * g2_ref[...], xhat, rstd)
         mg_ref[...] = mg
-        gate, sel = gate_ref[...], sel_ref[...]
-        branch = (gate * sel) * mg
-        gb_ref[...] = jnp.sum(branch, axis=0, keepdims=True)
-        br_ref[...] = branch.astype(BF16)
-        logit = sel * jnp.sum(mg * att_ref[...], axis=-1, keepdims=True) * gate * (1.0 - gate)
-        logit_ref[...] = logit
-        first, _ = norm_parts(x_ref[...].astype(F32))
-        normed = first * g1_ref[...] + s1_ref[...]
-        gr_ref[...] = jnp.sum(normed * logit, axis=0, keepdims=True)
-
-    vec = (sds((1, p.width), F32), VMEM)
-    return call(
-        body,
-        [
-            (sds((p.rows, p.width), BF16), VMEM),
-            (sds((p.pad, p.width), F32), VMEM),
-            (sds((p.pad, p.width), BF16), VMEM),
-            (sds((p.pad, 1), F32), VMEM),
-            vec, vec, vec, vec,
-        ],
-        [
-            (a, VMEM)
-            for a in (
-                patches, out_grad, mixed, out_sum, back_sum, attended, gate, sel,
-                gain_one, shift_one, gain_two, b_down,
-            )
-        ],
-        micros=2.6,
+        br_ref[...] = (sg_ref[...] * mg).astype(BF16)
+
+    return call(
+        body,
+        [(sds((p.pad, p.width), F32), VMEM), (sds((p.pad, p.width), BF16), VMEM)],
+        [(a, VMEM) for a in (out_grad, mixed, back_sum, sel_gate, gain_two)],
+        micros=2.0,
         name="middle",
     )
 
 
-def attention_values(p, pos, weights, other, branch, probs):
+def attention_values(p, weights, branch, probs):
     win, pad, lh, hd = p.win, p.pad, p.local_heads, p.hd
     lead = p.cw - p.cols
 
-    def body(*refs):
-        nw = len(weights)
-        pos_ref, w_refs = refs[0], refs[1 : 1 + nw]
-        br_ref, prob_ref, dc_ref, dv_ref, bias_ref, wbuf, gv = refs[1 + nw :]
-        gather_blocks(p, w_refs, wbuf, pos_ref, other, slice(0, p.cw))
+    def body(w_ref, br_ref, prob_ref, dc_ref, dv_ref, bias_ref, gv):
         for b in range(2):
-            dc_ref[b] = dot(br_ref[...], wbuf[b]).astype(BF16)
+            dc_ref[b] = dot(br_ref[...], w_ref[b, :, : p.cw]).astype(BF16)
             gv[...] = jnp.zeros((pad, p.cw), F32)
             for img in range(p.images):
                 here = slice(p.base[img], p.base[img] + win)
@@ -431,26 +394,23 @@
             (sds((2, pad, p.cw), BF16), VMEM),
             (sds((2, 1, p.cw), F32), VMEM),
         ],
-        [(pos, SMEM)] + [(w, VMEM) for w in weights] + [(branch, VMEM), (probs, VMEM)],
-        [pltpu.VMEM((2, p.width, p.cw), BF16), pltpu.VMEM((pad, p.cw), F32)],
+        [(a, VMEM) for a in (weights, branch, probs)],
+        [pltpu.VMEM((pad, p.cw), F32)],
         micros=2.5,
         name="attn_values",
     )
 
 
-def attention_backward(p, pos, weights, other, dc, dv, qkv, probs, carry):
+def attention_backward(p, weights, dc, dv, qkv, probs, carry):
     win, pad, lh, hd, cols = p.win, p.pad, p.local_heads, p.hd, p.cols
     lead = p.cw - p.cols
 
     def body(*refs):
-        nw = len(weights)
-        pos_ref, w_refs = refs[0], refs[1 : 1 + nw]
-        dc_ref, dv_ref, qkv_ref, prob_ref = refs[1 + nw : 5 + nw]
-        rest = list(refs[5 + nw :])
+        w_ref, dc_ref, dv_ref, qkv_ref, prob_ref = refs[:5]
+        rest = list(refs[5:])
         if carry is not None:
             carry_ref, rest = rest[0], rest[1:]
-        low_ref, n1_ref, bias_ref, wbuf, gq = rest
-        gather_blocks(p, w_refs, wbuf, pos_ref, other, slice(p.off, None))
+        low_ref, n1_ref, bias_ref, gq = rest
         total = None
         for b in range(2):
             gq[...] = jnp.zeros((pad, 2 * cols), F32)
@@ -465,9 +425,12 @@
                     v = qkv_ref[b, here, qs + 2 * cols : qs + 2 * cols + hd]
                     d = dc_ref[b, here, hd * j : hd * j + hd]
                     soft = prob_ref[(b * p.images + img) * lh + j].astype(F32)
-                    pg = dot(d, v, NT)
+                    if p.exact:
+                        pg = dot(d * jnp.asarray(p.scale, BF16), v, NT)
+                    else:
+                        pg = dot(d, v, NT) * p.scale
                     row = jnp.sum(soft * pg, axis=-1, keepdims=True)
-                    s = (soft * (pg - row) * p.scale).astype(BF16)
+                    s = (soft * (pg - row)).astype(BF16)
                     dqs.append(dot(s, k))
                     dks.append(dot(s, q, TN))
                 gq[here, :] += jnp.concatenate(dqs + dks, axis=1)
@@ -477,14 +440,13 @@
             low_ref[b] = low
             start = [jnp.zeros((pad, p.lo), BF16)] if p.lo else []
             gl = jnp.concatenate(start + [low, dv_ref[b][:, lead:]], axis=1)
-            part = dot(gl, wbuf[b], NT)
+            part = dot(gl, w_ref[b, :, p.off :], NT)
             total = part if total is None else total + part
         if carry is not None:
             total = total + carry_ref[...]
         n1_ref[...] = total
 
-    ins = [(pos, SMEM)] + [(w, VMEM) for w in weights]
-    ins += [(a, VMEM) for a in (dc, dv, qkv, probs)]
+    ins = [(a, VMEM) for a in (weights, dc, dv, qkv, probs)]
     if carry is not None:
         ins.append((carry, VMEM))
     return call(
@@ -495,32 +457,45 @@
             (sds((2, 1, 2 * cols), F32), VMEM),
         ],
         ins,
-        [pltpu.VMEM((2, p.width, p.nq), BF16), pltpu.VMEM((pad, 2 * cols), F32)],
+        [pltpu.VMEM((pad, 2 * cols), F32)],
         micros=6.0,
         name="attn_bwd",
     )
 
 
-def exit_kernel(p, patches, back, logit, router, gain_one, mixed_grad, common, query, value, up):
+def exit_kernel(p, arrays, query, value, up):
+    names = tuple(arrays)
     half = p.cols
     at = p.cw - p.cols
 
     def body(*refs):
-        x_ref, n_ref, l_ref, r_ref, g_ref, mg_ref = refs[:6]
-        c_refs = refs[6 : 6 + len(common)]
-        rest = list(refs[6 + len(common) :])
+        a = dict(zip(names, refs))
+        rest = list(refs[len(names) :])
         q_refs, v_refs, u_refs = (rest[i * p.pairs : (i + 1) * p.pairs] for i in range(3))
-        out_ref, *vec_refs = rest[3 * p.pairs :]
-        xhat, rstd = norm_parts(x_ref[...].astype(F32))
-        grad = n_ref[...] + l_ref[...] * r_ref[...]
-        g_gain = jnp.sum(grad * xhat, axis=0, keepdims=True)
-        g_shift = jnp.sum(grad, axis=0, keepdims=True)
-        total = mg_ref[...] + norm_back(grad * g_ref[...], xhat, rstd)
+        tok_ref, out_ref, *vec_refs = rest[3 * p.pairs :]
+        mixed = a["mixed"][...]
+        tok_ref[...] = (mixed + a["out"][...] + a["b_down"][...])[: p.rows].astype(BF16)
+        xhat, _ = norm_parts(mixed)
+        back = a["back"][...]
+        g_gain2 = jnp.sum(back * xhat, axis=0, keepdims=True)
+        g_shift2 = jnp.sum(back, axis=0, keepdims=True)
+        mg, gate, sel = a["mixed_grad"][...], a["gate"][...], a["sel"][...]
+        g_out = jnp.sum((sel * gate) * mg, axis=0, keepdims=True)
+        rows = jnp.sum(mg * a["attended"][...], axis=-1, keepdims=True)
+        logit = sel * rows * gate * (1.0 - gate)
+        xhat, rstd = norm_parts(a["patches"][...].astype(F32))
+        normed = xhat * a["gain_one"][...] + a["shift_one"][...]
+        g_router = jnp.sum(normed * logit, axis=0, keepdims=True)
+        grad = a["input"][...] + logit * a["router"][...]
+        g_gain1 = jnp.sum(grad * xhat, axis=0, keepdims=True)
+        g_shift1 = jnp.sum(grad, axis=0, keepdims=True)
+        total = mg + norm_back(grad * a["gain_one"][...], xhat, rstd)
         out_ref[...] = total[: p.rows].astype(BF16)
+        common = [g_gain1, g_shift1, g_router, g_out, g_gain2, g_shift2, a["g_down"][...]]
         for i in range(p.pairs):
             vec = vec_refs[i]
             vec[...] = jnp.zeros(vec.shape, F32)
-            for j, r in enumerate([g_gain, g_shift] + [c[...] for c in c_refs]):
+            for j, r in enumerate(common):
                 vec[j : j + 1, :] = r
             for b in range(2):
                 row = 8 + 2 * b
@@ -530,18 +505,10 @@
 
     return call(
         body,
-        [(sds((p.rows, p.width), BF16), VMEM)] + [(sds((12, p.width), F32), VMEM)] * p.pairs,
-        [
-            (a, VMEM)
-            for a in (
-                [patches, back, logit, router, gain_one, mixed_grad]
-                + list(common)
-                + list(query)
-                + list(value)
-                + list(up)
-            )
-        ],
-        micros=EXIT,
+        [(sds((p.rows, p.width), BF16), VMEM)] * 2
+        + [(sds((12, p.width), F32), VMEM)] * p.pairs,
+        [(v, VMEM) for v in list(arrays.values()) + list(query) + list(value) + list(up)],
+        micros=5.0,
         name="exit",
     )
 
@@ -571,6 +538,23 @@
         [(mine, VMEM), (got, VMEM)],
         micros=4.0,
         name="parts",
+    )
+
+
+def total_kernel(pieces, cuts):
+    def body(*refs):
+        total = sum((r[...].astype(F32) for r in refs[1:4]), refs[0][...].astype(F32))
+        for (first, last, turned), ref in zip(cuts, refs[4:]):
+            part = total[:, first:last]
+            ref[...] = part.T if turned else part
+
+    rows = pieces[0].shape[0]
+    return call(
+        body,
+        [(sds((b - a, rows) if t else (rows, b - a), F32), VMEM) for a, b, t in cuts],
+        [(v, VMEM) for v in pieces],
+        micros=4.0,
+        name="total",
     )
 
 
@@ -650,8 +634,7 @@
 
 
 def along_chips(pieces, *others):
-    got = [after(send(pieces[s], along_z(-s)), *others) for s in (1, 2, 3)]
-    return sum([g.astype(F32) for g in got], pieces[0].astype(F32))
+    return [pieces[0]] + [after(send(pieces[s], along_z(-s)), *others) for s in (1, 2, 3)]
 
 
 def gather_head(p, vector):
@@ -673,7 +656,7 @@
         self.keep, self.away = vecs
 
     def over_cores(self, *others):
-        self.vec = self.keep + after(send(self.away, core), *others)
+        self.vec = self.keep + send(after(self.away, *others), core)
 
     def over_z(self, step, *others):
         got = send(self.vec, lambda z, x, y, c: (z ^ step, x, y, c))
@@ -751,7 +734,7 @@
         attn_w, up_w, down_w = (gather_whole(p, v) for v in (attn_shard, w_up, w_down.T))
     sel_gate = gate * sel_col
 
-    qkvs, probs, ctxs, carry = [], [], [], None
+    qkvs, probs, ctxs, attn_full, carry = [], [], [], [], None
     for i in range(p.pairs):
         tail = (x_pad, sel_gate, b_out, gain_two, shift_two) if i == p.pairs - 1 else None
         if fast and i == 1:
@@ -764,55 +747,47 @@
         probs.append(got[1])
         ctxs.append(got[2])
         carry = got[3]
-    attended, mixed, mlp_in = got[3], got[4], got[5]
-
-    acts, slopes = [], []
-    up_in = mlp_in
-    for i in range(p.pairs):
-        act, slope = up_kernel(p, pos, up_w[i], i, up_in, up_bias[2 * i : 2 * i + 2])
-        acts.append(act)
-        slopes.append(slope)
+        attn_full.append(got[4])
+    attended, mixed, mlp_in = got[3], got[5], got[6]
+
+    def up(i, rows):
+        return up_kernel(p, pos, up_w[i], i, rows, up_bias[2 * i : 2 * i + 2])
 
     def values(i, branch):
-        return attention_values(p, pos, attn_w[i], i if fast else 0, branch, probs[i])
+        return attention_values(p, attn_full[i], branch, probs[i])
 
     def backward(i, dc, dv, carry):
-        return attention_backward(
-            p, pos, attn_w[i], i if fast else 0, dc, dv, qkvs[i], probs[i], carry
-        )
-
-    def grads(pairs, received, name, other, turned=False):
-        return weight_grad(p, pos, other, pairs, received, name, turned)
+        return attention_backward(p, attn_full[i], dc, dv, qkvs[i], probs[i], carry)
+
+    def grads(pairs, received, name, other):
+        return weight_grad(p, pos, other, pairs, received, name)
 
     def attention_pairs(i, dv, low):
         return [(branch, ctxs[i], 0), (rows_low, dv, p.off), (rows_low, low, 2 * cols)]
 
     def down(i, grad_in, carry):
-        return down_kernel(p, pos, up_w[i], down_w[i], i, acts[i], slopes[i], grad_in, carry)
-
-    def middle(back, out):
-        return middle_kernel(
-            p, x_pad, og_pad, mixed, out, back, attended, gate, sel_col,
-            (gain_one, shift_one, gain_two, b_down),
+        return down_kernel(p, pos, up_full[i], down_w[i], i, acts[i], slopes[i], grad_in, carry)
+
+    def leave(back, qsums, vsums, up_sums):
+        arrays = dict(
+            patches=x_pad, mixed=mixed, out=out_sum, back=back_sum, mixed_grad=mixed_grad,
+            attended=attended, input=back, gate=gate, sel=sel_col, gain_one=gain_one,
+            shift_one=shift_one, router=router, b_down=b_down, g_down=g_down_bias,
         )
-
-    def leave(back, qsums, vsums, up_sums):
-        common = (g_router, g_out_bias, g_gain2, g_shift2, g_down_bias)
-        return exit_kernel(
-            p, x_pad, back, logit, router, gain_one, mixed_grad, common, qsums, vsums, up_sums
-        )
+        return exit_kernel(p, arrays, qsums, vsums, up_sums)
 
     if fast:
-        down_w = both_cores(down_eight, down_rest, acts[1])
-        gd1 = grads([(og_pad, acts[1], 0)], None, "grad_down", 1)
+        act1, slope1, full1 = up(1, mlp_in)
+        gd1 = grads([(og_pad, act1, 0)], None, "grad_down", 1)
         gd1_got = [send(o, core) for o in gd1]
-        out_sum, back_sum, low0, sum0 = down(0, after(og_pad, *gd1), None)
-        gd0 = grads([(after(og_pad, low0), acts[0], 0)], gd1_got, "grad_down", 0)
+        act0, slope0, full0 = up(0, after(mlp_in, *gd1))
+        acts, slopes, up_full = (act0, act1), (slope0, slope1), (full0, full1)
+        down_w = both_cores(down_eight, down_rest, act0)
+        gd0 = grads([(og_pad, act0, 0)], gd1_got, "grad_down", 0)
+        out_sum, back_sum, low0, sum0 = down(0, after(og_pad, *gd0), None)
         down_sum = Scatter(*gd0)
         out_sum, back_sum, low1, sum1 = down(1, after(og_pad, *gd0), (out_sum, back_sum))
-        tokens, mixed_grad, branch, logit, g_gain2, g_shift2, g_out_bias, g_router = middle(
-            back_sum, out_sum
-        )
+        mixed_grad, branch = middle_kernel(p, og_pad, mixed, back_sum, sel_gate, gain_two)
         gu1 = grads([(after(mlp_in, branch), low1, 0)], None, "grad_up", 1)
         gu1_got = [send(o, core) for o in gu1]
         dc1, dv1, vsum1 = values(1, after(branch, *gu1))
@@ -831,29 +806,35 @@
         ga0 = grads(attention_pairs(0, dv0, low0), ga1_got, "grad_attn", 0)
         attn_sum = Scatter(*ga0)
         carry = after(carry, *ga0)
-        grad_patches, *vecs = leave(carry, (qsum0, qsum1), (vsum0, vsum1), (sum0, sum1))
+        tokens, grad_patches, *vecs = leave(carry, (qsum0, qsum1), (vsum0, vsum1), (sum0, sum1))
         vec_sum = VectorSum(vecs)
-        grad_down = along_chips(down_sum.pieces, grad_patches)
-        vec_sum.over_cores(grad_down)
-        up_sum.second(vec_sum.vec)
-        vec_sum.vec = after(vec_sum.vec, *up_sum.pieces)
-        attn_sum.first(*up_sum.pieces)
-        grad_up = along_chips(up_sum.pieces, attn_sum.other)
-        vec_sum.over_z(1, grad_up)
+        down_parts = along_chips(down_sum.pieces, grad_patches)
+        up_sum.second(*down_parts)
+        vec_sum.over_cores(*up_sum.pieces)
+        attn_sum.first(vec_sum.vec)
+        down_parts[0] = after(down_parts[0], attn_sum.other)
+        (grad_down,) = total_kernel(down_parts, [(0, p.hid, True)])
+        up_parts = along_chips(up_sum.pieces, grad_down)
+        vec_sum.over_z(1, *up_parts)
         attn_sum.second(vec_sum.vec)
         vec_sum.over_z(2, *attn_sum.pieces)
-        grad_attn = along_chips(attn_sum.pieces, vec_sum.vec)
-        summed = vec_sum.over_xy(grad_attn)
+        up_parts[0] = after(up_parts[0], *attn_sum.pieces)
+        (grad_up,) = total_kernel(up_parts, [(0, p.hid, False)])
+        attn_parts = along_chips(attn_sum.pieces, grad_up)
+        summed = vec_sum.over_xy(grad_up)
+        grad_out, grad_value, grad_query, grad_key = total_kernel(
+            attn_parts, [(i * cols, (i + 1) * cols, i == 0) for i in range(4)]
+        )
     else:
+        acts, slopes, up_full = zip(*(up(i, mlp_in) for i in range(p.pairs)))
         carry, lows, up_sums = None, [], []
         for i in range(p.pairs):
             got = down(i, og_pad, carry)
             carry = (got[0], got[1])
             lows.append(got[2])
             up_sums.append(got[3])
-        tokens, mixed_grad, branch, logit, g_gain2, g_shift2, g_out_bias, g_router = middle(
-            carry[1], carry[0]
-        )
+        out_sum, back_sum = carry
+        mixed_grad, branch = middle_kernel(p, og_pad, mixed, back_sum, sel_gate, gain_two)
         carry, blocks, vsums, qsums = None, [], [], []
         for i in range(p.pairs):
             dc, dv, vsum = values(i, branch)
@@ -861,7 +842,7 @@
             blocks += grads(attention_pairs(i, dv, low), None, "grad_attn", 0)
             vsums.append(vsum)
             qsums.append(qsum)
-        grad_patches, *vecs = leave(carry, qsums, vsums, up_sums)
+        tokens, grad_patches, *vecs = leave(carry, qsums, vsums, up_sums)
         grad_down, grad_up, grad_attn = (
             scatter_whole(p, g)
             for g in (
@@ -870,6 +851,11 @@
                 blocks,
             )
         )
+        grad_down = grad_down.T
+        grad_out, grad_value, grad_query, grad_key = (
+            grad_attn[:, i * cols : (i + 1) * cols] for i in range(4)
+        )
+        grad_out = grad_out.T
         summed = sum_vectors(p, vecs)
 
     vecs = [summed[i] for i in range(7)]
@@ -880,18 +866,18 @@
         vecs[0],
         vecs[1],
         vecs[2],
-        grad_attn[:, 2 * cols : 3 * cols],
+        grad_query,
         owned[:cols],
-        grad_attn[:, 3 * cols :],
-        grad_attn[:, cols : 2 * cols],
+        grad_key,
+        grad_value,
         owned[cols : 2 * cols],
-        grad_attn[:, :cols].T,
+        grad_out,
         vecs[3],
         vecs[4],
         vecs[5],
         grad_up,
         hidden_sum,
-        grad_down.T,
+        grad_down,
         vecs[6],
     )
 

time: 197 us -> 183 us (0.929)
  waiting for transfers between devices: 56.2 us -> 43.8 us
    ppermute x50, waiting for transfers between devices: 56.2 us -> 43.8 us  [send(): return lax.ppermute(v, ('dp', 'head'), table(move))]
    pallas_call x25 -> x28, Pallas kernels: 60.1 us -> 58.7 us  [call(): pl.pallas_call(body, out_shape=[o for o, _ in outs], in_specs=[s for _, s...]
  transfers between devices with their start and end apart: 50 -> 50, of which waited for: 17 -> 17; matrix products, arithmetic and copies ran while one was open for 4% -> 4% of each run, Pallas kernels for 31% -> 32%
where the time goes in v4:
time: 183 us; the launch traced here: 179 us
  starting transfers between devices  65.2 us (36%)
  Pallas kernels  58.7 us (32%)
  waiting for transfers between devices  43.8 us (24%)
  local copies, waits for them, and re-layouts  6.79 us (4%)
  other arithmetic  3.4 us (2%)
    ppermute x50, starting transfers between devices, send(): return lax.ppermute(v, ('dp', 'head'), table(move))  65.2 us
    pallas_call x28, Pallas kernels, call(): pl.pallas_call(body, out_shape=[o for o, _ in outs], in_specs=[s for _, s...  58.7 us
    ppermute x50, waiting for transfers between devices, send(): return lax.ppermute(v, ('dp', 'head'), table(move))  43.8 us
  transfers between devices with their start and end apart: 50, of which 17 were waited for; matrix products, arithmetic and copies ran while one was open for 4% of the time, Pallas kernels for 32%

profile of v4, /device:TPU:0, one launch (start us, length us, event | category | flops | bytes accessed | tf_op | source)
XLA Modules:
  0.0 179.4 jit_solution(16961208882467026123)
XLA Ops:
  2.6 3.1 %collective-permute-start = (bf16[96,768]{1,0:T(8,128)(2,1)S(1)}, bf16[96,768]{1,0:T(8,128)(2,1)S(1)}, u32[]{:S(2)}, u32[]{:S(2)}) collective-permute-start(bf16[96,768]{1,0:T(8,128)(2,1)S(1)} %pad_maximum_fusion.6), channel_id=1, source_target_pairs={{0,8},{1,9},{2,10},{3,11},{4,12},{5,13},{6,14},{7,15},{8,16},{9,17... | collective-permute-start | bytes 442376 | tf_op jit(solution)/shard_map/ppermute | solution.py:576
  5.7 2.6 %collective-permute-start.1 = (bf16[96,768]{1,0:T(8,128)(2,1)S(1)}, bf16[96,768]{1,0:T(8,128)(2,1)S(1)}, u32[]{:S(2)}, u32[]{:S(2)}) collective-permute-start(bf16[96,768]{1,0:T(8,128)(2,1)S(1)} %pad_maximum_fusion.6), channel_id=1, source_target_pairs={{0,16},{1,17},{2,18},{3,19},{4,20},{5,21},{6,22},{7,23},{8,24},{9,... | collective-permute-start | bytes 442376 | tf_op jit(solution)/shard_map/ppermute | solution.py:576
  9.6 2.1 %concatenate.17 = bf16[1152]{0:T(1024)(128)(2,1)S(1)} concatenate(bf16[192]{0:T(256)(128)(2,1)} %param.26, bf16[192]{0:T(256)(128)(2,1)} %param.29, bf16[768]{0:T(1024)(128)(2,1)} %param.35), dimensions={0} | concatenate | bytes 4608 | tf_op jit(solution)/shard_map/concatenate | solution.py:688
  20.2 3.2 %collective-permute-start.7 = (bf16[96,768]{1,0:T(8,128)(2,1)S(1)}, bf16[96,768]{1,0:T(8,128)(2,1)S(1)}, u32[]{:S(2)}, u32[]{:S(2)}) collective-permute-start(bf16[96,768]{1,0:T(8,128)(2,1)S(1)} %copy-done.10), channel_id=1, source_target_pairs={{0,8},{1,9},{2,10},{3,11},{4,12},{5,13},{6,14},{7,15},{8,16},{9,17... | collective-permute-start | bytes 442376 | tf_op jit(solution)/shard_map/ppermute | solution.py:576
  30.9 3.2 %collective-permute-done.9 = bf16[96,768]{1,0:T(8,128)(2,1)S(1)} collective-permute-done((bf16[96,768]{1,0:T(8,128)(2,1)S(1)}, bf16[96,768]{1,0:T(8,128)(2,1)S(1)}, u32[]{:S(2)}, u32[]{:S(2)}) %collective-permute-start.9) | collective-permute-done | bytes 147488 | tf_op jit(solution)/shard_map/ppermute | solution.py:576
  35.3 3.7 %collective-permute-start.15 = (bf16[2,96,768]{2,1,0:T(8,128)(2,1)S(1)}, bf16[2,96,768]{2,1,0:T(8,128)(2,1)S(1)}, u32[]{:S(2)}, u32[]{:S(2)}) collective-permute-start(bf16[2,96,768]{2,1,0:T(8,128)(2,1)S(1)} %pad_maximum_fusion.5), channel_id=1, source_target_pairs={{0,8},{1,9},{2,10},{3,11},{4,12},{5,13},{6,14},{7,15},{8,16},{9,17... | collective-permute-start | bytes 884744 | tf_op jit(solution)/shard_map/ppermute | solution.py:576
  39.1 2.4 %collective-permute-start.16 = (bf16[2,96,768]{2,1,0:T(8,128)(2,1)S(1)}, bf16[2,96,768]{2,1,0:T(8,128)(2,1)S(1)}, u32[]{:S(2)}, u32[]{:S(2)}) collective-permute-start(bf16[2,96,768]{2,1,0:T(8,128)(2,1)S(1)} %pad_maximum_fusion.5), channel_id=1, source_target_pairs={{0,16},{1,17},{2,18},{3,19},{4,20},{5,21},{6,22},{7,23},{8,24},{9,... | collective-permute-start | bytes 884744 | tf_op jit(solution)/shard_map/ppermute | solution.py:576
  41.7 7.6 %collective-permute-done.11 = bf16[4,96,768]{2,1,0:T(8,128)(2,1)S(1)} collective-permute-done((bf16[4,96,768]{2,1,0:T(8,128)(2,1)S(1)}, bf16[4,96,768]{2,1,0:T(8,128)(2,1)S(1)}, u32[]{:S(2)}, u32[]{:S(2)}) %collective-permute-start.11) | collective-permute-done | bytes 589856 | tf_op jit(solution)/shard_map/ppermute | solution.py:576
  49.6 2.0 %collective-permute-done.12.refs_2_ = bf16[2,4,96,768]{3,2,1,0:T(8,128)(2,1)S(1)} collective-permute-done((bf16[2,4,96,768]{3,2,1,0:T(8,128)(2,1)S(1)}, bf16[2,4,96,768]{3,2,1,0:T(8,128)(2,1)S(1)}, u32[]{:S(2)}, u32[]{:S(2)}) %collective-permute-start.12) | collective-permute-done | bytes 1179680 | tf_op jit(solution)/shard_map/ppermute | solution.py:576
  53.3 4.9 %attn_fwd.2 = (bf16[2,400,640]{2,1,0:T(8,128)(2,1)S(1)}, bf16[12,208,208]{2,1,0:T(8,128)(2,1)S(1)}, bf16[2,400,256]{2,1,0:T(8,128)(2,1)S(1)}, f32[400,768]{1,0:T(8,128)S(1)}, bf16[2,768,768]{2,1,0:T(8,128)(2,1)S(1)}) custom-call(s32[3]{0:T(128)S(1)} %pad_add_fusion.refs_0_, bf16[2,4,96,768]{3,2,1,0:T(8,128)(2,1)S(1)} %pad_maximum_fusion.refs_1_, ...), custom_call_target="tpu_custom_call" | custom-call | flops 22000001024 | tf_op jit(solution)/shard_map/attn_fwd/pallas_call | solution.py:36
  60.5 7.4 %collective-permute-done.13.refs_2_ = bf16[2,4,96,768]{3,2,1,0:T(8,128)(2,1)S(1)} collective-permute-done((bf16[2,4,96,768]{3,2,1,0:T(8,128)(2,1)S(1)}, bf16[2,4,96,768]{3,2,1,0:T(8,128)(2,1)S(1)}, u32[]{:S(2)}, u32[]{:S(2)}) %collective-permute-start.13) | collective-permute-done | bytes 1179680 | tf_op jit(solution)/shard_map/ppermute | solution.py:576
  67.9 5.4 %attn_fwd.3 = (bf16[2,400,640]{2,1,0:T(8,128)(2,1)S(1)}, bf16[12,208,208]{2,1,0:T(8,128)(2,1)S(1)}, bf16[2,400,256]{2,1,0:T(8,128)(2,1)S(1)}, f32[400,768]{1,0:T...) custom-call(s32[3]{0:T(128)S(1)} %pad_add_fusion.refs_0_, ...), custom_call_target="tpu_custom_call" | custom-call | flops 22000001024 | tf_op jit(solution)/shard_map/attn_fwd/pallas_call | solution.py:36
  73.3 2.5 %up.2 = (bf16[2,400,768]{2,1,0:T(8,128)(2,1)S(1)}, bf16[2,400,768]{2,1,0:T(8,128)(2,1)S(1)}, bf16[2,768,768]{2,1,0:T(8,128)(2,1)S(1)}) custom-call(s32[3]{0:T(128)S(1)} %pad_add_fusion.refs_0_, bf16[2,4,96,768]{3,2,1,0:T(8,128)(2,1)S(1)} %collective-permute-done.18.refs_1_, bf16[2,4,96,768]{3,2,1,0:T(8,128)(2,1)S(1)} %collective-permute-done.19.refs_2_, ...), custom_call_target="tpu_custom_call" | custom-call | flops 10000000000 | tf_op jit(solution)/shard_map/up/pallas_call | solution.py:36
  75.9 2.2 %grad_down.2 = (bf16[2,4,96,768]{3,2,1,0:T(8,128)(2,1)S(1)}, bf16[2,4,96,768]{3,2,1,0:T(8,128)(2,1)S(1)}) custom-call(s32[3]{0:T(128)S(1)} %pad_add_fusion.refs_0_, bf16[400,768]{1,0:T(8,128)(2,1)S(1)} %pad.20.og_ref.refs_1_.refs_6_, bf16[2,400,768]{2,1,0:T(8,128)(2,1)S(1)} %get-tuple-element.165.refs_2_.refs_4_), custom_call_target="tpu_custom_call" | custom-call | flops 9200000000 | tf_op jit(solution)/shard_map/grad_down/pallas_call | solution.py:36
  78.7 2.8 %up.3 = (bf16[2,400,768]{2,1,0:T(8,128)(2,1)S(1)}, bf16[2,400,768]{2,1,0:T(8,128)(2,1)S(1)}, bf16[2,768,768]{2,1,0:T(8,128)(2,1)S(1)}) custom-call(s32[3]{0:T(128)S(1)} %pad_add_fusion.refs_0_, bf16[2,4,96,768]{3,2,1,0:T(8,128)(2,1)S(1)} %pad_maximum_fusion.1.refs_1_, bf16[2,4,96,768]{3,2,1,0:T(8,128)(2,1)S(1)} %collective-permute-done.13.refs_2_, ...), custom_call_target="tpu_custom_call" | custom-call | flops 10000000000 | tf_op jit(solution)/shard_map/up/pallas_call | solution.py:36
  82.8 2.5 %grad_down.3 = (bf16[2,4,96,768]{3,2,1,0:T(8,128)(2,1)S(1)}, bf16[2,4,96,768]{3,2,1,0:T(8,128)(2,1)S(1)}) custom-call(s32[3]{0:T(128)S(1)} %pad_add_fusion.refs_0_, bf16[400,768]{1,0:T(8,128)(2,1)S(1)} %pad.20.og_ref.refs_1_.refs_6_, bf16[2,400,768]{2,1,0:T(8,128)(2,1)S(1)} %get-tuple-element.169.refs_2_.refs_4_, ...), custom_call_target="tpu_custom_call" | custom-call | flops 9200000000 | tf_op jit(solution)/shard_map/grad_down/pallas_call | solution.py:36
  87.0 3.9 %down.2 = (f32[400,768]{1,0:T(8,128)S(1)}, f32[400,768]{1,0:T(8,128)S(1)}, bf16[2,400,768]{2,1,0:T(8,128)(2,1)S(1)}, f32[2,1,768]{2,1,0:T(1,128)S(1)}) custom-call(s32[3]{0:T(128)S(1)} %pad_add_fusion.refs_0_, bf16[4,2,96,768]{3,2,1,0:T(8,128)(2,1)S(1)} %pad_maximum_fusion.2.refs_1_, bf16[4,2,96,768]{3,2,1,0:T(8,128)(2,1)S(1)} %collective-permute-done.21.refs_2_, ...), custom_call_target="tpu_custom_call" | custom-call | flops 20000000000 | tf_op jit(solution)/shard_map/down/pallas_call | solution.py:36
  91.0 4.0 %down.3 = (f32[400,768]{1,0:T(8,128)S(1)}, f32[400,768]{1,0:T(8,128)S(1)}, bf16[2,400,768]{2,1,0:T(8,128)(2,1)S(1)}, f32[2,1,768]{2,1,0:T(1,128)S(1)}) custom-call(s32[3]{0:T(128)S(1)} %pad_add_fusion.refs_0_, bf16[4,2,96,768]{3,2,1,0:T(8,128)(2,1)S(1)} %collective-permute-done.20.refs_1_, bf16[4,2,96,768]{3,2,1,0:T(8,128)(2,1)S(1)} %collective-permute-done.22.refs_2_, ...), custom_call_target="tpu_custom_call" | custom-call | flops 20000000000 | tf_op jit(solution)/shard_map/down/pallas_call | solution.py:36
  96.0 2.2 %grad_up.2 = (bf16[2,4,96,768]{3,2,1,0:T(8,128)(2,1)S(1)}, bf16[2,4,96,768]{3,2,1,0:T(8,128)(2,1)S(1)}) custom-call(s32[3]{0:T(128)S(1)} %pad_add_fusion.refs_0_, bf16[400,768]{1,0:T(8,128)(2,1)S(1)} %get-tuple-element.188.refs_3_.refs_1_, bf16[2,400,768]{2,1,0:T(8,128)(2,1)S(1)} %get-tuple-element.189.refs_2_), custom_call_target="tpu_custom_call" | custom-call | flops 9200000000 | tf_op jit(solution)/shard_map/grad_up/pallas_call | solution.py:36
  103.0 2.5 %grad_up.3 = (bf16[2,4,96,768]{3,2,1,0:T(8,128)(2,1)S(1)}, bf16[2,4,96,768]{3,2,1,0:T(8,128)(2,1)S(1)}) custom-call(s32[3]{0:T(128)S(1)} %pad_add_fusion.refs_0_, bf16[400,768]{1,0:T(8,128)(2,1)S(1)} %get-tuple-element.188.refs_3_.refs_1_, bf16[2,400,768]{2,1,0:T(8,128)(2,1)S(1)} %get-tuple-element.200.refs_2_, ...), custom_call_target="tpu_custom_call" | custom-call | flops 9200000000 | tf_op jit(solution)/shard_map/grad_up/pallas_call | solution.py:36
  106.6 4.8 %attn_bwd.2 = (bf16[2,400,384]{2,1,0:T(8,128)(2,1)S(1)}, f32[400,768]{1,0:T(8,128)S(1)}, f32[2,1,384]{2,1,0:T(1,128)S(1)}) custom-call(bf16[2,768,768]{2,1,0:T(8,128)(2,1)S(1)} %get-tuple-element.187.w_ref.refs_0_, bf16[2,400,256]{2,1,0:T(8,128)(2,1)S(1)} %get-tuple-element.207.refs_1_, bf16[2,400,256]{2,1,0:T(8,128)(2,1)S(1)} %get-tuple-element.194.refs_2_.refs_4_, ...), custom_call_target="tpu_custom_call" | custom-call | flops 24000000000 | tf_op jit(solution)/shard_map/attn_bwd/pallas_call | solution.py:36
  111.4 2.6 %grad_attn.2 = (bf16[2,4,96,768]{3,2,1,0:T(8,128)(2,1)S(1)}, bf16[2,4,96,768]{3,2,1,0:T(8,128)(2,1)S(1)}) custom-call(s32[3]{0:T(128)S(1)} %pad_add_fusion.refs_0_, bf16[400,768]{1,0:T(8,128)(2,1)S(1)} %get-tuple-element.195.br_ref.refs_1_, bf16[2,400,256]{2,1,0:T(8,128)(2,1)S(1)} %get-tuple-element.198.refs_2_, bf16[400,768]{1,0:T(8,128)(2,1)S(1)} %copy-done.3, ...), custom_call_target="tpu_custom_call" | custom-call | flops 9200000000 | tf_op jit(solution)/shard_map/grad_attn/pallas_call | solution.py:36
  116.1 4.6 %collective-permute-start.35 = (bf16[96,768]{1,0:T(8,128)(2,1)S(1)}, bf16[96,768]{1,0:T(8,128)(2,1)S(1)}, u32[]{:S(2)}, u32[]{:S(2)}) collective-permute-start(bf16[96,768]{1,0:T(8,128)(2,1)S(1)} %get-tuple-element.216), channel_id=1, source_target_pairs={{0,8},{1,9},{2,10},{3,11},{4,12},{5,13},{6,14},{7,15},{8,16},{9,17... | collective-permute-start | bytes 442376 | tf_op jit(solution)/shard_map/ppermute | solution.py:576
  122.1 4.8 %attn_bwd.3 = (bf16[2,400,384]{2,1,0:T(8,128)(2,1)S(1)}, f32[400,768]{1,0:T(8,128)S(1)}, f32[2,1,384]{2,1,0:T(1,128)S(1)}) custom-call(bf16[2,768,768]{2,1,0:T(8,128)(2,1)S(1)} %get-tuple-element.185.w_ref.refs_0_, bf16[2,400,256]{2,1,0:T(8,128)(2,1)S(1)} %get-tuple-element.217.refs_1_, bf16[2,400,256]{2,1,0:T(8,128)(2,1)S(1)} %get-tuple-element.201.refs_2_.refs_4_, ...), custom_call_target="tpu_custom_call" | custom-call | flops 24000000000 | tf_op jit(solution)/shard_map/attn_bwd/pallas_call | solution.py:36
  126.9 2.9 %collective-permute-start.33 = (bf16[96,768]{1,0:T(8,128)(2,1)S(1)}, bf16[96,768]{1,0:T(8,128)(2,1)S(1)}, u32[]{:S(2)}, u32[]{:S(2)}) collective-permute-start(bf16[96,768]{1,0:T(8,128)(2,1)S(1)} %get-tuple-element.214), channel_id=1, source_target_pairs={{0,24},{1,25},{2,26},{3,27},{4,28},{5,29},{6,30},{7,31},{8,0},{9,1... | collective-permute-start | bytes 442376 | tf_op jit(solution)/shard_map/ppermute | solution.py:576
  130.2 2.9 %grad_attn.3 = (bf16[2,4,96,768]{3,2,1,0:T(8,128)(2,1)S(1)}, bf16[2,4,96,768]{3,2,1,0:T(8,128)(2,1)S(1)}) custom-call(s32[3]{0:T(128)S(1)} %pad_add_fusion.refs_0_, bf16[400,768]{1,0:T(8,128)(2,1)S(1)} %get-tuple-element.195.br_ref.refs_1_, bf16[2,400,256]{2,1,0:T(8,128)(2,1)S(1)} %get-tuple-element.221.refs_2_, bf16[400,768]{1,0:T(8,128)(2,1)S(1)} %copy-done.3, ...), custom_call_target="tpu_custom_call" | custom-call | flops 9200000000 | tf_op jit(solution)/shard_map/grad_attn/pallas_call | solution.py:36
  134.8 3.0 %exit.1 = (bf16[394,768]{1,0:T(8,128)(2,1)}, bf16[394,768]{1,0:T(8,128)(2,1)}, f32[12,768]{1,0:T(8,128)S(1)}, f32[12,768]{1,0:T(8,128)S(1)}) custom-call(bf16[400,768]{1,0:T(8,128)(2,1)S(1)} %pad.19.x_ref.refs_7_.refs_0_, f32[400,768]{1,0:T(8,128)S(1)} %get-tuple-element.159.mix_ref.refs_1_, f32[400,768]{1,0:T(8,128)S(1)} %get-tuple-element.181.refs_2_, ...), custom_call_target="tpu_custom_call" | custom-call | flops 20000000000 | tf_op jit(solution)/shard_map/exit/pallas_call | solution.py:36
  137.8 7.3 %collective-permute-done.32.g_ref = bf16[4,96,768]{2,1,0:T(8,128)(2,1)S(1)} collective-permute-done((bf16[4,96,768]{2,1,0:T(8,128)(2,1)S(1)}, bf16[4,96,768]{2,1,0:T(8,128)(2,1)S(1)}, u32[]{:S(2)}, u32[]{:S(2)}) %collective-permute-start.32) | collective-permute-done | bytes 589856 | tf_op jit(solution)/shard_map/ppermute | solution.py:576
  145.5 3.7 %collective-permute-start.38 = (bf16[96,768]{1,0:T(8,128)(2,1)S(1)}, bf16[96,768]{1,0:T(8,128)(2,1)S(1)}, u32[]{:S(2)}, u32[]{:S(2)}) collective-permute-start(bf16[96,768]{1,0:T(8,128)(2,1)S(1)} %get-tuple-element.247), channel_id=1, source_target_pairs={{0,24},{1,25},{2,26},{3,27},{4,28},{5,29},{6,30},{7,31},{8,0},{9,1... | collective-permute-start | bytes 442376 | tf_op jit(solution)/shard_map/ppermute | solution.py:576
  154.0 5.5 %collective-permute-done.40.refs_2_ = bf16[96,768]{1,0:T(8,128)(2,1)S(1)} collective-permute-done((bf16[96,768]{1,0:T(8,128)(2,1)S(1)}, bf16[96,768]{1,0:T(8,128)(2,1)S(1)}, u32[]{:S(2)}, u32[]{:S(2)}) %collective-permute-start.40) | collective-permute-done | bytes 147488 | tf_op jit(solution)/shard_map/ppermute | solution.py:576
  163.2 2.6 %collective-permute-start.48 = (bf16[96,768]{1,0:T(8,128)(2,1)S(1)}, bf16[96,768]{1,0:T(8,128)(2,1)S(1)}, u32[]{:S(2)}, u32[]{:S(2)}) collective-permute-start(bf16[96,768]{1,0:T(8,128)(2,1)S(1)} %get-tuple-element.262), channel_id=1, source_target_pairs={{0,16},{1,17},{2,18},{3,19},{4,20},{5,21},{6,22},{7,23},{8,24},{9,... | collective-permute-start | bytes 442376 | tf_op jit(solution)/shard_map/ppermute | solution.py:576
  172.6 2.7 %collective-permute-start.47 = (bf16[96,768]{1,0:T(8,128)(2,1)S(1)}, bf16[96,768]{1,0:T(8,128)(2,1)S(1)}, u32[]{:S(2)}, u32[]{:S(2)}) collective-permute-start(bf16[96,768]{1,0:T(8,128)(2,1)S(1)} %get-tuple-element.261), channel_id=1, source_target_pairs={{0,24},{1,25},{2,26},{3,27},{4,28},{5,29},{6,30},{7,31},{8,0},{9,1... | collective-permute-start | bytes 442376 | tf_op jit(solution)/shard_map/ppermute | solution.py:576
  (188 shorter events, 60.3 us)
Async XLA Ops:
  2.6 15.2 %collective-permute-start = (bf16[96,768]{1,0:T(8,128)(2,1)S(1)}, bf16[96,768]{1,0:T(8,128)(2,1)S(1)}, u32[]{:S(2)}, u32[]{:S(2)}) collective-permute-start(bf16[96,768]{1,0:T(8,128)(2,1)S(1)} %pad_maximum_fusion.6), channel_id=1, source_target_pairs={{0,8},{1,9},{2,10},{3,11},{4,12},{5,13},{6,14},{7,15},{8,16},{9,17... | collective-permute-start | bytes 442376 | tf_op jit(solution)/shard_map/ppermute | solution.py:576
  5.7 12.3 %collective-permute-start.1 = (bf16[96,768]{1,0:T(8,128)(2,1)S(1)}, bf16[96,768]{1,0:T(8,128)(2,1)S(1)}, u32[]{:S(2)}, u32[]{:S(2)}) collective-permute-start(bf16[96,768]{1,0:T(8,128)(2,1)S(1)} %pad_maximum_fusion.6), channel_id=1, source_target_pairs={{0,16},{1,17},{2,18},{3,19},{4,20},{5,21},{6,22},{7,23},{8,24},{9,... | collective-permute-start | bytes 442376 | tf_op jit(solution)/shard_map/ppermute | solution.py:576
  8.3 9.7 %collective-permute-start.2 = (bf16[96,768]{1,0:T(8,128)(2,1)S(1)}, bf16[96,768]{1,0:T(8,128)(2,1)S(1)}, u32[]{:S(2)}, u32[]{:S(2)}) collective-permute-start(bf16[96,768]{1,0:T(8,128)(2,1)S(1)} %pad_maximum_fusion.6), channel_id=1, source_target_pairs={{0,24},{1,25},{2,26},{3,27},{4,28},{5,29},{6,30},{7,31},{8,0},{9,1... | collective-permute-start | bytes 442376 | tf_op jit(solution)/shard_map/ppermute | solution.py:576
  18.6 9.9 %collective-permute-start.6 = (bf16[4,96,768]{2,1,0:T(8,128)(2,1)S(1)}, bf16[4,96,768]{2,1,0:T(8,128)(2,1)S(1)}, u32[]{:S(2)}, u32[]{:S(2)}) collective-permute-start(bf16[4,96,768]{2,1,0:T(8,128)(2,1)S(1)} %pad_maximum_fusion.3), channel_id=1, source_target_pairs={{0,4},{1,3},{2,6},{3,1},{4,0},{5,7},{6,2},{7,5},{8,12},{9,11},{10,... | collective-permute-start | bytes 1769480 | tf_op jit(solution)/shard_map/ppermute | solution.py:576
  23.4 10.6 %collective-permute-start.9 = (bf16[96,768]{1,0:T(8,128)(2,1)S(1)}, bf16[96,768]{1,0:T(8,128)(2,1)S(1)}, u32[]{:S(2)}, u32[]{:S(2)}) collective-permute-start(bf16[96,768]{1,0:T(8,128)(2,1)S(1)} %copy-done.10), channel_id=1, source_target_pairs={{0,16},{1,17},{2,18},{3,19},{4,20},{5,21},{6,22},{7,23},{8,24},{9,... | collective-permute-start | bytes 442376 | tf_op jit(solution)/shard_map/ppermute | solution.py:576
  29.1 22.5 %collective-permute-start.12 = (bf16[2,4,96,768]{3,2,1,0:T(8,128)(2,1)S(1)}, bf16[2,4,96,768]{3,2,1,0:T(8,128)(2,1)S(1)}, u32[]{:S(2)}, u32[]{:S(2)}) collective-permute-start(bf16[2,4,96,768]{3,2,1,0:T(8,128)(2,1)S(1)} %pad_maximum_fusion.refs_1_), channel_id=1, source_target_pairs={{0,2},{1,5},{2,0},{3,7},{4,6},{5,1},{6,4},{7,3},{8,10},{9,13},{10,... | collective-permute-start | bytes 3538952 | tf_op jit(solution)/shard_map/ppermute | solution.py:576
  34.1 15.1 %collective-permute-start.11 = (bf16[4,96,768]{2,1,0:T(8,128)(2,1)S(1)}, bf16[4,96,768]{2,1,0:T(8,128)(2,1)S(1)}, u32[]{:S(2)}, u32[]{:S(2)}) collective-permute-start(bf16[4,96,768]{2,1,0:T(8,128)(2,1)S(1)} %pad_maximum_fusion.4), channel_id=1, source_target_pairs={{0,4},{1,3},{2,6},{3,1},{4,0},{5,7},{6,2},{7,5},{8,12},{9,11},{10,... | collective-permute-start | bytes 1769480 | tf_op jit(solution)/shard_map/ppermute | solution.py:576
  35.3 18.0 %collective-permute-start.15 = (bf16[2,96,768]{2,1,0:T(8,128)(2,1)S(1)}, bf16[2,96,768]{2,1,0:T(8,128)(2,1)S(1)}, u32[]{:S(2)}, u32[]{:S(2)}) collective-permute-start(bf16[2,96,768]{2,1,0:T(8,128)(2,1)S(1)} %pad_maximum_fusion.5), channel_id=1, source_target_pairs={{0,8},{1,9},{2,10},{3,11},{4,12},{5,13},{6,14},{7,15},{8,16},{9,17... | collective-permute-start | bytes 884744 | tf_op jit(solution)/shard_map/ppermute | solution.py:576
  39.1 19.4 %collective-permute-start.16 = (bf16[2,96,768]{2,1,0:T(8,128)(2,1)S(1)}, bf16[2,96,768]{2,1,0:T(8,128)(2,1)S(1)}, u32[]{:S(2)}, u32[]{:S(2)}) collective-permute-start(bf16[2,96,768]{2,1,0:T(8,128)(2,1)S(1)} %pad_maximum_fusion.5), channel_id=1, source_target_pairs={{0,16},{1,17},{2,18},{3,19},{4,20},{5,21},{6,22},{7,23},{8,24},{9,... | collective-permute-start | bytes 884744 | tf_op jit(solution)/shard_map/ppermute | solution.py:576
  41.4 17.4 %collective-permute-start.17 = (bf16[2,96,768]{2,1,0:T(8,128)(2,1)S(1)}, bf16[2,96,768]{2,1,0:T(8,128)(2,1)S(1)}, u32[]{:S(2)}, u32[]{:S(2)}) collective-permute-start(bf16[2,96,768]{2,1,0:T(8,128)(2,1)S(1)} %pad_maximum_fusion.5), channel_id=1, source_target_pairs={{0,24},{1,25},{2,26},{3,27},{4,28},{5,29},{6,30},{7,31},{8,0},{9,1... | collective-permute-start | bytes 884744 | tf_op jit(solution)/shard_map/ppermute | solution.py:576
  49.2 18.6 %collective-permute-start.8 = (bf16[2,4,96,768]{3,2,1,0:T(8,128)(2,1)S(1)}, bf16[2,4,96,768]{3,2,1,0:T(8,128)(2,1)S(1)}, u32[]{:S(2)}, u32[]{:S(2)}) collective-permute-start(bf16[2,4,96,768]{3,2,1,0:T(8,128)(2,1)S(1)} %pad_maximum_fusion.refs_1_), channel_id=1, source_target_pairs={{0,1},{1,0},{2,3},{3,2},{4,5},{5,4},{6,7},{7,6},{8,9},{9,8},{10,11... | collective-permute-start | bytes 3538952 | tf_op jit(solution)/shard_map/ppermute | solution.py:576
  51.7 16.2 %collective-permute-start.13 = (bf16[2,4,96,768]{3,2,1,0:T(8,128)(2,1)S(1)}, bf16[2,4,96,768]{3,2,1,0:T(8,128)(2,1)S(1)}, u32[]{:S(2)}, u32[]{:S(2)}) collective-permute-start(bf16[2,4,96,768]{3,2,1,0:T(8,128)(2,1)S(1)} %pad_maximum_fusion.1.refs_1_), channel_id=1, source_target_pairs={{0,2},{1,5},{2,0},{3,7},{4,6},{5,1},{6,4},{7,3},{8,10},{9,13},{10,... | collective-permute-start | bytes 3538952 | tf_op jit(solution)/shard_map/ppermute | solution.py:576
  53.3 14.6 %collective-permute-start.14 = (bf16[2,4,96,768]{3,2,1,0:T(8,128)(2,1)S(1)}, bf16[2,4,96,768]{3,2,1,0:T(8,128)(2,1)S(1)}, u32[]{:S(2)}, u32[]{:S(2)}) collective-permute-start(bf16[2,4,96,768]{3,2,1,0:T(8,128)(2,1)S(1)} %collective-permute-done.12.refs_2_), channel_id=1, source_target_pairs={{0,1},{1,0},{2,3},{3,2},{4,5},{5,4},{6,7},{7,6},{8,9},{9,8},{10,11... | collective-permute-start | bytes 3538952 | tf_op jit(solution)/shard_map/ppermute | solution.py:576
  58.5 14.8 %collective-permute-start.18 = (bf16[2,4,96,768]{3,2,1,0:T(8,128)(2,1)S(1)}, bf16[2,4,96,768]{3,2,1,0:T(8,128)(2,1)S(1)}, u32[]{:S(2)}, u32[]{:S(2)}) collective-permute-start(bf16[2,4,96,768]{3,2,1,0:T(8,128)(2,1)S(1)} %pad_maximum_fusion.1.refs_1_), channel_id=1, source_target_pairs={{0,1},{1,0},{2,3},{3,2},{4,5},{5,4},{6,7},{7,6},{8,9},{9,8},{10,11... | collective-permute-start | bytes 3538952 | tf_op jit(solution)/shard_map/ppermute | solution.py:576
  59.2 22.3 %collective-permute-start.21 = (bf16[4,2,96,768]{3,2,1,0:T(8,128)(2,1)S(1)}, bf16[4,2,96,768]{3,2,1,0:T(8,128)(2,1)S(1)}, u32[]{:S(2)}, u32[]{:S(2)}) collective-permute-start(bf16[4,2,96,768]{3,2,1,0:T(8,128)(2,1)S(1)} %pad_maximum_fusion.2.refs_1_), channel_id=1, source_target_pairs={{0,2},{1,5},{2,0},{3,7},{4,6},{5,1},{6,4},{7,3},{8,10},{9,13},{10,... | collective-permute-start | bytes 3538952 | tf_op jit(solution)/shard_map/ppermute | solution.py:576
  85.3 16.5 %collective-permute-start.26 = (bf16[2,4,96,768]{3,2,1,0:T(8,128)(2,1)S(1)}, bf16[2,4,96,768]{3,2,1,0:T(8,128)(2,1)S(1)}, u32[]{:S(2)}, u32[]{:S(2)}) collective-permute-start(bf16[2,4,96,768]{3,2,1,0:T(8,128)(2,1)S(1)} %get-tuple-element.175), channel_id=1, source_target_pairs={{0,2},{1,5},{2,0},{3,7},{4,6},{5,1},{6,4},{7,3},{8,10},{9,13},{10,... | collective-permute-start | bytes 3538952 | tf_op jit(solution)/shard_map/ppermute | solution.py:576
  102.1 13.8 %collective-permute-start.28 = (bf16[4,96,768]{2,1,0:T(8,128)(2,1)S(1)}, bf16[4,96,768]{2,1,0:T(8,128)(2,1)S(1)}, u32[]{:S(2)}, u32[]{:S(2)}) collective-permute-start(bf16[4,96,768]{2,1,0:T(8,128)(2,1)S(1)} %get-tuple-element.202), channel_id=1, source_target_pairs={{0,4},{1,3},{2,6},{3,1},{4,0},{5,7},{6,2},{7,5},{8,12},{9,11},{10,... | collective-permute-start | bytes 1769480 | tf_op jit(solution)/shard_map/ppermute | solution.py:576
  105.5 21.4 %collective-permute-start.30 = (bf16[2,4,96,768]{3,2,1,0:T(8,128)(2,1)S(1)}, bf16[2,4,96,768]{3,2,1,0:T(8,128)(2,1)S(1)}, u32[]{:S(2)}, u32[]{:S(2)}) collective-permute-start(bf16[2,4,96,768]{3,2,1,0:T(8,128)(2,1)S(1)} %get-tuple-element.206), channel_id=1, source_target_pairs={{0,2},{1,5},{2,0},{3,7},{4,6},{5,1},{6,4},{7,3},{8,10},{9,13},{10,... | collective-permute-start | bytes 3538952 | tf_op jit(solution)/shard_map/ppermute | solution.py:576
  114.0 16.1 %collective-permute-start.31 = (bf16[2,4,96,768]{3,2,1,0:T(8,128)(2,1)S(1)}, bf16[2,4,96,768]{3,2,1,0:T(8,128)(2,1)S(1)}, u32[]{:S(2)}, u32[]{:S(2)}) collective-permute-start(bf16[2,4,96,768]{3,2,1,0:T(8,128)(2,1)S(1)} %get-tuple-element.211), channel_id=1, source_target_pairs={{0,1},{1,0},{2,3},{3,2},{4,5},{5,4},{6,7},{7,6},{8,9},{9,8},{10,11... | collective-permute-start | bytes 3538952 | tf_op jit(solution)/shard_map/ppermute | solution.py:576
  114.1 16.2 %collective-permute-start.29 = (bf16[2,4,96,768]{3,2,1,0:T(8,128)(2,1)S(1)}, bf16[2,4,96,768]{3,2,1,0:T(8,128)(2,1)S(1)}, u32[]{:S(2)}, u32[]{:S(2)}) collective-permute-start(bf16[2,4,96,768]{3,2,1,0:T(8,128)(2,1)S(1)} %get-tuple-element.210), channel_id=1, source_target_pairs={{0,1},{1,0},{2,3},{3,2},{4,5},{5,4},{6,7},{7,6},{8,9},{9,8},{10,11... | collective-permute-start | bytes 3538952 | tf_op jit(solution)/shard_map/ppermute | solution.py:576
  116.1 21.7 %collective-permute-start.35 = (bf16[96,768]{1,0:T(8,128)(2,1)S(1)}, bf16[96,768]{1,0:T(8,128)(2,1)S(1)}, u32[]{:S(2)}, u32[]{:S(2)}) collective-permute-start(bf16[96,768]{1,0:T(8,128)(2,1)S(1)} %get-tuple-element.216), channel_id=1, source_target_pairs={{0,8},{1,9},{2,10},{3,11},{4,12},{5,13},{6,14},{7,15},{8,16},{9,17... | collective-permute-start | bytes 442376 | tf_op jit(solution)/shard_map/ppermute | solution.py:576
  120.7 17.1 %collective-permute-start.34 = (bf16[96,768]{1,0:T(8,128)(2,1)S(1)}, bf16[96,768]{1,0:T(8,128)(2,1)S(1)}, u32[]{:S(2)}, u32[]{:S(2)}) collective-permute-start(bf16[96,768]{1,0:T(8,128)(2,1)S(1)} %get-tuple-element.215), channel_id=1, source_target_pairs={{0,16},{1,17},{2,18},{3,19},{4,20},{5,21},{6,22},{7,23},{8,24},{9,... | collective-permute-start | bytes 442376 | tf_op jit(solution)/shard_map/ppermute | solution.py:576
  126.9 10.9 %collective-permute-start.33 = (bf16[96,768]{1,0:T(8,128)(2,1)S(1)}, bf16[96,768]{1,0:T(8,128)(2,1)S(1)}, u32[]{:S(2)}, u32[]{:S(2)}) collective-permute-start(bf16[96,768]{1,0:T(8,128)(2,1)S(1)} %get-tuple-element.214), channel_id=1, source_target_pairs={{0,24},{1,25},{2,26},{3,27},{4,28},{5,29},{6,30},{7,31},{8,0},{9,1... | collective-permute-start | bytes 442376 | tf_op jit(solution)/shard_map/ppermute | solution.py:576
  130.1 15.0 %collective-permute-start.32 = (bf16[4,96,768]{2,1,0:T(8,128)(2,1)S(1)}, bf16[4,96,768]{2,1,0:T(8,128)(2,1)S(1)}, u32[]{:S(2)}, u32[]{:S(2)}) collective-permute-start(bf16[4,96,768]{2,1,0:T(8,128)(2,1)S(1)} %get-tuple-element.224), channel_id=1, source_target_pairs={{0,4},{1,3},{2,6},{3,1},{4,0},{5,7},{6,2},{7,5},{8,12},{9,11},{10,... | collective-permute-start | bytes 1769480 | tf_op jit(solution)/shard_map/ppermute | solution.py:576
  133.2 16.7 %collective-permute-start.39 = (bf16[2,4,96,768]{3,2,1,0:T(8,128)(2,1)S(1)}, bf16[2,4,96,768]{3,2,1,0:T(8,128)(2,1)S(1)}, u32[]{:S(2)}, u32[]{:S(2)}) collective-permute-start(bf16[2,4,96,768]{3,2,1,0:T(8,128)(2,1)S(1)} %get-tuple-element.228), channel_id=1, source_target_pairs={{0,2},{1,5},{2,0},{3,7},{4,6},{5,1},{6,4},{7,3},{8,10},{9,13},{10,... | collective-permute-start | bytes 3538952 | tf_op jit(solution)/shard_map/ppermute | solution.py:576
  145.4 14.1 %collective-permute-start.40 = (bf16[96,768]{1,0:T(8,128)(2,1)S(1)}, bf16[96,768]{1,0:T(8,128)(2,1)S(1)}, u32[]{:S(2)}, u32[]{:S(2)}) collective-permute-start(bf16[96,768]{1,0:T(8,128)(2,1)S(1)} %get-tuple-element.248), channel_id=1, source_target_pairs={{0,16},{1,17},{2,18},{3,19},{4,20},{5,21},{6,22},{7,23},{8,24},{9,... | collective-permute-start | bytes 442376 | tf_op jit(solution)/shard_map/ppermute | solution.py:576
  145.5 14.0 %collective-permute-start.38 = (bf16[96,768]{1,0:T(8,128)(2,1)S(1)}, bf16[96,768]{1,0:T(8,128)(2,1)S(1)}, u32[]{:S(2)}, u32[]{:S(2)}) collective-permute-start(bf16[96,768]{1,0:T(8,128)(2,1)S(1)} %get-tuple-element.247), channel_id=1, source_target_pairs={{0,24},{1,25},{2,26},{3,27},{4,28},{5,29},{6,30},{7,31},{8,0},{9,1... | collective-permute-start | bytes 442376 | tf_op jit(solution)/shard_map/ppermute | solution.py:576
  149.2 10.6 %collective-permute-start.37 = (f32[12,768]{1,0:T(8,128)S(1)}, f32[12,768]{1,0:T(8,128)S(1)}, u32[]{:S(2)}, u32[]{:S(2)}) collective-permute-start(f32[12,768]{1,0:T(8,128)S(1)} %add.38), channel_id=1, source_target_pairs={{0,8},{1,9},{2,10},{3,11},{4,12},{5,13},{6,14},{7,15},{8,0},{9,1},... | collective-permute-start | bytes 110600 | tf_op jit(solution)/shard_map/ppermute | solution.py:576
  150.1 11.5 %collective-permute-start.43 = (bf16[4,96,768]{2,1,0:T(8,128)(2,1)S(1)}, bf16[4,96,768]{2,1,0:T(8,128)(2,1)S(1)}, u32[]{:S(2)}, u32[]{:S(2)}) collective-permute-start(bf16[4,96,768]{2,1,0:T(8,128)(2,1)S(1)} %get-tuple-element.252), channel_id=1, source_target_pairs={{0,4},{1,3},{2,6},{3,1},{4,0},{5,7},{6,2},{7,5},{8,12},{9,11},{10,... | collective-permute-start | bytes 1769480 | tf_op jit(solution)/shard_map/ppermute | solution.py:576
  161.8 14.8 %collective-permute-start.49 = (bf16[96,768]{1,0:T(8,128)(2,1)S(1)}, bf16[96,768]{1,0:T(8,128)(2,1)S(1)}, u32[]{:S(2)}, u32[]{:S(2)}) collective-permute-start(bf16[96,768]{1,0:T(8,128)(2,1)S(1)} %get-tuple-element.263), channel_id=1, source_target_pairs={{0,8},{1,9},{2,10},{3,11},{4,12},{5,13},{6,14},{7,15},{8,16},{9,17... | collective-permute-start | bytes 442376 | tf_op jit(solution)/shard_map/ppermute | solution.py:576
  163.2 13.5 %collective-permute-start.48 = (bf16[96,768]{1,0:T(8,128)(2,1)S(1)}, bf16[96,768]{1,0:T(8,128)(2,1)S(1)}, u32[]{:S(2)}, u32[]{:S(2)}) collective-permute-start(bf16[96,768]{1,0:T(8,128)(2,1)S(1)} %get-tuple-element.262), channel_id=1, source_target_pairs={{0,16},{1,17},{2,18},{3,19},{4,20},{5,21},{6,22},{7,23},{8,24},{9,... | collective-permute-start | bytes 442376 | tf_op jit(solution)/shard_map/ppermute | solution.py:576
  165.9 9.4 %collective-permute-start.46 = (f32[10,768]{1,0:T(8,128)S(1)}, f32[10,768]{1,0:T(8,128)S(1)}, u32[]{:S(2)}, u32[]{:S(2)}) collective-permute-start(f32[10,768]{1,0:T(8,128)S(1)} %pad_maximum_fusion.7), channel_id=1, source_target_pairs={{0,6},{1,7},{2,4},{3,5},{4,2},{5,3},{6,0},{7,1},{8,14},{9,15},{10,... | collective-permute-start | bytes 92168 | tf_op jit(solution)/shard_map/ppermute | solution.py:576
  (37 other events, 232.6 us)

commit v5 on v4

--- a/solution.py
+++ b/solution.py
@@ -799,9 +799,9 @@
         low1, carry, qsum1 = backward(1, after(dc1, *gu0), dv1, None)
         ga1 = grads(attention_pairs(1, dv1, low1), None, "grad_attn", 1)
         ga1_got = [send(o, core) for o in ga1]
-        down_sum.second()
-        low0, carry, qsum0 = backward(0, after(dc0, *ga1, *down_sum.pieces), dv0, carry)
-        up_sum.first(low0)
+        low0, carry, qsum0 = backward(0, after(dc0, *ga1), dv0, carry)
+        down_sum.second(low0)
+        up_sum.first(*down_sum.pieces)
         ga1_got = [after(g, up_sum.other) for g in ga1_got]
         ga0 = grads(attention_pairs(0, dv0, low0), ga1_got, "grad_attn", 0)
         attn_sum = Scatter(*ga0)

time: 183 us -> 181 us (0.989)
  transfers between devices with their start and end apart: 50 -> 50, of which waited for: 17 -> 18; matrix products, arithmetic and copies ran while one was open for 4% -> 4% of each run, Pallas kernels for 32% -> 33%
where the time goes in v5:
time: 181 us; the launch traced here: 178 us
  starting transfers between devices  63.6 us (35%)
  Pallas kernels  58.8 us (32%)
  waiting for transfers between devices  43.9 us (24%)
  local copies, waits for them, and re-layouts  6.79 us (4%)
  other arithmetic  3.4 us (2%)
    ppermute x50, starting transfers between devices, send(): return lax.ppermute(v, ('dp', 'head'), table(move))  63.6 us
    pallas_call x28, Pallas kernels, call(): pl.pallas_call(body, out_shape=[o for o, _ in outs], in_specs=[s for _, s...  58.8 us
    ppermute x50, waiting for transfers between devices, send(): return lax.ppermute(v, ('dp', 'head'), table(move))  43.9 us
  transfers between devices with their start and end apart: 50, of which 18 were waited for; matrix products, arithmetic and copies ran while one was open for 4% of the time, Pallas kernels for 33%

profile of v5, /device:TPU:0, one launch (start us, length us, event | category | flops | bytes accessed | tf_op | source)
XLA Modules:
  0.0 178.1 jit_solution(12208314980417260738)
XLA Ops:
  2.6 3.1 %collective-permute-start = (bf16[96,768]{1,0:T(8,128)(2,1)S(1)}, bf16[96,768]{1,0:T(8,128)(2,1)S(1)}, u32[]{:S(2)}, u32[]{:S(2)}) collective-permute-start(bf16[96,768]{1,0:T(8,128)(2,1)S(1)} %pad_maximum_fusion.6), channel_id=1, source_target_pairs={{0,8},{1,9},{2,10},{3,11},{4,12},{5,13},{6,14},{7,15},{8,16},{9,17... | collective-permute-start | bytes 442376 | tf_op jit(solution)/shard_map/ppermute | solution.py:576
  5.7 2.6 %collective-permute-start.1 = (bf16[96,768]{1,0:T(8,128)(2,1)S(1)}, bf16[96,768]{1,0:T(8,128)(2,1)S(1)}, u32[]{:S(2)}, u32[]{:S(2)}) collective-permute-start(bf16[96,768]{1,0:T(8,128)(2,1)S(1)} %pad_maximum_fusion.6), channel_id=1, source_target_pairs={{0,16},{1,17},{2,18},{3,19},{4,20},{5,21},{6,22},{7,23},{8,24},{9,... | collective-permute-start | bytes 442376 | tf_op jit(solution)/shard_map/ppermute | solution.py:576
  20.2 3.2 %collective-permute-start.7 = (bf16[96,768]{1,0:T(8,128)(2,1)S(1)}, bf16[96,768]{1,0:T(8,128)(2,1)S(1)}, u32[]{:S(2)}, u32[]{:S(2)}) collective-permute-start(bf16[96,768]{1,0:T(8,128)(2,1)S(1)} %copy-done.10), channel_id=1, source_target_pairs={{0,8},{1,9},{2,10},{3,11},{4,12},{5,13},{6,14},{7,15},{8,16},{9,17... | collective-permute-start | bytes 442376 | tf_op jit(solution)/shard_map/ppermute | solution.py:576
  30.9 3.2 %collective-permute-done.9 = bf16[96,768]{1,0:T(8,128)(2,1)S(1)} collective-permute-done((bf16[96,768]{1,0:T(8,128)(2,1)S(1)}, bf16[96,768]{1,0:T(8,128)(2,1)S(1)}, u32[]{:S(2)}, u32[]{:S(2)}) %collective-permute-start.9) | collective-permute-done | bytes 147488 | tf_op jit(solution)/shard_map/ppermute | solution.py:576
  35.3 3.7 %collective-permute-start.15 = (bf16[2,96,768]{2,1,0:T(8,128)(2,1)S(1)}, bf16[2,96,768]{2,1,0:T(8,128)(2,1)S(1)}, u32[]{:S(2)}, u32[]{:S(2)}) collective-permute-start(bf16[2,96,768]{2,1,0:T(8,128)(2,1)S(1)} %pad_maximum_fusion.5), channel_id=1, source_target_pairs={{0,8},{1,9},{2,10},{3,11},{4,12},{5,13},{6,14},{7,15},{8,16},{9,17... | collective-permute-start | bytes 884744 | tf_op jit(solution)/shard_map/ppermute | solution.py:576
  39.1 2.4 %collective-permute-start.16 = (bf16[2,96,768]{2,1,0:T(8,128)(2,1)S(1)}, bf16[2,96,768]{2,1,0:T(8,128)(2,1)S(1)}, u32[]{:S(2)}, u32[]{:S(2)}) collective-permute-start(bf16[2,96,768]{2,1,0:T(8,128)(2,1)S(1)} %pad_maximum_fusion.5), channel_id=1, source_target_pairs={{0,16},{1,17},{2,18},{3,19},{4,20},{5,21},{6,22},{7,23},{8,24},{9,... | collective-permute-start | bytes 884744 | tf_op jit(solution)/shard_map/ppermute | solution.py:576
  41.7 7.6 %collective-permute-done.11 = bf16[4,96,768]{2,1,0:T(8,128)(2,1)S(1)} collective-permute-done((bf16[4,96,768]{2,1,0:T(8,128)(2,1)S(1)}, bf16[4,96,768]{2,1,0:T(8,128)(2,1)S(1)}, u32[]{:S(2)}, u32[]{:S(2)}) %collective-permute-start.11) | collective-permute-done | bytes 589856 | tf_op jit(solution)/shard_map/ppermute | solution.py:576
  53.3 4.9 %attn_fwd.2 = (bf16[2,400,640]{2,1,0:T(8,128)(2,1)S(1)}, bf16[12,208,208]{2,1,0:T(8,128)(2,1)S(1)}, bf16[2,400,256]{2,1,0:T(8,128)(2,1)S(1)}, f32[400,768]{1,0:T(8,128)S(1)}, bf16[2,768,768]{2,1,0:T(8,128)(2,1)S(1)}) custom-call(s32[3]{0:T(128)S(1)} %pad_add_fusion.refs_0_, bf16[2,4,96,768]{3,2,1,0:T(8,128)(2,1)S(1)} %pad_maximum_fusion.refs_1_, ...), custom_call_target="tpu_custom_call" | custom-call | flops 22000001024 | tf_op jit(solution)/shard_map/attn_fwd/pallas_call | solution.py:36
  60.5 7.4 %collective-permute-done.13.refs_2_ = bf16[2,4,96,768]{3,2,1,0:T(8,128)(2,1)S(1)} collective-permute-done((bf16[2,4,96,768]{3,2,1,0:T(8,128)(2,1)S(1)}, bf16[2,4,96,768]{3,2,1,0:T(8,128)(2,1)S(1)}, u32[]{:S(2)}, u32[]{:S(2)}) %collective-permute-start.13) | collective-permute-done | bytes 1179680 | tf_op jit(solution)/shard_map/ppermute | solution.py:576
  67.9 5.4 %attn_fwd.3 = (bf16[2,400,640]{2,1,0:T(8,128)(2,1)S(1)}, bf16[12,208,208]{2,1,0:T(8,128)(2,1)S(1)}, bf16[2,400,256]{2,1,0:T(8,128)(2,1)S(1)}, f32[400,768]{1,0:T...) custom-call(s32[3]{0:T(128)S(1)} %pad_add_fusion.refs_0_, ...), custom_call_target="tpu_custom_call" | custom-call | flops 22000001024 | tf_op jit(solution)/shard_map/attn_fwd/pallas_call | solution.py:36
  73.3 2.5 %up.2 = (bf16[2,400,768]{2,1,0:T(8,128)(2,1)S(1)}, bf16[2,400,768]{2,1,0:T(8,128)(2,1)S(1)}, bf16[2,768,768]{2,1,0:T(8,128)(2,1)S(1)}) custom-call(s32[3]{0:T(128)S(1)} %pad_add_fusion.refs_0_, bf16[2,4,96,768]{3,2,1,0:T(8,128)(2,1)S(1)} %collective-permute-done.18.refs_1_, bf16[2,4,96,768]{3,2,1,0:T(8,128)(2,1)S(1)} %collective-permute-done.19.refs_2_, ...), custom_call_target="tpu_custom_call" | custom-call | flops 10000000000 | tf_op jit(solution)/shard_map/up/pallas_call | solution.py:36
  75.9 2.2 %grad_down.2 = (bf16[2,4,96,768]{3,2,1,0:T(8,128)(2,1)S(1)}, bf16[2,4,96,768]{3,2,1,0:T(8,128)(2,1)S(1)}) custom-call(s32[3]{0:T(128)S(1)} %pad_add_fusion.refs_0_, bf16[400,768]{1,0:T(8,128)(2,1)S(1)} %pad.20.og_ref.refs_1_.refs_6_, bf16[2,400,768]{2,1,0:T(8,128)(2,1)S(1)} %get-tuple-element.166.refs_2_.refs_4_), custom_call_target="tpu_custom_call" | custom-call | flops 9200000000 | tf_op jit(solution)/shard_map/grad_down/pallas_call | solution.py:36
  78.7 2.8 %up.3 = (bf16[2,400,768]{2,1,0:T(8,128)(2,1)S(1)}, bf16[2,400,768]{2,1,0:T(8,128)(2,1)S(1)}, bf16[2,768,768]{2,1,0:T(8,128)(2,1)S(1)}) custom-call(s32[3]{0:T(128)S(1)} %pad_add_fusion.refs_0_, bf16[2,4,96,768]{3,2,1,0:T(8,128)(2,1)S(1)} %pad_maximum_fusion.1.refs_1_, bf16[2,4,96,768]{3,2,1,0:T(8,128)(2,1)S(1)} %collective-permute-done.13.refs_2_, ...), custom_call_target="tpu_custom_call" | custom-call | flops 10000000000 | tf_op jit(solution)/shard_map/up/pallas_call | solution.py:36
  82.8 2.5 %grad_down.3 = (bf16[2,4,96,768]{3,2,1,0:T(8,128)(2,1)S(1)}, bf16[2,4,96,768]{3,2,1,0:T(8,128)(2,1)S(1)}) custom-call(s32[3]{0:T(128)S(1)} %pad_add_fusion.refs_0_, bf16[400,768]{1,0:T(8,128)(2,1)S(1)} %pad.20.og_ref.refs_1_.refs_6_, bf16[2,400,768]{2,1,0:T(8,128)(2,1)S(1)} %get-tuple-element.170.refs_2_.refs_4_, ...), custom_call_target="tpu_custom_call" | custom-call | flops 9200000000 | tf_op jit(solution)/shard_map/grad_down/pallas_call | solution.py:36
  87.0 3.9 %down.2 = (f32[400,768]{1,0:T(8,128)S(1)}, f32[400,768]{1,0:T(8,128)S(1)}, bf16[2,400,768]{2,1,0:T(8,128)(2,1)S(1)}, f32[2,1,768]{2,1,0:T(1,128)S(1)}) custom-call(s32[3]{0:T(128)S(1)} %pad_add_fusion.refs_0_, bf16[4,2,96,768]{3,2,1,0:T(8,128)(2,1)S(1)} %pad_maximum_fusion.2.refs_1_, bf16[4,2,96,768]{3,2,1,0:T(8,128)(2,1)S(1)} %collective-permute-done.21.refs_2_, ...), custom_call_target="tpu_custom_call" | custom-call | flops 20000000000 | tf_op jit(solution)/shard_map/down/pallas_call | solution.py:36
  91.0 4.0 %down.3 = (f32[400,768]{1,0:T(8,128)S(1)}, f32[400,768]{1,0:T(8,128)S(1)}, bf16[2,400,768]{2,1,0:T(8,128)(2,1)S(1)}, f32[2,1,768]{2,1,0:T(1,128)S(1)}) custom-call(s32[3]{0:T(128)S(1)} %pad_add_fusion.refs_0_, bf16[4,2,96,768]{3,2,1,0:T(8,128)(2,1)S(1)} %collective-permute-done.20.refs_1_, bf16[4,2,96,768]{3,2,1,0:T(8,128)(2,1)S(1)} %collective-permute-done.22.refs_2_, ...), custom_call_target="tpu_custom_call" | custom-call | flops 20000000000 | tf_op jit(solution)/shard_map/down/pallas_call | solution.py:36
  96.0 2.2 %grad_up.2 = (bf16[2,4,96,768]{3,2,1,0:T(8,128)(2,1)S(1)}, bf16[2,4,96,768]{3,2,1,0:T(8,128)(2,1)S(1)}) custom-call(s32[3]{0:T(128)S(1)} %pad_add_fusion.refs_0_, bf16[400,768]{1,0:T(8,128)(2,1)S(1)} %get-tuple-element.189.refs_3_.refs_1_, bf16[2,400,768]{2,1,0:T(8,128)(2,1)S(1)} %get-tuple-element.190.refs_2_), custom_call_target="tpu_custom_call" | custom-call | flops 9200000000 | tf_op jit(solution)/shard_map/grad_up/pallas_call | solution.py:36
  103.0 2.5 %grad_up.3 = (bf16[2,4,96,768]{3,2,1,0:T(8,128)(2,1)S(1)}, bf16[2,4,96,768]{3,2,1,0:T(8,128)(2,1)S(1)}) custom-call(s32[3]{0:T(128)S(1)} %pad_add_fusion.refs_0_, bf16[400,768]{1,0:T(8,128)(2,1)S(1)} %get-tuple-element.189.refs_3_.refs_1_, bf16[2,400,768]{2,1,0:T(8,128)(2,1)S(1)} %get-tuple-element.201.refs_2_, ...), custom_call_target="tpu_custom_call" | custom-call | flops 9200000000 | tf_op jit(solution)/shard_map/grad_up/pallas_call | solution.py:36
  106.6 4.8 %attn_bwd.2 = (bf16[2,400,384]{2,1,0:T(8,128)(2,1)S(1)}, f32[400,768]{1,0:T(8,128)S(1)}, f32[2,1,384]{2,1,0:T(1,128)S(1)}) custom-call(bf16[2,768,768]{2,1,0:T(8,128)(2,1)S(1)} %get-tuple-element.188.w_ref.refs_0_, bf16[2,400,256]{2,1,0:T(8,128)(2,1)S(1)} %get-tuple-element.208.refs_1_, bf16[2,400,256]{2,1,0:T(8,128)(2,1)S(1)} %get-tuple-element.195.refs_2_.refs_4_, ...), custom_call_target="tpu_custom_call" | custom-call | flops 24000000000 | tf_op jit(solution)/shard_map/attn_bwd/pallas_call | solution.py:36
  111.4 2.6 %grad_attn.2 = (bf16[2,4,96,768]{3,2,1,0:T(8,128)(2,1)S(1)}, bf16[2,4,96,768]{3,2,1,0:T(8,128)(2,1)S(1)}) custom-call(s32[3]{0:T(128)S(1)} %pad_add_fusion.refs_0_, bf16[400,768]{1,0:T(8,128)(2,1)S(1)} %get-tuple-element.196.br_ref.refs_1_, bf16[2,400,256]{2,1,0:T(8,128)(2,1)S(1)} %get-tuple-element.199.refs_2_, bf16[400,768]{1,0:T(8,128)(2,1)S(1)} %copy-done.3, ...), custom_call_target="tpu_custom_call" | custom-call | flops 9200000000 | tf_op jit(solution)/shard_map/grad_attn/pallas_call | solution.py:36
  114.6 4.9 %attn_bwd.3 = (bf16[2,400,384]{2,1,0:T(8,128)(2,1)S(1)}, f32[400,768]{1,0:T(8,128)S(1)}, f32[2,1,384]{2,1,0:T(1,128)S(1)}) custom-call(bf16[2,768,768]{2,1,0:T(8,128)(2,1)S(1)} %get-tuple-element.186.w_ref.refs_0_, bf16[2,400,256]{2,1,0:T(8,128)(2,1)S(1)} %get-tuple-element.213.refs_1_, bf16[2,400,256]{2,1,0:T(8,128)(2,1)S(1)} %get-tuple-element.202.refs_2_.refs_4_, ...), custom_call_target="tpu_custom_call" | custom-call | flops 24000000000 | tf_op jit(solution)/shard_map/attn_bwd/pallas_call | solution.py:36
  119.7 4.3 %collective-permute-start.35 = (bf16[96,768]{1,0:T(8,128)(2,1)S(1)}, bf16[96,768]{1,0:T(8,128)(2,1)S(1)}, u32[]{:S(2)}, u32[]{:S(2)}) collective-permute-start(bf16[96,768]{1,0:T(8,128)(2,1)S(1)} %get-tuple-element.224), channel_id=1, source_target_pairs={{0,8},{1,9},{2,10},{3,11},{4,12},{5,13},{6,14},{7,15},{8,16},{9,17... | collective-permute-start | bytes 442376 | tf_op jit(solution)/shard_map/ppermute | solution.py:576
  125.2 2.9 %collective-permute-start.33 = (bf16[96,768]{1,0:T(8,128)(2,1)S(1)}, bf16[96,768]{1,0:T(8,128)(2,1)S(1)}, u32[]{:S(2)}, u32[]{:S(2)}) collective-permute-start(bf16[96,768]{1,0:T(8,128)(2,1)S(1)} %get-tuple-element.222), channel_id=1, source_target_pairs={{0,24},{1,25},{2,26},{3,27},{4,28},{5,29},{6,30},{7,31},{8,0},{9,1... | collective-permute-start | bytes 442376 | tf_op jit(solution)/shard_map/ppermute | solution.py:576
  130.2 2.9 %grad_attn.3 = (bf16[2,4,96,768]{3,2,1,0:T(8,128)(2,1)S(1)}, bf16[2,4,96,768]{3,2,1,0:T(8,128)(2,1)S(1)}) custom-call(s32[3]{0:T(128)S(1)} %pad_add_fusion.refs_0_, bf16[400,768]{1,0:T(8,128)(2,1)S(1)} %get-tuple-element.196.br_ref.refs_1_, bf16[2,400,256]{2,1,0:T(8,128)(2,1)S(1)} %get-tuple-element.217.refs_2_, bf16[400,768]{1,0:T(8,128)(2,1)S(1)} %copy-done.3, ...), custom_call_target="tpu_custom_call" | custom-call | flops 9200000000 | tf_op jit(solution)/shard_map/grad_attn/pallas_call | solution.py:36
  133.9 3.0 %exit.1 = (bf16[394,768]{1,0:T(8,128)(2,1)}, bf16[394,768]{1,0:T(8,128)(2,1)}, f32[12,768]{1,0:T(8,128)S(1)}, f32[12,768]{1,0:T(8,128)S(1)}) custom-call(bf16[400,768]{1,0:T(8,128)(2,1)S(1)} %pad.19.x_ref.refs_7_.refs_0_, f32[400,768]{1,0:T(8,128)S(1)} %get-tuple-element.160.mix_ref.refs_1_, f32[400,768]{1,0:T(8,128)S(1)} %get-tuple-element.182.refs_2_, ...), custom_call_target="tpu_custom_call" | custom-call | flops 20000000000 | tf_op jit(solution)/shard_map/exit/pallas_call | solution.py:36
  136.9 4.5 %collective-permute-done.32.g_ref = bf16[4,96,768]{2,1,0:T(8,128)(2,1)S(1)} collective-permute-done((bf16[4,96,768]{2,1,0:T(8,128)(2,1)S(1)}, bf16[4,96,768]{2,1,0:T(8,128)(2,1)S(1)}, u32[]{:S(2)}, u32[]{:S(2)}) %collective-permute-start.32) | collective-permute-done | bytes 589856 | tf_op jit(solution)/shard_map/ppermute | solution.py:576
  141.7 2.6 %collective-permute-start.40 = (bf16[96,768]{1,0:T(8,128)(2,1)S(1)}, bf16[96,768]{1,0:T(8,128)(2,1)S(1)}, u32[]{:S(2)}, u32[]{:S(2)}) collective-permute-start(bf16[96,768]{1,0:T(8,128)(2,1)S(1)} %get-tuple-element.250), channel_id=1, source_target_pairs={{0,16},{1,17},{2,18},{3,19},{4,20},{5,21},{6,22},{7,23},{8,24},{9,... | collective-permute-start | bytes 442376 | tf_op jit(solution)/shard_map/ppermute | solution.py:576
  146.5 3.7 %collective-permute-done.39.g_ref = bf16[2,4,96,768]{3,2,1,0:T(8,128)(2,1)S(1)} collective-permute-done((bf16[2,4,96,768]{3,2,1,0:T(8,128)(2,1)S(1)}, bf16[2,4,96,768]{3,2,1,0:T(8,128)(2,1)S(1)}, u32[]{:S(2)}, u32[]{:S(2)}) %collective-permute-start.39) | collective-permute-done | bytes 1179680 | tf_op jit(solution)/shard_map/ppermute | solution.py:576
  152.7 3.1 %collective-permute-done.40.refs_2_ = bf16[96,768]{1,0:T(8,128)(2,1)S(1)} collective-permute-done((bf16[96,768]{1,0:T(8,128)(2,1)S(1)}, bf16[96,768]{1,0:T(8,128)(2,1)S(1)}, u32[]{:S(2)}, u32[]{:S(2)}) %collective-permute-start.40) | collective-permute-done | bytes 147488 | tf_op jit(solution)/shard_map/ppermute | solution.py:576
  158.0 2.4 %collective-permute-done.43.g_ref = bf16[4,96,768]{2,1,0:T(8,128)(2,1)S(1)} collective-permute-done((bf16[4,96,768]{2,1,0:T(8,128)(2,1)S(1)}, bf16[4,96,768]{2,1,0:T(8,128)(2,1)S(1)}, u32[]{:S(2)}, u32[]{:S(2)}) %collective-permute-start.43) | collective-permute-done | bytes 589856 | tf_op jit(solution)/shard_map/ppermute | solution.py:576
  161.6 3.0 %collective-permute-start.48 = (bf16[96,768]{1,0:T(8,128)(2,1)S(1)}, bf16[96,768]{1,0:T(8,128)(2,1)S(1)}, u32[]{:S(2)}, u32[]{:S(2)}) collective-permute-start(bf16[96,768]{1,0:T(8,128)(2,1)S(1)} %get-tuple-element.264), channel_id=1, source_target_pairs={{0,16},{1,17},{2,18},{3,19},{4,20},{5,21},{6,22},{7,23},{8,24},{9,... | collective-permute-start | bytes 442376 | tf_op jit(solution)/shard_map/ppermute | solution.py:576
  174.7 2.4 %collective-permute-done.47.refs_1_ = bf16[96,768]{1,0:T(8,128)(2,1)S(1)} collective-permute-done((bf16[96,768]{1,0:T(8,128)(2,1)S(1)}, bf16[96,768]{1,0:T(8,128)(2,1)S(1)}, u32[]{:S(2)}, u32[]{:S(2)}) %collective-permute-start.47) | collective-permute-done | bytes 147488 | tf_op jit(solution)/shard_map/ppermute | solution.py:576
  (188 shorter events, 63.6 us)
Async XLA Ops:
  2.6 15.2 %collective-permute-start = (bf16[96,768]{1,0:T(8,128)(2,1)S(1)}, bf16[96,768]{1,0:T(8,128)(2,1)S(1)}, u32[]{:S(2)}, u32[]{:S(2)}) collective-permute-start(bf16[96,768]{1,0:T(8,128)(2,1)S(1)} %pad_maximum_fusion.6), channel_id=1, source_target_pairs={{0,8},{1,9},{2,10},{3,11},{4,12},{5,13},{6,14},{7,15},{8,16},{9,17... | collective-permute-start | bytes 442376 | tf_op jit(solution)/shard_map/ppermute | solution.py:576
  5.7 12.3 %collective-permute-start.1 = (bf16[96,768]{1,0:T(8,128)(2,1)S(1)}, bf16[96,768]{1,0:T(8,128)(2,1)S(1)}, u32[]{:S(2)}, u32[]{:S(2)}) collective-permute-start(bf16[96,768]{1,0:T(8,128)(2,1)S(1)} %pad_maximum_fusion.6), channel_id=1, source_target_pairs={{0,16},{1,17},{2,18},{3,19},{4,20},{5,21},{6,22},{7,23},{8,24},{9,... | collective-permute-start | bytes 442376 | tf_op jit(solution)/shard_map/ppermute | solution.py:576
  8.3 9.7 %collective-permute-start.2 = (bf16[96,768]{1,0:T(8,128)(2,1)S(1)}, bf16[96,768]{1,0:T(8,128)(2,1)S(1)}, u32[]{:S(2)}, u32[]{:S(2)}) collective-permute-start(bf16[96,768]{1,0:T(8,128)(2,1)S(1)} %pad_maximum_fusion.6), channel_id=1, source_target_pairs={{0,24},{1,25},{2,26},{3,27},{4,28},{5,29},{6,30},{7,31},{8,0},{9,1... | collective-permute-start | bytes 442376 | tf_op jit(solution)/shard_map/ppermute | solution.py:576
  18.6 9.9 %collective-permute-start.6 = (bf16[4,96,768]{2,1,0:T(8,128)(2,1)S(1)}, bf16[4,96,768]{2,1,0:T(8,128)(2,1)S(1)}, u32[]{:S(2)}, u32[]{:S(2)}) collective-permute-start(bf16[4,96,768]{2,1,0:T(8,128)(2,1)S(1)} %pad_maximum_fusion.3), channel_id=1, source_target_pairs={{0,4},{1,3},{2,6},{3,1},{4,0},{5,7},{6,2},{7,5},{8,12},{9,11},{10,... | collective-permute-start | bytes 1769480 | tf_op jit(solution)/shard_map/ppermute | solution.py:576
  23.4 10.6 %collective-permute-start.9 = (bf16[96,768]{1,0:T(8,128)(2,1)S(1)}, bf16[96,768]{1,0:T(8,128)(2,1)S(1)}, u32[]{:S(2)}, u32[]{:S(2)}) collective-permute-start(bf16[96,768]{1,0:T(8,128)(2,1)S(1)} %copy-done.10), channel_id=1, source_target_pairs={{0,16},{1,17},{2,18},{3,19},{4,20},{5,21},{6,22},{7,23},{8,24},{9,... | collective-permute-start | bytes 442376 | tf_op jit(solution)/shard_map/ppermute | solution.py:576
  29.1 22.5 %collective-permute-start.12 = (bf16[2,4,96,768]{3,2,1,0:T(8,128)(2,1)S(1)}, bf16[2,4,96,768]{3,2,1,0:T(8,128)(2,1)S(1)}, u32[]{:S(2)}, u32[]{:S(2)}) collective-permute-start(bf16[2,4,96,768]{3,2,1,0:T(8,128)(2,1)S(1)} %pad_maximum_fusion.refs_1_), channel_id=1, source_target_pairs={{0,2},{1,5},{2,0},{3,7},{4,6},{5,1},{6,4},{7,3},{8,10},{9,13},{10,... | collective-permute-start | bytes 3538952 | tf_op jit(solution)/shard_map/ppermute | solution.py:576
  34.1 15.1 %collective-permute-start.11 = (bf16[4,96,768]{2,1,0:T(8,128)(2,1)S(1)}, bf16[4,96,768]{2,1,0:T(8,128)(2,1)S(1)}, u32[]{:S(2)}, u32[]{:S(2)}) collective-permute-start(bf16[4,96,768]{2,1,0:T(8,128)(2,1)S(1)} %pad_maximum_fusion.4), channel_id=1, source_target_pairs={{0,4},{1,3},{2,6},{3,1},{4,0},{5,7},{6,2},{7,5},{8,12},{9,11},{10,... | collective-permute-start | bytes 1769480 | tf_op jit(solution)/shard_map/ppermute | solution.py:576
  35.3 18.0 %collective-permute-start.15 = (bf16[2,96,768]{2,1,0:T(8,128)(2,1)S(1)}, bf16[2,96,768]{2,1,0:T(8,128)(2,1)S(1)}, u32[]{:S(2)}, u32[]{:S(2)}) collective-permute-start(bf16[2,96,768]{2,1,0:T(8,128)(2,1)S(1)} %pad_maximum_fusion.5), channel_id=1, source_target_pairs={{0,8},{1,9},{2,10},{3,11},{4,12},{5,13},{6,14},{7,15},{8,16},{9,17... | collective-permute-start | bytes 884744 | tf_op jit(solution)/shard_map/ppermute | solution.py:576
  39.1 19.4 %collective-permute-start.16 = (bf16[2,96,768]{2,1,0:T(8,128)(2,1)S(1)}, bf16[2,96,768]{2,1,0:T(8,128)(2,1)S(1)}, u32[]{:S(2)}, u32[]{:S(2)}) collective-permute-start(bf16[2,96,768]{2,1,0:T(8,128)(2,1)S(1)} %pad_maximum_fusion.5), channel_id=1, source_target_pairs={{0,16},{1,17},{2,18},{3,19},{4,20},{5,21},{6,22},{7,23},{8,24},{9,... | collective-permute-start | bytes 884744 | tf_op jit(solution)/shard_map/ppermute | solution.py:576
  41.4 17.4 %collective-permute-start.17 = (bf16[2,96,768]{2,1,0:T(8,128)(2,1)S(1)}, bf16[2,96,768]{2,1,0:T(8,128)(2,1)S(1)}, u32[]{:S(2)}, u32[]{:S(2)}) collective-permute-start(bf16[2,96,768]{2,1,0:T(8,128)(2,1)S(1)} %pad_maximum_fusion.5), channel_id=1, source_target_pairs={{0,24},{1,25},{2,26},{3,27},{4,28},{5,29},{6,30},{7,31},{8,0},{9,1... | collective-permute-start | bytes 884744 | tf_op jit(solution)/shard_map/ppermute | solution.py:576
  49.2 18.6 %collective-permute-start.8 = (bf16[2,4,96,768]{3,2,1,0:T(8,128)(2,1)S(1)}, bf16[2,4,96,768]{3,2,1,0:T(8,128)(2,1)S(1)}, u32[]{:S(2)}, u32[]{:S(2)}) collective-permute-start(bf16[2,4,96,768]{3,2,1,0:T(8,128)(2,1)S(1)} %pad_maximum_fusion.refs_1_), channel_id=1, source_target_pairs={{0,1},{1,0},{2,3},{3,2},{4,5},{5,4},{6,7},{7,6},{8,9},{9,8},{10,11... | collective-permute-start | bytes 3538952 | tf_op jit(solution)/shard_map/ppermute | solution.py:576
  51.7 16.2 %collective-permute-start.13 = (bf16[2,4,96,768]{3,2,1,0:T(8,128)(2,1)S(1)}, bf16[2,4,96,768]{3,2,1,0:T(8,128)(2,1)S(1)}, u32[]{:S(2)}, u32[]{:S(2)}) collective-permute-start(bf16[2,4,96,768]{3,2,1,0:T(8,128)(2,1)S(1)} %pad_maximum_fusion.1.refs_1_), channel_id=1, source_target_pairs={{0,2},{1,5},{2,0},{3,7},{4,6},{5,1},{6,4},{7,3},{8,10},{9,13},{10,... | collective-permute-start | bytes 3538952 | tf_op jit(solution)/shard_map/ppermute | solution.py:576
  53.3 14.6 %collective-permute-start.14 = (bf16[2,4,96,768]{3,2,1,0:T(8,128)(2,1)S(1)}, bf16[2,4,96,768]{3,2,1,0:T(8,128)(2,1)S(1)}, u32[]{:S(2)}, u32[]{:S(2)}) collective-permute-start(bf16[2,4,96,768]{3,2,1,0:T(8,128)(2,1)S(1)} %collective-permute-done.12.refs_2_), channel_id=1, source_target_pairs={{0,1},{1,0},{2,3},{3,2},{4,5},{5,4},{6,7},{7,6},{8,9},{9,8},{10,11... | collective-permute-start | bytes 3538952 | tf_op jit(solution)/shard_map/ppermute | solution.py:576
  58.5 14.8 %collective-permute-start.18 = (bf16[2,4,96,768]{3,2,1,0:T(8,128)(2,1)S(1)}, bf16[2,4,96,768]{3,2,1,0:T(8,128)(2,1)S(1)}, u32[]{:S(2)}, u32[]{:S(2)}) collective-permute-start(bf16[2,4,96,768]{3,2,1,0:T(8,128)(2,1)S(1)} %pad_maximum_fusion.1.refs_1_), channel_id=1, source_target_pairs={{0,1},{1,0},{2,3},{3,2},{4,5},{5,4},{6,7},{7,6},{8,9},{9,8},{10,11... | collective-permute-start | bytes 3538952 | tf_op jit(solution)/shard_map/ppermute | solution.py:576
  59.2 22.3 %collective-permute-start.21 = (bf16[4,2,96,768]{3,2,1,0:T(8,128)(2,1)S(1)}, bf16[4,2,96,768]{3,2,1,0:T(8,128)(2,1)S(1)}, u32[]{:S(2)}, u32[]{:S(2)}) collective-permute-start(bf16[4,2,96,768]{3,2,1,0:T(8,128)(2,1)S(1)} %pad_maximum_fusion.2.refs_1_), channel_id=1, source_target_pairs={{0,2},{1,5},{2,0},{3,7},{4,6},{5,1},{6,4},{7,3},{8,10},{9,13},{10,... | collective-permute-start | bytes 3538952 | tf_op jit(solution)/shard_map/ppermute | solution.py:576
  85.3 16.5 %collective-permute-start.26 = (bf16[2,4,96,768]{3,2,1,0:T(8,128)(2,1)S(1)}, bf16[2,4,96,768]{3,2,1,0:T(8,128)(2,1)S(1)}, u32[]{:S(2)}, u32[]{:S(2)}) collective-permute-start(bf16[2,4,96,768]{3,2,1,0:T(8,128)(2,1)S(1)} %get-tuple-element.176), channel_id=1, source_target_pairs={{0,2},{1,5},{2,0},{3,7},{4,6},{5,1},{6,4},{7,3},{8,10},{9,13},{10,... | collective-permute-start | bytes 3538952 | tf_op jit(solution)/shard_map/ppermute | solution.py:576
  102.1 17.4 %collective-permute-start.30 = (bf16[4,96,768]{2,1,0:T(8,128)(2,1)S(1)}, bf16[4,96,768]{2,1,0:T(8,128)(2,1)S(1)}, u32[]{:S(2)}, u32[]{:S(2)}) collective-permute-start(bf16[4,96,768]{2,1,0:T(8,128)(2,1)S(1)} %get-tuple-element.203), channel_id=1, source_target_pairs={{0,4},{1,3},{2,6},{3,1},{4,0},{5,7},{6,2},{7,5},{8,12},{9,11},{10,... | collective-permute-start | bytes 1769480 | tf_op jit(solution)/shard_map/ppermute | solution.py:576
  105.5 19.8 %collective-permute-start.29 = (bf16[2,4,96,768]{3,2,1,0:T(8,128)(2,1)S(1)}, bf16[2,4,96,768]{3,2,1,0:T(8,128)(2,1)S(1)}, u32[]{:S(2)}, u32[]{:S(2)}) collective-permute-start(bf16[2,4,96,768]{3,2,1,0:T(8,128)(2,1)S(1)} %get-tuple-element.207), channel_id=1, source_target_pairs={{0,2},{1,5},{2,0},{3,7},{4,6},{5,1},{6,4},{7,3},{8,10},{9,13},{10,... | collective-permute-start | bytes 3538952 | tf_op jit(solution)/shard_map/ppermute | solution.py:576
  114.0 14.4 %collective-permute-start.31 = (bf16[2,4,96,768]{3,2,1,0:T(8,128)(2,1)S(1)}, bf16[2,4,96,768]{3,2,1,0:T(8,128)(2,1)S(1)}, u32[]{:S(2)}, u32[]{:S(2)}) collective-permute-start(bf16[2,4,96,768]{3,2,1,0:T(8,128)(2,1)S(1)} %get-tuple-element.212), channel_id=1, source_target_pairs={{0,1},{1,0},{2,3},{3,2},{4,5},{5,4},{6,7},{7,6},{8,9},{9,8},{10,11... | collective-permute-start | bytes 3538952 | tf_op jit(solution)/shard_map/ppermute | solution.py:576
  114.1 16.1 %collective-permute-start.28 = (bf16[2,4,96,768]{3,2,1,0:T(8,128)(2,1)S(1)}, bf16[2,4,96,768]{3,2,1,0:T(8,128)(2,1)S(1)}, u32[]{:S(2)}, u32[]{:S(2)}) collective-permute-start(bf16[2,4,96,768]{3,2,1,0:T(8,128)(2,1)S(1)} %get-tuple-element.211), channel_id=1, source_target_pairs={{0,1},{1,0},{2,3},{3,2},{4,5},{5,4},{6,7},{7,6},{8,9},{9,8},{10,11... | collective-permute-start | bytes 3538952 | tf_op jit(solution)/shard_map/ppermute | solution.py:576
  119.7 17.2 %collective-permute-start.35 = (bf16[96,768]{1,0:T(8,128)(2,1)S(1)}, bf16[96,768]{1,0:T(8,128)(2,1)S(1)}, u32[]{:S(2)}, u32[]{:S(2)}) collective-permute-start(bf16[96,768]{1,0:T(8,128)(2,1)S(1)} %get-tuple-element.224), channel_id=1, source_target_pairs={{0,8},{1,9},{2,10},{3,11},{4,12},{5,13},{6,14},{7,15},{8,16},{9,17... | collective-permute-start | bytes 442376 | tf_op jit(solution)/shard_map/ppermute | solution.py:576
  124.0 12.9 %collective-permute-start.34 = (bf16[96,768]{1,0:T(8,128)(2,1)S(1)}, bf16[96,768]{1,0:T(8,128)(2,1)S(1)}, u32[]{:S(2)}, u32[]{:S(2)}) collective-permute-start(bf16[96,768]{1,0:T(8,128)(2,1)S(1)} %get-tuple-element.223), channel_id=1, source_target_pairs={{0,16},{1,17},{2,18},{3,19},{4,20},{5,21},{6,22},{7,23},{8,24},{9,... | collective-permute-start | bytes 442376 | tf_op jit(solution)/shard_map/ppermute | solution.py:576
  125.2 11.7 %collective-permute-start.33 = (bf16[96,768]{1,0:T(8,128)(2,1)S(1)}, bf16[96,768]{1,0:T(8,128)(2,1)S(1)}, u32[]{:S(2)}, u32[]{:S(2)}) collective-permute-start(bf16[96,768]{1,0:T(8,128)(2,1)S(1)} %get-tuple-element.222), channel_id=1, source_target_pairs={{0,24},{1,25},{2,26},{3,27},{4,28},{5,29},{6,30},{7,31},{8,0},{9,1... | collective-permute-start | bytes 442376 | tf_op jit(solution)/shard_map/ppermute | solution.py:576
  128.4 13.0 %collective-permute-start.32 = (bf16[4,96,768]{2,1,0:T(8,128)(2,1)S(1)}, bf16[4,96,768]{2,1,0:T(8,128)(2,1)S(1)}, u32[]{:S(2)}, u32[]{:S(2)}) collective-permute-start(bf16[4,96,768]{2,1,0:T(8,128)(2,1)S(1)} %get-tuple-element.226), channel_id=1, source_target_pairs={{0,4},{1,3},{2,6},{3,1},{4,0},{5,7},{6,2},{7,5},{8,12},{9,11},{10,... | collective-permute-start | bytes 1769480 | tf_op jit(solution)/shard_map/ppermute | solution.py:576
  133.1 17.0 %collective-permute-start.39 = (bf16[2,4,96,768]{3,2,1,0:T(8,128)(2,1)S(1)}, bf16[2,4,96,768]{3,2,1,0:T(8,128)(2,1)S(1)}, u32[]{:S(2)}, u32[]{:S(2)}) collective-permute-start(bf16[2,4,96,768]{3,2,1,0:T(8,128)(2,1)S(1)} %get-tuple-element.230), channel_id=1, source_target_pairs={{0,2},{1,5},{2,0},{3,7},{4,6},{5,1},{6,4},{7,3},{8,10},{9,13},{10,... | collective-permute-start | bytes 3538952 | tf_op jit(solution)/shard_map/ppermute | solution.py:576
  141.7 11.1 %collective-permute-start.41 = (bf16[96,768]{1,0:T(8,128)(2,1)S(1)}, bf16[96,768]{1,0:T(8,128)(2,1)S(1)}, u32[]{:S(2)}, u32[]{:S(2)}) collective-permute-start(bf16[96,768]{1,0:T(8,128)(2,1)S(1)} %get-tuple-element.251), channel_id=1, source_target_pairs={{0,8},{1,9},{2,10},{3,11},{4,12},{5,13},{6,14},{7,15},{8,16},{9,17... | collective-permute-start | bytes 442376 | tf_op jit(solution)/shard_map/ppermute | solution.py:576
  141.7 14.1 %collective-permute-start.40 = (bf16[96,768]{1,0:T(8,128)(2,1)S(1)}, bf16[96,768]{1,0:T(8,128)(2,1)S(1)}, u32[]{:S(2)}, u32[]{:S(2)}) collective-permute-start(bf16[96,768]{1,0:T(8,128)(2,1)S(1)} %get-tuple-element.250), channel_id=1, source_target_pairs={{0,16},{1,17},{2,18},{3,19},{4,20},{5,21},{6,22},{7,23},{8,24},{9,... | collective-permute-start | bytes 442376 | tf_op jit(solution)/shard_map/ppermute | solution.py:576
  144.4 11.4 %collective-permute-start.38 = (bf16[96,768]{1,0:T(8,128)(2,1)S(1)}, bf16[96,768]{1,0:T(8,128)(2,1)S(1)}, u32[]{:S(2)}, u32[]{:S(2)}) collective-permute-start(bf16[96,768]{1,0:T(8,128)(2,1)S(1)} %get-tuple-element.249), channel_id=1, source_target_pairs={{0,24},{1,25},{2,26},{3,27},{4,28},{5,29},{6,30},{7,31},{8,0},{9,1... | collective-permute-start | bytes 442376 | tf_op jit(solution)/shard_map/ppermute | solution.py:576
  145.7 10.5 %collective-permute-start.37 = (f32[12,768]{1,0:T(8,128)S(1)}, f32[12,768]{1,0:T(8,128)S(1)}, u32[]{:S(2)}, u32[]{:S(2)}) collective-permute-start(f32[12,768]{1,0:T(8,128)S(1)} %add.38), channel_id=1, source_target_pairs={{0,8},{1,9},{2,10},{3,11},{4,12},{5,13},{6,14},{7,15},{8,0},{9,1},... | collective-permute-start | bytes 110600 | tf_op jit(solution)/shard_map/ppermute | solution.py:576
  150.4 9.9 %collective-permute-start.43 = (bf16[4,96,768]{2,1,0:T(8,128)(2,1)S(1)}, bf16[4,96,768]{2,1,0:T(8,128)(2,1)S(1)}, u32[]{:S(2)}, u32[]{:S(2)}) collective-permute-start(bf16[4,96,768]{2,1,0:T(8,128)(2,1)S(1)} %get-tuple-element.254), channel_id=1, source_target_pairs={{0,4},{1,3},{2,6},{3,1},{4,0},{5,7},{6,2},{7,5},{8,12},{9,11},{10,... | collective-permute-start | bytes 1769480 | tf_op jit(solution)/shard_map/ppermute | solution.py:576
  160.5 12.7 %collective-permute-start.49 = (bf16[96,768]{1,0:T(8,128)(2,1)S(1)}, bf16[96,768]{1,0:T(8,128)(2,1)S(1)}, u32[]{:S(2)}, u32[]{:S(2)}) collective-permute-start(bf16[96,768]{1,0:T(8,128)(2,1)S(1)} %get-tuple-element.265), channel_id=1, source_target_pairs={{0,8},{1,9},{2,10},{3,11},{4,12},{5,13},{6,14},{7,15},{8,16},{9,17... | collective-permute-start | bytes 442376 | tf_op jit(solution)/shard_map/ppermute | solution.py:576
  161.6 13.2 %collective-permute-start.48 = (bf16[96,768]{1,0:T(8,128)(2,1)S(1)}, bf16[96,768]{1,0:T(8,128)(2,1)S(1)}, u32[]{:S(2)}, u32[]{:S(2)}) collective-permute-start(bf16[96,768]{1,0:T(8,128)(2,1)S(1)} %get-tuple-element.264), channel_id=1, source_target_pairs={{0,16},{1,17},{2,18},{3,19},{4,20},{5,21},{6,22},{7,23},{8,24},{9,... | collective-permute-start | bytes 442376 | tf_op jit(solution)/shard_map/ppermute | solution.py:576
  (37 other events, 228.1 us)

commit v6 on v5

--- a/solution.py
+++ b/solution.py
@@ -821,7 +821,7 @@
         up_parts[0] = after(up_parts[0], *attn_sum.pieces)
         (grad_up,) = total_kernel(up_parts, [(0, p.hid, False)])
         attn_parts = along_chips(attn_sum.pieces, grad_up)
-        summed = vec_sum.over_xy(grad_up)
+        summed = vec_sum.over_xy(*attn_parts)
         grad_out, grad_value, grad_query, grad_key = total_kernel(
             attn_parts, [(i * cols, (i + 1) * cols, i == 0) for i in range(4)]
         )

time: 181 us -> 180 us (level)
  transfers between devices with their start and end apart: 50 -> 50, of which waited for: 18 -> 17; matrix products, arithmetic and copies ran while one was open for 4% -> 3% of each run, Pallas kernels for 33% -> 33%
where the time goes in v6:
time: 180 us; the launch traced here: 177 us
  starting transfers between devices  63 us (35%)
  Pallas kernels  58.8 us (33%)
  waiting for transfers between devices  43.5 us (24%)
  local copies, waits for them, and re-layouts  6.79 us (4%)
  other arithmetic  3.4 us (2%)
    ppermute x50, starting transfers between devices, send(): return lax.ppermute(v, ('dp', 'head'), table(move))  63 us
    pallas_call x28, Pallas kernels, call(): pl.pallas_call(body, out_shape=[o for o, _ in outs], in_specs=[s for _, s...  58.8 us
    ppermute x50, waiting for transfers between devices, send(): return lax.ppermute(v, ('dp', 'head'), table(move))  43.5 us
  transfers between devices with their start and end apart: 50, of which 17 were waited for; matrix products, arithmetic and copies ran while one was open for 3% of the time, Pallas kernels for 33%

profile of v6, /device:TPU:0, one launch (start us, length us, event | category | flops | bytes accessed | tf_op | source)
XLA Modules:
  0.0 177.1 jit_solution(5412172998424126620)
XLA Ops:
  2.6 3.1 %collective-permute-start = (bf16[96,768]{1,0:T(8,128)(2,1)S(1)}, bf16[96,768]{1,0:T(8,128)(2,1)S(1)}, u32[]{:S(2)}, u32[]{:S(2)}) collective-permute-start(bf16[96,768]{1,0:T(8,128)(2,1)S(1)} %pad_maximum_fusion.6), channel_id=1, source_target_pairs={{0,8},{1,9},{2,10},{3,11},{4,12},{5,13},{6,14},{7,15},{8,16},{9,17... | collective-permute-start | bytes 442376 | tf_op jit(solution)/shard_map/ppermute | solution.py:576
  5.7 2.6 %collective-permute-start.1 = (bf16[96,768]{1,0:T(8,128)(2,1)S(1)}, bf16[96,768]{1,0:T(8,128)(2,1)S(1)}, u32[]{:S(2)}, u32[]{:S(2)}) collective-permute-start(bf16[96,768]{1,0:T(8,128)(2,1)S(1)} %pad_maximum_fusion.6), channel_id=1, source_target_pairs={{0,16},{1,17},{2,18},{3,19},{4,20},{5,21},{6,22},{7,23},{8,24},{9,... | collective-permute-start | bytes 442376 | tf_op jit(solution)/shard_map/ppermute | solution.py:576
  20.2 3.2 %collective-permute-start.7 = (bf16[96,768]{1,0:T(8,128)(2,1)S(1)}, bf16[96,768]{1,0:T(8,128)(2,1)S(1)}, u32[]{:S(2)}, u32[]{:S(2)}) collective-permute-start(bf16[96,768]{1,0:T(8,128)(2,1)S(1)} %copy-done.10), channel_id=1, source_target_pairs={{0,8},{1,9},{2,10},{3,11},{4,12},{5,13},{6,14},{7,15},{8,16},{9,17... | collective-permute-start | bytes 442376 | tf_op jit(solution)/shard_map/ppermute | solution.py:576
  30.9 3.2 %collective-permute-done.9 = bf16[96,768]{1,0:T(8,128)(2,1)S(1)} collective-permute-done((bf16[96,768]{1,0:T(8,128)(2,1)S(1)}, bf16[96,768]{1,0:T(8,128)(2,1)S(1)}, u32[]{:S(2)}, u32[]{:S(2)}) %collective-permute-start.9) | collective-permute-done | bytes 147488 | tf_op jit(solution)/shard_map/ppermute | solution.py:576
  35.3 3.7 %collective-permute-start.15 = (bf16[2,96,768]{2,1,0:T(8,128)(2,1)S(1)}, bf16[2,96,768]{2,1,0:T(8,128)(2,1)S(1)}, u32[]{:S(2)}, u32[]{:S(2)}) collective-permute-start(bf16[2,96,768]{2,1,0:T(8,128)(2,1)S(1)} %pad_maximum_fusion.5), channel_id=1, source_target_pairs={{0,8},{1,9},{2,10},{3,11},{4,12},{5,13},{6,14},{7,15},{8,16},{9,17... | collective-permute-start | bytes 884744 | tf_op jit(solution)/shard_map/ppermute | solution.py:576
  39.1 2.4 %collective-permute-start.16 = (bf16[2,96,768]{2,1,0:T(8,128)(2,1)S(1)}, bf16[2,96,768]{2,1,0:T(8,128)(2,1)S(1)}, u32[]{:S(2)}, u32[]{:S(2)}) collective-permute-start(bf16[2,96,768]{2,1,0:T(8,128)(2,1)S(1)} %pad_maximum_fusion.5), channel_id=1, source_target_pairs={{0,16},{1,17},{2,18},{3,19},{4,20},{5,21},{6,22},{7,23},{8,24},{9,... | collective-permute-start | bytes 884744 | tf_op jit(solution)/shard_map/ppermute | solution.py:576
  41.7 7.6 %collective-permute-done.11 = bf16[4,96,768]{2,1,0:T(8,128)(2,1)S(1)} collective-permute-done((bf16[4,96,768]{2,1,0:T(8,128)(2,1)S(1)}, bf16[4,96,768]{2,1,0:T(8,128)(2,1)S(1)}, u32[]{:S(2)}, u32[]{:S(2)}) %collective-permute-start.11) | collective-permute-done | bytes 589856 | tf_op jit(solution)/shard_map/ppermute | solution.py:576
  53.3 4.9 %attn_fwd.2 = (bf16[2,400,640]{2,1,0:T(8,128)(2,1)S(1)}, bf16[12,208,208]{2,1,0:T(8,128)(2,1)S(1)}, bf16[2,400,256]{2,1,0:T(8,128)(2,1)S(1)}, f32[400,768]{1,0:T(8,128)S(1)}, bf16[2,768,768]{2,1,0:T(8,128)(2,1)S(1)}) custom-call(s32[3]{0:T(128)S(1)} %pad_add_fusion.refs_0_, bf16[2,4,96,768]{3,2,1,0:T(8,128)(2,1)S(1)} %pad_maximum_fusion.refs_1_, ...), custom_call_target="tpu_custom_call" | custom-call | flops 22000001024 | tf_op jit(solution)/shard_map/attn_fwd/pallas_call | solution.py:36
  60.5 7.4 %collective-permute-done.13.refs_2_ = bf16[2,4,96,768]{3,2,1,0:T(8,128)(2,1)S(1)} collective-permute-done((bf16[2,4,96,768]{3,2,1,0:T(8,128)(2,1)S(1)}, bf16[2,4,96,768]{3,2,1,0:T(8,128)(2,1)S(1)}, u32[]{:S(2)}, u32[]{:S(2)}) %collective-permute-start.13) | collective-permute-done | bytes 1179680 | tf_op jit(solution)/shard_map/ppermute | solution.py:576
  67.9 5.4 %attn_fwd.3 = (bf16[2,400,640]{2,1,0:T(8,128)(2,1)S(1)}, bf16[12,208,208]{2,1,0:T(8,128)(2,1)S(1)}, bf16[2,400,256]{2,1,0:T(8,128)(2,1)S(1)}, f32[400,768]{1,0:T...) custom-call(s32[3]{0:T(128)S(1)} %pad_add_fusion.refs_0_, ...), custom_call_target="tpu_custom_call" | custom-call | flops 22000001024 | tf_op jit(solution)/shard_map/attn_fwd/pallas_call | solution.py:36
  73.3 2.5 %up.2 = (bf16[2,400,768]{2,1,0:T(8,128)(2,1)S(1)}, bf16[2,400,768]{2,1,0:T(8,128)(2,1)S(1)}, bf16[2,768,768]{2,1,0:T(8,128)(2,1)S(1)}) custom-call(s32[3]{0:T(128)S(1)} %pad_add_fusion.refs_0_, bf16[2,4,96,768]{3,2,1,0:T(8,128)(2,1)S(1)} %collective-permute-done.18.refs_1_, bf16[2,4,96,768]{3,2,1,0:T(8,128)(2,1)S(1)} %collective-permute-done.19.refs_2_, ...), custom_call_target="tpu_custom_call" | custom-call | flops 10000000000 | tf_op jit(solution)/shard_map/up/pallas_call | solution.py:36
  75.9 2.2 %grad_down.2 = (bf16[2,4,96,768]{3,2,1,0:T(8,128)(2,1)S(1)}, bf16[2,4,96,768]{3,2,1,0:T(8,128)(2,1)S(1)}) custom-call(s32[3]{0:T(128)S(1)} %pad_add_fusion.refs_0_, bf16[400,768]{1,0:T(8,128)(2,1)S(1)} %pad.20.og_ref.refs_1_.refs_6_, bf16[2,400,768]{2,1,0:T(8,128)(2,1)S(1)} %get-tuple-element.166.refs_2_.refs_4_), custom_call_target="tpu_custom_call" | custom-call | flops 9200000000 | tf_op jit(solution)/shard_map/grad_down/pallas_call | solution.py:36
  78.7 2.8 %up.3 = (bf16[2,400,768]{2,1,0:T(8,128)(2,1)S(1)}, bf16[2,400,768]{2,1,0:T(8,128)(2,1)S(1)}, bf16[2,768,768]{2,1,0:T(8,128)(2,1)S(1)}) custom-call(s32[3]{0:T(128)S(1)} %pad_add_fusion.refs_0_, bf16[2,4,96,768]{3,2,1,0:T(8,128)(2,1)S(1)} %pad_maximum_fusion.1.refs_1_, bf16[2,4,96,768]{3,2,1,0:T(8,128)(2,1)S(1)} %collective-permute-done.13.refs_2_, ...), custom_call_target="tpu_custom_call" | custom-call | flops 10000000000 | tf_op jit(solution)/shard_map/up/pallas_call | solution.py:36
  82.8 2.5 %grad_down.3 = (bf16[2,4,96,768]{3,2,1,0:T(8,128)(2,1)S(1)}, bf16[2,4,96,768]{3,2,1,0:T(8,128)(2,1)S(1)}) custom-call(s32[3]{0:T(128)S(1)} %pad_add_fusion.refs_0_, bf16[400,768]{1,0:T(8,128)(2,1)S(1)} %pad.20.og_ref.refs_1_.refs_6_, bf16[2,400,768]{2,1,0:T(8,128)(2,1)S(1)} %get-tuple-element.170.refs_2_.refs_4_, ...), custom_call_target="tpu_custom_call" | custom-call | flops 9200000000 | tf_op jit(solution)/shard_map/grad_down/pallas_call | solution.py:36
  87.0 3.9 %down.2 = (f32[400,768]{1,0:T(8,128)S(1)}, f32[400,768]{1,0:T(8,128)S(1)}, bf16[2,400,768]{2,1,0:T(8,128)(2,1)S(1)}, f32[2,1,768]{2,1,0:T(1,128)S(1)}) custom-call(s32[3]{0:T(128)S(1)} %pad_add_fusion.refs_0_, bf16[4,2,96,768]{3,2,1,0:T(8,128)(2,1)S(1)} %pad_maximum_fusion.2.refs_1_, bf16[4,2,96,768]{3,2,1,0:T(8,128)(2,1)S(1)} %collective-permute-done.21.refs_2_, ...), custom_call_target="tpu_custom_call" | custom-call | flops 20000000000 | tf_op jit(solution)/shard_map/down/pallas_call | solution.py:36
  91.0 4.0 %down.3 = (f32[400,768]{1,0:T(8,128)S(1)}, f32[400,768]{1,0:T(8,128)S(1)}, bf16[2,400,768]{2,1,0:T(8,128)(2,1)S(1)}, f32[2,1,768]{2,1,0:T(1,128)S(1)}) custom-call(s32[3]{0:T(128)S(1)} %pad_add_fusion.refs_0_, bf16[4,2,96,768]{3,2,1,0:T(8,128)(2,1)S(1)} %collective-permute-done.20.refs_1_, bf16[4,2,96,768]{3,2,1,0:T(8,128)(2,1)S(1)} %collective-permute-done.22.refs_2_, ...), custom_call_target="tpu_custom_call" | custom-call | flops 20000000000 | tf_op jit(solution)/shard_map/down/pallas_call | solution.py:36
  96.0 2.2 %grad_up.2 = (bf16[2,4,96,768]{3,2,1,0:T(8,128)(2,1)S(1)}, bf16[2,4,96,768]{3,2,1,0:T(8,128)(2,1)S(1)}) custom-call(s32[3]{0:T(128)S(1)} %pad_add_fusion.refs_0_, bf16[400,768]{1,0:T(8,128)(2,1)S(1)} %get-tuple-element.189.refs_3_.refs_1_, bf16[2,400,768]{2,1,0:T(8,128)(2,1)S(1)} %get-tuple-element.190.refs_2_), custom_call_target="tpu_custom_call" | custom-call | flops 9200000000 | tf_op jit(solution)/shard_map/grad_up/pallas_call | solution.py:36
  103.0 2.5 %grad_up.3 = (bf16[2,4,96,768]{3,2,1,0:T(8,128)(2,1)S(1)}, bf16[2,4,96,768]{3,2,1,0:T(8,128)(2,1)S(1)}) custom-call(s32[3]{0:T(128)S(1)} %pad_add_fusion.refs_0_, bf16[400,768]{1,0:T(8,128)(2,1)S(1)} %get-tuple-element.189.refs_3_.refs_1_, bf16[2,400,768]{2,1,0:T(8,128)(2,1)S(1)} %get-tuple-element.201.refs_2_, ...), custom_call_target="tpu_custom_call" | custom-call | flops 9200000000 | tf_op jit(solution)/shard_map/grad_up/pallas_call | solution.py:36
  106.6 4.8 %attn_bwd.2 = (bf16[2,400,384]{2,1,0:T(8,128)(2,1)S(1)}, f32[400,768]{1,0:T(8,128)S(1)}, f32[2,1,384]{2,1,0:T(1,128)S(1)}) custom-call(bf16[2,768,768]{2,1,0:T(8,128)(2,1)S(1)} %get-tuple-element.188.w_ref.refs_0_, bf16[2,400,256]{2,1,0:T(8,128)(2,1)S(1)} %get-tuple-element.208.refs_1_, bf16[2,400,256]{2,1,0:T(8,128)(2,1)S(1)} %get-tuple-element.195.refs_2_.refs_4_, ...), custom_call_target="tpu_custom_call" | custom-call | flops 24000000000 | tf_op jit(solution)/shard_map/attn_bwd/pallas_call | solution.py:36
  111.4 2.6 %grad_attn.2 = (bf16[2,4,96,768]{3,2,1,0:T(8,128)(2,1)S(1)}, bf16[2,4,96,768]{3,2,1,0:T(8,128)(2,1)S(1)}) custom-call(s32[3]{0:T(128)S(1)} %pad_add_fusion.refs_0_, bf16[400,768]{1,0:T(8,128)(2,1)S(1)} %get-tuple-element.196.br_ref.refs_1_, bf16[2,400,256]{2,1,0:T(8,128)(2,1)S(1)} %get-tuple-element.199.refs_2_, bf16[400,768]{1,0:T(8,128)(2,1)S(1)} %copy-done.3, ...), custom_call_target="tpu_custom_call" | custom-call | flops 9200000000 | tf_op jit(solution)/shard_map/grad_attn/pallas_call | solution.py:36
  114.6 4.9 %attn_bwd.3 = (bf16[2,400,384]{2,1,0:T(8,128)(2,1)S(1)}, f32[400,768]{1,0:T(8,128)S(1)}, f32[2,1,384]{2,1,0:T(1,128)S(1)}) custom-call(bf16[2,768,768]{2,1,0:T(8,128)(2,1)S(1)} %get-tuple-element.186.w_ref.refs_0_, bf16[2,400,256]{2,1,0:T(8,128)(2,1)S(1)} %get-tuple-element.213.refs_1_, bf16[2,400,256]{2,1,0:T(8,128)(2,1)S(1)} %get-tuple-element.202.refs_2_.refs_4_, ...), custom_call_target="tpu_custom_call" | custom-call | flops 24000000000 | tf_op jit(solution)/shard_map/attn_bwd/pallas_call | solution.py:36
  119.7 4.3 %collective-permute-start.35 = (bf16[96,768]{1,0:T(8,128)(2,1)S(1)}, bf16[96,768]{1,0:T(8,128)(2,1)S(1)}, u32[]{:S(2)}, u32[]{:S(2)}) collective-permute-start(bf16[96,768]{1,0:T(8,128)(2,1)S(1)} %get-tuple-element.224), channel_id=1, source_target_pairs={{0,8},{1,9},{2,10},{3,11},{4,12},{5,13},{6,14},{7,15},{8,16},{9,17... | collective-permute-start | bytes 442376 | tf_op jit(solution)/shard_map/ppermute | solution.py:576
  125.2 2.9 %collective-permute-start.33 = (bf16[96,768]{1,0:T(8,128)(2,1)S(1)}, bf16[96,768]{1,0:T(8,128)(2,1)S(1)}, u32[]{:S(2)}, u32[]{:S(2)}) collective-permute-start(bf16[96,768]{1,0:T(8,128)(2,1)S(1)} %get-tuple-element.222), channel_id=1, source_target_pairs={{0,24},{1,25},{2,26},{3,27},{4,28},{5,29},{6,30},{7,31},{8,0},{9,1... | collective-permute-start | bytes 442376 | tf_op jit(solution)/shard_map/ppermute | solution.py:576
  130.2 2.9 %grad_attn.3 = (bf16[2,4,96,768]{3,2,1,0:T(8,128)(2,1)S(1)}, bf16[2,4,96,768]{3,2,1,0:T(8,128)(2,1)S(1)}) custom-call(s32[3]{0:T(128)S(1)} %pad_add_fusion.refs_0_, bf16[400,768]{1,0:T(8,128)(2,1)S(1)} %get-tuple-element.196.br_ref.refs_1_, bf16[2,400,256]{2,1,0:T(8,128)(2,1)S(1)} %get-tuple-element.217.refs_2_, bf16[400,768]{1,0:T(8,128)(2,1)S(1)} %copy-done.3, ...), custom_call_target="tpu_custom_call" | custom-call | flops 9200000000 | tf_op jit(solution)/shard_map/grad_attn/pallas_call | solution.py:36
  133.9 3.0 %exit.1 = (bf16[394,768]{1,0:T(8,128)(2,1)}, bf16[394,768]{1,0:T(8,128)(2,1)}, f32[12,768]{1,0:T(8,128)S(1)}, f32[12,768]{1,0:T(8,128)S(1)}) custom-call(bf16[400,768]{1,0:T(8,128)(2,1)S(1)} %pad.19.x_ref.refs_7_.refs_0_, f32[400,768]{1,0:T(8,128)S(1)} %get-tuple-element.160.mix_ref.refs_1_, f32[400,768]{1,0:T(8,128)S(1)} %get-tuple-element.182.refs_2_, ...), custom_call_target="tpu_custom_call" | custom-call | flops 20000000000 | tf_op jit(solution)/shard_map/exit/pallas_call | solution.py:36
  136.9 4.5 %collective-permute-done.32.g_ref = bf16[4,96,768]{2,1,0:T(8,128)(2,1)S(1)} collective-permute-done((bf16[4,96,768]{2,1,0:T(8,128)(2,1)S(1)}, bf16[4,96,768]{2,1,0:T(8,128)(2,1)S(1)}, u32[]{:S(2)}, u32[]{:S(2)}) %collective-permute-start.32) | collective-permute-done | bytes 589856 | tf_op jit(solution)/shard_map/ppermute | solution.py:576
  141.7 2.6 %collective-permute-start.40 = (bf16[96,768]{1,0:T(8,128)(2,1)S(1)}, bf16[96,768]{1,0:T(8,128)(2,1)S(1)}, u32[]{:S(2)}, u32[]{:S(2)}) collective-permute-start(bf16[96,768]{1,0:T(8,128)(2,1)S(1)} %get-tuple-element.250), channel_id=1, source_target_pairs={{0,16},{1,17},{2,18},{3,19},{4,20},{5,21},{6,22},{7,23},{8,24},{9,... | collective-permute-start | bytes 442376 | tf_op jit(solution)/shard_map/ppermute | solution.py:576
  146.5 3.7 %collective-permute-done.39.g_ref = bf16[2,4,96,768]{3,2,1,0:T(8,128)(2,1)S(1)} collective-permute-done((bf16[2,4,96,768]{3,2,1,0:T(8,128)(2,1)S(1)}, bf16[2,4,96,768]{3,2,1,0:T(8,128)(2,1)S(1)}, u32[]{:S(2)}, u32[]{:S(2)}) %collective-permute-start.39) | collective-permute-done | bytes 1179680 | tf_op jit(solution)/shard_map/ppermute | solution.py:576
  152.7 3.1 %collective-permute-done.40.refs_2_ = bf16[96,768]{1,0:T(8,128)(2,1)S(1)} collective-permute-done((bf16[96,768]{1,0:T(8,128)(2,1)S(1)}, bf16[96,768]{1,0:T(8,128)(2,1)S(1)}, u32[]{:S(2)}, u32[]{:S(2)}) %collective-permute-start.40) | collective-permute-done | bytes 147488 | tf_op jit(solution)/shard_map/ppermute | solution.py:576
  158.0 2.4 %collective-permute-done.43.g_ref = bf16[4,96,768]{2,1,0:T(8,128)(2,1)S(1)} collective-permute-done((bf16[4,96,768]{2,1,0:T(8,128)(2,1)S(1)}, bf16[4,96,768]{2,1,0:T(8,128)(2,1)S(1)}, u32[]{:S(2)}, u32[]{:S(2)}) %collective-permute-start.43) | collective-permute-done | bytes 589856 | tf_op jit(solution)/shard_map/ppermute | solution.py:576
  161.6 3.0 %collective-permute-start.46 = (bf16[96,768]{1,0:T(8,128)(2,1)S(1)}, bf16[96,768]{1,0:T(8,128)(2,1)S(1)}, u32[]{:S(2)}, u32[]{:S(2)}) collective-permute-start(bf16[96,768]{1,0:T(8,128)(2,1)S(1)} %get-tuple-element.264), channel_id=1, source_target_pairs={{0,16},{1,17},{2,18},{3,19},{4,20},{5,21},{6,22},{7,23},{8,24},{9,... | collective-permute-start | bytes 442376 | tf_op jit(solution)/shard_map/ppermute | solution.py:576
  170.4 4.3 %collective-permute-done.46.refs_2_ = bf16[96,768]{1,0:T(8,128)(2,1)S(1)} collective-permute-done((bf16[96,768]{1,0:T(8,128)(2,1)S(1)}, bf16[96,768]{1,0:T(8,128)(2,1)S(1)}, u32[]{:S(2)}, u32[]{:S(2)}) %collective-permute-start.46) | collective-permute-done | bytes 147488 | tf_op jit(solution)/shard_map/ppermute | solution.py:576
  (188 shorter events, 60.5 us)
Async XLA Ops:
  2.6 15.2 %collective-permute-start = (bf16[96,768]{1,0:T(8,128)(2,1)S(1)}, bf16[96,768]{1,0:T(8,128)(2,1)S(1)}, u32[]{:S(2)}, u32[]{:S(2)}) collective-permute-start(bf16[96,768]{1,0:T(8,128)(2,1)S(1)} %pad_maximum_fusion.6), channel_id=1, source_target_pairs={{0,8},{1,9},{2,10},{3,11},{4,12},{5,13},{6,14},{7,15},{8,16},{9,17... | collective-permute-start | bytes 442376 | tf_op jit(solution)/shard_map/ppermute | solution.py:576
  5.7 12.3 %collective-permute-start.1 = (bf16[96,768]{1,0:T(8,128)(2,1)S(1)}, bf16[96,768]{1,0:T(8,128)(2,1)S(1)}, u32[]{:S(2)}, u32[]{:S(2)}) collective-permute-start(bf16[96,768]{1,0:T(8,128)(2,1)S(1)} %pad_maximum_fusion.6), channel_id=1, source_target_pairs={{0,16},{1,17},{2,18},{3,19},{4,20},{5,21},{6,22},{7,23},{8,24},{9,... | collective-permute-start | bytes 442376 | tf_op jit(solution)/shard_map/ppermute | solution.py:576
  18.6 9.9 %collective-permute-start.6 = (bf16[4,96,768]{2,1,0:T(8,128)(2,1)S(1)}, bf16[4,96,768]{2,1,0:T(8,128)(2,1)S(1)}, u32[]{:S(2)}, u32[]{:S(2)}) collective-permute-start(bf16[4,96,768]{2,1,0:T(8,128)(2,1)S(1)} %pad_maximum_fusion.3), channel_id=1, source_target_pairs={{0,4},{1,3},{2,6},{3,1},{4,0},{5,7},{6,2},{7,5},{8,12},{9,11},{10,... | collective-permute-start | bytes 1769480 | tf_op jit(solution)/shard_map/ppermute | solution.py:576
  23.4 10.6 %collective-permute-start.9 = (bf16[96,768]{1,0:T(8,128)(2,1)S(1)}, bf16[96,768]{1,0:T(8,128)(2,1)S(1)}, u32[]{:S(2)}, u32[]{:S(2)}) collective-permute-start(bf16[96,768]{1,0:T(8,128)(2,1)S(1)} %copy-done.10), channel_id=1, source_target_pairs={{0,16},{1,17},{2,18},{3,19},{4,20},{5,21},{6,22},{7,23},{8,24},{9,... | collective-permute-start | bytes 442376 | tf_op jit(solution)/shard_map/ppermute | solution.py:576
  29.1 22.5 %collective-permute-start.12 = (bf16[2,4,96,768]{3,2,1,0:T(8,128)(2,1)S(1)}, bf16[2,4,96,768]{3,2,1,0:T(8,128)(2,1)S(1)}, u32[]{:S(2)}, u32[]{:S(2)}) collective-permute-start(bf16[2,4,96,768]{3,2,1,0:T(8,128)(2,1)S(1)} %pad_maximum_fusion.refs_1_), channel_id=1, source_target_pairs={{0,2},{1,5},{2,0},{3,7},{4,6},{5,1},{6,4},{7,3},{8,10},{9,13},{10,... | collective-permute-start | bytes 3538952 | tf_op jit(solution)/shard_map/ppermute | solution.py:576
  34.1 15.1 %collective-permute-start.11 = (bf16[4,96,768]{2,1,0:T(8,128)(2,1)S(1)}, bf16[4,96,768]{2,1,0:T(8,128)(2,1)S(1)}, u32[]{:S(2)}, u32[]{:S(2)}) collective-permute-start(bf16[4,96,768]{2,1,0:T(8,128)(2,1)S(1)} %pad_maximum_fusion.4), channel_id=1, source_target_pairs={{0,4},{1,3},{2,6},{3,1},{4,0},{5,7},{6,2},{7,5},{8,12},{9,11},{10,... | collective-permute-start | bytes 1769480 | tf_op jit(solution)/shard_map/ppermute | solution.py:576
  35.3 18.0 %collective-permute-start.15 = (bf16[2,96,768]{2,1,0:T(8,128)(2,1)S(1)}, bf16[2,96,768]{2,1,0:T(8,128)(2,1)S(1)}, u32[]{:S(2)}, u32[]{:S(2)}) collective-permute-start(bf16[2,96,768]{2,1,0:T(8,128)(2,1)S(1)} %pad_maximum_fusion.5), channel_id=1, source_target_pairs={{0,8},{1,9},{2,10},{3,11},{4,12},{5,13},{6,14},{7,15},{8,16},{9,17... | collective-permute-start | bytes 884744 | tf_op jit(solution)/shard_map/ppermute | solution.py:576
  39.1 19.4 %collective-permute-start.16 = (bf16[2,96,768]{2,1,0:T(8,128)(2,1)S(1)}, bf16[2,96,768]{2,1,0:T(8,128)(2,1)S(1)}, u32[]{:S(2)}, u32[]{:S(2)}) collective-permute-start(bf16[2,96,768]{2,1,0:T(8,128)(2,1)S(1)} %pad_maximum_fusion.5), channel_id=1, source_target_pairs={{0,16},{1,17},{2,18},{3,19},{4,20},{5,21},{6,22},{7,23},{8,24},{9,... | collective-permute-start | bytes 884744 | tf_op jit(solution)/shard_map/ppermute | solution.py:576
  41.4 17.4 %collective-permute-start.17 = (bf16[2,96,768]{2,1,0:T(8,128)(2,1)S(1)}, bf16[2,96,768]{2,1,0:T(8,128)(2,1)S(1)}, u32[]{:S(2)}, u32[]{:S(2)}) collective-permute-start(bf16[2,96,768]{2,1,0:T(8,128)(2,1)S(1)} %pad_maximum_fusion.5), channel_id=1, source_target_pairs={{0,24},{1,25},{2,26},{3,27},{4,28},{5,29},{6,30},{7,31},{8,0},{9,1... | collective-permute-start | bytes 884744 | tf_op jit(solution)/shard_map/ppermute | solution.py:576
  49.2 18.6 %collective-permute-start.8 = (bf16[2,4,96,768]{3,2,1,0:T(8,128)(2,1)S(1)}, bf16[2,4,96,768]{3,2,1,0:T(8,128)(2,1)S(1)}, u32[]{:S(2)}, u32[]{:S(2)}) collective-permute-start(bf16[2,4,96,768]{3,2,1,0:T(8,128)(2,1)S(1)} %pad_maximum_fusion.refs_1_), channel_id=1, source_target_pairs={{0,1},{1,0},{2,3},{3,2},{4,5},{5,4},{6,7},{7,6},{8,9},{9,8},{10,11... | collective-permute-start | bytes 3538952 | tf_op jit(solution)/shard_map/ppermute | solution.py:576
  51.7 16.2 %collective-permute-start.13 = (bf16[2,4,96,768]{3,2,1,0:T(8,128)(2,1)S(1)}, bf16[2,4,96,768]{3,2,1,0:T(8,128)(2,1)S(1)}, u32[]{:S(2)}, u32[]{:S(2)}) collective-permute-start(bf16[2,4,96,768]{3,2,1,0:T(8,128)(2,1)S(1)} %pad_maximum_fusion.1.refs_1_), channel_id=1, source_target_pairs={{0,2},{1,5},{2,0},{3,7},{4,6},{5,1},{6,4},{7,3},{8,10},{9,13},{10,... | collective-permute-start | bytes 3538952 | tf_op jit(solution)/shard_map/ppermute | solution.py:576
  53.3 14.6 %collective-permute-start.14 = (bf16[2,4,96,768]{3,2,1,0:T(8,128)(2,1)S(1)}, bf16[2,4,96,768]{3,2,1,0:T(8,128)(2,1)S(1)}, u32[]{:S(2)}, u32[]{:S(2)}) collective-permute-start(bf16[2,4,96,768]{3,2,1,0:T(8,128)(2,1)S(1)} %collective-permute-done.12.refs_2_), channel_id=1, source_target_pairs={{0,1},{1,0},{2,3},{3,2},{4,5},{5,4},{6,7},{7,6},{8,9},{9,8},{10,11... | collective-permute-start | bytes 3538952 | tf_op jit(solution)/shard_map/ppermute | solution.py:576
  58.5 14.8 %collective-permute-start.18 = (bf16[2,4,96,768]{3,2,1,0:T(8,128)(2,1)S(1)}, bf16[2,4,96,768]{3,2,1,0:T(8,128)(2,1)S(1)}, u32[]{:S(2)}, u32[]{:S(2)}) collective-permute-start(bf16[2,4,96,768]{3,2,1,0:T(8,128)(2,1)S(1)} %pad_maximum_fusion.1.refs_1_), channel_id=1, source_target_pairs={{0,1},{1,0},{2,3},{3,2},{4,5},{5,4},{6,7},{7,6},{8,9},{9,8},{10,11... | collective-permute-start | bytes 3538952 | tf_op jit(solution)/shard_map/ppermute | solution.py:576
  59.2 22.3 %collective-permute-start.21 = (bf16[4,2,96,768]{3,2,1,0:T(8,128)(2,1)S(1)}, bf16[4,2,96,768]{3,2,1,0:T(8,128)(2,1)S(1)}, u32[]{:S(2)}, u32[]{:S(2)}) collective-permute-start(bf16[4,2,96,768]{3,2,1,0:T(8,128)(2,1)S(1)} %pad_maximum_fusion.2.refs_1_), channel_id=1, source_target_pairs={{0,2},{1,5},{2,0},{3,7},{4,6},{5,1},{6,4},{7,3},{8,10},{9,13},{10,... | collective-permute-start | bytes 3538952 | tf_op jit(solution)/shard_map/ppermute | solution.py:576
  85.3 16.5 %collective-permute-start.26 = (bf16[2,4,96,768]{3,2,1,0:T(8,128)(2,1)S(1)}, bf16[2,4,96,768]{3,2,1,0:T(8,128)(2,1)S(1)}, u32[]{:S(2)}, u32[]{:S(2)}) collective-permute-start(bf16[2,4,96,768]{3,2,1,0:T(8,128)(2,1)S(1)} %get-tuple-element.176), channel_id=1, source_target_pairs={{0,2},{1,5},{2,0},{3,7},{4,6},{5,1},{6,4},{7,3},{8,10},{9,13},{10,... | collective-permute-start | bytes 3538952 | tf_op jit(solution)/shard_map/ppermute | solution.py:576
  102.1 17.4 %collective-permute-start.30 = (bf16[4,96,768]{2,1,0:T(8,128)(2,1)S(1)}, bf16[4,96,768]{2,1,0:T(8,128)(2,1)S(1)}, u32[]{:S(2)}, u32[]{:S(2)}) collective-permute-start(bf16[4,96,768]{2,1,0:T(8,128)(2,1)S(1)} %get-tuple-element.203), channel_id=1, source_target_pairs={{0,4},{1,3},{2,6},{3,1},{4,0},{5,7},{6,2},{7,5},{8,12},{9,11},{10,... | collective-permute-start | bytes 1769480 | tf_op jit(solution)/shard_map/ppermute | solution.py:576
  105.5 19.8 %collective-permute-start.29 = (bf16[2,4,96,768]{3,2,1,0:T(8,128)(2,1)S(1)}, bf16[2,4,96,768]{3,2,1,0:T(8,128)(2,1)S(1)}, u32[]{:S(2)}, u32[]{:S(2)}) collective-permute-start(bf16[2,4,96,768]{3,2,1,0:T(8,128)(2,1)S(1)} %get-tuple-element.207), channel_id=1, source_target_pairs={{0,2},{1,5},{2,0},{3,7},{4,6},{5,1},{6,4},{7,3},{8,10},{9,13},{10,... | collective-permute-start | bytes 3538952 | tf_op jit(solution)/shard_map/ppermute | solution.py:576
  114.0 14.4 %collective-permute-start.31 = (bf16[2,4,96,768]{3,2,1,0:T(8,128)(2,1)S(1)}, bf16[2,4,96,768]{3,2,1,0:T(8,128)(2,1)S(1)}, u32[]{:S(2)}, u32[]{:S(2)}) collective-permute-start(bf16[2,4,96,768]{3,2,1,0:T(8,128)(2,1)S(1)} %get-tuple-element.212), channel_id=1, source_target_pairs={{0,1},{1,0},{2,3},{3,2},{4,5},{5,4},{6,7},{7,6},{8,9},{9,8},{10,11... | collective-permute-start | bytes 3538952 | tf_op jit(solution)/shard_map/ppermute | solution.py:576
  114.1 16.1 %collective-permute-start.28 = (bf16[2,4,96,768]{3,2,1,0:T(8,128)(2,1)S(1)}, bf16[2,4,96,768]{3,2,1,0:T(8,128)(2,1)S(1)}, u32[]{:S(2)}, u32[]{:S(2)}) collective-permute-start(bf16[2,4,96,768]{3,2,1,0:T(8,128)(2,1)S(1)} %get-tuple-element.211), channel_id=1, source_target_pairs={{0,1},{1,0},{2,3},{3,2},{4,5},{5,4},{6,7},{7,6},{8,9},{9,8},{10,11... | collective-permute-start | bytes 3538952 | tf_op jit(solution)/shard_map/ppermute | solution.py:576
  119.7 17.2 %collective-permute-start.35 = (bf16[96,768]{1,0:T(8,128)(2,1)S(1)}, bf16[96,768]{1,0:T(8,128)(2,1)S(1)}, u32[]{:S(2)}, u32[]{:S(2)}) collective-permute-start(bf16[96,768]{1,0:T(8,128)(2,1)S(1)} %get-tuple-element.224), channel_id=1, source_target_pairs={{0,8},{1,9},{2,10},{3,11},{4,12},{5,13},{6,14},{7,15},{8,16},{9,17... | collective-permute-start | bytes 442376 | tf_op jit(solution)/shard_map/ppermute | solution.py:576
  124.0 12.9 %collective-permute-start.34 = (bf16[96,768]{1,0:T(8,128)(2,1)S(1)}, bf16[96,768]{1,0:T(8,128)(2,1)S(1)}, u32[]{:S(2)}, u32[]{:S(2)}) collective-permute-start(bf16[96,768]{1,0:T(8,128)(2,1)S(1)} %get-tuple-element.223), channel_id=1, source_target_pairs={{0,16},{1,17},{2,18},{3,19},{4,20},{5,21},{6,22},{7,23},{8,24},{9,... | collective-permute-start | bytes 442376 | tf_op jit(solution)/shard_map/ppermute | solution.py:576
  125.2 11.7 %collective-permute-start.33 = (bf16[96,768]{1,0:T(8,128)(2,1)S(1)}, bf16[96,768]{1,0:T(8,128)(2,1)S(1)}, u32[]{:S(2)}, u32[]{:S(2)}) collective-permute-start(bf16[96,768]{1,0:T(8,128)(2,1)S(1)} %get-tuple-element.222), channel_id=1, source_target_pairs={{0,24},{1,25},{2,26},{3,27},{4,28},{5,29},{6,30},{7,31},{8,0},{9,1... | collective-permute-start | bytes 442376 | tf_op jit(solution)/shard_map/ppermute | solution.py:576
  128.4 13.0 %collective-permute-start.32 = (bf16[4,96,768]{2,1,0:T(8,128)(2,1)S(1)}, bf16[4,96,768]{2,1,0:T(8,128)(2,1)S(1)}, u32[]{:S(2)}, u32[]{:S(2)}) collective-permute-start(bf16[4,96,768]{2,1,0:T(8,128)(2,1)S(1)} %get-tuple-element.226), channel_id=1, source_target_pairs={{0,4},{1,3},{2,6},{3,1},{4,0},{5,7},{6,2},{7,5},{8,12},{9,11},{10,... | collective-permute-start | bytes 1769480 | tf_op jit(solution)/shard_map/ppermute | solution.py:576
  133.1 17.0 %collective-permute-start.39 = (bf16[2,4,96,768]{3,2,1,0:T(8,128)(2,1)S(1)}, bf16[2,4,96,768]{3,2,1,0:T(8,128)(2,1)S(1)}, u32[]{:S(2)}, u32[]{:S(2)}) collective-permute-start(bf16[2,4,96,768]{3,2,1,0:T(8,128)(2,1)S(1)} %get-tuple-element.230), channel_id=1, source_target_pairs={{0,2},{1,5},{2,0},{3,7},{4,6},{5,1},{6,4},{7,3},{8,10},{9,13},{10,... | collective-permute-start | bytes 3538952 | tf_op jit(solution)/shard_map/ppermute | solution.py:576
  141.7 11.1 %collective-permute-start.41 = (bf16[96,768]{1,0:T(8,128)(2,1)S(1)}, bf16[96,768]{1,0:T(8,128)(2,1)S(1)}, u32[]{:S(2)}, u32[]{:S(2)}) collective-permute-start(bf16[96,768]{1,0:T(8,128)(2,1)S(1)} %get-tuple-element.251), channel_id=1, source_target_pairs={{0,8},{1,9},{2,10},{3,11},{4,12},{5,13},{6,14},{7,15},{8,16},{9,17... | collective-permute-start | bytes 442376 | tf_op jit(solution)/shard_map/ppermute | solution.py:576
  141.7 14.1 %collective-permute-start.40 = (bf16[96,768]{1,0:T(8,128)(2,1)S(1)}, bf16[96,768]{1,0:T(8,128)(2,1)S(1)}, u32[]{:S(2)}, u32[]{:S(2)}) collective-permute-start(bf16[96,768]{1,0:T(8,128)(2,1)S(1)} %get-tuple-element.250), channel_id=1, source_target_pairs={{0,16},{1,17},{2,18},{3,19},{4,20},{5,21},{6,22},{7,23},{8,24},{9,... | collective-permute-start | bytes 442376 | tf_op jit(solution)/shard_map/ppermute | solution.py:576
  144.4 11.4 %collective-permute-start.38 = (bf16[96,768]{1,0:T(8,128)(2,1)S(1)}, bf16[96,768]{1,0:T(8,128)(2,1)S(1)}, u32[]{:S(2)}, u32[]{:S(2)}) collective-permute-start(bf16[96,768]{1,0:T(8,128)(2,1)S(1)} %get-tuple-element.249), channel_id=1, source_target_pairs={{0,24},{1,25},{2,26},{3,27},{4,28},{5,29},{6,30},{7,31},{8,0},{9,1... | collective-permute-start | bytes 442376 | tf_op jit(solution)/shard_map/ppermute | solution.py:576
  145.7 10.5 %collective-permute-start.37 = (f32[12,768]{1,0:T(8,128)S(1)}, f32[12,768]{1,0:T(8,128)S(1)}, u32[]{:S(2)}, u32[]{:S(2)}) collective-permute-start(f32[12,768]{1,0:T(8,128)S(1)} %add.38), channel_id=1, source_target_pairs={{0,8},{1,9},{2,10},{3,11},{4,12},{5,13},{6,14},{7,15},{8,0},{9,1},... | collective-permute-start | bytes 110600 | tf_op jit(solution)/shard_map/ppermute | solution.py:576
  150.4 9.9 %collective-permute-start.43 = (bf16[4,96,768]{2,1,0:T(8,128)(2,1)S(1)}, bf16[4,96,768]{2,1,0:T(8,128)(2,1)S(1)}, u32[]{:S(2)}, u32[]{:S(2)}) collective-permute-start(bf16[4,96,768]{2,1,0:T(8,128)(2,1)S(1)} %get-tuple-element.254), channel_id=1, source_target_pairs={{0,4},{1,3},{2,6},{3,1},{4,0},{5,7},{6,2},{7,5},{8,12},{9,11},{10,... | collective-permute-start | bytes 1769480 | tf_op jit(solution)/shard_map/ppermute | solution.py:576
  161.6 13.1 %collective-permute-start.46 = (bf16[96,768]{1,0:T(8,128)(2,1)S(1)}, bf16[96,768]{1,0:T(8,128)(2,1)S(1)}, u32[]{:S(2)}, u32[]{:S(2)}) collective-permute-start(bf16[96,768]{1,0:T(8,128)(2,1)S(1)} %get-tuple-element.264), channel_id=1, source_target_pairs={{0,16},{1,17},{2,18},{3,19},{4,20},{5,21},{6,22},{7,23},{8,24},{9,... | collective-permute-start | bytes 442376 | tf_op jit(solution)/shard_map/ppermute | solution.py:576
  164.6 10.1 %collective-permute-start.45 = (bf16[96,768]{1,0:T(8,128)(2,1)S(1)}, bf16[96,768]{1,0:T(8,128)(2,1)S(1)}, u32[]{:S(2)}, u32[]{:S(2)}) collective-permute-start(bf16[96,768]{1,0:T(8,128)(2,1)S(1)} %get-tuple-element.263), channel_id=1, source_target_pairs={{0,24},{1,25},{2,26},{3,27},{4,28},{5,29},{6,30},{7,31},{8,0},{9,1... | collective-permute-start | bytes 442376 | tf_op jit(solution)/shard_map/ppermute | solution.py:576
  165.8 9.8 %collective-permute-start.49 = (f32[10,768]{1,0:T(8,128)S(1)}, f32[10,768]{1,0:T(8,128)S(1)}, u32[]{:S(2)}, u32[]{:S(2)}) collective-permute-start(f32[10,768]{1,0:T(8,128)S(1)} %pad_maximum_fusion.7), channel_id=1, source_target_pairs={{0,6},{1,7},{2,4},{3,5},{4,2},{5,3},{6,0},{7,1},{8,14},{9,15},{10,... | collective-permute-start | bytes 92168 | tf_op jit(solution)/shard_map/ppermute | solution.py:576
  (37 other events, 238.7 us)
